TPU v7x, 32 devices: a whole 2x2x4 slice. The times are simulated.
32 devices in a mesh: row: 8 (over y, x, core), pair: 4 (over z).
Axes of the slice: x: 2, y: 2, z: 4, core: 2. Of those that a mesh axis runs over, the one named last changes fastest.
Arguments:
- basis: float32 [2048, 1024], P('row', 'pair'), may hold values from -48 to 48
Outputs:
- rotated: float32 [2048, 1024], P('row', 'pair')
All inputs are finite; a program needn't handle non-finite values.
Results may differ from a plain program's by a relative error of at most 0.0003.
Values sent between devices are 32-bit elements; how exact they have to be, the bound alone decides.
No kernel may reach another device: no remote copies, remote signals or barrier semaphores. Data moves between devices by JAX's collectives and lax.ppermute only.
A program may use at most 64 MiB of HBM per device.

v0:
```python
import jax
import jax.numpy as jnp
import numpy as np
from jax import lax
from jax.sharding import PartitionSpec as P

ROUNDS = 4
JSTEPS = 6


def from_behind(x, axis, by):
    size = lax.axis_size(axis)
    pairs = [(i, i + by) for i in range(size) if 0 <= i + by < size]
    return lax.ppermute(x, axis, pairs)


def tournament_order(pair_count):
    ordering = np.zeros(2 * pair_count, dtype=np.int64)
    ordering[0] = 0
    ordering[2] = 1
    for slot in range(2, pair_count):
        ordering[2 * slot] = 2 * (slot - 1)
    for slot in range(pair_count - 1):
        ordering[2 * slot + 1] = 2 * (slot + 1) + 1
    ordering[2 * pair_count - 1] = 2 * (pair_count - 1)
    return ordering


def jacobi_angle(diag_even, diag_odd, coupling):
    spread = diag_even - diag_odd
    radius = jnp.sqrt(spread * spread + 4.0 * coupling * coupling)
    widened = radius + jnp.abs(spread)
    larger = jnp.sqrt(widened / (2.0 * radius))
    smaller = coupling / (radius * larger)
    forward = spread >= 0.0
    cosine = jnp.where(forward, larger, jnp.abs(smaller))
    sine_part = jnp.where(forward, smaller, jnp.sign(coupling) * larger)
    return (cosine, sine_part)


def jacobi_turns(gram_mat):
    hp = lax.Precision.HIGHEST
    width = gram_mat.shape[0]
    halves = width // 2
    ordering = tournament_order(halves)
    source = jnp.asarray(ordering.astype(np.int32))[None, :]
    even_source = source % 2 == 0
    row_ids = lax.broadcasted_iota(jnp.int32, (width, width), 0)
    on_diag = row_ids == source
    below = jnp.logical_and(even_source, row_ids == source + 1)
    above = jnp.logical_and(jnp.logical_not(even_source), row_ids == source - 1)
    tracked = np.arange(width)
    rotation = jnp.eye(width, dtype=gram_mat.dtype)
    for step_index in range(JSTEPS):
        diagonal_all = jnp.diagonal(gram_mat)
        diag_even = diagonal_all[0::2]
        diag_odd = diagonal_all[1::2]
        coupling = jnp.diagonal(gram_mat, offset=1)[0::2]
        cosine, sine_part = jacobi_angle(diag_even, diag_odd, coupling)
        cosine_cols = jnp.repeat(cosine, 2)[ordering][None, :]
        sine_cols = jnp.repeat(sine_part, 2)[ordering][None, :]
        turner = jnp.where(
            on_diag, cosine_cols, jnp.where(below, sine_cols, jnp.where(above, -sine_cols, 0.0))
        )
        half_turned = jnp.dot(gram_mat, turner, precision=hp)
        gram_mat = lax.dot_general(turner, half_turned, (((0,), (0,)), ((), ())), precision=hp)
        rotation = jnp.dot(rotation, turner, precision=hp)
        tracked = tracked[ordering]
    inverse = np.argsort(tracked)
    return (rotation[:, inverse], gram_mat[inverse][:, inverse])


def inner_products(left_rows, right_rows):
    return lax.dot_general(
        left_rows, right_rows, (((0,), (0,)), ((), ())), precision=lax.Precision.HIGHEST
    )


def per_device(basis):
    block_cols = basis.shape[1] // 2
    pair_index = lax.axis_index("pair")
    pair_total = lax.axis_size("pair")
    is_first = pair_index == 0
    is_last = pair_index == pair_total - 1
    top_block = basis[:, :block_cols]
    bottom = basis[:, block_cols:]
    for round_index in range(ROUNDS):
        slab_rows = jnp.concatenate((top_block, bottom), axis=1)
        gram_mat = lax.psum(inner_products(slab_rows, slab_rows), "row")
        rotation, turned = jacobi_turns(gram_mat)
        slab_rows = jnp.dot(slab_rows, rotation, precision=lax.Precision.HIGHEST)
        top_block = slab_rows[:, :block_cols]
        bottom = slab_rows[:, block_cols:]
        leading = jnp.where(is_first, bottom, top_block)
        incoming = from_behind(leading, "pair", 1)
        following = from_behind(bottom, "pair", -1)
        new_top = jnp.where(is_first, top_block, incoming)
        new_bottom = jnp.where(is_last, top_block, following)
        top_block, bottom = (new_top, new_bottom)
    return jnp.concatenate((top_block, bottom), axis=1)


def solution(mesh):
    return jax.shard_map(
        per_device,
        mesh=mesh,
        in_specs=(P("row", "pair"),),
        out_specs=P("row", "pair"),
        check_vma=False,
    )
```

profile of v0, /device:TPU:0, one launch (start us, length us, event | category | flops | bytes accessed | tf_op | source)
XLA Modules:
  0.0 584.2 jit_solution(17007935162492651728)
XLA Ops:
  10.2 56.5 %all-reduce.5.cloned.1.call-done = f32[256,256]{1,0:T(8,128)} async-done(((f32[256,256]{1,0:T(8,128)}), f32[256,256]{1,0:T(8,128)}) %all-reduce.5.cloned.1.call-update) | async-done | bytes 262160 | tf_op jit(solution)/shard_map/psum | solution.py:89
  69.8 3.6 gather_fusion.76
  82.0 3.6 gather_fusion.77
  94.2 3.6 gather_fusion.78
  106.4 3.9 gather_fusion.79
  118.9 3.6 gather_fusion.80
  130.6 3.6 gather_fusion.81
  149.6 4.4 collective-permute-done.1
  155.2 52.1 %all-reduce.7.cloned.1.call-done = f32[256,256]{1,0:T(8,128)} async-done(((f32[256,256]{1,0:T(8,128)}), f32[256,256]{1,0:T(8,128)}) %all-reduce.7.cloned.1.call-update) | async-done | bytes 262160 | tf_op jit(solution)/shard_map/psum | solution.py:89
  210.4 3.7 gather_fusion.82
  222.8 3.6 gather_fusion.83
  234.9 3.6 gather_fusion.84
  247.1 4.0 gather_fusion.85
  259.6 3.6 gather_fusion.86
  271.4 3.6 gather_fusion.87
  290.4 4.4 collective-permute-done.3
  296.0 52.1 %all-reduce.9.cloned.1.call-done = f32[256,256]{1,0:T(8,128)} async-done(((f32[256,256]{1,0:T(8,128)}), f32[256,256]{1,0:T(8,128)}) %all-reduce.9.cloned.1.call-update) | async-done | bytes 262160 | tf_op jit(solution)/shard_map/psum | solution.py:89
  351.2 3.7 gather_fusion.88
  363.5 3.6 gather_fusion.89
  375.7 3.6 gather_fusion.90
  387.8 4.0 gather_fusion.91
  400.4 3.6 gather_fusion.92
  412.1 3.6 gather_fusion.93
  431.2 4.4 collective-permute-done.5
  436.7 52.1 %all-reduce.11.cloned.1.call-done = f32[256,256]{1,0:T(8,128)} async-done(((f32[256,256]{1,0:T(8,128)}), f32[256,256]{1,0:T(8,128)}) %all-reduce.11.cloned.1.call-update) | async-done | bytes 262160 | tf_op jit(solution)/shard_map/psum | solution.py:89
  491.9 3.7 gather_fusion.94
  504.3 3.6 gather_fusion.95
  516.4 3.6 gather_fusion.96
  528.6 3.8 gather_fusion.97
  541.0 3.6 gather_fusion.98
  552.7 3.6 gather_fusion.99
  572.0 4.4 collective-permute-done.7
  (444 shorter events, 250.8 us)
Async XLA Ops:
  6.5 1.0 copy-start
  6.5 60.1 %all-reduce.5.cloned.1.call-start = ((), (), s32[]{:S(2)}) async-start(), calls=%async_computation | async-start | bytes 524288 | tf_op jit(solution)/shard_map/psum | solution.py:89
  8.8 0.7 copy-start.5
  8.8 198.5 %all-reduce.7.cloned.1.call-start = ((), (), s32[]{:S(2)}) async-start(), calls=%async_computation.1 | async-start | bytes 524288 | tf_op jit(solution)/shard_map/psum | solution.py:89
  9.5 0.7 copy-start.6
  66.7 3.1 copy-start.1
  76.0 2.0 copy-start.7
  76.0 2.0 copy-start.8
  76.1 2.0 copy-start.9
  76.1 2.0 copy-start.10
  143.7 5.9 %collective-permute-start = (f32[256,128]{0,1:T(8,128)S(1)}, f32[256,128]{0,1:T(8,128)S(1)}, u32[]{:S(2)}, u32[]{:S(2)}) collective-permute-start(f32[256,128]{0,1:T(8,128)S(1)} %get-tuple-element.116), channel_id=1, source_target_pairs={{0,1},{1,2},{2,3},{4,5},{5,6},{6,7},{8,9},{9,10},{10,11},{12,13},{... | collective-permute-start | bytes 393224 | tf_op jit(solution)/shard_map/ppermute | solution.py:14
  147.1 6.9 %collective-permute-start.1 = (f32[256,128]{0,1:T(8,128)S(1)}, f32[256,128]{0,1:T(8,128)S(1)}, u32[]{:S(2)}, u32[]{:S(2)}) collective-permute-start(f32[256,128]{0,1:T(8,128)S(1)} %get-tuple-element.117), channel_id=1, source_target_pairs={{1,0},{2,1},{3,2},{5,4},{6,5},{7,6},{9,8},{10,9},{11,10},{13,12},{... | collective-permute-start | bytes 393224 | tf_op jit(solution)/shard_map/ppermute | solution.py:14
  155.2 192.9 %all-reduce.9.cloned.1.call-start = ((), (), s32[]{:S(2)}) async-start(), calls=%async_computation.2 | async-start | bytes 524288 | tf_op jit(solution)/shard_map/psum | solution.py:89
  207.3 3.1 copy-start.2
  284.5 5.9 %collective-permute-start.2 = (f32[256,128]{0,1:T(8,128)S(1)}, f32[256,128]{0,1:T(8,128)S(1)}, u32[]{:S(2)}, u32[]{:S(2)}) collective-permute-start(f32[256,128]{0,1:T(8,128)S(1)} %get-tuple-element.112), channel_id=1, source_target_pairs={{0,1},{1,2},{2,3},{4,5},{5,6},{6,7},{8,9},{9,10},{10,11},{12,13},{... | collective-permute-start | bytes 393224 | tf_op jit(solution)/shard_map/ppermute | solution.py:14
  287.9 6.9 %collective-permute-start.3 = (f32[256,128]{0,1:T(8,128)S(1)}, f32[256,128]{0,1:T(8,128)S(1)}, u32[]{:S(2)}, u32[]{:S(2)}) collective-permute-start(f32[256,128]{0,1:T(8,128)S(1)} %get-tuple-element.113), channel_id=1, source_target_pairs={{1,0},{2,1},{3,2},{5,4},{6,5},{7,6},{9,8},{10,9},{11,10},{13,12},{... | collective-permute-start | bytes 393224 | tf_op jit(solution)/shard_map/ppermute | solution.py:14
  295.9 192.9 %all-reduce.11.cloned.1.call-start = ((), (), s32[]{:S(2)}) async-start(), calls=%async_computation.3 | async-start | bytes 524288 | tf_op jit(solution)/shard_map/psum | solution.py:89
  348.1 3.1 copy-start.3
  425.3 5.9 %collective-permute-start.4 = (f32[256,128]{0,1:T(8,128)S(1)}, f32[256,128]{0,1:T(8,128)S(1)}, u32[]{:S(2)}, u32[]{:S(2)}) collective-permute-start(f32[256,128]{0,1:T(8,128)S(1)} %get-tuple-element.108), channel_id=1, source_target_pairs={{0,1},{1,2},{2,3},{4,5},{5,6},{6,7},{8,9},{9,10},{10,11},{12,13},{... | collective-permute-start | bytes 393224 | tf_op jit(solution)/shard_map/ppermute | solution.py:14
  428.7 6.9 %collective-permute-start.5 = (f32[256,128]{0,1:T(8,128)S(1)}, f32[256,128]{0,1:T(8,128)S(1)}, u32[]{:S(2)}, u32[]{:S(2)}) collective-permute-start(f32[256,128]{0,1:T(8,128)S(1)} %get-tuple-element.109), channel_id=1, source_target_pairs={{1,0},{2,1},{3,2},{5,4},{6,5},{7,6},{9,8},{10,9},{11,10},{13,12},{... | collective-permute-start | bytes 393224 | tf_op jit(solution)/shard_map/ppermute | solution.py:14
  488.8 3.1 copy-start.4
  566.1 5.9 %collective-permute-start.6 = (f32[256,128]{0,1:T(8,128)S(1)}, f32[256,128]{0,1:T(8,128)S(1)}, u32[]{:S(2)}, u32[]{:S(2)}) collective-permute-start(f32[256,128]{0,1:T(8,128)S(1)} %get-tuple-element.104), channel_id=1, source_target_pairs={{0,1},{1,2},{2,3},{4,5},{5,6},{6,7},{8,9},{9,10},{10,11},{12,13},{... | collective-permute-start | bytes 393224 | tf_op jit(solution)/shard_map/ppermute | solution.py:14
  569.5 6.9 %collective-permute-start.7 = (f32[256,128]{0,1:T(8,128)S(1)}, f32[256,128]{0,1:T(8,128)S(1)}, u32[]{:S(2)}, u32[]{:S(2)}) collective-permute-start(f32[256,128]{0,1:T(8,128)S(1)} %get-tuple-element.105), channel_id=1, source_target_pairs={{1,0},{2,1},{3,2},{5,4},{6,5},{7,6},{9,8},{10,9},{11,10},{13,12},{... | collective-permute-start | bytes 393224 | tf_op jit(solution)/shard_map/ppermute | solution.py:14
Sparse Core Ops, SparseCore 0:
  10.4 56.2 all-reduce.4
  155.3 51.9 all-reduce.6
  296.1 51.9 all-reduce.8
  436.8 51.9 all-reduce.10
where the time goes:
time: 594 us; the launch traced here: 584 us
  local copies, waits for them, and re-layouts  272 us (46%)
  waiting for transfers between devices  235 us (40%)
  matrix products  41 us (7%)
  starting transfers between devices  18.9 us (3%)
  between operations  15.8 us (3%)
    psum x4, waiting for transfers between devices, per_device(): gram_mat = lax.psum(inner_products(slab_rows, slab_rows), 'row')  213 us
    gather x24, local copies, waits for them, and re-layouts, jacobi_turns(): coupling = jnp.diagonal(gram_mat, offset=1)[0::2]  87.3 us
    gather x24, local copies, waits for them, and re-layouts, jacobi_turns(): diagonal_all = jnp.diagonal(gram_mat)  57.4 us
    gather x24, local copies, waits for them, and re-layouts, jacobi_turns(): cosine_cols = jnp.repeat(cosine, 2)[ordering][None, :]  46.9 us
    gather x24, local copies, waits for them, and re-layouts, jacobi_turns(): sine_cols = jnp.repeat(sine_part, 2)[ordering][None, :]  46.7 us
    ppermute x8, waiting for transfers between devices, from_behind(): return lax.ppermute(x, axis, pairs)  22.2 us
    ppermute x8, starting transfers between devices, from_behind(): return lax.ppermute(x, axis, pairs)  18.8 us
    dot_general x20, matrix products, jacobi_turns(): lax.dot_general(turner, half_turned, (((0,), (0,)), ((), ())), precision=hp)  13 us
  transfers between devices with their start and end apart: 12, of which 12 were waited for; matrix products, arithmetic and copies ran while one was open for 0% of the time, Pallas kernels for 0%

commit v1 on v0

v1 whole, which is shorter than its diff:
```python
import functools

import jax
import jax.numpy as jnp
import numpy as np
from jax import lax
from jax.experimental import pallas as pl
from jax.experimental.pallas import tpu as pltpu
from jax.sharding import PartitionSpec as P

ROUNDS = 4
JSTEPS = 6
REACH = 2 * (JSTEPS - 1) + 1
DIAGS = 16


def tournament_order(pair_count):
    ordering = np.zeros(2 * pair_count, dtype=np.int64)
    ordering[0] = 0
    ordering[2] = 1
    for slot in range(2, pair_count):
        ordering[2 * slot] = 2 * (slot - 1)
    for slot in range(pair_count - 1):
        ordering[2 * slot + 1] = 2 * (slot + 1) + 1
    ordering[2 * pair_count - 1] = 2 * (pair_count - 1)
    return ordering


def host_of(pair, pair_total, round_index):
    if round_index % 2 == 0 or pair == 0:
        return pair
    return min(pair + 1, pair_total - 1) if pair % 2 else pair - 1


def moves(pair_total):
    ordering = tournament_order(pair_total)
    plans = []
    for round_index in range(ROUNDS):
        sends, sends_first, gets_first = [], set(), set()
        for pair in range(pair_total):
            target = host_of(pair, pair_total, round_index + 1)
            for place in (0, 1):
                old = int(ordering[2 * pair + place])
                source = host_of(old // 2, pair_total, round_index)
                if source == target:
                    continue
                sends.append((source, target))
                if old % 2 == 0:
                    sends_first.add(source)
                if place == 0:
                    gets_first.add(target)
        assert len({s for s, _ in sends}) == len(sends) == len({t for _, t in sends})
        plans.append((sends, sends_first, gets_first))
    return plans


def among(members):
    here = lax.axis_index("pair")
    return functools.reduce(
        jnp.logical_or, [here == member for member in sorted(members)], here < 0
    )


def left(x, by):
    width = x.shape[1]
    return pltpu.roll(x, (width - by) % width, 1) if by % width else x


def right(x, by):
    width = x.shape[1]
    return pltpu.roll(x, by % width, 1) if by % width else x


def down(x, by):
    return pltpu.roll(x, by % x.shape[0], 0)


def lanes_of(x):
    return lax.broadcasted_iota(jnp.int32, x.shape, 1)


def split_pair(first, second):
    half = first.shape[1] // 2
    low = lanes_of(first) < half
    even = jnp.where(low, first, right(second, half))
    odd = jnp.where(low, right(first, half), second)
    return even, odd


def join_pair(even, odd):
    half = even.shape[1] // 2
    low = lanes_of(even) < half
    return jnp.where(low, even, right(odd, half)), jnp.where(low, right(even, half), odd)


def separator(width, back):
    rows = lax.broadcasted_iota(jnp.int32, (width, width), 0)
    cols = lax.broadcasted_iota(jnp.int32, (width, width), 1)
    if back:
        rows, cols = cols, rows
    half = width // 2
    source = jnp.where(cols < half, 2 * cols, 2 * (cols - half) + 1)
    return jnp.where(rows == source, 1.0, 0.0).astype(jnp.float32)


def reorder(block, table):
    return jnp.dot(
        block, table, precision=lax.Precision.HIGHEST, preferred_element_type=jnp.float32
    )


def store_bands(even, odd, band_ref):
    rows = even.shape[0]
    sums = [[None] * 4 for _ in range(REACH)]
    for start in range(0, rows, 8):
        e, o = even[start : start + 8], odd[start : start + 8]
        for d in range(REACH):
            e_near, o_near = right(e, d), right(o, d)
            parts = (e_near * e, e_near * o, o_near * e, o_near * o)
            for q in range(4):
                if d == 0 and q == 2:
                    continue
                sums[d][q] = parts[q] if start == 0 else sums[d][q] + parts[q]
    sums[0][2] = sums[0][1]
    for q in range(4):
        for d in range(REACH):
            band_ref[q, d : d + 1, :] = jnp.sum(sums[d][q], axis=0, keepdims=True)
        band_ref[q, REACH:, :] = jnp.zeros((DIAGS - REACH, even.shape[1]), jnp.float32)


def open_kernel(basis_ref, even_ref, odd_ref, band_ref):
    width = basis_ref.shape[1] // 2
    table = separator(width, False)
    first = reorder(basis_ref[:, :width], table)
    second = reorder(basis_ref[:, width:], table)
    even, odd = split_pair(first, second)
    even_ref[...] = even
    odd_ref[...] = odd
    store_bands(even, odd, band_ref)


def pair_kernel(gets_first, kept_ref, came_ref, even_ref, odd_ref, band_ref):
    flag = among(gets_first)
    kept, came = kept_ref[...], came_ref[...]
    even, odd = split_pair(jnp.where(flag, came, kept), jnp.where(flag, kept, came))
    even_ref[...] = even
    odd_ref[...] = odd
    store_bands(even, odd, band_ref)


def jacobi_angle(diag_even, diag_odd, coupling):
    spread = diag_even - diag_odd
    radius = jnp.sqrt(spread * spread + 4.0 * coupling * coupling)
    widened = radius + jnp.abs(spread)
    larger = jnp.sqrt(widened / (2.0 * radius))
    smaller = coupling / (radius * larger)
    forward = spread >= 0.0
    sign = jnp.where(coupling > 0.0, 1.0, jnp.where(coupling < 0.0, -1.0, 0.0))
    cosine = jnp.where(forward, larger, jnp.abs(smaller))
    sine_part = jnp.where(forward, smaller, sign * larger)
    return cosine, sine_part


def turn_bands(ee, eo, oe, oo, cosine, sine):
    cl, sl = jnp.broadcast_to(cosine, ee.shape), jnp.broadcast_to(sine, ee.shape)
    ck = pltpu.roll(cl, 0, 1, stride=1, stride_axis=0)
    sk = pltpu.roll(sl, 0, 1, stride=1, stride_axis=0)
    ee, oe = ck * ee + sk * oe, ck * oe - sk * ee
    eo, oo = ck * eo + sk * oo, ck * oo - sk * eo
    ee, eo = cl * ee + sl * eo, cl * eo - sl * ee
    oe, oo = cl * oe + sl * oo, cl * oo - sl * oe
    return ee, eo, oe, oo


def move_bands(ee, eo, oe, oo):
    lane = lanes_of(ee)
    diag = lax.broadcasted_iota(jnp.int32, ee.shape, 0)
    last = lane == ee.shape[1] - 1
    first, second = lane == diag, lane == diag + 1
    on, next_on = diag == 0, diag == 1

    ee_new = right(ee, 1)
    ee_new = jnp.where(second, right(jnp.where(on, oo, oe), 1), ee_new)
    near = jnp.where(next_on, down(eo, 1), down(ee, 1))
    ee_new = jnp.where(first, jnp.where(on, ee, right(near, 1)), ee_new)

    eo_new = left(down(eo, -2), 1)
    eo_new = jnp.where(second, left(down(oo, -2), 1), eo_new)
    eo_new = jnp.where(first, left(down(eo, -1), 1), eo_new)
    eo_new = jnp.where(last, down(ee, -1), eo_new)

    oo_new = jnp.where(last, jnp.where(on, ee, down(oe, 1)), left(oo, 1))

    oe_new = right(down(oe, 2), 1)
    oe_new = jnp.where(next_on, jnp.where(first, oo, eo), oe_new)
    oe_new = jnp.where(on, eo_new, oe_new)
    return ee_new, eo_new, oe_new, oo_new


def move_columns(even, odd):
    lane = lanes_of(even)
    first, last = lane == 0, lane == even.shape[1] - 1
    even_new = jnp.where(first, even, right(jnp.where(first, odd, even), 1))
    odd_new = jnp.where(last, even, left(odd, 1))
    return even_new, odd_new


def move_columns_back(even, odd):
    lane = lanes_of(even)
    first, last = lane == 0, lane == even.shape[1] - 1
    back = left(even, 1)
    even_old = jnp.where(first, even, jnp.where(last, odd, back))
    odd_old = jnp.where(first, back, right(odd, 1))
    return even_old, odd_old


def turn_kernel(sends_first, is_last, even_ref, odd_ref, *refs):
    *band_refs, kept_ref, sent_ref = refs
    bands = [ref[...] for ref in band_refs]
    while len(bands) > 1:
        bands = [bands[i] + bands[i + 1] for i in range(0, len(bands), 2)]
    ee, eo, oe, oo = (bands[0][q] for q in range(4))
    even, odd = even_ref[...], odd_ref[...]
    for step in range(JSTEPS):
        cosine, sine = jacobi_angle(ee[0:1], oo[0:1], eo[0:1])
        even, odd = cosine * even + sine * odd, cosine * odd - sine * even
        if step < JSTEPS - 1:
            ee, eo, oe, oo = move_bands(*turn_bands(ee, eo, oe, oo, cosine, sine))
            even, odd = move_columns(even, odd)
    for step in range(JSTEPS - 1):
        even, odd = move_columns_back(even, odd)
    first, second = join_pair(even, odd)
    if is_last:
        table = separator(first.shape[1], True)
        first, second = reorder(first, table), reorder(second, table)
    flag = among(sends_first)
    kept_ref[...] = jnp.where(flag, second, first)
    sent_ref[...] = jnp.where(flag, first, second)


def exchange_groups(x, axis):
    size = lax.axis_size(axis)
    bits = [1 << b for b in range(size.bit_length() - 1)]
    groups = [bits[:1]] + [bits[i : i + 2] for i in range(1, len(bits), 2)]
    arrays = [x]
    for group in groups:
        while len(arrays) > 1:
            arrays = [arrays[i] + arrays[i + 1] for i in range(0, len(arrays), 2)]
        x = arrays[0]
        masks = [group[0]] if len(group) == 1 else [group[0], group[1], group[0] | group[1]]
        arrays = [x] + [
            lax.ppermute(x, axis, [(i, i ^ mask) for i in range(size)]) for mask in masks
        ]
    return arrays


def call(kernel, shapes, *args):
    out = [jax.ShapeDtypeStruct(shape, jnp.float32) for shape in shapes]
    return pl.pallas_call(
        kernel,
        out_shape=out,
        compiler_params=pltpu.CompilerParams(vmem_limit_bytes=32 * 1024 * 1024),
    )(*args)


def per_device(basis):
    rows, cols = basis.shape
    width = cols // 2
    column = (rows, width)
    band = (4, DIAGS, width)
    plans = moves(lax.axis_size("pair"))
    even, odd, partial = call(open_kernel, (column, column, band), basis)
    for round_index, (sends, sends_first, gets_first) in enumerate(plans):
        is_last = round_index == ROUNDS - 1
        arrays = exchange_groups(partial, "row")
        kept, sent = call(
            functools.partial(turn_kernel, sends_first, is_last),
            (column, column),
            even,
            odd,
            *arrays,
        )
        came = lax.ppermute(sent, "pair", sends)
        if not is_last:
            even, odd, partial = call(
                functools.partial(pair_kernel, gets_first), (column, column, band), kept, came
            )
    flag = among(gets_first)
    first = jnp.where(flag, came, kept)
    second = jnp.where(flag, kept, came)
    return jnp.concatenate((first, second), axis=1)


def solution(mesh):
    return jax.shard_map(
        per_device,
        mesh=mesh,
        in_specs=(P("row", "pair"),),
        out_specs=P("row", "pair"),
        check_vma=False,
    )
```

time: 594 us -> 69.4 us (0.12); the launches traced: 584 us -> 69.3 us
  local copies, waits for them, and re-layouts: 272 us -> 0.95 us
  waiting for transfers between devices: 235 us -> 31.7 us
  matrix products: 41 us -> 0 us
  between operations: 15.8 us -> 0.11 us
  Pallas kernels: 0 us -> 11.2 us
    gather x100 -> x0, local copies, waits for them, and re-layouts: 242 us -> none  [the longest x24 87.3 us: jacobi_turns(): coupling = jnp.diagonal(gram_mat, offset=1)[0::2]]
    psum x4 -> x0, waiting for transfers between devices: 213 us -> none  [per_device(): gram_mat = lax.psum(inner_products(slab_rows, slab_rows), 'row')]
    dot_general x72 -> x0, matrix products: 41 us -> none  [the longest x20 13 us: jacobi_turns(): lax.dot_general(turner, half_turned, (((0,), (0,)), ((), ())), precision=hp)]
    slice x72 -> x0, local copies, waits for them, and re-layouts: 16 us -> none  [the longest x24 5.41 us: jacobi_turns(): diag_odd = diagonal_all[1::2]]
    pallas_call x0 -> x8, Pallas kernels: none -> 11.2 us  [call(): pl.pallas_call(kernel, out_shape=out, compiler_params=pltpu.CompilerParam...]
    ppermute x8 -> x20, waiting for transfers between devices: 22.2 us -> 31.7 us  [the longest x16 18.3 us: exchange_groups(): lax.ppermute(x, axis, [(i, i ^ mask) for i in range(size)])]
    reshape x48 -> x0, local copies, waits for them, and re-layouts: 7.33 us -> none  [the longest x24 3.75 us: jacobi_turns(): sine_cols = jnp.repeat(sine_part, 2)[ordering][None, :]]
    ppermute x8 -> x20, starting transfers between devices: 18.8 us -> 24.6 us  [the longest x16 15.6 us: exchange_groups(): lax.ppermute(x, axis, [(i, i ^ mask) for i in range(size)])]
  transfers between devices with their start and end apart: 12 -> 20, of which waited for: 12 -> 20; matrix products, arithmetic and copies ran while one was open for 0% -> 0% of each run, Pallas kernels for 0% -> 0%
where the time goes in v1:
time: 69.4 us; the launch traced here: 69.3 us
  waiting for transfers between devices  31.7 us (46%)
  starting transfers between devices  24.6 us (35%)
  Pallas kernels  11.2 us (16%)
  local copies, waits for them, and re-layouts  0.95 us (1%)
  other arithmetic  0.76 us (1%)
    ppermute x16, waiting for transfers between devices, exchange_groups(): lax.ppermute(x, axis, [(i, i ^ mask) for i in range(size)])  18.3 us
    ppermute x16, starting transfers between devices, exchange_groups(): lax.ppermute(x, axis, [(i, i ^ mask) for i in range(size)])  15.6 us
    ppermute x4, waiting for transfers between devices, per_device(): came = lax.ppermute(sent, 'pair', sends)  13.4 us
    pallas_call x8, Pallas kernels, call(): pl.pallas_call(kernel, out_shape=out, compiler_params=pltpu.CompilerParam...  11.2 us
    ppermute x4, starting transfers between devices, per_device(): came = lax.ppermute(sent, 'pair', sends)  9.06 us
  transfers between devices with their start and end apart: 20, of which 20 were waited for; matrix products, arithmetic and copies ran while one was open for 0% of the time, Pallas kernels for 0%

profile of v1, /device:TPU:0, one launch (start us, length us, event | category | flops | bytes accessed | tf_op | source)
XLA Modules:
  0.0 69.3 jit_solution(3713587948845953091)
XLA Ops:
  0.0 0.9 %copy-done = f32[256,256]{1,0:T(8,128)S(1)} copy-done((f32[256,256]{1,0:T(8,128)S(1)}, f32[256,256]{1,0:T(8,128)}, u32[]{:S(2)}) %copy-start) | copy-done | bytes 262168
  1.0 1.2 %shard_map.17 = (f32[256,128]{1,0:T(8,128)S(1)}, f32[256,128]{1,0:T(8,128)S(1)}, f32[4,16,128]{2,1,0:T(8,128)S(1)}) custom-call(f32[256,256]{1,0:T(8,128)S(1)} %copy-done), custom_call_target="tpu_custom_call" | custom-call | tf_op jit(solution)/shard_map/pallas_call | solution.py:259
  3.5 2.8 %collective-permute-start.1 = (f32[4,16,128]{2,1,0:T(8,128)S(1)}, f32[4,16,128]{2,1,0:T(8,128)S(1)}, u32[]{:S(2)}, u32[]{:S(2)}) collective-permute-start(f32[4,16,128]{2,1,0:T(8,128)S(1)} %add.12.refs_0_), channel_id=1, source_target_pairs={{0,8},{4,12},{8,0},{12,4},{16,24},{20,28},{24,16},{28,20},{1,9},{5... | collective-permute-start | bytes 98312 | tf_op jit(solution)/shard_map/ppermute | solution.py:252
  6.4 1.5 %collective-permute-start.2 = (f32[4,16,128]{2,1,0:T(8,128)S(1)}, f32[4,16,128]{2,1,0:T(8,128)S(1)}, u32[]{:S(2)}, u32[]{:S(2)}) collective-permute-start(f32[4,16,128]{2,1,0:T(8,128)S(1)} %add.12.refs_0_), channel_id=1, source_target_pairs={{0,16},{4,20},{8,24},{12,28},{16,0},{20,4},{24,8},{28,12},{1,17},{... | collective-permute-start | bytes 98312 | tf_op jit(solution)/shard_map/ppermute | solution.py:252
  8.2 2.0 %collective-permute-done.2.refs_2_ = f32[4,16,128]{2,1,0:T(8,128)S(1)} collective-permute-done((f32[4,16,128]{2,1,0:T(8,128)S(1)}, f32[4,16,128]{2,1,0:T(8,128)S(1)}, u32[]{:S(2)}, u32[]{:S(2)}) %collective-permute-start.2) | collective-permute-done | bytes 32800 | tf_op jit(solution)/shard_map/ppermute | solution.py:252
  10.3 2.4 %collective-permute-done.3.refs_3_ = f32[4,16,128]{2,1,0:T(8,128)S(1)} collective-permute-done((f32[4,16,128]{2,1,0:T(8,128)S(1)}, f32[4,16,128]{2,1,0:T(8,128)S(1)}, u32[]{:S(2)}, u32[]{:S(2)}) %collective-permute-start.3) | collective-permute-done | bytes 32800 | tf_op jit(solution)/shard_map/ppermute | solution.py:252
  12.7 1.7 %shard_map.18 = (f32[256,128]{1,0:T(8,128)S(1)}, f32[256,128]{1,0:T(8,128)S(1)}) custom-call(f32[256,128]{1,0:T(8,128)S(1)} %get-tuple-element.25.even_ref, f32[256,128]{1,0:T(8,128)S(1)} %get-tuple-element.26.odd_ref, f32[4,16,128]{2,1,0:T(8,128)S(1)} %add.12.refs_0_, f32[4,16,128]{2,1,0:T(8,128)S(1)} %collective-permute-done.1.refs_1_, ...), custom_call_target="tpu_custom_call" | custom-call | tf_op jit(solution)/shard_map/pallas_call | solution.py:259
  14.4 2.6 %collective-permute-start.4 = (f32[256,128]{1,0:T(8,128)S(1)}, f32[256,128]{1,0:T(8,128)S(1)}, u32[]{:S(2)}, u32[]{:S(2)}) collective-permute-start(f32[256,128]{1,0:T(8,128)S(1)} %get-tuple-element.29), channel_id=1, source_target_pairs={{1,0},{0,2},{3,1},{2,3},{5,4},{4,6},{7,5},{6,7},{9,8},{8,10},{11,9... | collective-permute-start | bytes 393224 | tf_op jit(solution)/shard_map/ppermute | solution.py:283
  17.1 2.5 %collective-permute-done.4.came_ref = f32[256,128]{1,0:T(8,128)S(1)} collective-permute-done((f32[256,128]{1,0:T(8,128)S(1)}, f32[256,128]{1,0:T(8,128)S(1)}, u32[]{:S(2)}, u32[]{:S(2)}) %collective-permute-start.4) | collective-permute-done | bytes 131104 | tf_op jit(solution)/shard_map/ppermute | solution.py:283
  20.6 1.2 %collective-permute-done.5 = f32[4,16,128]{2,1,0:T(8,128)S(1)} collective-permute-done((f32[4,16,128]{2,1,0:T(8,128)S(1)}, f32[4,16,128]{2,1,0:T(8,128)S(1)}, u32[]{:S(2)}, u32[]{:S(2)}) %collective-permute-start.5) | collective-permute-done | bytes 32800 | tf_op jit(solution)/shard_map/ppermute | solution.py:252
  22.8 2.4 %collective-permute-start.8 = (f32[4,16,128]{2,1,0:T(8,128)S(1)}, f32[4,16,128]{2,1,0:T(8,128)S(1)}, u32[]{:S(2)}, u32[]{:S(2)}) collective-permute-start(f32[4,16,128]{2,1,0:T(8,128)S(1)} %add.13.refs_0_), channel_id=1, source_target_pairs={{0,24},{4,28},{8,16},{12,20},{16,8},{20,12},{24,0},{28,4},{1,25},{... | collective-permute-start | bytes 98312 | tf_op jit(solution)/shard_map/ppermute | solution.py:252
  25.7 0.9 %collective-permute-done.7.refs_2_ = f32[4,16,128]{2,1,0:T(8,128)S(1)} collective-permute-done((f32[4,16,128]{2,1,0:T(8,128)S(1)}, f32[4,16,128]{2,1,0:T(8,128)S(1)}, u32[]{:S(2)}, u32[]{:S(2)}) %collective-permute-start.7) | collective-permute-done | bytes 32800 | tf_op jit(solution)/shard_map/ppermute | solution.py:252
  26.6 1.1 %collective-permute-done.8.refs_3_ = f32[4,16,128]{2,1,0:T(8,128)S(1)} collective-permute-done((f32[4,16,128]{2,1,0:T(8,128)S(1)}, f32[4,16,128]{2,1,0:T(8,128)S(1)}, u32[]{:S(2)}, u32[]{:S(2)}) %collective-permute-start.8) | collective-permute-done | bytes 32800 | tf_op jit(solution)/shard_map/ppermute | solution.py:252
  27.6 1.7 %shard_map.20 = (f32[256,128]{1,0:T(8,128)S(1)}, f32[256,128]{1,0:T(8,128)S(1)}) custom-call(f32[256,128]{1,0:T(8,128)S(1)} %get-tuple-element.30.even_ref, f32[256,128]{1,0:T(8,128)S(1)} %get-tuple-element.31.odd_ref, f32[4,16,128]{2,1,0:T(8,128)S(1)} %add.13.refs_0_, f32[4,16,128]{2,1,0:T(8,128)S(1)} %collective-permute-done.6.refs_1_, ...), custom_call_target="tpu_custom_call" | custom-call | tf_op jit(solution)/shard_map/pallas_call | solution.py:259
  29.4 2.4 %collective-permute-start.9 = (f32[256,128]{1,0:T(8,128)S(1)}, f32[256,128]{1,0:T(8,128)S(1)}, u32[]{:S(2)}, u32[]{:S(2)}) collective-permute-start(f32[256,128]{1,0:T(8,128)S(1)} %get-tuple-element.34), channel_id=1, source_target_pairs={{2,0},{0,1},{3,2},{1,3},{6,4},{4,5},{7,6},{5,7},{10,8},{8,9},{11,1... | collective-permute-start | bytes 393224 | tf_op jit(solution)/shard_map/ppermute | solution.py:283
  31.8 4.0 %collective-permute-done.9.came_ref = f32[256,128]{1,0:T(8,128)S(1)} collective-permute-done((f32[256,128]{1,0:T(8,128)S(1)}, f32[256,128]{1,0:T(8,128)S(1)}, u32[]{:S(2)}, u32[]{:S(2)}) %collective-permute-start.9) | collective-permute-done | bytes 131104 | tf_op jit(solution)/shard_map/ppermute | solution.py:283
  35.7 0.9 %shard_map.21 = (f32[256,128]{1,0:T(8,128)S(1)}, f32[256,128]{1,0:T(8,128)S(1)}, f32[4,16,128]{2,1,0:T(8,128)S(1)}) custom-call(f32[256,128]{1,0:T(8,128)S(1)} %get-tuple-element.33.kept_ref, f32[256,128]{1,0:T(8,128)S(1)} %collective-permute-done.9.came_ref), custom_call_target="tpu_custom_call" | custom-call | tf_op jit(solution)/shard_map/pallas_call | solution.py:259
  36.7 1.2 %collective-permute-done.10 = f32[4,16,128]{2,1,0:T(8,128)S(1)} collective-permute-done((f32[4,16,128]{2,1,0:T(8,128)S(1)}, f32[4,16,128]{2,1,0:T(8,128)S(1)}, u32[]{:S(2)}, u32[]{:S(2)}) %collective-permute-start.10) | collective-permute-done | bytes 32800 | tf_op jit(solution)/shard_map/ppermute | solution.py:252
  37.9 1.5 %collective-permute-start.11 = (f32[4,16,128]{2,1,0:T(8,128)S(1)}, f32[4,16,128]{2,1,0:T(8,128)S(1)}, u32[]{:S(2)}, u32[]{:S(2)}) collective-permute-start(f32[4,16,128]{2,1,0:T(8,128)S(1)} %add.14.refs_0_), channel_id=1, source_target_pairs={{0,8},{4,12},{8,0},{12,4},{16,24},{20,28},{24,16},{28,20},{1,9},{5... | collective-permute-start | bytes 98312 | tf_op jit(solution)/shard_map/ppermute | solution.py:252
  39.4 1.5 %collective-permute-start.12 = (f32[4,16,128]{2,1,0:T(8,128)S(1)}, f32[4,16,128]{2,1,0:T(8,128)S(1)}, u32[]{:S(2)}, u32[]{:S(2)}) collective-permute-start(f32[4,16,128]{2,1,0:T(8,128)S(1)} %add.14.refs_0_), channel_id=1, source_target_pairs={{0,16},{4,20},{8,24},{12,28},{16,0},{20,4},{24,8},{28,12},{1,17},{... | collective-permute-start | bytes 98312 | tf_op jit(solution)/shard_map/ppermute | solution.py:252
  41.8 1.5 %collective-permute-done.12.refs_2_ = f32[4,16,128]{2,1,0:T(8,128)S(1)} collective-permute-done((f32[4,16,128]{2,1,0:T(8,128)S(1)}, f32[4,16,128]{2,1,0:T(8,128)S(1)}, u32[]{:S(2)}, u32[]{:S(2)}) %collective-permute-start.12) | collective-permute-done | bytes 32800 | tf_op jit(solution)/shard_map/ppermute | solution.py:252
  43.3 2.4 %collective-permute-done.13.refs_3_ = f32[4,16,128]{2,1,0:T(8,128)S(1)} collective-permute-done((f32[4,16,128]{2,1,0:T(8,128)S(1)}, f32[4,16,128]{2,1,0:T(8,128)S(1)}, u32[]{:S(2)}, u32[]{:S(2)}) %collective-permute-start.13) | collective-permute-done | bytes 32800 | tf_op jit(solution)/shard_map/ppermute | solution.py:252
  45.7 1.7 %shard_map.22 = (f32[256,128]{1,0:T(8,128)S(1)}, f32[256,128]{1,0:T(8,128)S(1)}) custom-call(f32[256,128]{1,0:T(8,128)S(1)} %get-tuple-element.35.even_ref, f32[256,128]{1,0:T(8,128)S(1)} %get-tuple-element.36.odd_ref, f32[4,16,128]{2,1,0:T(8,128)S(1)} %add.14.refs_0_, f32[4,16,128]{2,1,0:T(8,128)S(1)} %collective-permute-done.11.refs_1_, ...), custom_call_target="tpu_custom_call" | custom-call | tf_op jit(solution)/shard_map/pallas_call | solution.py:259
  47.5 2.1 %collective-permute-start.14 = (f32[256,128]{1,0:T(8,128)S(1)}, f32[256,128]{1,0:T(8,128)S(1)}, u32[]{:S(2)}, u32[]{:S(2)}) collective-permute-start(f32[256,128]{1,0:T(8,128)S(1)} %get-tuple-element.39), channel_id=1, source_target_pairs={{1,0},{0,2},{3,1},{2,3},{5,4},{4,6},{7,5},{6,7},{9,8},{8,10},{11,9... | collective-permute-start | bytes 393224 | tf_op jit(solution)/shard_map/ppermute | solution.py:283
  49.5 2.9 %collective-permute-done.14.came_ref = f32[256,128]{1,0:T(8,128)S(1)} collective-permute-done((f32[256,128]{1,0:T(8,128)S(1)}, f32[256,128]{1,0:T(8,128)S(1)}, u32[]{:S(2)}, u32[]{:S(2)}) %collective-permute-start.14) | collective-permute-done | bytes 131104 | tf_op jit(solution)/shard_map/ppermute | solution.py:283
  53.5 1.2 %collective-permute-done.15 = f32[4,16,128]{2,1,0:T(8,128)S(1)} collective-permute-done((f32[4,16,128]{2,1,0:T(8,128)S(1)}, f32[4,16,128]{2,1,0:T(8,128)S(1)}, u32[]{:S(2)}, u32[]{:S(2)}) %collective-permute-start.15) | collective-permute-done | bytes 32800 | tf_op jit(solution)/shard_map/ppermute | solution.py:252
  55.7 2.4 %collective-permute-start.18 = (f32[4,16,128]{2,1,0:T(8,128)S(1)}, f32[4,16,128]{2,1,0:T(8,128)S(1)}, u32[]{:S(2)}, u32[]{:S(2)}) collective-permute-start(f32[4,16,128]{2,1,0:T(8,128)S(1)} %add.15.refs_0_), channel_id=1, source_target_pairs={{0,24},{4,28},{8,16},{12,20},{16,8},{20,12},{24,0},{28,4},{1,25},{... | collective-permute-start | bytes 98312 | tf_op jit(solution)/shard_map/ppermute | solution.py:252
  58.6 0.9 %collective-permute-done.17.refs_2_ = f32[4,16,128]{2,1,0:T(8,128)S(1)} collective-permute-done((f32[4,16,128]{2,1,0:T(8,128)S(1)}, f32[4,16,128]{2,1,0:T(8,128)S(1)}, u32[]{:S(2)}, u32[]{:S(2)}) %collective-permute-start.17) | collective-permute-done | bytes 32800 | tf_op jit(solution)/shard_map/ppermute | solution.py:252
  59.5 1.1 %collective-permute-done.18.refs_3_ = f32[4,16,128]{2,1,0:T(8,128)S(1)} collective-permute-done((f32[4,16,128]{2,1,0:T(8,128)S(1)}, f32[4,16,128]{2,1,0:T(8,128)S(1)}, u32[]{:S(2)}, u32[]{:S(2)}) %collective-permute-start.18) | collective-permute-done | bytes 32800 | tf_op jit(solution)/shard_map/ppermute | solution.py:252
  60.5 2.1 %shard_map.24 = (f32[256,128]{1,0:T(8,128)S(1)}, f32[256,128]{1,0:T(8,128)S(1)}) custom-call(f32[256,128]{1,0:T(8,128)S(1)} %get-tuple-element.40.even_ref, f32[256,128]{1,0:T(8,128)S(1)} %get-tuple-element.41.odd_ref, f32[4,16,128]{2,1,0:T(8,128)S(1)} %add.15.refs_0_, f32[4,16,128]{2,1,0:T(8,128)S(1)} %collective-permute-done.16.refs_1_, ...), custom_call_target="tpu_custom_call" | custom-call | tf_op jit(solution)/shard_map/pallas_call | solution.py:259
  62.6 2.0 %collective-permute-start.19 = (f32[256,128]{1,0:T(8,128)S(1)}, f32[256,128]{1,0:T(8,128)S(1)}, u32[]{:S(2)}, u32[]{:S(2)}) collective-permute-start(f32[256,128]{1,0:T(8,128)S(1)} %get-tuple-element.43), channel_id=1, source_target_pairs={{2,0},{0,1},{3,2},{1,3},{6,4},{4,5},{7,6},{5,7},{10,8},{8,9},{11,1... | collective-permute-start | bytes 393224 | tf_op jit(solution)/shard_map/ppermute | solution.py:283
  64.6 4.0 %collective-permute-done.19 = f32[256,128]{1,0:T(8,128)S(1)} collective-permute-done((f32[256,128]{1,0:T(8,128)S(1)}, f32[256,128]{1,0:T(8,128)S(1)}, u32[]{:S(2)}, u32[]{:S(2)}) %collective-permute-start.19) | collective-permute-done | bytes 131104 | tf_op jit(solution)/shard_map/ppermute | solution.py:283
  (24 shorter events, 8.3 us)
Async XLA Ops:
  0.0 0.9 %copy-start = (f32[256,256]{1,0:T(8,128)S(1)}, f32[256,256]{1,0:T(8,128)}, u32[]{:S(2)}) copy-start(f32[256,256]{1,0:T(8,128)} %basis_ref.1) | copy-start | bytes 786436
  2.1 1.4 %collective-permute-start = (f32[4,16,128]{2,1,0:T(8,128)S(1)}, f32[4,16,128]{2,1,0:T(8,128)S(1)}, u32[]{:S(2)}, u32[]{:S(2)}) collective-permute-start(f32[4,16,128]{2,1,0:T(8,128)S(1)} %get-tuple-element.27), channel_id=1, source_target_pairs={{0,4},{4,0},{8,12},{12,8},{16,20},{20,16},{24,28},{28,24},{1,5},{5... | collective-permute-start | bytes 98312 | tf_op jit(solution)/shard_map/ppermute | solution.py:252
  3.5 4.7 %collective-permute-start.1 = (f32[4,16,128]{2,1,0:T(8,128)S(1)}, f32[4,16,128]{2,1,0:T(8,128)S(1)}, u32[]{:S(2)}, u32[]{:S(2)}) collective-permute-start(f32[4,16,128]{2,1,0:T(8,128)S(1)} %add.12.refs_0_), channel_id=1, source_target_pairs={{0,8},{4,12},{8,0},{12,4},{16,24},{20,28},{24,16},{28,20},{1,9},{5... | collective-permute-start | bytes 98312 | tf_op jit(solution)/shard_map/ppermute | solution.py:252
  6.4 3.9 %collective-permute-start.2 = (f32[4,16,128]{2,1,0:T(8,128)S(1)}, f32[4,16,128]{2,1,0:T(8,128)S(1)}, u32[]{:S(2)}, u32[]{:S(2)}) collective-permute-start(f32[4,16,128]{2,1,0:T(8,128)S(1)} %add.12.refs_0_), channel_id=1, source_target_pairs={{0,16},{4,20},{8,24},{12,28},{16,0},{20,4},{24,8},{28,12},{1,17},{... | collective-permute-start | bytes 98312 | tf_op jit(solution)/shard_map/ppermute | solution.py:252
  7.9 4.8 %collective-permute-start.3 = (f32[4,16,128]{2,1,0:T(8,128)S(1)}, f32[4,16,128]{2,1,0:T(8,128)S(1)}, u32[]{:S(2)}, u32[]{:S(2)}) collective-permute-start(f32[4,16,128]{2,1,0:T(8,128)S(1)} %add.12.refs_0_), channel_id=1, source_target_pairs={{0,24},{4,28},{8,16},{12,20},{16,8},{20,12},{24,0},{28,4},{1,25},{... | collective-permute-start | bytes 98312 | tf_op jit(solution)/shard_map/ppermute | solution.py:252
  14.4 5.2 %collective-permute-start.4 = (f32[256,128]{1,0:T(8,128)S(1)}, f32[256,128]{1,0:T(8,128)S(1)}, u32[]{:S(2)}, u32[]{:S(2)}) collective-permute-start(f32[256,128]{1,0:T(8,128)S(1)} %get-tuple-element.29), channel_id=1, source_target_pairs={{1,0},{0,2},{3,1},{2,3},{5,4},{4,6},{7,5},{6,7},{9,8},{8,10},{11,9... | collective-permute-start | bytes 393224 | tf_op jit(solution)/shard_map/ppermute | solution.py:283
  20.5 1.3 %collective-permute-start.5 = (f32[4,16,128]{2,1,0:T(8,128)S(1)}, f32[4,16,128]{2,1,0:T(8,128)S(1)}, u32[]{:S(2)}, u32[]{:S(2)}) collective-permute-start(f32[4,16,128]{2,1,0:T(8,128)S(1)} %get-tuple-element.32), channel_id=1, source_target_pairs={{0,4},{4,0},{8,12},{12,8},{16,20},{20,16},{24,28},{28,24},{1,5},{5... | collective-permute-start | bytes 98312 | tf_op jit(solution)/shard_map/ppermute | solution.py:252
  21.8 3.9 %collective-permute-start.6 = (f32[4,16,128]{2,1,0:T(8,128)S(1)}, f32[4,16,128]{2,1,0:T(8,128)S(1)}, u32[]{:S(2)}, u32[]{:S(2)}) collective-permute-start(f32[4,16,128]{2,1,0:T(8,128)S(1)} %add.13.refs_0_), channel_id=1, source_target_pairs={{0,8},{4,12},{8,0},{12,4},{16,24},{20,28},{24,16},{28,20},{1,9},{5... | collective-permute-start | bytes 98312 | tf_op jit(solution)/shard_map/ppermute | solution.py:252
  22.3 4.3 %collective-permute-start.7 = (f32[4,16,128]{2,1,0:T(8,128)S(1)}, f32[4,16,128]{2,1,0:T(8,128)S(1)}, u32[]{:S(2)}, u32[]{:S(2)}) collective-permute-start(f32[4,16,128]{2,1,0:T(8,128)S(1)} %add.13.refs_0_), channel_id=1, source_target_pairs={{0,16},{4,20},{8,24},{12,28},{16,0},{20,4},{24,8},{28,12},{1,17},{... | collective-permute-start | bytes 98312 | tf_op jit(solution)/shard_map/ppermute | solution.py:252
  22.8 4.8 %collective-permute-start.8 = (f32[4,16,128]{2,1,0:T(8,128)S(1)}, f32[4,16,128]{2,1,0:T(8,128)S(1)}, u32[]{:S(2)}, u32[]{:S(2)}) collective-permute-start(f32[4,16,128]{2,1,0:T(8,128)S(1)} %add.13.refs_0_), channel_id=1, source_target_pairs={{0,24},{4,28},{8,16},{12,20},{16,8},{20,12},{24,0},{28,4},{1,25},{... | collective-permute-start | bytes 98312 | tf_op jit(solution)/shard_map/ppermute | solution.py:252
  29.4 6.3 %collective-permute-start.9 = (f32[256,128]{1,0:T(8,128)S(1)}, f32[256,128]{1,0:T(8,128)S(1)}, u32[]{:S(2)}, u32[]{:S(2)}) collective-permute-start(f32[256,128]{1,0:T(8,128)S(1)} %get-tuple-element.34), channel_id=1, source_target_pairs={{2,0},{0,1},{3,2},{1,3},{6,4},{4,5},{7,6},{5,7},{10,8},{8,9},{11,1... | collective-permute-start | bytes 393224 | tf_op jit(solution)/shard_map/ppermute | solution.py:283
  36.6 1.3 %collective-permute-start.10 = (f32[4,16,128]{2,1,0:T(8,128)S(1)}, f32[4,16,128]{2,1,0:T(8,128)S(1)}, u32[]{:S(2)}, u32[]{:S(2)}) collective-permute-start(f32[4,16,128]{2,1,0:T(8,128)S(1)} %get-tuple-element.37), channel_id=1, source_target_pairs={{0,4},{4,0},{8,12},{12,8},{16,20},{20,16},{24,28},{28,24},{1,5},{5... | collective-permute-start | bytes 98312 | tf_op jit(solution)/shard_map/ppermute | solution.py:252
  37.9 3.9 %collective-permute-start.11 = (f32[4,16,128]{2,1,0:T(8,128)S(1)}, f32[4,16,128]{2,1,0:T(8,128)S(1)}, u32[]{:S(2)}, u32[]{:S(2)}) collective-permute-start(f32[4,16,128]{2,1,0:T(8,128)S(1)} %add.14.refs_0_), channel_id=1, source_target_pairs={{0,8},{4,12},{8,0},{12,4},{16,24},{20,28},{24,16},{28,20},{1,9},{5... | collective-permute-start | bytes 98312 | tf_op jit(solution)/shard_map/ppermute | solution.py:252
  39.4 3.9 %collective-permute-start.12 = (f32[4,16,128]{2,1,0:T(8,128)S(1)}, f32[4,16,128]{2,1,0:T(8,128)S(1)}, u32[]{:S(2)}, u32[]{:S(2)}) collective-permute-start(f32[4,16,128]{2,1,0:T(8,128)S(1)} %add.14.refs_0_), channel_id=1, source_target_pairs={{0,16},{4,20},{8,24},{12,28},{16,0},{20,4},{24,8},{28,12},{1,17},{... | collective-permute-start | bytes 98312 | tf_op jit(solution)/shard_map/ppermute | solution.py:252
  40.9 4.8 %collective-permute-start.13 = (f32[4,16,128]{2,1,0:T(8,128)S(1)}, f32[4,16,128]{2,1,0:T(8,128)S(1)}, u32[]{:S(2)}, u32[]{:S(2)}) collective-permute-start(f32[4,16,128]{2,1,0:T(8,128)S(1)} %add.14.refs_0_), channel_id=1, source_target_pairs={{0,24},{4,28},{8,16},{12,20},{16,8},{20,12},{24,0},{28,4},{1,25},{... | collective-permute-start | bytes 98312 | tf_op jit(solution)/shard_map/ppermute | solution.py:252
  47.5 5.0 %collective-permute-start.14 = (f32[256,128]{1,0:T(8,128)S(1)}, f32[256,128]{1,0:T(8,128)S(1)}, u32[]{:S(2)}, u32[]{:S(2)}) collective-permute-start(f32[256,128]{1,0:T(8,128)S(1)} %get-tuple-element.39), channel_id=1, source_target_pairs={{1,0},{0,2},{3,1},{2,3},{5,4},{4,6},{7,5},{6,7},{9,8},{8,10},{11,9... | collective-permute-start | bytes 393224 | tf_op jit(solution)/shard_map/ppermute | solution.py:283
  53.4 1.3 %collective-permute-start.15 = (f32[4,16,128]{2,1,0:T(8,128)S(1)}, f32[4,16,128]{2,1,0:T(8,128)S(1)}, u32[]{:S(2)}, u32[]{:S(2)}) collective-permute-start(f32[4,16,128]{2,1,0:T(8,128)S(1)} %get-tuple-element.42), channel_id=1, source_target_pairs={{0,4},{4,0},{8,12},{12,8},{16,20},{20,16},{24,28},{28,24},{1,5},{5... | collective-permute-start | bytes 98312 | tf_op jit(solution)/shard_map/ppermute | solution.py:252
  54.7 3.9 %collective-permute-start.16 = (f32[4,16,128]{2,1,0:T(8,128)S(1)}, f32[4,16,128]{2,1,0:T(8,128)S(1)}, u32[]{:S(2)}, u32[]{:S(2)}) collective-permute-start(f32[4,16,128]{2,1,0:T(8,128)S(1)} %add.15.refs_0_), channel_id=1, source_target_pairs={{0,8},{4,12},{8,0},{12,4},{16,24},{20,28},{24,16},{28,20},{1,9},{5... | collective-permute-start | bytes 98312 | tf_op jit(solution)/shard_map/ppermute | solution.py:252
  55.2 4.3 %collective-permute-start.17 = (f32[4,16,128]{2,1,0:T(8,128)S(1)}, f32[4,16,128]{2,1,0:T(8,128)S(1)}, u32[]{:S(2)}, u32[]{:S(2)}) collective-permute-start(f32[4,16,128]{2,1,0:T(8,128)S(1)} %add.15.refs_0_), channel_id=1, source_target_pairs={{0,16},{4,20},{8,24},{12,28},{16,0},{20,4},{24,8},{28,12},{1,17},{... | collective-permute-start | bytes 98312 | tf_op jit(solution)/shard_map/ppermute | solution.py:252
  55.7 4.8 %collective-permute-start.18 = (f32[4,16,128]{2,1,0:T(8,128)S(1)}, f32[4,16,128]{2,1,0:T(8,128)S(1)}, u32[]{:S(2)}, u32[]{:S(2)}) collective-permute-start(f32[4,16,128]{2,1,0:T(8,128)S(1)} %add.15.refs_0_), channel_id=1, source_target_pairs={{0,24},{4,28},{8,16},{12,20},{16,8},{20,12},{24,0},{28,4},{1,25},{... | collective-permute-start | bytes 98312 | tf_op jit(solution)/shard_map/ppermute | solution.py:252
  62.6 5.9 %collective-permute-start.19 = (f32[256,128]{1,0:T(8,128)S(1)}, f32[256,128]{1,0:T(8,128)S(1)}, u32[]{:S(2)}, u32[]{:S(2)}) collective-permute-start(f32[256,128]{1,0:T(8,128)S(1)} %get-tuple-element.43), channel_id=1, source_target_pairs={{2,0},{0,1},{3,2},{1,3},{6,4},{4,5},{7,6},{5,7},{10,8},{8,9},{11,1... | collective-permute-start | bytes 393224 | tf_op jit(solution)/shard_map/ppermute | solution.py:283

commit v2 on v1

--- a/solution.py
+++ b/solution.py
@@ -12,6 +12,10 @@
 JSTEPS = 6
 REACH = 2 * (JSTEPS - 1) + 1
 DIAGS = 16
+FAR_REACH = 6 * (JSTEPS - 1) - 1
+FAR_DIAGS = 32
+WINDOW = 32
+NEAR = 16
 
 
 def tournament_order(pair_count):
@@ -54,6 +58,59 @@
     return plans
 
 
+def fused_moves(pair_total):
+    ordering = tournament_order(pair_total)
+    before, last = ROUNDS - 3, ROUNDS - 1
+    needs, edges, seconds = {}, [], ({}, {})
+    for pair in range(pair_total):
+        here = host_of(pair, pair_total, last)
+        needs[here] = []
+        for place in (0, 1):
+            source = int(ordering[2 * pair + place])
+            seconds[place][here] = source % 2
+            for half in (0, 1):
+                old = int(ordering[2 * (source // 2) + half])
+                there = host_of(old // 2, pair_total, before)
+                needs[here].append((there, old % 2))
+                if there != here:
+                    edges.append((there, old % 2, here))
+    turn, left_over = {}, list(edges)
+    while left_over:
+        edge, by_target = left_over[0], True
+        number = 0
+        while edge is not None:
+            turn[edge] = number
+            left_over.remove(edge)
+            key = 2 if by_target else 0
+            edge = next((e for e in left_over if e[key] == edge[key]), None)
+            by_target, number = not by_target, 1 - number
+    sends = [[(e[0], e[2]) for e in edges if turn[e] == i] for i in (0, 1)]
+    for chosen in sends:
+        assert len({a for a, _ in chosen}) == len({b for _, b in chosen}) == pair_total
+    sends_first = {e[0] for e in edges if turn[e] == 0 and e[1] == 0}
+    picks = []
+    for slot in range(4):
+        pick = {}
+        for here in range(pair_total):
+            there, half = needs[here][slot]
+            if there == here:
+                pick[here] = 0 if (half == 0) == (here in sends_first) else 1
+            else:
+                pick[here] = 2 + turn[(there, half, here)]
+        picks.append(pick)
+    is_second = [{h for h, place in table.items() if place} for table in seconds]
+    return sends, sends_first, picks, is_second
+
+
+def choose(pick, arrays):
+    chosen = arrays[0]
+    for number in range(1, len(arrays)):
+        members = {here for here, value in pick.items() if value == number}
+        if members:
+            chosen = jnp.where(among(members), arrays[number], chosen)
+    return chosen
+
+
 def among(members):
     here = lax.axis_index("pair")
     return functools.reduce(
@@ -109,23 +166,26 @@
     )
 
 
-def store_bands(even, odd, band_ref):
-    rows = even.shape[0]
-    sums = [[None] * 4 for _ in range(REACH)]
-    for start in range(0, rows, 8):
-        e, o = even[start : start + 8], odd[start : start + 8]
-        for d in range(REACH):
+def store_bands(even, odd, band_ref, reach, diags, base=0):
+    rows, width = even.shape
+    for d in range(reach):
+        sums = [None] * 4
+        for start in range(0, rows, 8):
+            e, o = even[start : start + 8], odd[start : start + 8]
             e_near, o_near = right(e, d), right(o, d)
-            parts = (e_near * e, e_near * o, o_near * e, o_near * o)
+            parts = (e_near * e, e_near * o, o_near * e if d else None, o_near * o)
             for q in range(4):
-                if d == 0 and q == 2:
-                    continue
-                sums[d][q] = parts[q] if start == 0 else sums[d][q] + parts[q]
-    sums[0][2] = sums[0][1]
+                if parts[q] is not None:
+                    sums[q] = parts[q] if start == 0 else sums[q] + parts[q]
+        if d == 0:
+            sums[2] = sums[1]
+        for q in range(4):
+            row = base + q * diags + d
+            band_ref[row : row + 1, :] = jnp.sum(sums[q], axis=0, keepdims=True)
     for q in range(4):
-        for d in range(REACH):
-            band_ref[q, d : d + 1, :] = jnp.sum(sums[d][q], axis=0, keepdims=True)
-        band_ref[q, REACH:, :] = jnp.zeros((DIAGS - REACH, even.shape[1]), jnp.float32)
+        band_ref[base + q * diags + reach : base + (q + 1) * diags, :] = jnp.zeros(
+            (diags - reach, width), jnp.float32
+        )
 
 
 def open_kernel(basis_ref, even_ref, odd_ref, band_ref):
@@ -136,7 +196,7 @@
     even, odd = split_pair(first, second)
     even_ref[...] = even
     odd_ref[...] = odd
-    store_bands(even, odd, band_ref)
+    store_bands(even, odd, band_ref, REACH, DIAGS)
 
 
 def pair_kernel(gets_first, kept_ref, came_ref, even_ref, odd_ref, band_ref):
@@ -145,7 +205,7 @@
     even, odd = split_pair(jnp.where(flag, came, kept), jnp.where(flag, kept, came))
     even_ref[...] = even
     odd_ref[...] = odd
-    store_bands(even, odd, band_ref)
+    store_bands(even, odd, band_ref, REACH, DIAGS)
 
 
 def jacobi_angle(diag_even, diag_odd, coupling):
@@ -197,6 +257,30 @@
     return ee_new, eo_new, oe_new, oo_new
 
 
+def move_bands_back(ee, eo, oe, oo):
+    lane = lanes_of(ee)
+    diag = lax.broadcasted_iota(jnp.int32, ee.shape, 0)
+    last, first = lane == ee.shape[1] - 1, lane == diag
+    on, next_on = diag == 0, diag == 1
+    ee_left, oe_left = left(ee, 1), left(down(oe, -2), 1)
+    ee_far, eo_far = left(down(ee, -1), 1), right(down(eo, 2), 1)
+
+    ee_old = jnp.where(first, jnp.where(on, ee, ee_far), ee_left)
+    ee_old = jnp.where(last, jnp.where(on, oo, down(eo, 1)), ee_old)
+
+    eo_old = jnp.where(on, oe_left, jnp.where(next_on, oe, eo_far))
+    eo_old = jnp.where(first, jnp.where(on, ee_far, right(down(eo, 1), 1)), eo_old)
+    eo_old = jnp.where(jnp.logical_and(last, on), down(oo, -1), eo_old)
+
+    oe_old = jnp.where(first, ee_left, oe_left)
+    oe_old = jnp.where(last, down(oo, -1), oe_old)
+    oe_old = jnp.where(on, eo_old, oe_old)
+
+    near = jnp.where(on, ee_left, jnp.where(next_on, oe, eo_far))
+    oo_old = jnp.where(first, near, right(oo, 1))
+    return ee_old, eo_old, oe_old, oo_old
+
+
 def move_columns(even, odd):
     lane = lanes_of(even)
     first, last = lane == 0, lane == even.shape[1] - 1
@@ -214,51 +298,203 @@
     return even_old, odd_old
 
 
-def turn_kernel(sends_first, is_last, even_ref, odd_ref, *refs):
+def angles_of(bands, carried):
+    angles = []
+    for step in range(JSTEPS):
+        ee, eo, oe, oo = bands
+        cosine, sine = jacobi_angle(ee[0:1], oo[0:1], eo[0:1])
+        angles.append((cosine, sine))
+        if carried or step < JSTEPS - 1:
+            bands = turn_bands(ee, eo, oe, oo, cosine, sine)
+        if step < JSTEPS - 1:
+            bands = move_bands(*bands)
+    if carried:
+        for step in range(JSTEPS - 1):
+            bands = move_bands_back(*bands)
+    return angles, bands
+
+
+def turn_columns(even, odd, angles):
+    for step, (cosine, sine) in enumerate(angles):
+        even, odd = cosine * even + sine * odd, cosine * odd - sine * even
+        if step < JSTEPS - 1:
+            even, odd = move_columns(even, odd)
+    for step in range(JSTEPS - 1):
+        even, odd = move_columns_back(even, odd)
+    return even, odd
+
+
+def turn_kernel(sends_first, even_ref, odd_ref, *refs):
     *band_refs, kept_ref, sent_ref = refs
     bands = [ref[...] for ref in band_refs]
     while len(bands) > 1:
         bands = [bands[i] + bands[i + 1] for i in range(0, len(bands), 2)]
-    ee, eo, oe, oo = (bands[0][q] for q in range(4))
-    even, odd = even_ref[...], odd_ref[...]
-    for step in range(JSTEPS):
-        cosine, sine = jacobi_angle(ee[0:1], oo[0:1], eo[0:1])
-        even, odd = cosine * even + sine * odd, cosine * odd - sine * even
-        if step < JSTEPS - 1:
-            ee, eo, oe, oo = move_bands(*turn_bands(ee, eo, oe, oo, cosine, sine))
-            even, odd = move_columns(even, odd)
-    for step in range(JSTEPS - 1):
-        even, odd = move_columns_back(even, odd)
-    first, second = join_pair(even, odd)
-    if is_last:
-        table = separator(first.shape[1], True)
-        first, second = reorder(first, table), reorder(second, table)
+    bands = [bands[0][q * DIAGS : (q + 1) * DIAGS] for q in range(4)]
+    angles, _ = angles_of(bands, False)
+    first, second = join_pair(*turn_columns(even_ref[...], odd_ref[...], angles))
     flag = among(sends_first)
     kept_ref[...] = jnp.where(flag, second, first)
     sent_ref[...] = jnp.where(flag, first, second)
 
 
-def exchange_groups(x, axis):
-    size = lax.axis_size(axis)
-    bits = [1 << b for b in range(size.bit_length() - 1)]
-    groups = [bits[:1]] + [bits[i : i + 2] for i in range(1, len(bits), 2)]
+def near_starts(width):
+    half = width // 2
+    reach = REACH - 1
+    return (half - 2 * reach, width - WINDOW), (0, half - reach)
+
+
+def cross_partial(x_even, x_odd, y_even, y_odd, x_second, y_second):
+    rows, width = x_even.shape
+    x_starts, y_starts = near_starts(width)
+    lane = lanes_of(x_even)
+
+    def window(even, odd, flag, starts):
+        at_zero = jnp.where(flag, left(even, starts[1]), left(even, starts[0]))
+        at_next = jnp.where(flag, left(odd, starts[1] - WINDOW), left(odd, starts[0] - WINDOW))
+        return jnp.where(lane < WINDOW, at_zero, jnp.where(lane < 2 * WINDOW, at_next, 0.0))
+
+    corner = lax.dot_general(
+        window(y_even, y_odd, y_second, y_starts),
+        window(x_even, x_odd, x_second, x_starts),
+        (((0,), (0,)), ((), ())),
+        precision=lax.Precision.HIGHEST,
+        preferred_element_type=jnp.float32,
+    )
+    low = lax.broadcasted_iota(jnp.int32, (WINDOW, width), 1) < 2 * WINDOW
+    return jnp.where(low, corner[:WINDOW], right(corner[WINDOW : 2 * WINDOW], 2 * WINDOW))
+
+
+def spread(packed, place, flag, starts):
+    at = place * WINDOW
+    return jnp.where(flag, right(packed, starts[1] - at), right(packed, starts[0] - at))
+
+
+def cross_bands(corner, x_angles, y_angles, x_second, y_second):
+    width = corner.shape[1]
+    half = width // 2
+    x_starts, y_starts = near_starts(width)
+    even = jnp.concatenate([spread(corner, p, x_second, x_starts) for p in (0, 2)], axis=0)
+    odd = jnp.concatenate([spread(corner, p, x_second, x_starts) for p in (1, 3)], axis=0)
+    even, odd = turn_columns(even, odd, x_angles)
+    stacked = jnp.concatenate((even, odd), axis=0)
+    ends = jnp.where(x_second, left(stacked, width - NEAR), left(stacked, half - NEAR))
+    ends = jnp.transpose(ends)[:NEAR]
+    even = jnp.concatenate([spread(ends, p, y_second, y_starts) for p in (0, 2)], axis=0)
+    odd = jnp.concatenate([spread(ends, p, y_second, y_starts) for p in (1, 3)], axis=0)
+    even, odd = turn_columns(even, odd, y_angles)
+    even = jnp.where(y_second, even, right(even, half))
+    odd = jnp.where(y_second, odd, right(odd, half))
+    quadrants = (even[:NEAR], odd[:NEAR], even[NEAR:], odd[NEAR:])
+    offset = lanes_of(ends) - lax.broadcasted_iota(jnp.int32, ends.shape, 0) - (half - NEAR)
+    diag = lax.broadcasted_iota(jnp.int32, (DIAGS, width), 0)
+    bands = [jnp.zeros((DIAGS, width), jnp.float32) for _ in quadrants]
+    for d in range(1, REACH):
+        here = offset == d
+        for q, quadrant in enumerate(quadrants):
+            line = jnp.sum(jnp.where(here, quadrant, 0.0), axis=0, keepdims=True)
+            bands[q] = jnp.where(diag == d, line, bands[q])
+    return bands
+
+
+def fused_open(picks, is_second, kept_ref, sent_ref, came0_ref, came1_ref, *refs):
+    *column_refs, mine_ref, other_ref, parts = refs
+    arrays = [ref[...] for ref in (sent_ref, kept_ref, came0_ref, came1_ref)]
+    blocks = [choose(pick, arrays) for pick in picks]
+    columns = split_pair(*blocks[:2]) + split_pair(*blocks[2:])
+    for ref, value in zip(column_refs, columns):
+        ref[...] = value
+    corner = cross_partial(*columns, among(is_second[0]), among(is_second[1]))
+    for i in (0, 1):
+        store_bands(*columns[2 * i : 2 * i + 2], parts.at[i], FAR_REACH, FAR_DIAGS)
+        parts[i, 4 * FAR_DIAGS :, :] = corner[i * NEAR : (i + 1) * NEAR]
+    odd_core = lax.axis_index("row") % 2
+    mine_ref[...] = parts[odd_core]
+    other_ref[...] = parts[1 - odd_core]
+
+
+def fused_turn(x_even, x_odd, y_even, y_odd, x_part, y_part, x_second, y_second):
+    half = x_even.shape[1] // 2
+
+    def quadrants(part):
+        return [part[q * FAR_DIAGS : (q + 1) * FAR_DIAGS] for q in range(4)]
+
+    x_angles, x_bands = angles_of(quadrants(x_part), True)
+    y_angles, y_bands = angles_of(quadrants(y_part), True)
+    corner = jnp.concatenate((x_part[4 * FAR_DIAGS :], y_part[4 * FAR_DIAGS :]), axis=0)
+    middle = cross_bands(corner, x_angles, y_angles, x_second, y_second)
+
+    def first_half(x):
+        return jnp.where(x_second, right(x, half), x)
+
+    def second_half(y):
+        return jnp.where(y_second, y, right(y, half))
+
+    lane = lanes_of(middle[0])
+    diag = lax.broadcasted_iota(jnp.int32, middle[0].shape, 0)
+    bands = [
+        jnp.where(
+            lane < half,
+            first_half(x_bands[q][:DIAGS]),
+            jnp.where(lane - diag < half, middle[q], second_half(y_bands[q][:DIAGS])),
+        )
+        for q in range(4)
+    ]
+    x_turned = turn_columns(x_even, x_odd, x_angles)
+    y_turned = turn_columns(y_even, y_odd, y_angles)
+    low = lanes_of(x_even) < half
+    even, odd = (
+        jnp.where(low, first_half(x), second_half(y)) for x, y in zip(x_turned, y_turned)
+    )
+    angles, _ = angles_of(bands, False)
+    return join_pair(*turn_columns(even, odd, angles))
+
+
+def fused_kernel(is_second, sends_first, *refs):
+    *column_refs, mine_ref, other_ref, kept_ref, sent_ref = refs
+    mine, other = mine_ref[...], other_ref[...]
+    odd_core = lax.axis_index("row") % 2 == 1
+    parts = jnp.where(odd_core, other, mine), jnp.where(odd_core, mine, other)
+    first, second = fused_turn(
+        *(ref[...] for ref in column_refs),
+        *parts,
+        among(is_second[0]),
+        among(is_second[1]),
+    )
+    table = separator(first.shape[1], True)
+    first, second = reorder(first, table), reorder(second, table)
+    flag = among(sends_first)
+    kept_ref[...] = jnp.where(flag, second, first)
+    sent_ref[...] = jnp.where(flag, first, second)
+
+
+def pair_sums(arrays):
+    while len(arrays) > 1:
+        arrays = [arrays[i] + arrays[i + 1] for i in range(0, len(arrays), 2)]
+    return arrays[0]
+
+
+def swap(x, axis, mask):
+    return lax.ppermute(x, axis, [(i, i ^ mask) for i in range(lax.axis_size(axis))])
+
+
+def exchange_groups(x, axis, first_bit=0):
+    count = lax.axis_size(axis).bit_length() - 1
+    bits = [1 << b for b in range(count)]
+    groups = [bits[:1]] + [bits[i : i + 2] for i in range(1, count, 2)]
     arrays = [x]
-    for group in groups:
-        while len(arrays) > 1:
-            arrays = [arrays[i] + arrays[i + 1] for i in range(0, len(arrays), 2)]
-        x = arrays[0]
+    for group in groups[first_bit:]:
+        x = pair_sums(arrays)
         masks = [group[0]] if len(group) == 1 else [group[0], group[1], group[0] | group[1]]
-        arrays = [x] + [
-            lax.ppermute(x, axis, [(i, i ^ mask) for i in range(size)]) for mask in masks
-        ]
+        arrays = [x] + [swap(x, axis, mask) for mask in masks]
     return arrays
 
 
-def call(kernel, shapes, *args):
+def call(kernel, shapes, *args, scratch=()):
     out = [jax.ShapeDtypeStruct(shape, jnp.float32) for shape in shapes]
     return pl.pallas_call(
         kernel,
         out_shape=out,
+        scratch_shapes=[pltpu.VMEM(shape, jnp.float32) for shape in scratch],
         compiler_params=pltpu.CompilerParams(vmem_limit_bytes=32 * 1024 * 1024),
     )(*args)
 
@@ -266,25 +502,43 @@
 def per_device(basis):
     rows, cols = basis.shape
     width = cols // 2
+    pair_total = lax.axis_size("pair")
     column = (rows, width)
-    band = (4, DIAGS, width)
-    plans = moves(lax.axis_size("pair"))
+    band = (4 * DIAGS, width)
+    part = (4 * FAR_DIAGS + NEAR, width)
+    plans = moves(pair_total)
+    fused_sends, fused_first, picks, is_second = fused_moves(pair_total)
     even, odd, partial = call(open_kernel, (column, column, band), basis)
-    for round_index, (sends, sends_first, gets_first) in enumerate(plans):
-        is_last = round_index == ROUNDS - 1
+    for round_index in range(ROUNDS - 2):
+        sends, sends_first, gets_first = plans[round_index]
+        ahead = round_index == ROUNDS - 3
         arrays = exchange_groups(partial, "row")
-        kept, sent = call(
-            functools.partial(turn_kernel, sends_first, is_last),
-            (column, column),
-            even,
-            odd,
-            *arrays,
-        )
-        came = lax.ppermute(sent, "pair", sends)
-        if not is_last:
-            even, odd, partial = call(
-                functools.partial(pair_kernel, gets_first), (column, column, band), kept, came
-            )
+        turn = functools.partial(turn_kernel, fused_first if ahead else sends_first)
+        kept, sent = call(turn, (column, column), even, odd, *arrays)
+        if not ahead:
+            came = lax.ppermute(sent, "pair", sends)
+            opening = functools.partial(pair_kernel, gets_first)
+            even, odd, partial = call(opening, (column, column, band), kept, came)
+    came = [lax.ppermute(x, "pair", s) for x, s in zip((sent, kept), fused_sends)]
+    *columns, mine, other = call(
+        functools.partial(fused_open, picks, is_second),
+        (column,) * 4 + (part,) * 2,
+        kept,
+        sent,
+        *came,
+        scratch=((2,) + part,),
+    )
+    mine = pair_sums(exchange_groups(mine + swap(other, "row", 1), "row", 1))
+    other = swap(mine, "row", 1)
+    sends, sends_first, gets_first = plans[-1]
+    kept, sent = call(
+        functools.partial(fused_kernel, is_second, sends_first),
+        (column, column),
+        *columns,
+        mine,
+        other,
+    )
+    came = lax.ppermute(sent, "pair", sends)
     flag = among(gets_first)
     first = jnp.where(flag, came, kept)
     second = jnp.where(flag, kept, came)

time: 69.4 us -> 67.8 us (0.977)
  starting transfers between devices: 24.6 us -> 19.6 us
  Pallas kernels: 11.2 us -> 15.6 us
  waiting for transfers between devices: 31.7 us -> 30.7 us
    ppermute x4 -> x2, starting transfers between devices: 9.06 us -> 3.35 us  [per_device(): came = lax.ppermute(sent, 'pair', sends)]
    ppermute x4 -> x2, waiting for transfers between devices: 13.4 us -> 8.5 us  [per_device(): came = lax.ppermute(sent, 'pair', sends)]
    pallas_call x8 -> x6, Pallas kernels: 11.2 us -> 15.6 us  [call(): pl.pallas_call(kernel, out_shape=out, scratch_shapes=[pltpu.VMEM(shape, j...]
    ppermute x16 -> x15, waiting for transfers between devices: 18.3 us -> 22.1 us  [the longest x13 16.4 us: swap(): lax.ppermute(x, axis, [(i, i ^ mask) for i in range(lax.axis_size(axis))])]
    ppermute x16 -> x15, starting transfers between devices: 15.6 us -> 16.2 us  [the longest x13 12.1 us: swap(): lax.ppermute(x, axis, [(i, i ^ mask) for i in range(lax.axis_size(axis))])]
  transfers between devices with their start and end apart: 20 -> 17, of which waited for: 20 -> 17; matrix products, arithmetic and copies ran while one was open for 0% -> 0% of each run, Pallas kernels for 0% -> 0%
where the time goes in v2:
time: 67.8 us; the launch traced here: 67.6 us
  waiting for transfers between devices  30.7 us (45%)
  starting transfers between devices  19.6 us (29%)
  Pallas kernels  15.6 us (23%)
  local copies, waits for them, and re-layouts  0.95 us (1%)
  other arithmetic  0.78 us (1%)
    ppermute x13, waiting for transfers between devices, swap(): lax.ppermute(x, axis, [(i, i ^ mask) for i in range(lax.axis_size(axis))])  16.4 us
    pallas_call x6, Pallas kernels, call(): pl.pallas_call(kernel, out_shape=out, scratch_shapes=[pltpu.VMEM(shape, j...  15.6 us
    ppermute x13, starting transfers between devices, swap(): lax.ppermute(x, axis, [(i, i ^ mask) for i in range(lax.axis_size(axis))])  12.1 us
    ppermute x2, waiting for transfers between devices, per_device(): came = lax.ppermute(sent, 'pair', sends)  8.5 us
    ppermute x2, waiting for transfers between devices, per_device(): lax.ppermute(x, 'pair', s)  5.77 us
    ppermute x2, starting transfers between devices, per_device(): lax.ppermute(x, 'pair', s)  4.09 us
    ppermute x2, starting transfers between devices, per_device(): came = lax.ppermute(sent, 'pair', sends)  3.35 us
  transfers between devices with their start and end apart: 17, of which 17 were waited for; matrix products, arithmetic and copies ran while one was open for 0% of the time, Pallas kernels for 0%

profile of v2, /device:TPU:0, one launch (start us, length us, event | category | flops | bytes accessed | tf_op | source)
XLA Modules:
  0.0 67.6 jit_solution(454348149781063230)
XLA Ops:
  0.0 0.9 %copy-done = f32[256,256]{1,0:T(8,128)S(1)} copy-done((f32[256,256]{1,0:T(8,128)S(1)}, f32[256,256]{1,0:T(8,128)}, u32[]{:S(2)}) %copy-start) | copy-done | bytes 262168
  1.0 1.1 %shard_map.17 = (f32[256,128]{1,0:T(8,128)S(1)}, f32[256,128]{1,0:T(8,128)S(1)}, f32[64,128]{1,0:T(8,128)S(1)}) custom-call(f32[256,256]{1,0:T(8,128)S(1)} %copy-done), custom_call_target="tpu_custom_call" | custom-call | tf_op jit(solution)/shard_map/pallas_call | solution.py:494
  2.6 0.9 %collective-permute-done = f32[64,128]{1,0:T(8,128)S(1)} collective-permute-done((f32[64,128]{1,0:T(8,128)S(1)}, f32[64,128]{1,0:T(8,128)S(1)}, u32[]{:S(2)}, u32[]{:S(2)}) %collective-permute-start) | collective-permute-done | bytes 32800 | tf_op jit(solution)/shard_map/ppermute | solution.py:477
  3.5 2.8 %collective-permute-start.1 = (f32[64,128]{1,0:T(8,128)S(1)}, f32[64,128]{1,0:T(8,128)S(1)}, u32[]{:S(2)}, u32[]{:S(2)}) collective-permute-start(f32[64,128]{1,0:T(8,128)S(1)} %add.18.refs_0_), channel_id=1, source_target_pairs={{0,8},{4,12},{8,0},{12,4},{16,24},{20,28},{24,16},{28,20},{1,9},{5... | collective-permute-start | bytes 98312 | tf_op jit(solution)/shard_map/ppermute | solution.py:477
  6.3 1.5 %collective-permute-start.2 = (f32[64,128]{1,0:T(8,128)S(1)}, f32[64,128]{1,0:T(8,128)S(1)}, u32[]{:S(2)}, u32[]{:S(2)}) collective-permute-start(f32[64,128]{1,0:T(8,128)S(1)} %add.18.refs_0_), channel_id=1, source_target_pairs={{0,16},{4,20},{8,24},{12,28},{16,0},{20,4},{24,8},{28,12},{1,17},{... | collective-permute-start | bytes 98312 | tf_op jit(solution)/shard_map/ppermute | solution.py:477
  8.2 2.0 %collective-permute-done.2.refs_2_ = f32[64,128]{1,0:T(8,128)S(1)} collective-permute-done((f32[64,128]{1,0:T(8,128)S(1)}, f32[64,128]{1,0:T(8,128)S(1)}, u32[]{:S(2)}, u32[]{:S(2)}) %collective-permute-start.2) | collective-permute-done | bytes 32800 | tf_op jit(solution)/shard_map/ppermute | solution.py:477
  10.2 2.4 %collective-permute-done.3.refs_3_ = f32[64,128]{1,0:T(8,128)S(1)} collective-permute-done((f32[64,128]{1,0:T(8,128)S(1)}, f32[64,128]{1,0:T(8,128)S(1)}, u32[]{:S(2)}, u32[]{:S(2)}) %collective-permute-start.3) | collective-permute-done | bytes 32800 | tf_op jit(solution)/shard_map/ppermute | solution.py:477
  12.7 1.7 %shard_map.18 = (f32[256,128]{1,0:T(8,128)S(1)}, f32[256,128]{1,0:T(8,128)S(1)}) custom-call(f32[256,128]{1,0:T(8,128)S(1)} %get-tuple-element.23.even_ref, f32[256,128]{1,0:T(8,128)S(1)} %get-tuple-element.24.odd_ref, f32[64,128]{1,0:T(8,128)S(1)} %add.18.refs_0_, f32[64,128]{1,0:T(8,128)S(1)} %collective-permute-done.1.refs_1_, ...), custom_call_target="tpu_custom_call" | custom-call | tf_op jit(solution)/shard_map/pallas_call | solution.py:494
  14.4 2.8 %collective-permute-start.4 = (f32[256,128]{1,0:T(8,128)S(1)}, f32[256,128]{1,0:T(8,128)S(1)}, u32[]{:S(2)}, u32[]{:S(2)}) collective-permute-start(f32[256,128]{1,0:T(8,128)S(1)} %get-tuple-element.27), channel_id=1, source_target_pairs={{1,0},{0,2},{3,1},{2,3},{5,4},{4,6},{7,5},{6,7},{9,8},{8,10},{11,9... | collective-permute-start | bytes 393224 | tf_op jit(solution)/shard_map/ppermute | solution.py:519
  17.2 2.5 %collective-permute-done.4.came_ref = f32[256,128]{1,0:T(8,128)S(1)} collective-permute-done((f32[256,128]{1,0:T(8,128)S(1)}, f32[256,128]{1,0:T(8,128)S(1)}, u32[]{:S(2)}, u32[]{:S(2)}) %collective-permute-start.4) | collective-permute-done | bytes 131104 | tf_op jit(solution)/shard_map/ppermute | solution.py:519
  19.7 0.9 %shard_map.19 = (f32[256,128]{1,0:T(8,128)S(1)}, f32[256,128]{1,0:T(8,128)S(1)}, f32[64,128]{1,0:T(8,128)S(1)}) custom-call(f32[256,128]{1,0:T(8,128)S(1)} %get-tuple-element.26.kept_ref, f32[256,128]{1,0:T(8,128)S(1)} %collective-permute-done.4.came_ref), custom_call_target="tpu_custom_call" | custom-call | tf_op jit(solution)/shard_map/pallas_call | solution.py:494
  20.7 1.2 %collective-permute-done.5 = f32[64,128]{1,0:T(8,128)S(1)} collective-permute-done((f32[64,128]{1,0:T(8,128)S(1)}, f32[64,128]{1,0:T(8,128)S(1)}, u32[]{:S(2)}, u32[]{:S(2)}) %collective-permute-start.5) | collective-permute-done | bytes 32800 | tf_op jit(solution)/shard_map/ppermute | solution.py:477
  22.9 2.4 %collective-permute-start.8 = (f32[64,128]{1,0:T(8,128)S(1)}, f32[64,128]{1,0:T(8,128)S(1)}, u32[]{:S(2)}, u32[]{:S(2)}) collective-permute-start(f32[64,128]{1,0:T(8,128)S(1)} %add.19.refs_0_), channel_id=1, source_target_pairs={{0,24},{4,28},{8,16},{12,20},{16,8},{20,12},{24,0},{28,4},{1,25},{... | collective-permute-start | bytes 98312 | tf_op jit(solution)/shard_map/ppermute | solution.py:477
  25.8 0.9 %collective-permute-done.7.refs_2_ = f32[64,128]{1,0:T(8,128)S(1)} collective-permute-done((f32[64,128]{1,0:T(8,128)S(1)}, f32[64,128]{1,0:T(8,128)S(1)}, u32[]{:S(2)}, u32[]{:S(2)}) %collective-permute-start.7) | collective-permute-done | bytes 32800 | tf_op jit(solution)/shard_map/ppermute | solution.py:477
  26.7 1.1 %collective-permute-done.8.refs_3_ = f32[64,128]{1,0:T(8,128)S(1)} collective-permute-done((f32[64,128]{1,0:T(8,128)S(1)}, f32[64,128]{1,0:T(8,128)S(1)}, u32[]{:S(2)}, u32[]{:S(2)}) %collective-permute-start.8) | collective-permute-done | bytes 32800 | tf_op jit(solution)/shard_map/ppermute | solution.py:477
  27.7 1.7 %shard_map.20 = (f32[256,128]{1,0:T(8,128)S(1)}, f32[256,128]{1,0:T(8,128)S(1)}) custom-call(f32[256,128]{1,0:T(8,128)S(1)} %get-tuple-element.28.even_ref, f32[256,128]{1,0:T(8,128)S(1)} %get-tuple-element.29.odd_ref, f32[64,128]{1,0:T(8,128)S(1)} %add.19.refs_0_, f32[64,128]{1,0:T(8,128)S(1)} %collective-permute-done.6.refs_1_, ...), custom_call_target="tpu_custom_call" | custom-call | tf_op jit(solution)/shard_map/pallas_call | solution.py:494
  29.5 2.4 %collective-permute-start.10 = (f32[256,128]{1,0:T(8,128)S(1)}, f32[256,128]{1,0:T(8,128)S(1)}, u32[]{:S(2)}, u32[]{:S(2)}) collective-permute-start(f32[256,128]{1,0:T(8,128)S(1)} %get-tuple-element.31.kept_ref), channel_id=1, source_target_pairs={{1,0},{3,2},{0,1},{2,3},{5,4},{7,6},{4,5},{6,7},{9,8},{11,10},{8,9... | collective-permute-start | bytes 393224 | tf_op jit(solution)/shard_map/ppermute | solution.py:522
  31.9 1.7 %collective-permute-start.9 = (f32[256,128]{1,0:T(8,128)S(1)}, f32[256,128]{1,0:T(8,128)S(1)}, u32[]{:S(2)}, u32[]{:S(2)}) collective-permute-start(f32[256,128]{1,0:T(8,128)S(1)} %get-tuple-element.32.sent_ref), channel_id=1, source_target_pairs={{2,0},{0,2},{3,1},{1,3},{6,4},{4,6},{7,5},{5,7},{10,8},{8,10},{11,... | collective-permute-start | bytes 393224 | tf_op jit(solution)/shard_map/ppermute | solution.py:522
  33.6 2.6 %collective-permute-done.10.came1_ref = f32[256,128]{1,0:T(8,128)S(1)} collective-permute-done((f32[256,128]{1,0:T(8,128)S(1)}, f32[256,128]{1,0:T(8,128)S(1)}, u32[]{:S(2)}, u32[]{:S(2)}) %collective-permute-start.10) | collective-permute-done | bytes 131104 | tf_op jit(solution)/shard_map/ppermute | solution.py:522
  36.2 3.2 %collective-permute-done.9.came0_ref = f32[256,128]{1,0:T(8,128)S(1)} collective-permute-done((f32[256,128]{1,0:T(8,128)S(1)}, f32[256,128]{1,0:T(8,128)S(1)}, u32[]{:S(2)}, u32[]{:S(2)}) %collective-permute-start.9) | collective-permute-done | bytes 131104 | tf_op jit(solution)/shard_map/ppermute | solution.py:522
  39.3 4.8 %shard_map.21 = (f32[256,128]{1,0:T(8,128)S(1)}, f32[256,128]{1,0:T(8,128)S(1)}, f32[256,128]{1,0:T(8,128)S(1)}, f32[256,128]{1,0:T(8,128)S(1)}, f32[144,128]{1,0:T(8,128)S(1)}, /*index=5*/f32[144,128]{1,0:T(8,128)S(1)}) custom-call(f32[256,128]{1,0:T(8,128)S(1)} %get-tuple-element.31.kept_ref, f32[256,128]{1,0:T(8,128)S(1)} %get-tuple-element.32.sent_ref, ...), custom_call_target="tpu_custom_call" | custom-call | tf_op jit(solution)/shard_map/pallas_call | solution.py:494
  44.2 1.3 %collective-permute-done.11 = f32[144,128]{1,0:T(8,128)S(1)} collective-permute-done((f32[144,128]{1,0:T(8,128)S(1)}, f32[144,128]{1,0:T(8,128)S(1)}, u32[]{:S(2)}, u32[]{:S(2)}) %collective-permute-start.11) | collective-permute-done | bytes 73760 | tf_op jit(solution)/shard_map/ppermute | solution.py:477
  45.5 1.6 %collective-permute-start.12 = (f32[144,128]{1,0:T(8,128)S(1)}, f32[144,128]{1,0:T(8,128)S(1)}, u32[]{:S(2)}, u32[]{:S(2)}) collective-permute-start(f32[144,128]{1,0:T(8,128)S(1)} %add.20), channel_id=1, source_target_pairs={{0,8},{4,12},{8,0},{12,4},{16,24},{20,28},{24,16},{28,20},{1,9},{5... | collective-permute-start | bytes 221192 | tf_op jit(solution)/shard_map/ppermute | solution.py:477
  47.0 1.4 %collective-permute-start.13 = (f32[144,128]{1,0:T(8,128)S(1)}, f32[144,128]{1,0:T(8,128)S(1)}, u32[]{:S(2)}, u32[]{:S(2)}) collective-permute-start(f32[144,128]{1,0:T(8,128)S(1)} %add.20), channel_id=1, source_target_pairs={{0,16},{4,20},{8,24},{12,28},{16,0},{20,4},{24,8},{28,12},{1,17},{... | collective-permute-start | bytes 221192 | tf_op jit(solution)/shard_map/ppermute | solution.py:477
  48.4 0.6 collective-permute-start.14
  49.0 0.9 %collective-permute-done.12 = f32[144,128]{1,0:T(8,128)S(1)} collective-permute-done((f32[144,128]{1,0:T(8,128)S(1)}, f32[144,128]{1,0:T(8,128)S(1)}, u32[]{:S(2)}, u32[]{:S(2)}) %collective-permute-start.12) | collective-permute-done | bytes 73760 | tf_op jit(solution)/shard_map/ppermute | solution.py:477
  49.9 1.5 %collective-permute-done.13 = f32[144,128]{1,0:T(8,128)S(1)} collective-permute-done((f32[144,128]{1,0:T(8,128)S(1)}, f32[144,128]{1,0:T(8,128)S(1)}, u32[]{:S(2)}, u32[]{:S(2)}) %collective-permute-start.13) | collective-permute-done | bytes 73760 | tf_op jit(solution)/shard_map/ppermute | solution.py:477
  51.4 2.3 %collective-permute-done.14 = f32[144,128]{1,0:T(8,128)S(1)} collective-permute-done((f32[144,128]{1,0:T(8,128)S(1)}, f32[144,128]{1,0:T(8,128)S(1)}, u32[]{:S(2)}, u32[]{:S(2)}) %collective-permute-start.14) | collective-permute-done | bytes 73760 | tf_op jit(solution)/shard_map/ppermute | solution.py:477
  53.8 1.3 %collective-permute-done.15.refs_5_ = f32[144,128]{1,0:T(8,128)S(1)} collective-permute-done((f32[144,128]{1,0:T(8,128)S(1)}, f32[144,128]{1,0:T(8,128)S(1)}, u32[]{:S(2)}, u32[]{:S(2)}) %collective-permute-start.15) | collective-permute-done | bytes 73760 | tf_op jit(solution)/shard_map/ppermute | solution.py:477
  55.0 5.3 %shard_map.22 = (f32[256,128]{1,0:T(8,128)S(1)}, f32[256,128]{1,0:T(8,128)S(1)}) custom-call(f32[256,128]{1,0:T(8,128)S(1)} %get-tuple-element.33.refs_0_, f32[256,128]{1,0:T(8,128)S(1)} %get-tuple-element.34.refs_1_, f32[256,128]{1,0:T(8,128)S(1)} %get-tuple-element.35.refs_2_, f32[256,128]{1,0:T(8,128)S(1)} %get-tuple-element.36.refs_3_, ...), custom_call_target="tpu_custom_call" | custom-call | tf_op jit(solution)/shard_map/pallas_call | solution.py:494
  60.9 6.0 %collective-permute-done.16 = f32[256,128]{1,0:T(8,128)S(1)} collective-permute-done((f32[256,128]{1,0:T(8,128)S(1)}, f32[256,128]{1,0:T(8,128)S(1)}, u32[]{:S(2)}, u32[]{:S(2)}) %collective-permute-start.16) | collective-permute-done | bytes 131104 | tf_op jit(solution)/shard_map/ppermute | solution.py:541
  66.9 0.7 %pad_maximum_fusion = f32[256,256]{1,0:T(8,128)} fusion(f32[256,128]{1,0:T(8,128)S(1)} %get-tuple-element.42, f32[256,128]{1,0:T(8,128)S(1)} %get-tuple-element.41), kind=kLoop, calls=%fused_computation | loop fusion | flops 65536 | bytes 524288 | tf_op jit(solution)/shard_map/concatenate | solution.py:545
  (16 shorter events, 3.2 us)
Async XLA Ops:
  0.0 0.9 %copy-start = (f32[256,256]{1,0:T(8,128)S(1)}, f32[256,256]{1,0:T(8,128)}, u32[]{:S(2)}) copy-start(f32[256,256]{1,0:T(8,128)} %basis_ref.1) | copy-start | bytes 786436
  2.1 1.4 %collective-permute-start = (f32[64,128]{1,0:T(8,128)S(1)}, f32[64,128]{1,0:T(8,128)S(1)}, u32[]{:S(2)}, u32[]{:S(2)}) collective-permute-start(f32[64,128]{1,0:T(8,128)S(1)} %get-tuple-element.25), channel_id=1, source_target_pairs={{0,4},{4,0},{8,12},{12,8},{16,20},{20,16},{24,28},{28,24},{1,5},{5... | collective-permute-start | bytes 98312 | tf_op jit(solution)/shard_map/ppermute | solution.py:477
  3.5 4.7 %collective-permute-start.1 = (f32[64,128]{1,0:T(8,128)S(1)}, f32[64,128]{1,0:T(8,128)S(1)}, u32[]{:S(2)}, u32[]{:S(2)}) collective-permute-start(f32[64,128]{1,0:T(8,128)S(1)} %add.18.refs_0_), channel_id=1, source_target_pairs={{0,8},{4,12},{8,0},{12,4},{16,24},{20,28},{24,16},{28,20},{1,9},{5... | collective-permute-start | bytes 98312 | tf_op jit(solution)/shard_map/ppermute | solution.py:477
  6.3 3.9 %collective-permute-start.2 = (f32[64,128]{1,0:T(8,128)S(1)}, f32[64,128]{1,0:T(8,128)S(1)}, u32[]{:S(2)}, u32[]{:S(2)}) collective-permute-start(f32[64,128]{1,0:T(8,128)S(1)} %add.18.refs_0_), channel_id=1, source_target_pairs={{0,16},{4,20},{8,24},{12,28},{16,0},{20,4},{24,8},{28,12},{1,17},{... | collective-permute-start | bytes 98312 | tf_op jit(solution)/shard_map/ppermute | solution.py:477
  7.8 4.8 %collective-permute-start.3 = (f32[64,128]{1,0:T(8,128)S(1)}, f32[64,128]{1,0:T(8,128)S(1)}, u32[]{:S(2)}, u32[]{:S(2)}) collective-permute-start(f32[64,128]{1,0:T(8,128)S(1)} %add.18.refs_0_), channel_id=1, source_target_pairs={{0,24},{4,28},{8,16},{12,20},{16,8},{20,12},{24,0},{28,4},{1,25},{... | collective-permute-start | bytes 98312 | tf_op jit(solution)/shard_map/ppermute | solution.py:477
  14.4 5.3 %collective-permute-start.4 = (f32[256,128]{1,0:T(8,128)S(1)}, f32[256,128]{1,0:T(8,128)S(1)}, u32[]{:S(2)}, u32[]{:S(2)}) collective-permute-start(f32[256,128]{1,0:T(8,128)S(1)} %get-tuple-element.27), channel_id=1, source_target_pairs={{1,0},{0,2},{3,1},{2,3},{5,4},{4,6},{7,5},{6,7},{9,8},{8,10},{11,9... | collective-permute-start | bytes 393224 | tf_op jit(solution)/shard_map/ppermute | solution.py:519
  20.6 1.3 %collective-permute-start.5 = (f32[64,128]{1,0:T(8,128)S(1)}, f32[64,128]{1,0:T(8,128)S(1)}, u32[]{:S(2)}, u32[]{:S(2)}) collective-permute-start(f32[64,128]{1,0:T(8,128)S(1)} %get-tuple-element.30), channel_id=1, source_target_pairs={{0,4},{4,0},{8,12},{12,8},{16,20},{20,16},{24,28},{28,24},{1,5},{5... | collective-permute-start | bytes 98312 | tf_op jit(solution)/shard_map/ppermute | solution.py:477
  21.9 3.9 %collective-permute-start.6 = (f32[64,128]{1,0:T(8,128)S(1)}, f32[64,128]{1,0:T(8,128)S(1)}, u32[]{:S(2)}, u32[]{:S(2)}) collective-permute-start(f32[64,128]{1,0:T(8,128)S(1)} %add.19.refs_0_), channel_id=1, source_target_pairs={{0,8},{4,12},{8,0},{12,4},{16,24},{20,28},{24,16},{28,20},{1,9},{5... | collective-permute-start | bytes 98312 | tf_op jit(solution)/shard_map/ppermute | solution.py:477
  22.4 4.3 %collective-permute-start.7 = (f32[64,128]{1,0:T(8,128)S(1)}, f32[64,128]{1,0:T(8,128)S(1)}, u32[]{:S(2)}, u32[]{:S(2)}) collective-permute-start(f32[64,128]{1,0:T(8,128)S(1)} %add.19.refs_0_), channel_id=1, source_target_pairs={{0,16},{4,20},{8,24},{12,28},{16,0},{20,4},{24,8},{28,12},{1,17},{... | collective-permute-start | bytes 98312 | tf_op jit(solution)/shard_map/ppermute | solution.py:477
  22.9 4.8 %collective-permute-start.8 = (f32[64,128]{1,0:T(8,128)S(1)}, f32[64,128]{1,0:T(8,128)S(1)}, u32[]{:S(2)}, u32[]{:S(2)}) collective-permute-start(f32[64,128]{1,0:T(8,128)S(1)} %add.19.refs_0_), channel_id=1, source_target_pairs={{0,24},{4,28},{8,16},{12,20},{16,8},{20,12},{24,0},{28,4},{1,25},{... | collective-permute-start | bytes 98312 | tf_op jit(solution)/shard_map/ppermute | solution.py:477
  29.5 6.7 %collective-permute-start.10 = (f32[256,128]{1,0:T(8,128)S(1)}, f32[256,128]{1,0:T(8,128)S(1)}, u32[]{:S(2)}, u32[]{:S(2)}) collective-permute-start(f32[256,128]{1,0:T(8,128)S(1)} %get-tuple-element.31.kept_ref), channel_id=1, source_target_pairs={{1,0},{3,2},{0,1},{2,3},{5,4},{7,6},{4,5},{6,7},{9,8},{11,10},{8,9... | collective-permute-start | bytes 393224 | tf_op jit(solution)/shard_map/ppermute | solution.py:522
  31.9 7.5 %collective-permute-start.9 = (f32[256,128]{1,0:T(8,128)S(1)}, f32[256,128]{1,0:T(8,128)S(1)}, u32[]{:S(2)}, u32[]{:S(2)}) collective-permute-start(f32[256,128]{1,0:T(8,128)S(1)} %get-tuple-element.32.sent_ref), channel_id=1, source_target_pairs={{2,0},{0,2},{3,1},{1,3},{6,4},{4,6},{7,5},{5,7},{10,8},{8,10},{11,... | collective-permute-start | bytes 393224 | tf_op jit(solution)/shard_map/ppermute | solution.py:522
  44.1 1.3 %collective-permute-start.11 = (f32[144,128]{1,0:T(8,128)S(1)}, f32[144,128]{1,0:T(8,128)S(1)}, u32[]{:S(2)}, u32[]{:S(2)}) collective-permute-start(f32[144,128]{1,0:T(8,128)S(1)} %get-tuple-element.38), channel_id=1, source_target_pairs={{0,4},{4,0},{8,12},{12,8},{16,20},{20,16},{24,28},{28,24},{1,5},{5... | collective-permute-start | bytes 221192 | tf_op jit(solution)/shard_map/ppermute | solution.py:477
  45.5 4.4 %collective-permute-start.12 = (f32[144,128]{1,0:T(8,128)S(1)}, f32[144,128]{1,0:T(8,128)S(1)}, u32[]{:S(2)}, u32[]{:S(2)}) collective-permute-start(f32[144,128]{1,0:T(8,128)S(1)} %add.20), channel_id=1, source_target_pairs={{0,8},{4,12},{8,0},{12,4},{16,24},{20,28},{24,16},{28,20},{1,9},{5... | collective-permute-start | bytes 221192 | tf_op jit(solution)/shard_map/ppermute | solution.py:477
  47.0 4.4 %collective-permute-start.13 = (f32[144,128]{1,0:T(8,128)S(1)}, f32[144,128]{1,0:T(8,128)S(1)}, u32[]{:S(2)}, u32[]{:S(2)}) collective-permute-start(f32[144,128]{1,0:T(8,128)S(1)} %add.20), channel_id=1, source_target_pairs={{0,16},{4,20},{8,24},{12,28},{16,0},{20,4},{24,8},{28,12},{1,17},{... | collective-permute-start | bytes 221192 | tf_op jit(solution)/shard_map/ppermute | solution.py:477
  48.4 5.3 %collective-permute-start.14 = (f32[144,128]{1,0:T(8,128)S(1)}, f32[144,128]{1,0:T(8,128)S(1)}, u32[]{:S(2)}, u32[]{:S(2)}) collective-permute-start(f32[144,128]{1,0:T(8,128)S(1)} %add.20), channel_id=1, source_target_pairs={{0,24},{4,28},{8,16},{12,20},{16,8},{20,12},{24,0},{28,4},{1,25},{... | collective-permute-start | bytes 221192 | tf_op jit(solution)/shard_map/ppermute | solution.py:477
  53.7 1.3 %collective-permute-start.15 = (f32[144,128]{1,0:T(8,128)S(1)}, f32[144,128]{1,0:T(8,128)S(1)}, u32[]{:S(2)}, u32[]{:S(2)}) collective-permute-start(f32[144,128]{1,0:T(8,128)S(1)} %add_add_fusion.refs_4_), channel_id=1, source_target_pairs={{0,4},{4,0},{8,12},{12,8},{16,20},{20,16},{24,28},{28,24},{1,5},{5... | collective-permute-start | bytes 221192 | tf_op jit(solution)/shard_map/ppermute | solution.py:477
  60.4 6.5 %collective-permute-start.16 = (f32[256,128]{1,0:T(8,128)S(1)}, f32[256,128]{1,0:T(8,128)S(1)}, u32[]{:S(2)}, u32[]{:S(2)}) collective-permute-start(f32[256,128]{1,0:T(8,128)S(1)} %get-tuple-element.39), channel_id=1, source_target_pairs={{2,0},{0,1},{3,2},{1,3},{6,4},{4,5},{7,6},{5,7},{10,8},{8,9},{11,1... | collective-permute-start | bytes 393224 | tf_op jit(solution)/shard_map/ppermute | solution.py:541

commit v3 on v2

--- a/solution.py
+++ b/solution.py
@@ -188,6 +188,28 @@
         )
 
 
+def backwards(x):
+    return jnp.take_along_axis(x, x.shape[1] - 1 - lanes_of(x), axis=1)
+
+
+def dense_bands(even, odd, diags):
+    width = even.shape[1]
+    gram = lax.dot_general(
+        jnp.concatenate((even, odd), axis=1),
+        jnp.concatenate((backwards(even), backwards(odd)), axis=1),
+        (((0,), (0,)), ((), ())),
+        precision=lax.Precision.HIGHEST,
+        preferred_element_type=jnp.float32,
+    )
+    bands = []
+    for near in (0, width):
+        for far in (0, width):
+            quadrant = gram[far : far + width, near : near + width]
+            aligned = pltpu.roll(quadrant, 1, 1, stride=1, stride_axis=0)
+            bands.append(jnp.transpose(aligned)[:diags])
+    return bands
+
+
 def open_kernel(basis_ref, even_ref, odd_ref, band_ref):
     width = basis_ref.shape[1] // 2
     table = separator(width, False)
@@ -210,10 +232,12 @@
 
 def jacobi_angle(diag_even, diag_odd, coupling):
     spread = diag_even - diag_odd
-    radius = jnp.sqrt(spread * spread + 4.0 * coupling * coupling)
-    widened = radius + jnp.abs(spread)
-    larger = jnp.sqrt(widened / (2.0 * radius))
-    smaller = coupling / (radius * larger)
+    square = spread * spread + 4.0 * coupling * coupling
+    inverse = lax.rsqrt(square)
+    larger_square = (square * inverse + jnp.abs(spread)) * (0.5 * inverse)
+    larger_inverse = lax.rsqrt(larger_square)
+    larger = larger_square * larger_inverse
+    smaller = coupling * inverse * larger_inverse
     forward = spread >= 0.0
     sign = jnp.where(coupling > 0.0, 1.0, jnp.where(coupling < 0.0, -1.0, 0.0))
     cosine = jnp.where(forward, larger, jnp.abs(smaller))
@@ -289,28 +313,39 @@
     return even_new, odd_new
 
 
-def move_columns_back(even, odd):
+def columns_home(even, odd):
     lane = lanes_of(even)
-    first, last = lane == 0, lane == even.shape[1] - 1
-    back = left(even, 1)
-    even_old = jnp.where(first, even, jnp.where(last, odd, back))
-    odd_old = jnp.where(first, back, right(odd, 1))
-    return even_old, odd_old
+    by, end = JSTEPS - 1, even.shape[1] - 1
+    mixed = jnp.where(jnp.logical_and(lane >= 1, lane <= by), right(odd, by + 1), even)
+    source = jnp.where(lane <= end - by, lane + by, end + 1 - lane)
+    even_home = jnp.take_along_axis(mixed, jnp.where(lane == 0, 0, source), axis=1)
+    mixed = jnp.where(lane > end - by, left(even, by + 1), odd)
+    source = jnp.where(lane >= by, lane - by, end - lane)
+    odd_home = jnp.take_along_axis(mixed, source, axis=1)
+    return even_home, odd_home
+
+
+def trim(bands, reach):
+    rows = min(bands[0].shape[0], -(-(reach + 1) // 8) * 8)
+    return [band[:rows] for band in bands]
 
 
 def angles_of(bands, carried):
     angles = []
+    ahead = 2 * (JSTEPS - 1)
+    kept = 2 * ahead if carried else 0
     for step in range(JSTEPS):
-        ee, eo, oe, oo = bands
+        ee, eo, oe, oo = trim(bands, kept + ahead - 2 * step)
         cosine, sine = jacobi_angle(ee[0:1], oo[0:1], eo[0:1])
         angles.append((cosine, sine))
+        bands = ee, eo, oe, oo
         if carried or step < JSTEPS - 1:
             bands = turn_bands(ee, eo, oe, oo, cosine, sine)
         if step < JSTEPS - 1:
             bands = move_bands(*bands)
     if carried:
         for step in range(JSTEPS - 1):
-            bands = move_bands_back(*bands)
+            bands = move_bands_back(*trim(bands, kept - 2 * step))
     return angles, bands
 
 
@@ -319,9 +354,7 @@
         even, odd = cosine * even + sine * odd, cosine * odd - sine * even
         if step < JSTEPS - 1:
             even, odd = move_columns(even, odd)
-    for step in range(JSTEPS - 1):
-        even, odd = move_columns_back(even, odd)
-    return even, odd
+    return columns_home(even, odd)
 
 
 def turn_kernel(sends_first, even_ref, odd_ref, *refs):
@@ -405,7 +438,8 @@
         ref[...] = value
     corner = cross_partial(*columns, among(is_second[0]), among(is_second[1]))
     for i in (0, 1):
-        store_bands(*columns[2 * i : 2 * i + 2], parts.at[i], FAR_REACH, FAR_DIAGS)
+        for q, band in enumerate(dense_bands(*columns[2 * i : 2 * i + 2], FAR_DIAGS)):
+            parts[i, q * FAR_DIAGS : (q + 1) * FAR_DIAGS, :] = band
         parts[i, 4 * FAR_DIAGS :, :] = corner[i * NEAR : (i + 1) * NEAR]
     odd_core = lax.axis_index("row") % 2
     mine_ref[...] = parts[odd_core]

time: 67.8 us -> 62.7 us (0.925)
  Pallas kernels: 15.6 us -> 10.7 us
    pallas_call x6, Pallas kernels: 15.6 us -> 10.7 us  [call(): pl.pallas_call(kernel, out_shape=out, scratch_shapes=[pltpu.VMEM(shape, j...]
where the time goes in v3:
time: 62.7 us; the launch traced here: 62.6 us
  waiting for transfers between devices  30.7 us (49%)
  starting transfers between devices  19.4 us (31%)
  Pallas kernels  10.7 us (17%)
  local copies, waits for them, and re-layouts  0.95 us (2%)
  other arithmetic  0.78 us (1%)
    ppermute x13, waiting for transfers between devices, swap(): lax.ppermute(x, axis, [(i, i ^ mask) for i in range(lax.axis_size(axis))])  16.4 us
    ppermute x13, starting transfers between devices, swap(): lax.ppermute(x, axis, [(i, i ^ mask) for i in range(lax.axis_size(axis))])  12.1 us
    pallas_call x6, Pallas kernels, call(): pl.pallas_call(kernel, out_shape=out, scratch_shapes=[pltpu.VMEM(shape, j...  10.7 us
    ppermute x2, waiting for transfers between devices, per_device(): came = lax.ppermute(sent, 'pair', sends)  8.51 us
    ppermute x2, waiting for transfers between devices, per_device(): lax.ppermute(x, 'pair', s)  5.77 us
    ppermute x2, starting transfers between devices, per_device(): lax.ppermute(x, 'pair', s)  4.09 us
    ppermute x2, starting transfers between devices, per_device(): came = lax.ppermute(sent, 'pair', sends)  3.16 us
  transfers between devices with their start and end apart: 17, of which 17 were waited for; matrix products, arithmetic and copies ran while one was open for 0% of the time, Pallas kernels for 0%

profile of v3, /device:TPU:0, one launch (start us, length us, event | category | flops | bytes accessed | tf_op | source)
XLA Modules:
  0.0 62.6 jit_solution(6908436291877111340)
XLA Ops:
  0.0 0.9 %copy-done = f32[256,256]{1,0:T(8,128)S(1)} copy-done((f32[256,256]{1,0:T(8,128)S(1)}, f32[256,256]{1,0:T(8,128)}, u32[]{:S(2)}) %copy-start) | copy-done | bytes 262168
  1.0 1.1 %shard_map.17 = (f32[256,128]{1,0:T(8,128)S(1)}, f32[256,128]{1,0:T(8,128)S(1)}, f32[64,128]{1,0:T(8,128)S(1)}) custom-call(f32[256,256]{1,0:T(8,128)S(1)} %copy-done), custom_call_target="tpu_custom_call" | custom-call | tf_op jit(solution)/shard_map/pallas_call | solution.py:528
  2.6 0.9 %collective-permute-done = f32[64,128]{1,0:T(8,128)S(1)} collective-permute-done((f32[64,128]{1,0:T(8,128)S(1)}, f32[64,128]{1,0:T(8,128)S(1)}, u32[]{:S(2)}, u32[]{:S(2)}) %collective-permute-start) | collective-permute-done | bytes 32800 | tf_op jit(solution)/shard_map/ppermute | solution.py:511
  3.5 2.8 %collective-permute-start.1 = (f32[64,128]{1,0:T(8,128)S(1)}, f32[64,128]{1,0:T(8,128)S(1)}, u32[]{:S(2)}, u32[]{:S(2)}) collective-permute-start(f32[64,128]{1,0:T(8,128)S(1)} %add.18.refs_0_), channel_id=1, source_target_pairs={{0,8},{4,12},{8,0},{12,4},{16,24},{20,28},{24,16},{28,20},{1,9},{5... | collective-permute-start | bytes 98312 | tf_op jit(solution)/shard_map/ppermute | solution.py:511
  6.3 1.5 %collective-permute-start.2 = (f32[64,128]{1,0:T(8,128)S(1)}, f32[64,128]{1,0:T(8,128)S(1)}, u32[]{:S(2)}, u32[]{:S(2)}) collective-permute-start(f32[64,128]{1,0:T(8,128)S(1)} %add.18.refs_0_), channel_id=1, source_target_pairs={{0,16},{4,20},{8,24},{12,28},{16,0},{20,4},{24,8},{28,12},{1,17},{... | collective-permute-start | bytes 98312 | tf_op jit(solution)/shard_map/ppermute | solution.py:511
  8.2 2.0 %collective-permute-done.2.refs_2_ = f32[64,128]{1,0:T(8,128)S(1)} collective-permute-done((f32[64,128]{1,0:T(8,128)S(1)}, f32[64,128]{1,0:T(8,128)S(1)}, u32[]{:S(2)}, u32[]{:S(2)}) %collective-permute-start.2) | collective-permute-done | bytes 32800 | tf_op jit(solution)/shard_map/ppermute | solution.py:511
  10.2 2.4 %collective-permute-done.3.refs_3_ = f32[64,128]{1,0:T(8,128)S(1)} collective-permute-done((f32[64,128]{1,0:T(8,128)S(1)}, f32[64,128]{1,0:T(8,128)S(1)}, u32[]{:S(2)}, u32[]{:S(2)}) %collective-permute-start.3) | collective-permute-done | bytes 32800 | tf_op jit(solution)/shard_map/ppermute | solution.py:511
  12.7 1.3 %shard_map.18 = (f32[256,128]{1,0:T(8,128)S(1)}, f32[256,128]{1,0:T(8,128)S(1)}) custom-call(f32[256,128]{1,0:T(8,128)S(1)} %get-tuple-element.23.even_ref, f32[256,128]{1,0:T(8,128)S(1)} %get-tuple-element.24.odd_ref, f32[64,128]{1,0:T(8,128)S(1)} %add.18.refs_0_, f32[64,128]{1,0:T(8,128)S(1)} %collective-permute-done.1.refs_1_, ...), custom_call_target="tpu_custom_call" | custom-call | tf_op jit(solution)/shard_map/pallas_call | solution.py:528
  13.9 2.6 %collective-permute-start.4 = (f32[256,128]{1,0:T(8,128)S(1)}, f32[256,128]{1,0:T(8,128)S(1)}, u32[]{:S(2)}, u32[]{:S(2)}) collective-permute-start(f32[256,128]{1,0:T(8,128)S(1)} %get-tuple-element.27), channel_id=1, source_target_pairs={{1,0},{0,2},{3,1},{2,3},{5,4},{4,6},{7,5},{6,7},{9,8},{8,10},{11,9... | collective-permute-start | bytes 393224 | tf_op jit(solution)/shard_map/ppermute | solution.py:553
  16.6 2.5 %collective-permute-done.4.came_ref = f32[256,128]{1,0:T(8,128)S(1)} collective-permute-done((f32[256,128]{1,0:T(8,128)S(1)}, f32[256,128]{1,0:T(8,128)S(1)}, u32[]{:S(2)}, u32[]{:S(2)}) %collective-permute-start.4) | collective-permute-done | bytes 131104 | tf_op jit(solution)/shard_map/ppermute | solution.py:553
  19.1 0.9 %shard_map.19 = (f32[256,128]{1,0:T(8,128)S(1)}, f32[256,128]{1,0:T(8,128)S(1)}, f32[64,128]{1,0:T(8,128)S(1)}) custom-call(f32[256,128]{1,0:T(8,128)S(1)} %get-tuple-element.26.kept_ref, f32[256,128]{1,0:T(8,128)S(1)} %collective-permute-done.4.came_ref), custom_call_target="tpu_custom_call" | custom-call | tf_op jit(solution)/shard_map/pallas_call | solution.py:528
  20.0 1.2 %collective-permute-done.5 = f32[64,128]{1,0:T(8,128)S(1)} collective-permute-done((f32[64,128]{1,0:T(8,128)S(1)}, f32[64,128]{1,0:T(8,128)S(1)}, u32[]{:S(2)}, u32[]{:S(2)}) %collective-permute-start.5) | collective-permute-done | bytes 32800 | tf_op jit(solution)/shard_map/ppermute | solution.py:511
  22.3 2.4 %collective-permute-start.8 = (f32[64,128]{1,0:T(8,128)S(1)}, f32[64,128]{1,0:T(8,128)S(1)}, u32[]{:S(2)}, u32[]{:S(2)}) collective-permute-start(f32[64,128]{1,0:T(8,128)S(1)} %add.19.refs_0_), channel_id=1, source_target_pairs={{0,24},{4,28},{8,16},{12,20},{16,8},{20,12},{24,0},{28,4},{1,25},{... | collective-permute-start | bytes 98312 | tf_op jit(solution)/shard_map/ppermute | solution.py:511
  25.1 0.9 %collective-permute-done.7.refs_2_ = f32[64,128]{1,0:T(8,128)S(1)} collective-permute-done((f32[64,128]{1,0:T(8,128)S(1)}, f32[64,128]{1,0:T(8,128)S(1)}, u32[]{:S(2)}, u32[]{:S(2)}) %collective-permute-start.7) | collective-permute-done | bytes 32800 | tf_op jit(solution)/shard_map/ppermute | solution.py:511
  26.0 1.1 %collective-permute-done.8.refs_3_ = f32[64,128]{1,0:T(8,128)S(1)} collective-permute-done((f32[64,128]{1,0:T(8,128)S(1)}, f32[64,128]{1,0:T(8,128)S(1)}, u32[]{:S(2)}, u32[]{:S(2)}) %collective-permute-start.8) | collective-permute-done | bytes 32800 | tf_op jit(solution)/shard_map/ppermute | solution.py:511
  27.1 1.3 %shard_map.20 = (f32[256,128]{1,0:T(8,128)S(1)}, f32[256,128]{1,0:T(8,128)S(1)}) custom-call(f32[256,128]{1,0:T(8,128)S(1)} %get-tuple-element.28.even_ref, f32[256,128]{1,0:T(8,128)S(1)} %get-tuple-element.29.odd_ref, f32[64,128]{1,0:T(8,128)S(1)} %add.19.refs_0_, f32[64,128]{1,0:T(8,128)S(1)} %collective-permute-done.6.refs_1_, ...), custom_call_target="tpu_custom_call" | custom-call | tf_op jit(solution)/shard_map/pallas_call | solution.py:528
  28.4 2.4 %collective-permute-start.10 = (f32[256,128]{1,0:T(8,128)S(1)}, f32[256,128]{1,0:T(8,128)S(1)}, u32[]{:S(2)}, u32[]{:S(2)}) collective-permute-start(f32[256,128]{1,0:T(8,128)S(1)} %get-tuple-element.31.kept_ref), channel_id=1, source_target_pairs={{1,0},{3,2},{0,1},{2,3},{5,4},{7,6},{4,5},{6,7},{9,8},{11,10},{8,9... | collective-permute-start | bytes 393224 | tf_op jit(solution)/shard_map/ppermute | solution.py:556
  30.8 1.7 %collective-permute-start.9 = (f32[256,128]{1,0:T(8,128)S(1)}, f32[256,128]{1,0:T(8,128)S(1)}, u32[]{:S(2)}, u32[]{:S(2)}) collective-permute-start(f32[256,128]{1,0:T(8,128)S(1)} %get-tuple-element.32.sent_ref), channel_id=1, source_target_pairs={{2,0},{0,2},{3,1},{1,3},{6,4},{4,6},{7,5},{5,7},{10,8},{8,10},{11,... | collective-permute-start | bytes 393224 | tf_op jit(solution)/shard_map/ppermute | solution.py:556
  32.4 2.6 %collective-permute-done.10.came1_ref = f32[256,128]{1,0:T(8,128)S(1)} collective-permute-done((f32[256,128]{1,0:T(8,128)S(1)}, f32[256,128]{1,0:T(8,128)S(1)}, u32[]{:S(2)}, u32[]{:S(2)}) %collective-permute-start.10) | collective-permute-done | bytes 131104 | tf_op jit(solution)/shard_map/ppermute | solution.py:556
  35.0 3.2 %collective-permute-done.9.came0_ref = f32[256,128]{1,0:T(8,128)S(1)} collective-permute-done((f32[256,128]{1,0:T(8,128)S(1)}, f32[256,128]{1,0:T(8,128)S(1)}, u32[]{:S(2)}, u32[]{:S(2)}) %collective-permute-start.9) | collective-permute-done | bytes 131104 | tf_op jit(solution)/shard_map/ppermute | solution.py:556
  38.2 2.0 %shard_map.21 = (f32[256,128]{1,0:T(8,128)S(1)}, f32[256,128]{1,0:T(8,128)S(1)}, f32[256,128]{1,0:T(8,128)S(1)}, f32[256,128]{1,0:T(8,128)S(1)}, f32[144,128]{1,0:T(8,128)S(1)}, /*index=5*/f32[144,128]{1,0:T(8,128)S(1)}) custom-call(f32[256,128]{1,0:T(8,128)S(1)} %get-tuple-element.31.kept_ref, f32[256,128]{1,0:T(8,128)S(1)} %get-tuple-element.32.sent_ref, ...), custom_call_target="tpu_custom_call" | custom-call | tf_op jit(solution)/shard_map/pallas_call | solution.py:528
  40.3 1.3 %collective-permute-done.11 = f32[144,128]{1,0:T(8,128)S(1)} collective-permute-done((f32[144,128]{1,0:T(8,128)S(1)}, f32[144,128]{1,0:T(8,128)S(1)}, u32[]{:S(2)}, u32[]{:S(2)}) %collective-permute-start.11) | collective-permute-done | bytes 73760 | tf_op jit(solution)/shard_map/ppermute | solution.py:511
  41.5 1.6 %collective-permute-start.12 = (f32[144,128]{1,0:T(8,128)S(1)}, f32[144,128]{1,0:T(8,128)S(1)}, u32[]{:S(2)}, u32[]{:S(2)}) collective-permute-start(f32[144,128]{1,0:T(8,128)S(1)} %add.20), channel_id=1, source_target_pairs={{0,8},{4,12},{8,0},{12,4},{16,24},{20,28},{24,16},{28,20},{1,9},{5... | collective-permute-start | bytes 221192 | tf_op jit(solution)/shard_map/ppermute | solution.py:511
  43.1 1.4 %collective-permute-start.13 = (f32[144,128]{1,0:T(8,128)S(1)}, f32[144,128]{1,0:T(8,128)S(1)}, u32[]{:S(2)}, u32[]{:S(2)}) collective-permute-start(f32[144,128]{1,0:T(8,128)S(1)} %add.20), channel_id=1, source_target_pairs={{0,16},{4,20},{8,24},{12,28},{16,0},{20,4},{24,8},{28,12},{1,17},{... | collective-permute-start | bytes 221192 | tf_op jit(solution)/shard_map/ppermute | solution.py:511
  44.5 0.6 collective-permute-start.14
  45.1 0.9 %collective-permute-done.12 = f32[144,128]{1,0:T(8,128)S(1)} collective-permute-done((f32[144,128]{1,0:T(8,128)S(1)}, f32[144,128]{1,0:T(8,128)S(1)}, u32[]{:S(2)}, u32[]{:S(2)}) %collective-permute-start.12) | collective-permute-done | bytes 73760 | tf_op jit(solution)/shard_map/ppermute | solution.py:511
  46.0 1.5 %collective-permute-done.13 = f32[144,128]{1,0:T(8,128)S(1)} collective-permute-done((f32[144,128]{1,0:T(8,128)S(1)}, f32[144,128]{1,0:T(8,128)S(1)}, u32[]{:S(2)}, u32[]{:S(2)}) %collective-permute-start.13) | collective-permute-done | bytes 73760 | tf_op jit(solution)/shard_map/ppermute | solution.py:511
  47.5 2.3 %collective-permute-done.14 = f32[144,128]{1,0:T(8,128)S(1)} collective-permute-done((f32[144,128]{1,0:T(8,128)S(1)}, f32[144,128]{1,0:T(8,128)S(1)}, u32[]{:S(2)}, u32[]{:S(2)}) %collective-permute-start.14) | collective-permute-done | bytes 73760 | tf_op jit(solution)/shard_map/ppermute | solution.py:511
  49.9 1.3 %collective-permute-done.15.refs_5_ = f32[144,128]{1,0:T(8,128)S(1)} collective-permute-done((f32[144,128]{1,0:T(8,128)S(1)}, f32[144,128]{1,0:T(8,128)S(1)}, u32[]{:S(2)}, u32[]{:S(2)}) %collective-permute-start.15) | collective-permute-done | bytes 73760 | tf_op jit(solution)/shard_map/ppermute | solution.py:511
  51.1 4.2 %shard_map.22 = (f32[256,128]{1,0:T(8,128)S(1)}, f32[256,128]{1,0:T(8,128)S(1)}) custom-call(f32[256,128]{1,0:T(8,128)S(1)} %get-tuple-element.33.refs_0_, f32[256,128]{1,0:T(8,128)S(1)} %get-tuple-element.34.refs_1_, f32[256,128]{1,0:T(8,128)S(1)} %get-tuple-element.35.refs_2_, f32[256,128]{1,0:T(8,128)S(1)} %get-tuple-element.36.refs_3_, ...), custom_call_target="tpu_custom_call" | custom-call | tf_op jit(solution)/shard_map/pallas_call | solution.py:528
  55.8 6.0 %collective-permute-done.16 = f32[256,128]{1,0:T(8,128)S(1)} collective-permute-done((f32[256,128]{1,0:T(8,128)S(1)}, f32[256,128]{1,0:T(8,128)S(1)}, u32[]{:S(2)}, u32[]{:S(2)}) %collective-permute-start.16) | collective-permute-done | bytes 131104 | tf_op jit(solution)/shard_map/ppermute | solution.py:575
  61.8 0.7 %pad_maximum_fusion = f32[256,256]{1,0:T(8,128)} fusion(f32[256,128]{1,0:T(8,128)S(1)} %get-tuple-element.42, f32[256,128]{1,0:T(8,128)S(1)} %get-tuple-element.41), kind=kLoop, calls=%fused_computation | loop fusion | flops 65536 | bytes 524288 | tf_op jit(solution)/shard_map/concatenate | solution.py:579
  (16 shorter events, 3.1 us)
Async XLA Ops:
  0.0 0.9 %copy-start = (f32[256,256]{1,0:T(8,128)S(1)}, f32[256,256]{1,0:T(8,128)}, u32[]{:S(2)}) copy-start(f32[256,256]{1,0:T(8,128)} %basis_ref.1) | copy-start | bytes 786436
  2.1 1.4 %collective-permute-start = (f32[64,128]{1,0:T(8,128)S(1)}, f32[64,128]{1,0:T(8,128)S(1)}, u32[]{:S(2)}, u32[]{:S(2)}) collective-permute-start(f32[64,128]{1,0:T(8,128)S(1)} %get-tuple-element.25), channel_id=1, source_target_pairs={{0,4},{4,0},{8,12},{12,8},{16,20},{20,16},{24,28},{28,24},{1,5},{5... | collective-permute-start | bytes 98312 | tf_op jit(solution)/shard_map/ppermute | solution.py:511
  3.5 4.7 %collective-permute-start.1 = (f32[64,128]{1,0:T(8,128)S(1)}, f32[64,128]{1,0:T(8,128)S(1)}, u32[]{:S(2)}, u32[]{:S(2)}) collective-permute-start(f32[64,128]{1,0:T(8,128)S(1)} %add.18.refs_0_), channel_id=1, source_target_pairs={{0,8},{4,12},{8,0},{12,4},{16,24},{20,28},{24,16},{28,20},{1,9},{5... | collective-permute-start | bytes 98312 | tf_op jit(solution)/shard_map/ppermute | solution.py:511
  6.3 3.9 %collective-permute-start.2 = (f32[64,128]{1,0:T(8,128)S(1)}, f32[64,128]{1,0:T(8,128)S(1)}, u32[]{:S(2)}, u32[]{:S(2)}) collective-permute-start(f32[64,128]{1,0:T(8,128)S(1)} %add.18.refs_0_), channel_id=1, source_target_pairs={{0,16},{4,20},{8,24},{12,28},{16,0},{20,4},{24,8},{28,12},{1,17},{... | collective-permute-start | bytes 98312 | tf_op jit(solution)/shard_map/ppermute | solution.py:511
  7.8 4.8 %collective-permute-start.3 = (f32[64,128]{1,0:T(8,128)S(1)}, f32[64,128]{1,0:T(8,128)S(1)}, u32[]{:S(2)}, u32[]{:S(2)}) collective-permute-start(f32[64,128]{1,0:T(8,128)S(1)} %add.18.refs_0_), channel_id=1, source_target_pairs={{0,24},{4,28},{8,16},{12,20},{16,8},{20,12},{24,0},{28,4},{1,25},{... | collective-permute-start | bytes 98312 | tf_op jit(solution)/shard_map/ppermute | solution.py:511
  13.9 5.2 %collective-permute-start.4 = (f32[256,128]{1,0:T(8,128)S(1)}, f32[256,128]{1,0:T(8,128)S(1)}, u32[]{:S(2)}, u32[]{:S(2)}) collective-permute-start(f32[256,128]{1,0:T(8,128)S(1)} %get-tuple-element.27), channel_id=1, source_target_pairs={{1,0},{0,2},{3,1},{2,3},{5,4},{4,6},{7,5},{6,7},{9,8},{8,10},{11,9... | collective-permute-start | bytes 393224 | tf_op jit(solution)/shard_map/ppermute | solution.py:553
  20.0 1.3 %collective-permute-start.5 = (f32[64,128]{1,0:T(8,128)S(1)}, f32[64,128]{1,0:T(8,128)S(1)}, u32[]{:S(2)}, u32[]{:S(2)}) collective-permute-start(f32[64,128]{1,0:T(8,128)S(1)} %get-tuple-element.30), channel_id=1, source_target_pairs={{0,4},{4,0},{8,12},{12,8},{16,20},{20,16},{24,28},{28,24},{1,5},{5... | collective-permute-start | bytes 98312 | tf_op jit(solution)/shard_map/ppermute | solution.py:511
  21.2 3.9 %collective-permute-start.6 = (f32[64,128]{1,0:T(8,128)S(1)}, f32[64,128]{1,0:T(8,128)S(1)}, u32[]{:S(2)}, u32[]{:S(2)}) collective-permute-start(f32[64,128]{1,0:T(8,128)S(1)} %add.19.refs_0_), channel_id=1, source_target_pairs={{0,8},{4,12},{8,0},{12,4},{16,24},{20,28},{24,16},{28,20},{1,9},{5... | collective-permute-start | bytes 98312 | tf_op jit(solution)/shard_map/ppermute | solution.py:511
  21.8 4.3 %collective-permute-start.7 = (f32[64,128]{1,0:T(8,128)S(1)}, f32[64,128]{1,0:T(8,128)S(1)}, u32[]{:S(2)}, u32[]{:S(2)}) collective-permute-start(f32[64,128]{1,0:T(8,128)S(1)} %add.19.refs_0_), channel_id=1, source_target_pairs={{0,16},{4,20},{8,24},{12,28},{16,0},{20,4},{24,8},{28,12},{1,17},{... | collective-permute-start | bytes 98312 | tf_op jit(solution)/shard_map/ppermute | solution.py:511
  22.3 4.8 %collective-permute-start.8 = (f32[64,128]{1,0:T(8,128)S(1)}, f32[64,128]{1,0:T(8,128)S(1)}, u32[]{:S(2)}, u32[]{:S(2)}) collective-permute-start(f32[64,128]{1,0:T(8,128)S(1)} %add.19.refs_0_), channel_id=1, source_target_pairs={{0,24},{4,28},{8,16},{12,20},{16,8},{20,12},{24,0},{28,4},{1,25},{... | collective-permute-start | bytes 98312 | tf_op jit(solution)/shard_map/ppermute | solution.py:511
  28.4 6.7 %collective-permute-start.10 = (f32[256,128]{1,0:T(8,128)S(1)}, f32[256,128]{1,0:T(8,128)S(1)}, u32[]{:S(2)}, u32[]{:S(2)}) collective-permute-start(f32[256,128]{1,0:T(8,128)S(1)} %get-tuple-element.31.kept_ref), channel_id=1, source_target_pairs={{1,0},{3,2},{0,1},{2,3},{5,4},{7,6},{4,5},{6,7},{9,8},{11,10},{8,9... | collective-permute-start | bytes 393224 | tf_op jit(solution)/shard_map/ppermute | solution.py:556
  30.8 7.5 %collective-permute-start.9 = (f32[256,128]{1,0:T(8,128)S(1)}, f32[256,128]{1,0:T(8,128)S(1)}, u32[]{:S(2)}, u32[]{:S(2)}) collective-permute-start(f32[256,128]{1,0:T(8,128)S(1)} %get-tuple-element.32.sent_ref), channel_id=1, source_target_pairs={{2,0},{0,2},{3,1},{1,3},{6,4},{4,6},{7,5},{5,7},{10,8},{8,10},{11,... | collective-permute-start | bytes 393224 | tf_op jit(solution)/shard_map/ppermute | solution.py:556
  40.2 1.3 %collective-permute-start.11 = (f32[144,128]{1,0:T(8,128)S(1)}, f32[144,128]{1,0:T(8,128)S(1)}, u32[]{:S(2)}, u32[]{:S(2)}) collective-permute-start(f32[144,128]{1,0:T(8,128)S(1)} %get-tuple-element.38), channel_id=1, source_target_pairs={{0,4},{4,0},{8,12},{12,8},{16,20},{20,16},{24,28},{28,24},{1,5},{5... | collective-permute-start | bytes 221192 | tf_op jit(solution)/shard_map/ppermute | solution.py:511
  41.5 4.4 %collective-permute-start.12 = (f32[144,128]{1,0:T(8,128)S(1)}, f32[144,128]{1,0:T(8,128)S(1)}, u32[]{:S(2)}, u32[]{:S(2)}) collective-permute-start(f32[144,128]{1,0:T(8,128)S(1)} %add.20), channel_id=1, source_target_pairs={{0,8},{4,12},{8,0},{12,4},{16,24},{20,28},{24,16},{28,20},{1,9},{5... | collective-permute-start | bytes 221192 | tf_op jit(solution)/shard_map/ppermute | solution.py:511
  43.1 4.4 %collective-permute-start.13 = (f32[144,128]{1,0:T(8,128)S(1)}, f32[144,128]{1,0:T(8,128)S(1)}, u32[]{:S(2)}, u32[]{:S(2)}) collective-permute-start(f32[144,128]{1,0:T(8,128)S(1)} %add.20), channel_id=1, source_target_pairs={{0,16},{4,20},{8,24},{12,28},{16,0},{20,4},{24,8},{28,12},{1,17},{... | collective-permute-start | bytes 221192 | tf_op jit(solution)/shard_map/ppermute | solution.py:511
  44.5 5.3 %collective-permute-start.14 = (f32[144,128]{1,0:T(8,128)S(1)}, f32[144,128]{1,0:T(8,128)S(1)}, u32[]{:S(2)}, u32[]{:S(2)}) collective-permute-start(f32[144,128]{1,0:T(8,128)S(1)} %add.20), channel_id=1, source_target_pairs={{0,24},{4,28},{8,16},{12,20},{16,8},{20,12},{24,0},{28,4},{1,25},{... | collective-permute-start | bytes 221192 | tf_op jit(solution)/shard_map/ppermute | solution.py:511
  49.8 1.3 %collective-permute-start.15 = (f32[144,128]{1,0:T(8,128)S(1)}, f32[144,128]{1,0:T(8,128)S(1)}, u32[]{:S(2)}, u32[]{:S(2)}) collective-permute-start(f32[144,128]{1,0:T(8,128)S(1)} %add_add_fusion.refs_4_), channel_id=1, source_target_pairs={{0,4},{4,0},{8,12},{12,8},{16,20},{20,16},{24,28},{28,24},{1,5},{5... | collective-permute-start | bytes 221192 | tf_op jit(solution)/shard_map/ppermute | solution.py:511
  55.3 6.5 %collective-permute-start.16 = (f32[256,128]{1,0:T(8,128)S(1)}, f32[256,128]{1,0:T(8,128)S(1)}, u32[]{:S(2)}, u32[]{:S(2)}) collective-permute-start(f32[256,128]{1,0:T(8,128)S(1)} %get-tuple-element.39), channel_id=1, source_target_pairs={{2,0},{0,1},{3,2},{1,3},{6,4},{4,5},{7,6},{5,7},{10,8},{8,9},{11,1... | collective-permute-start | bytes 393224 | tf_op jit(solution)/shard_map/ppermute | solution.py:575

commit v4 on v3

--- a/solution.py
+++ b/solution.py
@@ -12,7 +12,6 @@
 JSTEPS = 6
 REACH = 2 * (JSTEPS - 1) + 1
 DIAGS = 16
-FAR_REACH = 6 * (JSTEPS - 1) - 1
 FAR_DIAGS = 32
 WINDOW = 32
 NEAR = 16
@@ -76,14 +75,17 @@
                     edges.append((there, old % 2, here))
     turn, left_over = {}, list(edges)
     while left_over:
-        edge, by_target = left_over[0], True
-        number = 0
-        while edge is not None:
-            turn[edge] = number
-            left_over.remove(edge)
-            key = 2 if by_target else 0
-            edge = next((e for e in left_over if e[key] == edge[key]), None)
-            by_target, number = not by_target, 1 - number
+        source, _, target = left_over[0]
+        start = source
+        while True:
+            for number, one, other in ((0, source, target), (1, target, source)):
+                edge = next(e for e in left_over if (e[0], e[2]) == (one, other))
+                turn[edge] = number
+                left_over.remove(edge)
+            if target == start:
+                break
+            ahead = [e[2] for e in left_over if e[0] == target]
+            source, target = target, ahead[0]
     sends = [[(e[0], e[2]) for e in edges if turn[e] == i] for i in (0, 1)]
     for chosen in sends:
         assert len({a for a, _ in chosen}) == len({b for _, b in chosen}) == pair_total
@@ -166,28 +168,6 @@
     )
 
 
-def store_bands(even, odd, band_ref, reach, diags, base=0):
-    rows, width = even.shape
-    for d in range(reach):
-        sums = [None] * 4
-        for start in range(0, rows, 8):
-            e, o = even[start : start + 8], odd[start : start + 8]
-            e_near, o_near = right(e, d), right(o, d)
-            parts = (e_near * e, e_near * o, o_near * e if d else None, o_near * o)
-            for q in range(4):
-                if parts[q] is not None:
-                    sums[q] = parts[q] if start == 0 else sums[q] + parts[q]
-        if d == 0:
-            sums[2] = sums[1]
-        for q in range(4):
-            row = base + q * diags + d
-            band_ref[row : row + 1, :] = jnp.sum(sums[q], axis=0, keepdims=True)
-    for q in range(4):
-        band_ref[base + q * diags + reach : base + (q + 1) * diags, :] = jnp.zeros(
-            (diags - reach, width), jnp.float32
-        )
-
-
 def backwards(x):
     return jnp.take_along_axis(x, x.shape[1] - 1 - lanes_of(x), axis=1)
 
@@ -210,6 +190,11 @@
     return bands
 
 
+def store_bands(even, odd, band_ref):
+    for q, band in enumerate(dense_bands(even, odd, DIAGS)):
+        band_ref[q * DIAGS : (q + 1) * DIAGS, :] = band
+
+
 def open_kernel(basis_ref, even_ref, odd_ref, band_ref):
     width = basis_ref.shape[1] // 2
     table = separator(width, False)
@@ -218,7 +203,7 @@
     even, odd = split_pair(first, second)
     even_ref[...] = even
     odd_ref[...] = odd
-    store_bands(even, odd, band_ref, REACH, DIAGS)
+    store_bands(even, odd, band_ref)
 
 
 def pair_kernel(gets_first, kept_ref, came_ref, even_ref, odd_ref, band_ref):
@@ -227,7 +212,7 @@
     even, odd = split_pair(jnp.where(flag, came, kept), jnp.where(flag, kept, came))
     even_ref[...] = even
     odd_ref[...] = odd
-    store_bands(even, odd, band_ref, REACH, DIAGS)
+    store_bands(even, odd, band_ref)
 
 
 def jacobi_angle(diag_even, diag_odd, coupling):
@@ -260,23 +245,22 @@
     lane = lanes_of(ee)
     diag = lax.broadcasted_iota(jnp.int32, ee.shape, 0)
     last = lane == ee.shape[1] - 1
-    first, second = lane == diag, lane == diag + 1
     on, next_on = diag == 0, diag == 1
 
-    ee_new = right(ee, 1)
-    ee_new = jnp.where(second, right(jnp.where(on, oo, oe), 1), ee_new)
-    near = jnp.where(next_on, down(eo, 1), down(ee, 1))
-    ee_new = jnp.where(first, jnp.where(on, ee, right(near, 1)), ee_new)
-
-    eo_new = left(down(eo, -2), 1)
-    eo_new = jnp.where(second, left(down(oo, -2), 1), eo_new)
-    eo_new = jnp.where(first, left(down(eo, -1), 1), eo_new)
-    eo_new = jnp.where(last, down(ee, -1), eo_new)
+    near = down(jnp.where(on, eo, ee), 1)
+    turned = jnp.where(on, oo, oe)
+    mixed = jnp.where(lane == diag, turned, jnp.where(lane == diag - 1, near, ee))
+    ee_new = jnp.where(jnp.logical_and(on, lane == 0), ee, right(mixed, 1))
+
+    far = down(jnp.where(last, ee, eo), -1)
+    mixed = down(jnp.where(lane == diag, oo, eo), -2)
+    mixed = left(jnp.where(lane == diag + 1, far, mixed), 1)
+    eo_new = jnp.where(last, far, mixed)
 
     oo_new = jnp.where(last, jnp.where(on, ee, down(oe, 1)), left(oo, 1))
 
     oe_new = right(down(oe, 2), 1)
-    oe_new = jnp.where(next_on, jnp.where(first, oo, eo), oe_new)
+    oe_new = jnp.where(next_on, jnp.where(lane == diag, oo, eo), oe_new)
     oe_new = jnp.where(on, eo_new, oe_new)
     return ee_new, eo_new, oe_new, oo_new
 
@@ -286,22 +270,25 @@
     diag = lax.broadcasted_iota(jnp.int32, ee.shape, 0)
     last, first = lane == ee.shape[1] - 1, lane == diag
     on, next_on = diag == 0, diag == 1
-    ee_left, oe_left = left(ee, 1), left(down(oe, -2), 1)
-    ee_far, eo_far = left(down(ee, -1), 1), right(down(eo, 2), 1)
-
-    ee_old = jnp.where(first, jnp.where(on, ee, ee_far), ee_left)
-    ee_old = jnp.where(last, jnp.where(on, oo, down(eo, 1)), ee_old)
-
-    eo_old = jnp.where(on, oe_left, jnp.where(next_on, oe, eo_far))
-    eo_old = jnp.where(first, jnp.where(on, ee_far, right(down(eo, 1), 1)), eo_old)
-    eo_old = jnp.where(jnp.logical_and(last, on), down(oo, -1), eo_old)
-
-    oe_old = jnp.where(first, ee_left, oe_left)
-    oe_old = jnp.where(last, down(oo, -1), oe_old)
-    oe_old = jnp.where(on, eo_old, oe_old)
-
-    near = jnp.where(on, ee_left, jnp.where(next_on, oe, eo_far))
-    oo_old = jnp.where(first, near, right(oo, 1))
+    ahead, behind = lane == diag + 1, lane == diag - 1
+    eo_down, oo_up = down(eo, 1), down(oo, -1)
+    eo_twice = down(eo, 2)
+
+    ee_left = left(jnp.where(ahead, down(ee, -1), ee), 1)
+    ee_old = jnp.where(jnp.logical_and(first, on), ee, ee_left)
+    ee_old = jnp.where(last, jnp.where(on, oo, eo_down), ee_old)
+
+    oe_left = left(jnp.where(jnp.logical_and(ahead, diag > 0), ee, down(oe, -2)), 1)
+    eo_far = right(jnp.where(behind, eo_down, eo_twice), 1)
+    eo_old = jnp.where(on, jnp.where(last, oo_up, oe_left), eo_far)
+    eo_old = jnp.where(jnp.logical_and(next_on, lane > 1), oe, eo_old)
+    eo_old = jnp.where(jnp.logical_and(on, first), ee_left, eo_old)
+
+    oe_old = jnp.where(on, eo_old, jnp.where(last, oo_up, oe_left))
+
+    oo_old = right(jnp.where(behind, eo_twice, oo), 1)
+    oo_old = jnp.where(jnp.logical_and(next_on, first), oe, oo_old)
+    oo_old = jnp.where(jnp.logical_and(on, first), left(ee, 1), oo_old)
     return ee_old, eo_old, oe_old, oo_old
 
 

time: 62.7 us -> 62.1 us (level)
    ppermute x2, starting transfers between devices: 4.09 us -> 3.4 us  [per_device(): lax.ppermute(x, 'pair', s)]
where the time goes in v4:
time: 62.1 us; the launch traced here: 62 us
  waiting for transfers between devices  30.8 us (50%)
  starting transfers between devices  18.9 us (30%)
  Pallas kernels  10.5 us (17%)
  local copies, waits for them, and re-layouts  0.95 us (2%)
  other arithmetic  0.78 us (1%)
    ppermute x13, waiting for transfers between devices, swap(): lax.ppermute(x, axis, [(i, i ^ mask) for i in range(lax.axis_size(axis))])  16.4 us
    ppermute x13, starting transfers between devices, swap(): lax.ppermute(x, axis, [(i, i ^ mask) for i in range(lax.axis_size(axis))])  12.1 us
    pallas_call x6, Pallas kernels, call(): pl.pallas_call(kernel, out_shape=out, scratch_shapes=[pltpu.VMEM(shape, j...  10.5 us
    ppermute x2, waiting for transfers between devices, per_device(): came = lax.ppermute(sent, 'pair', sends)  8.3 us
    ppermute x2, waiting for transfers between devices, per_device(): lax.ppermute(x, 'pair', s)  6.09 us
    ppermute x2, starting transfers between devices, per_device(): lax.ppermute(x, 'pair', s)  3.4 us
    ppermute x2, starting transfers between devices, per_device(): came = lax.ppermute(sent, 'pair', sends)  3.37 us
  transfers between devices with their start and end apart: 17, of which 17 were waited for; matrix products, arithmetic and copies ran while one was open for 0% of the time, Pallas kernels for 0%

profile of v4, /device:TPU:0, one launch (start us, length us, event | category | flops | bytes accessed | tf_op | source)
XLA Modules:
  0.0 62.0 jit_solution(11637036241897020123)
XLA Ops:
  0.0 0.9 %copy-done = f32[256,256]{1,0:T(8,128)S(1)} copy-done((f32[256,256]{1,0:T(8,128)S(1)}, f32[256,256]{1,0:T(8,128)}, u32[]{:S(2)}) %copy-start) | copy-done | bytes 262168
  1.0 1.1 %shard_map.17 = (f32[256,128]{1,0:T(8,128)S(1)}, f32[256,128]{1,0:T(8,128)S(1)}, f32[64,128]{1,0:T(8,128)S(1)}) custom-call(f32[256,256]{1,0:T(8,128)S(1)} %copy-done), custom_call_target="tpu_custom_call" | custom-call | tf_op jit(solution)/shard_map/pallas_call | solution.py:515
  2.5 0.9 %collective-permute-done = f32[64,128]{1,0:T(8,128)S(1)} collective-permute-done((f32[64,128]{1,0:T(8,128)S(1)}, f32[64,128]{1,0:T(8,128)S(1)}, u32[]{:S(2)}, u32[]{:S(2)}) %collective-permute-start) | collective-permute-done | bytes 32800 | tf_op jit(solution)/shard_map/ppermute | solution.py:498
  3.4 2.8 %collective-permute-start.1 = (f32[64,128]{1,0:T(8,128)S(1)}, f32[64,128]{1,0:T(8,128)S(1)}, u32[]{:S(2)}, u32[]{:S(2)}) collective-permute-start(f32[64,128]{1,0:T(8,128)S(1)} %add.18.refs_0_), channel_id=1, source_target_pairs={{0,8},{4,12},{8,0},{12,4},{16,24},{20,28},{24,16},{28,20},{1,9},{5... | collective-permute-start | bytes 98312 | tf_op jit(solution)/shard_map/ppermute | solution.py:498
  6.2 1.5 %collective-permute-start.2 = (f32[64,128]{1,0:T(8,128)S(1)}, f32[64,128]{1,0:T(8,128)S(1)}, u32[]{:S(2)}, u32[]{:S(2)}) collective-permute-start(f32[64,128]{1,0:T(8,128)S(1)} %add.18.refs_0_), channel_id=1, source_target_pairs={{0,16},{4,20},{8,24},{12,28},{16,0},{20,4},{24,8},{28,12},{1,17},{... | collective-permute-start | bytes 98312 | tf_op jit(solution)/shard_map/ppermute | solution.py:498
  8.1 2.0 %collective-permute-done.2.refs_2_ = f32[64,128]{1,0:T(8,128)S(1)} collective-permute-done((f32[64,128]{1,0:T(8,128)S(1)}, f32[64,128]{1,0:T(8,128)S(1)}, u32[]{:S(2)}, u32[]{:S(2)}) %collective-permute-start.2) | collective-permute-done | bytes 32800 | tf_op jit(solution)/shard_map/ppermute | solution.py:498
  10.1 2.4 %collective-permute-done.3.refs_3_ = f32[64,128]{1,0:T(8,128)S(1)} collective-permute-done((f32[64,128]{1,0:T(8,128)S(1)}, f32[64,128]{1,0:T(8,128)S(1)}, u32[]{:S(2)}, u32[]{:S(2)}) %collective-permute-start.3) | collective-permute-done | bytes 32800 | tf_op jit(solution)/shard_map/ppermute | solution.py:498
  12.5 1.2 %shard_map.18 = (f32[256,128]{1,0:T(8,128)S(1)}, f32[256,128]{1,0:T(8,128)S(1)}) custom-call(f32[256,128]{1,0:T(8,128)S(1)} %get-tuple-element.23.even_ref, f32[256,128]{1,0:T(8,128)S(1)} %get-tuple-element.24.odd_ref, f32[64,128]{1,0:T(8,128)S(1)} %add.18.refs_0_, f32[64,128]{1,0:T(8,128)S(1)} %collective-permute-done.1.refs_1_, ...), custom_call_target="tpu_custom_call" | custom-call | tf_op jit(solution)/shard_map/pallas_call | solution.py:515
  13.8 2.6 %collective-permute-start.4 = (f32[256,128]{1,0:T(8,128)S(1)}, f32[256,128]{1,0:T(8,128)S(1)}, u32[]{:S(2)}, u32[]{:S(2)}) collective-permute-start(f32[256,128]{1,0:T(8,128)S(1)} %get-tuple-element.27), channel_id=1, source_target_pairs={{1,0},{0,2},{3,1},{2,3},{5,4},{4,6},{7,5},{6,7},{9,8},{8,10},{11,9... | collective-permute-start | bytes 393224 | tf_op jit(solution)/shard_map/ppermute | solution.py:540
  16.4 2.5 %collective-permute-done.4.came_ref = f32[256,128]{1,0:T(8,128)S(1)} collective-permute-done((f32[256,128]{1,0:T(8,128)S(1)}, f32[256,128]{1,0:T(8,128)S(1)}, u32[]{:S(2)}, u32[]{:S(2)}) %collective-permute-start.4) | collective-permute-done | bytes 131104 | tf_op jit(solution)/shard_map/ppermute | solution.py:540
  18.9 0.7 %shard_map.19 = (f32[256,128]{1,0:T(8,128)S(1)}, f32[256,128]{1,0:T(8,128)S(1)}, f32[64,128]{1,0:T(8,128)S(1)}) custom-call(f32[256,128]{1,0:T(8,128)S(1)} %get-tuple-element.26.kept_ref, f32[256,128]{1,0:T(8,128)S(1)} %collective-permute-done.4.came_ref), custom_call_target="tpu_custom_call" | custom-call | tf_op jit(solution)/shard_map/pallas_call | solution.py:515
  19.7 1.2 %collective-permute-done.5 = f32[64,128]{1,0:T(8,128)S(1)} collective-permute-done((f32[64,128]{1,0:T(8,128)S(1)}, f32[64,128]{1,0:T(8,128)S(1)}, u32[]{:S(2)}, u32[]{:S(2)}) %collective-permute-start.5) | collective-permute-done | bytes 32800 | tf_op jit(solution)/shard_map/ppermute | solution.py:498
  22.0 2.5 %collective-permute-start.8 = (f32[64,128]{1,0:T(8,128)S(1)}, f32[64,128]{1,0:T(8,128)S(1)}, u32[]{:S(2)}, u32[]{:S(2)}) collective-permute-start(f32[64,128]{1,0:T(8,128)S(1)} %add.19.refs_0_), channel_id=1, source_target_pairs={{0,24},{4,28},{8,16},{12,20},{16,8},{20,12},{24,0},{28,4},{1,25},{... | collective-permute-start | bytes 98312 | tf_op jit(solution)/shard_map/ppermute | solution.py:498
  24.9 0.9 %collective-permute-done.7.refs_2_ = f32[64,128]{1,0:T(8,128)S(1)} collective-permute-done((f32[64,128]{1,0:T(8,128)S(1)}, f32[64,128]{1,0:T(8,128)S(1)}, u32[]{:S(2)}, u32[]{:S(2)}) %collective-permute-start.7) | collective-permute-done | bytes 32800 | tf_op jit(solution)/shard_map/ppermute | solution.py:498
  25.7 1.1 %collective-permute-done.8.refs_3_ = f32[64,128]{1,0:T(8,128)S(1)} collective-permute-done((f32[64,128]{1,0:T(8,128)S(1)}, f32[64,128]{1,0:T(8,128)S(1)}, u32[]{:S(2)}, u32[]{:S(2)}) %collective-permute-start.8) | collective-permute-done | bytes 32800 | tf_op jit(solution)/shard_map/ppermute | solution.py:498
  26.8 1.2 %shard_map.20 = (f32[256,128]{1,0:T(8,128)S(1)}, f32[256,128]{1,0:T(8,128)S(1)}) custom-call(f32[256,128]{1,0:T(8,128)S(1)} %get-tuple-element.28.even_ref, f32[256,128]{1,0:T(8,128)S(1)} %get-tuple-element.29.odd_ref, f32[64,128]{1,0:T(8,128)S(1)} %add.19.refs_0_, f32[64,128]{1,0:T(8,128)S(1)} %collective-permute-done.6.refs_1_, ...), custom_call_target="tpu_custom_call" | custom-call | tf_op jit(solution)/shard_map/pallas_call | solution.py:515
  28.0 3.4 %collective-permute-start.10 = (f32[256,128]{1,0:T(8,128)S(1)}, f32[256,128]{1,0:T(8,128)S(1)}, u32[]{:S(2)}, u32[]{:S(2)}) collective-permute-start(f32[256,128]{1,0:T(8,128)S(1)} %get-tuple-element.31.kept_ref), channel_id=1, source_target_pairs={{1,0},{0,2},{3,1},{2,3},{5,4},{4,6},{7,5},{6,7},{9,8},{8,10},{11,9... | collective-permute-start | bytes 393224 | tf_op jit(solution)/shard_map/ppermute | solution.py:543
  31.4 2.9 %collective-permute-done.10.came1_ref = f32[256,128]{1,0:T(8,128)S(1)} collective-permute-done((f32[256,128]{1,0:T(8,128)S(1)}, f32[256,128]{1,0:T(8,128)S(1)}, u32[]{:S(2)}, u32[]{:S(2)}) %collective-permute-start.10) | collective-permute-done | bytes 131104 | tf_op jit(solution)/shard_map/ppermute | solution.py:543
  34.3 3.2 %collective-permute-done.9.came0_ref = f32[256,128]{1,0:T(8,128)S(1)} collective-permute-done((f32[256,128]{1,0:T(8,128)S(1)}, f32[256,128]{1,0:T(8,128)S(1)}, u32[]{:S(2)}, u32[]{:S(2)}) %collective-permute-start.9) | collective-permute-done | bytes 131104 | tf_op jit(solution)/shard_map/ppermute | solution.py:543
  37.5 2.0 %shard_map.21 = (f32[256,128]{1,0:T(8,128)S(1)}, f32[256,128]{1,0:T(8,128)S(1)}, f32[256,128]{1,0:T(8,128)S(1)}, f32[256,128]{1,0:T(8,128)S(1)}, f32[144,128]{1,0:T(8,128)S(1)}, /*index=5*/f32[144,128]{1,0:T(8,128)S(1)}) custom-call(f32[256,128]{1,0:T(8,128)S(1)} %get-tuple-element.31.kept_ref, f32[256,128]{1,0:T(8,128)S(1)} %get-tuple-element.32.sent_ref, ...), custom_call_target="tpu_custom_call" | custom-call | tf_op jit(solution)/shard_map/pallas_call | solution.py:515
  39.6 1.3 %collective-permute-done.11 = f32[144,128]{1,0:T(8,128)S(1)} collective-permute-done((f32[144,128]{1,0:T(8,128)S(1)}, f32[144,128]{1,0:T(8,128)S(1)}, u32[]{:S(2)}, u32[]{:S(2)}) %collective-permute-start.11) | collective-permute-done | bytes 73760 | tf_op jit(solution)/shard_map/ppermute | solution.py:498
  40.9 1.6 %collective-permute-start.12 = (f32[144,128]{1,0:T(8,128)S(1)}, f32[144,128]{1,0:T(8,128)S(1)}, u32[]{:S(2)}, u32[]{:S(2)}) collective-permute-start(f32[144,128]{1,0:T(8,128)S(1)} %add.20), channel_id=1, source_target_pairs={{0,8},{4,12},{8,0},{12,4},{16,24},{20,28},{24,16},{28,20},{1,9},{5... | collective-permute-start | bytes 221192 | tf_op jit(solution)/shard_map/ppermute | solution.py:498
  42.4 1.5 %collective-permute-start.13 = (f32[144,128]{1,0:T(8,128)S(1)}, f32[144,128]{1,0:T(8,128)S(1)}, u32[]{:S(2)}, u32[]{:S(2)}) collective-permute-start(f32[144,128]{1,0:T(8,128)S(1)} %add.20), channel_id=1, source_target_pairs={{0,16},{4,20},{8,24},{12,28},{16,0},{20,4},{24,8},{28,12},{1,17},{... | collective-permute-start | bytes 221192 | tf_op jit(solution)/shard_map/ppermute | solution.py:498
  43.9 0.5 collective-permute-start.14
  44.4 0.9 %collective-permute-done.12 = f32[144,128]{1,0:T(8,128)S(1)} collective-permute-done((f32[144,128]{1,0:T(8,128)S(1)}, f32[144,128]{1,0:T(8,128)S(1)}, u32[]{:S(2)}, u32[]{:S(2)}) %collective-permute-start.12) | collective-permute-done | bytes 73760 | tf_op jit(solution)/shard_map/ppermute | solution.py:498
  45.3 1.5 %collective-permute-done.13 = f32[144,128]{1,0:T(8,128)S(1)} collective-permute-done((f32[144,128]{1,0:T(8,128)S(1)}, f32[144,128]{1,0:T(8,128)S(1)}, u32[]{:S(2)}, u32[]{:S(2)}) %collective-permute-start.13) | collective-permute-done | bytes 73760 | tf_op jit(solution)/shard_map/ppermute | solution.py:498
  46.8 2.4 %collective-permute-done.14 = f32[144,128]{1,0:T(8,128)S(1)} collective-permute-done((f32[144,128]{1,0:T(8,128)S(1)}, f32[144,128]{1,0:T(8,128)S(1)}, u32[]{:S(2)}, u32[]{:S(2)}) %collective-permute-start.14) | collective-permute-done | bytes 73760 | tf_op jit(solution)/shard_map/ppermute | solution.py:498
  49.2 1.3 %collective-permute-done.15.refs_5_ = f32[144,128]{1,0:T(8,128)S(1)} collective-permute-done((f32[144,128]{1,0:T(8,128)S(1)}, f32[144,128]{1,0:T(8,128)S(1)}, u32[]{:S(2)}, u32[]{:S(2)}) %collective-permute-start.15) | collective-permute-done | bytes 73760 | tf_op jit(solution)/shard_map/ppermute | solution.py:498
  50.5 4.2 %shard_map.22 = (f32[256,128]{1,0:T(8,128)S(1)}, f32[256,128]{1,0:T(8,128)S(1)}) custom-call(f32[256,128]{1,0:T(8,128)S(1)} %get-tuple-element.33.refs_0_, f32[256,128]{1,0:T(8,128)S(1)} %get-tuple-element.34.refs_1_, f32[256,128]{1,0:T(8,128)S(1)} %get-tuple-element.35.refs_2_, f32[256,128]{1,0:T(8,128)S(1)} %get-tuple-element.36.refs_3_, ...), custom_call_target="tpu_custom_call" | custom-call | tf_op jit(solution)/shard_map/pallas_call | solution.py:515
  54.7 0.7 %collective-permute-start.16 = (f32[256,128]{1,0:T(8,128)S(1)}, f32[256,128]{1,0:T(8,128)S(1)}, u32[]{:S(2)}, u32[]{:S(2)}) collective-permute-start(f32[256,128]{1,0:T(8,128)S(1)} %get-tuple-element.39), channel_id=1, source_target_pairs={{2,0},{0,1},{3,2},{1,3},{6,4},{4,5},{7,6},{5,7},{10,8},{8,9},{11,1... | collective-permute-start | bytes 393224 | tf_op jit(solution)/shard_map/ppermute | solution.py:562
  55.4 5.8 %collective-permute-done.16 = f32[256,128]{1,0:T(8,128)S(1)} collective-permute-done((f32[256,128]{1,0:T(8,128)S(1)}, f32[256,128]{1,0:T(8,128)S(1)}, u32[]{:S(2)}, u32[]{:S(2)}) %collective-permute-start.16) | collective-permute-done | bytes 131104 | tf_op jit(solution)/shard_map/ppermute | solution.py:562
  61.2 0.7 %pad_maximum_fusion = f32[256,256]{1,0:T(8,128)} fusion(f32[256,128]{1,0:T(8,128)S(1)} %get-tuple-element.42, f32[256,128]{1,0:T(8,128)S(1)} %get-tuple-element.41), kind=kLoop, calls=%fused_computation | loop fusion | flops 65536 | bytes 524288 | tf_op jit(solution)/shard_map/concatenate | solution.py:566
  (16 shorter events, 2.6 us)
Async XLA Ops:
  0.0 0.9 %copy-start = (f32[256,256]{1,0:T(8,128)S(1)}, f32[256,256]{1,0:T(8,128)}, u32[]{:S(2)}) copy-start(f32[256,256]{1,0:T(8,128)} %basis_ref.1) | copy-start | bytes 786436
  2.0 1.4 %collective-permute-start = (f32[64,128]{1,0:T(8,128)S(1)}, f32[64,128]{1,0:T(8,128)S(1)}, u32[]{:S(2)}, u32[]{:S(2)}) collective-permute-start(f32[64,128]{1,0:T(8,128)S(1)} %get-tuple-element.25), channel_id=1, source_target_pairs={{0,4},{4,0},{8,12},{12,8},{16,20},{20,16},{24,28},{28,24},{1,5},{5... | collective-permute-start | bytes 98312 | tf_op jit(solution)/shard_map/ppermute | solution.py:498
  3.4 4.7 %collective-permute-start.1 = (f32[64,128]{1,0:T(8,128)S(1)}, f32[64,128]{1,0:T(8,128)S(1)}, u32[]{:S(2)}, u32[]{:S(2)}) collective-permute-start(f32[64,128]{1,0:T(8,128)S(1)} %add.18.refs_0_), channel_id=1, source_target_pairs={{0,8},{4,12},{8,0},{12,4},{16,24},{20,28},{24,16},{28,20},{1,9},{5... | collective-permute-start | bytes 98312 | tf_op jit(solution)/shard_map/ppermute | solution.py:498
  6.2 3.9 %collective-permute-start.2 = (f32[64,128]{1,0:T(8,128)S(1)}, f32[64,128]{1,0:T(8,128)S(1)}, u32[]{:S(2)}, u32[]{:S(2)}) collective-permute-start(f32[64,128]{1,0:T(8,128)S(1)} %add.18.refs_0_), channel_id=1, source_target_pairs={{0,16},{4,20},{8,24},{12,28},{16,0},{20,4},{24,8},{28,12},{1,17},{... | collective-permute-start | bytes 98312 | tf_op jit(solution)/shard_map/ppermute | solution.py:498
  7.7 4.8 %collective-permute-start.3 = (f32[64,128]{1,0:T(8,128)S(1)}, f32[64,128]{1,0:T(8,128)S(1)}, u32[]{:S(2)}, u32[]{:S(2)}) collective-permute-start(f32[64,128]{1,0:T(8,128)S(1)} %add.18.refs_0_), channel_id=1, source_target_pairs={{0,24},{4,28},{8,16},{12,20},{16,8},{20,12},{24,0},{28,4},{1,25},{... | collective-permute-start | bytes 98312 | tf_op jit(solution)/shard_map/ppermute | solution.py:498
  13.8 5.2 %collective-permute-start.4 = (f32[256,128]{1,0:T(8,128)S(1)}, f32[256,128]{1,0:T(8,128)S(1)}, u32[]{:S(2)}, u32[]{:S(2)}) collective-permute-start(f32[256,128]{1,0:T(8,128)S(1)} %get-tuple-element.27), channel_id=1, source_target_pairs={{1,0},{0,2},{3,1},{2,3},{5,4},{4,6},{7,5},{6,7},{9,8},{8,10},{11,9... | collective-permute-start | bytes 393224 | tf_op jit(solution)/shard_map/ppermute | solution.py:540
  19.7 1.3 %collective-permute-start.5 = (f32[64,128]{1,0:T(8,128)S(1)}, f32[64,128]{1,0:T(8,128)S(1)}, u32[]{:S(2)}, u32[]{:S(2)}) collective-permute-start(f32[64,128]{1,0:T(8,128)S(1)} %get-tuple-element.30), channel_id=1, source_target_pairs={{0,4},{4,0},{8,12},{12,8},{16,20},{20,16},{24,28},{28,24},{1,5},{5... | collective-permute-start | bytes 98312 | tf_op jit(solution)/shard_map/ppermute | solution.py:498
  20.9 3.9 %collective-permute-start.6 = (f32[64,128]{1,0:T(8,128)S(1)}, f32[64,128]{1,0:T(8,128)S(1)}, u32[]{:S(2)}, u32[]{:S(2)}) collective-permute-start(f32[64,128]{1,0:T(8,128)S(1)} %add.19.refs_0_), channel_id=1, source_target_pairs={{0,8},{4,12},{8,0},{12,4},{16,24},{20,28},{24,16},{28,20},{1,9},{5... | collective-permute-start | bytes 98312 | tf_op jit(solution)/shard_map/ppermute | solution.py:498
  21.5 4.3 %collective-permute-start.7 = (f32[64,128]{1,0:T(8,128)S(1)}, f32[64,128]{1,0:T(8,128)S(1)}, u32[]{:S(2)}, u32[]{:S(2)}) collective-permute-start(f32[64,128]{1,0:T(8,128)S(1)} %add.19.refs_0_), channel_id=1, source_target_pairs={{0,16},{4,20},{8,24},{12,28},{16,0},{20,4},{24,8},{28,12},{1,17},{... | collective-permute-start | bytes 98312 | tf_op jit(solution)/shard_map/ppermute | solution.py:498
  22.0 4.8 %collective-permute-start.8 = (f32[64,128]{1,0:T(8,128)S(1)}, f32[64,128]{1,0:T(8,128)S(1)}, u32[]{:S(2)}, u32[]{:S(2)}) collective-permute-start(f32[64,128]{1,0:T(8,128)S(1)} %add.19.refs_0_), channel_id=1, source_target_pairs={{0,24},{4,28},{8,16},{12,20},{16,8},{20,12},{24,0},{28,4},{1,25},{... | collective-permute-start | bytes 98312 | tf_op jit(solution)/shard_map/ppermute | solution.py:498
  28.0 6.3 %collective-permute-start.10 = (f32[256,128]{1,0:T(8,128)S(1)}, f32[256,128]{1,0:T(8,128)S(1)}, u32[]{:S(2)}, u32[]{:S(2)}) collective-permute-start(f32[256,128]{1,0:T(8,128)S(1)} %get-tuple-element.31.kept_ref), channel_id=1, source_target_pairs={{1,0},{0,2},{3,1},{2,3},{5,4},{4,6},{7,5},{6,7},{9,8},{8,10},{11,9... | collective-permute-start | bytes 393224 | tf_op jit(solution)/shard_map/ppermute | solution.py:543
  31.4 6.1 %collective-permute-start.9 = (f32[256,128]{1,0:T(8,128)S(1)}, f32[256,128]{1,0:T(8,128)S(1)}, u32[]{:S(2)}, u32[]{:S(2)}) collective-permute-start(f32[256,128]{1,0:T(8,128)S(1)} %get-tuple-element.32.sent_ref), channel_id=1, source_target_pairs={{2,0},{3,2},{0,1},{1,3},{6,4},{7,6},{4,5},{5,7},{10,8},{11,10},{8,... | collective-permute-start | bytes 393224 | tf_op jit(solution)/shard_map/ppermute | solution.py:543
  39.5 1.3 %collective-permute-start.11 = (f32[144,128]{1,0:T(8,128)S(1)}, f32[144,128]{1,0:T(8,128)S(1)}, u32[]{:S(2)}, u32[]{:S(2)}) collective-permute-start(f32[144,128]{1,0:T(8,128)S(1)} %get-tuple-element.38), channel_id=1, source_target_pairs={{0,4},{4,0},{8,12},{12,8},{16,20},{20,16},{24,28},{28,24},{1,5},{5... | collective-permute-start | bytes 221192 | tf_op jit(solution)/shard_map/ppermute | solution.py:498
  40.9 4.4 %collective-permute-start.12 = (f32[144,128]{1,0:T(8,128)S(1)}, f32[144,128]{1,0:T(8,128)S(1)}, u32[]{:S(2)}, u32[]{:S(2)}) collective-permute-start(f32[144,128]{1,0:T(8,128)S(1)} %add.20), channel_id=1, source_target_pairs={{0,8},{4,12},{8,0},{12,4},{16,24},{20,28},{24,16},{28,20},{1,9},{5... | collective-permute-start | bytes 221192 | tf_op jit(solution)/shard_map/ppermute | solution.py:498
  42.4 4.4 %collective-permute-start.13 = (f32[144,128]{1,0:T(8,128)S(1)}, f32[144,128]{1,0:T(8,128)S(1)}, u32[]{:S(2)}, u32[]{:S(2)}) collective-permute-start(f32[144,128]{1,0:T(8,128)S(1)} %add.20), channel_id=1, source_target_pairs={{0,16},{4,20},{8,24},{12,28},{16,0},{20,4},{24,8},{28,12},{1,17},{... | collective-permute-start | bytes 221192 | tf_op jit(solution)/shard_map/ppermute | solution.py:498
  43.9 5.3 %collective-permute-start.14 = (f32[144,128]{1,0:T(8,128)S(1)}, f32[144,128]{1,0:T(8,128)S(1)}, u32[]{:S(2)}, u32[]{:S(2)}) collective-permute-start(f32[144,128]{1,0:T(8,128)S(1)} %add.20), channel_id=1, source_target_pairs={{0,24},{4,28},{8,16},{12,20},{16,8},{20,12},{24,0},{28,4},{1,25},{... | collective-permute-start | bytes 221192 | tf_op jit(solution)/shard_map/ppermute | solution.py:498
  49.1 1.3 %collective-permute-start.15 = (f32[144,128]{1,0:T(8,128)S(1)}, f32[144,128]{1,0:T(8,128)S(1)}, u32[]{:S(2)}, u32[]{:S(2)}) collective-permute-start(f32[144,128]{1,0:T(8,128)S(1)} %add_add_fusion.refs_4_), channel_id=1, source_target_pairs={{0,4},{4,0},{8,12},{12,8},{16,20},{20,16},{24,28},{28,24},{1,5},{5... | collective-permute-start | bytes 221192 | tf_op jit(solution)/shard_map/ppermute | solution.py:498
  54.7 6.5 %collective-permute-start.16 = (f32[256,128]{1,0:T(8,128)S(1)}, f32[256,128]{1,0:T(8,128)S(1)}, u32[]{:S(2)}, u32[]{:S(2)}) collective-permute-start(f32[256,128]{1,0:T(8,128)S(1)} %get-tuple-element.39), channel_id=1, source_target_pairs={{2,0},{0,1},{3,2},{1,3},{6,4},{4,5},{7,6},{5,7},{10,8},{8,9},{11,1... | collective-permute-start | bytes 393224 | tf_op jit(solution)/shard_map/ppermute | solution.py:562

commit v5 on v4

--- a/solution.py
+++ b/solution.py
@@ -152,19 +152,22 @@
     return jnp.where(low, even, right(odd, half)), jnp.where(low, right(even, half), odd)
 
 
-def separator(width, back):
-    rows = lax.broadcasted_iota(jnp.int32, (width, width), 0)
-    cols = lax.broadcasted_iota(jnp.int32, (width, width), 1)
-    if back:
-        rows, cols = cols, rows
-    half = width // 2
-    source = jnp.where(cols < half, 2 * cols, 2 * (cols - half) + 1)
-    return jnp.where(rows == source, 1.0, 0.0).astype(jnp.float32)
-
-
-def reorder(block, table):
-    return jnp.dot(
-        block, table, precision=lax.Precision.HIGHEST, preferred_element_type=jnp.float32
+def take_lanes(x, source):
+    return jnp.take_along_axis(x, jnp.broadcast_to(source, x.shape), axis=1)
+
+
+def line_lanes(x):
+    return lax.broadcasted_iota(jnp.int32, (1, x.shape[1]), 1)
+
+
+def separate(first, second):
+    lane = line_lanes(first)
+    half = first.shape[1] // 2
+    low = lane < half
+    source = 2 * jnp.where(low, lane, lane - half)
+    return tuple(
+        jnp.where(low, take_lanes(first, source + odd), take_lanes(second, source + odd))
+        for odd in (0, 1)
     )
 
 
@@ -190,20 +193,17 @@
     return bands
 
 
-def store_bands(even, odd, band_ref):
-    for q, band in enumerate(dense_bands(even, odd, DIAGS)):
-        band_ref[q * DIAGS : (q + 1) * DIAGS, :] = band
+def store_bands(even, odd, band_ref, diags):
+    for q, band in enumerate(dense_bands(even, odd, diags)):
+        band_ref[q * diags : (q + 1) * diags, :] = band
 
 
 def open_kernel(basis_ref, even_ref, odd_ref, band_ref):
     width = basis_ref.shape[1] // 2
-    table = separator(width, False)
-    first = reorder(basis_ref[:, :width], table)
-    second = reorder(basis_ref[:, width:], table)
-    even, odd = split_pair(first, second)
+    even, odd = separate(basis_ref[:, :width], basis_ref[:, width:])
     even_ref[...] = even
     odd_ref[...] = odd
-    store_bands(even, odd, band_ref)
+    store_bands(even, odd, band_ref, DIAGS)
 
 
 def pair_kernel(gets_first, kept_ref, came_ref, even_ref, odd_ref, band_ref):
@@ -212,7 +212,7 @@
     even, odd = split_pair(jnp.where(flag, came, kept), jnp.where(flag, kept, came))
     even_ref[...] = even
     odd_ref[...] = odd
-    store_bands(even, odd, band_ref)
+    store_bands(even, odd, band_ref, DIAGS)
 
 
 def jacobi_angle(diag_even, diag_odd, coupling):
@@ -300,16 +300,42 @@
     return even_new, odd_new
 
 
-def columns_home(even, odd):
-    lane = lanes_of(even)
+def home_sources(even, odd):
+    lane = line_lanes(even)
     by, end = JSTEPS - 1, even.shape[1] - 1
-    mixed = jnp.where(jnp.logical_and(lane >= 1, lane <= by), right(odd, by + 1), even)
-    source = jnp.where(lane <= end - by, lane + by, end + 1 - lane)
-    even_home = jnp.take_along_axis(mixed, jnp.where(lane == 0, 0, source), axis=1)
-    mixed = jnp.where(lane > end - by, left(even, by + 1), odd)
-    source = jnp.where(lane >= by, lane - by, end - lane)
-    odd_home = jnp.take_along_axis(mixed, source, axis=1)
-    return even_home, odd_home
+    entered = jnp.logical_and(lane >= 1, lane <= by)
+    mixed_even = jnp.where(entered, right(odd, by + 1), even)
+    mixed_odd = jnp.where(lane > end - by, left(even, by + 1), odd)
+
+    def even_source(place):
+        moved = jnp.where(place <= end - by, place + by, end + 1 - place)
+        return jnp.where(place == 0, 0, moved)
+
+    def odd_source(place):
+        return jnp.where(place >= by, place - by, end - place)
+
+    return (mixed_even, even_source), (mixed_odd, odd_source)
+
+
+def columns_home(even, odd, shifted=None):
+    lane = line_lanes(even)
+    if shifted is not None:
+        half = even.shape[1] // 2
+        lane = jnp.where(shifted, jnp.where(lane < half, lane + half, lane - half), lane)
+    return tuple(take_lanes(x, source(lane)) for x, source in home_sources(even, odd))
+
+
+def blocks_home(even, odd):
+    lane = line_lanes(even)
+    (even, even_source), (odd, odd_source) = home_sources(even, odd)
+    blocks = []
+    for block in (0, 1):
+        place = block * (even.shape[1] // 2) + lane // 2
+        from_even, from_odd = (
+            take_lanes(x, source(place)) for x, source in ((even, even_source), (odd, odd_source))
+        )
+        blocks.append(jnp.where(lane % 2 == 0, from_even, from_odd))
+    return blocks
 
 
 def trim(bands, reach):
@@ -336,20 +362,23 @@
     return angles, bands
 
 
-def turn_columns(even, odd, angles):
+def turned(even, odd, angles):
     for step, (cosine, sine) in enumerate(angles):
         even, odd = cosine * even + sine * odd, cosine * odd - sine * even
         if step < JSTEPS - 1:
             even, odd = move_columns(even, odd)
-    return columns_home(even, odd)
+    return even, odd
+
+
+def turn_columns(even, odd, angles, shifted=None):
+    return columns_home(*turned(even, odd, angles), shifted)
 
 
 def turn_kernel(sends_first, even_ref, odd_ref, *refs):
     *band_refs, kept_ref, sent_ref = refs
     bands = [ref[...] for ref in band_refs]
-    while len(bands) > 1:
-        bands = [bands[i] + bands[i + 1] for i in range(0, len(bands), 2)]
-    bands = [bands[0][q * DIAGS : (q + 1) * DIAGS] for q in range(4)]
+    band = pair_sums(bands)
+    bands = [band[q * DIAGS : (q + 1) * DIAGS] for q in range(4)]
     angles, _ = angles_of(bands, False)
     first, second = join_pair(*turn_columns(even_ref[...], odd_ref[...], angles))
     flag = among(sends_first)
@@ -416,73 +445,99 @@
     return bands
 
 
+def halves_swapped(is_second):
+    return among(is_second[0]), jnp.logical_not(among(is_second[1]))
+
+
+def on_odd_core():
+    return lax.axis_index("row") % 2 == 1
+
+
 def fused_open(picks, is_second, kept_ref, sent_ref, came0_ref, came1_ref, *refs):
-    *column_refs, mine_ref, other_ref, parts = refs
+    *column_refs, corner_ref, other_ref = refs
     arrays = [ref[...] for ref in (sent_ref, kept_ref, came0_ref, came1_ref)]
     blocks = [choose(pick, arrays) for pick in picks]
-    columns = split_pair(*blocks[:2]) + split_pair(*blocks[2:])
-    for ref, value in zip(column_refs, columns):
+    x, y = split_pair(*blocks[:2]), split_pair(*blocks[2:])
+    corner = cross_partial(*x, *y, among(is_second[0]), among(is_second[1]))
+    flag = on_odd_core()
+    mine = [jnp.where(flag, b, a) for a, b in zip(x, y)]
+    theirs = [jnp.where(flag, a, b) for a, b in zip(x, y)]
+    for ref, value in zip(column_refs, mine + theirs):
         ref[...] = value
-    corner = cross_partial(*columns, among(is_second[0]), among(is_second[1]))
-    for i in (0, 1):
-        for q, band in enumerate(dense_bands(*columns[2 * i : 2 * i + 2], FAR_DIAGS)):
-            parts[i, q * FAR_DIAGS : (q + 1) * FAR_DIAGS, :] = band
-        parts[i, 4 * FAR_DIAGS :, :] = corner[i * NEAR : (i + 1) * NEAR]
-    odd_core = lax.axis_index("row") % 2
-    mine_ref[...] = parts[odd_core]
-    other_ref[...] = parts[1 - odd_core]
-
-
-def fused_turn(x_even, x_odd, y_even, y_odd, x_part, y_part, x_second, y_second):
-    half = x_even.shape[1] // 2
-
-    def quadrants(part):
-        return [part[q * FAR_DIAGS : (q + 1) * FAR_DIAGS] for q in range(4)]
-
-    x_angles, x_bands = angles_of(quadrants(x_part), True)
-    y_angles, y_bands = angles_of(quadrants(y_part), True)
-    corner = jnp.concatenate((x_part[4 * FAR_DIAGS :], y_part[4 * FAR_DIAGS :]), axis=0)
-    middle = cross_bands(corner, x_angles, y_angles, x_second, y_second)
-
-    def first_half(x):
-        return jnp.where(x_second, right(x, half), x)
-
-    def second_half(y):
-        return jnp.where(y_second, y, right(y, half))
-
+    corner_ref[...] = jnp.where(flag, corner[NEAR:], corner[:NEAR])
+    store_bands(*theirs, other_ref, FAR_DIAGS)
+    other_ref[4 * FAR_DIAGS :, :] = jnp.where(flag, corner[:NEAR], corner[NEAR:])
+
+
+def bands_kernel(even_ref, odd_ref, corner_ref, part_ref):
+    store_bands(even_ref[...], odd_ref[...], part_ref, FAR_DIAGS)
+    part_ref[4 * FAR_DIAGS :, :] = corner_ref[...]
+
+
+def angles_kernel(*refs):
+    *part_refs, found_ref = refs
+    part = pair_sums([ref[...] for ref in part_refs])
+    quadrants = [part[q * FAR_DIAGS : (q + 1) * FAR_DIAGS] for q in range(4)]
+    angles, bands = angles_of(quadrants, True)
+    for step, pair in enumerate(angles):
+        for i in (0, 1):
+            found_ref[2 * step + i : 2 * step + i + 1, :] = pair[i]
+    spare = NEAR - 2 * JSTEPS
+    found_ref[2 * JSTEPS : NEAR, :] = jnp.zeros((spare, part.shape[1]), jnp.float32)
+    for q in range(4):
+        found_ref[NEAR + q * DIAGS : NEAR + (q + 1) * DIAGS, :] = bands[q][:DIAGS]
+    found_ref[NEAR + 4 * DIAGS :, :] = part[4 * FAR_DIAGS :]
+
+
+def angles_in(found):
+    return [(found[2 * i : 2 * i + 1], found[2 * i + 1 : 2 * i + 2]) for i in range(JSTEPS)]
+
+
+def columns_kernel(is_second, even_ref, odd_ref, found_ref, *out_refs):
+    x_swapped, y_swapped = halves_swapped(is_second)
+    flag = on_odd_core()
+    swapped = jnp.logical_or(
+        jnp.logical_and(flag, y_swapped), jnp.logical_and(jnp.logical_not(flag), x_swapped)
+    )
+    columns = turn_columns(even_ref[...], odd_ref[...], angles_in(found_ref[...]), swapped)
+    for ref, value in zip(out_refs, columns):
+        ref[...] = value
+
+
+def last_bands(x_found, y_found, x_second, y_second):
+    corner = jnp.concatenate((x_found[NEAR + 4 * DIAGS :], y_found[NEAR + 4 * DIAGS :]), axis=0)
+    middle = cross_bands(corner, angles_in(x_found), angles_in(y_found), x_second, y_second)
+    half = corner.shape[1] // 2
     lane = lanes_of(middle[0])
     diag = lax.broadcasted_iota(jnp.int32, middle[0].shape, 0)
-    bands = [
-        jnp.where(
-            lane < half,
-            first_half(x_bands[q][:DIAGS]),
-            jnp.where(lane - diag < half, middle[q], second_half(y_bands[q][:DIAGS])),
-        )
-        for q in range(4)
-    ]
-    x_turned = turn_columns(x_even, x_odd, x_angles)
-    y_turned = turn_columns(y_even, y_odd, y_angles)
-    low = lanes_of(x_even) < half
-    even, odd = (
-        jnp.where(low, first_half(x), second_half(y)) for x, y in zip(x_turned, y_turned)
-    )
+    bands = []
+    for q in range(4):
+        rows = slice(NEAR + q * DIAGS, NEAR + (q + 1) * DIAGS)
+        x, y = x_found[rows], y_found[rows]
+        x = jnp.where(x_second, right(x, half), x)
+        y = jnp.where(y_second, y, right(y, half))
+        crossing = jnp.where(lane - diag < half, middle[q], y)
+        bands.append(jnp.where(lane < half, x, crossing))
+    return bands
+
+
+def last_kernel(is_second, sends_first, *refs):
+    mine_even, mine_odd, even_ref, odd_ref, found_ref, other_ref, kept_ref, sent_ref = refs
+    found, other = found_ref[...], other_ref[...]
+    flag = on_odd_core()
+    x_found, y_found = jnp.where(flag, other, found), jnp.where(flag, found, other)
+    bands = last_bands(x_found, y_found, among(is_second[0]), among(is_second[1]))
+    x_swapped, y_swapped = halves_swapped(is_second)
+    swapped = jnp.logical_or(
+        jnp.logical_and(flag, x_swapped), jnp.logical_and(jnp.logical_not(flag), y_swapped)
+    )
+    theirs = turn_columns(even_ref[...], odd_ref[...], angles_in(other), swapped)
+    low = line_lanes(found) < found.shape[1] // 2
+    from_mine = jnp.logical_xor(low, flag)
+    even = jnp.where(from_mine, mine_even[...], theirs[0])
+    odd = jnp.where(from_mine, mine_odd[...], theirs[1])
     angles, _ = angles_of(bands, False)
-    return join_pair(*turn_columns(even, odd, angles))
-
-
-def fused_kernel(is_second, sends_first, *refs):
-    *column_refs, mine_ref, other_ref, kept_ref, sent_ref = refs
-    mine, other = mine_ref[...], other_ref[...]
-    odd_core = lax.axis_index("row") % 2 == 1
-    parts = jnp.where(odd_core, other, mine), jnp.where(odd_core, mine, other)
-    first, second = fused_turn(
-        *(ref[...] for ref in column_refs),
-        *parts,
-        among(is_second[0]),
-        among(is_second[1]),
-    )
-    table = separator(first.shape[1], True)
-    first, second = reorder(first, table), reorder(second, table)
+    first, second = blocks_home(*turned(even, odd, angles))
     flag = among(sends_first)
     kept_ref[...] = jnp.where(flag, second, first)
     sent_ref[...] = jnp.where(flag, first, second)
@@ -510,12 +565,11 @@
     return arrays
 
 
-def call(kernel, shapes, *args, scratch=()):
+def call(kernel, shapes, *args):
     out = [jax.ShapeDtypeStruct(shape, jnp.float32) for shape in shapes]
     return pl.pallas_call(
         kernel,
         out_shape=out,
-        scratch_shapes=[pltpu.VMEM(shape, jnp.float32) for shape in scratch],
         compiler_params=pltpu.CompilerParams(vmem_limit_bytes=32 * 1024 * 1024),
     )(*args)
 
@@ -541,24 +595,24 @@
             opening = functools.partial(pair_kernel, gets_first)
             even, odd, partial = call(opening, (column, column, band), kept, came)
     came = [lax.ppermute(x, "pair", s) for x, s in zip((sent, kept), fused_sends)]
-    *columns, mine, other = call(
+    *columns, corner, other = call(
         functools.partial(fused_open, picks, is_second),
-        (column,) * 4 + (part,) * 2,
+        (column,) * 4 + ((NEAR, width), part),
         kept,
         sent,
         *came,
-        scratch=((2,) + part,),
-    )
-    mine = pair_sums(exchange_groups(mine + swap(other, "row", 1), "row", 1))
-    other = swap(mine, "row", 1)
+    )
+    other = swap(other, "row", 1)
+    (mine,) = call(bands_kernel, (part,), *columns[:2], corner)
+    (found,) = call(
+        angles_kernel, ((2 * NEAR + 4 * DIAGS, width),), *exchange_groups(mine + other, "row", 1)
+    )
+    other = swap(found, "row", 1)
+    turn = functools.partial(columns_kernel, is_second)
+    columns[:2] = call(turn, (column, column), *columns[:2], found)
     sends, sends_first, gets_first = plans[-1]
-    kept, sent = call(
-        functools.partial(fused_kernel, is_second, sends_first),
-        (column, column),
-        *columns,
-        mine,
-        other,
-    )
+    last = functools.partial(last_kernel, is_second, sends_first)
+    kept, sent = call(last, (column, column), *columns, found, other)
     came = lax.ppermute(sent, "pair", sends)
     flag = among(gets_first)
     first = jnp.where(flag, came, kept)

time: 62.1 us -> 60.8 us (0.979)
  waiting for transfers between devices: 30.8 us -> 29.4 us
    ppermute x13, waiting for transfers between devices: 16.4 us -> 15 us  [swap(): lax.ppermute(x, axis, [(i, i ^ mask) for i in range(lax.axis_size(axis))])]
    pallas_call x6 -> x9, Pallas kernels: 10.5 us -> 10.6 us  [call(): pl.pallas_call(kernel, out_shape=out, compiler_params=pltpu.CompilerParam...]
  transfers between devices with their start and end apart: 17 -> 17, of which waited for: 17 -> 17; matrix products, arithmetic and copies ran while one was open for 0% -> 0% of each run, Pallas kernels for 0% -> 2%
where the time goes in v5:
time: 60.8 us; the launch traced here: 60.6 us
  waiting for transfers between devices  29.4 us (48%)
  starting transfers between devices  18.8 us (31%)
  Pallas kernels  10.6 us (17%)
  local copies, waits for them, and re-layouts  0.95 us (2%)
  other arithmetic  0.76 us (1%)
    ppermute x13, waiting for transfers between devices, swap(): lax.ppermute(x, axis, [(i, i ^ mask) for i in range(lax.axis_size(axis))])  15 us
    ppermute x13, starting transfers between devices, swap(): lax.ppermute(x, axis, [(i, i ^ mask) for i in range(lax.axis_size(axis))])  12.1 us
    pallas_call x9, Pallas kernels, call(): pl.pallas_call(kernel, out_shape=out, compiler_params=pltpu.CompilerParam...  10.6 us
    ppermute x2, waiting for transfers between devices, per_device(): came = lax.ppermute(sent, 'pair', sends)  8.3 us
    ppermute x2, waiting for transfers between devices, per_device(): lax.ppermute(x, 'pair', s)  6.09 us
    ppermute x2, starting transfers between devices, per_device(): lax.ppermute(x, 'pair', s)  3.4 us
    ppermute x2, starting transfers between devices, per_device(): came = lax.ppermute(sent, 'pair', sends)  3.37 us
  transfers between devices with their start and end apart: 17, of which 17 were waited for; matrix products, arithmetic and copies ran while one was open for 0% of the time, Pallas kernels for 2%

profile of v5, /device:TPU:0, one launch (start us, length us, event | category | flops | bytes accessed | tf_op | source)
XLA Modules:
  0.0 60.6 jit_solution(5525432097041879286)
XLA Ops:
  0.0 0.9 %copy-done = f32[256,256]{1,0:T(8,128)S(1)} copy-done((f32[256,256]{1,0:T(8,128)S(1)}, f32[256,256]{1,0:T(8,128)}, u32[]{:S(2)}) %copy-start) | copy-done | bytes 262168
  1.0 0.8 %shard_map.17 = (f32[256,128]{1,0:T(8,128)S(1)}, f32[256,128]{1,0:T(8,128)S(1)}, f32[64,128]{1,0:T(8,128)S(1)}) custom-call(f32[256,256]{1,0:T(8,128)S(1)} %copy-done), custom_call_target="tpu_custom_call" | custom-call | tf_op jit(solution)/shard_map/pallas_call | solution.py:570
  2.3 0.9 %collective-permute-done = f32[64,128]{1,0:T(8,128)S(1)} collective-permute-done((f32[64,128]{1,0:T(8,128)S(1)}, f32[64,128]{1,0:T(8,128)S(1)}, u32[]{:S(2)}, u32[]{:S(2)}) %collective-permute-start) | collective-permute-done | bytes 32800 | tf_op jit(solution)/shard_map/ppermute | solution.py:553
  3.2 2.8 %collective-permute-start.1 = (f32[64,128]{1,0:T(8,128)S(1)}, f32[64,128]{1,0:T(8,128)S(1)}, u32[]{:S(2)}, u32[]{:S(2)}) collective-permute-start(f32[64,128]{1,0:T(8,128)S(1)} %add.9.refs_0_), channel_id=1, source_target_pairs={{0,8},{4,12},{8,0},{12,4},{16,24},{20,28},{24,16},{28,20},{1,9},{5... | collective-permute-start | bytes 98312 | tf_op jit(solution)/shard_map/ppermute | solution.py:553
  6.0 1.5 %collective-permute-start.2 = (f32[64,128]{1,0:T(8,128)S(1)}, f32[64,128]{1,0:T(8,128)S(1)}, u32[]{:S(2)}, u32[]{:S(2)}) collective-permute-start(f32[64,128]{1,0:T(8,128)S(1)} %add.9.refs_0_), channel_id=1, source_target_pairs={{0,16},{4,20},{8,24},{12,28},{16,0},{20,4},{24,8},{28,12},{1,17},{... | collective-permute-start | bytes 98312 | tf_op jit(solution)/shard_map/ppermute | solution.py:553
  7.9 2.0 %collective-permute-done.2.refs_2_ = f32[64,128]{1,0:T(8,128)S(1)} collective-permute-done((f32[64,128]{1,0:T(8,128)S(1)}, f32[64,128]{1,0:T(8,128)S(1)}, u32[]{:S(2)}, u32[]{:S(2)}) %collective-permute-start.2) | collective-permute-done | bytes 32800 | tf_op jit(solution)/shard_map/ppermute | solution.py:553
  9.9 2.4 %collective-permute-done.3.refs_3_ = f32[64,128]{1,0:T(8,128)S(1)} collective-permute-done((f32[64,128]{1,0:T(8,128)S(1)}, f32[64,128]{1,0:T(8,128)S(1)}, u32[]{:S(2)}, u32[]{:S(2)}) %collective-permute-start.3) | collective-permute-done | bytes 32800 | tf_op jit(solution)/shard_map/ppermute | solution.py:553
  12.3 1.2 %shard_map.18 = (f32[256,128]{1,0:T(8,128)S(1)}, f32[256,128]{1,0:T(8,128)S(1)}) custom-call(f32[256,128]{1,0:T(8,128)S(1)} %get-tuple-element.25.even_ref, f32[256,128]{1,0:T(8,128)S(1)} %get-tuple-element.26.odd_ref, f32[64,128]{1,0:T(8,128)S(1)} %add.9.refs_0_, f32[64,128]{1,0:T(8,128)S(1)} %collective-permute-done.1.refs_1_, ...), custom_call_target="tpu_custom_call" | custom-call | tf_op jit(solution)/shard_map/pallas_call | solution.py:570
  13.5 2.6 %collective-permute-start.4 = (f32[256,128]{1,0:T(8,128)S(1)}, f32[256,128]{1,0:T(8,128)S(1)}, u32[]{:S(2)}, u32[]{:S(2)}) collective-permute-start(f32[256,128]{1,0:T(8,128)S(1)} %get-tuple-element.29), channel_id=1, source_target_pairs={{1,0},{0,2},{3,1},{2,3},{5,4},{4,6},{7,5},{6,7},{9,8},{8,10},{11,9... | collective-permute-start | bytes 393224 | tf_op jit(solution)/shard_map/ppermute | solution.py:594
  16.2 2.5 %collective-permute-done.4.came_ref = f32[256,128]{1,0:T(8,128)S(1)} collective-permute-done((f32[256,128]{1,0:T(8,128)S(1)}, f32[256,128]{1,0:T(8,128)S(1)}, u32[]{:S(2)}, u32[]{:S(2)}) %collective-permute-start.4) | collective-permute-done | bytes 131104 | tf_op jit(solution)/shard_map/ppermute | solution.py:594
  18.7 0.7 %shard_map.19 = (f32[256,128]{1,0:T(8,128)S(1)}, f32[256,128]{1,0:T(8,128)S(1)}, f32[64,128]{1,0:T(8,128)S(1)}) custom-call(f32[256,128]{1,0:T(8,128)S(1)} %get-tuple-element.28.kept_ref, f32[256,128]{1,0:T(8,128)S(1)} %collective-permute-done.4.came_ref), custom_call_target="tpu_custom_call" | custom-call | tf_op jit(solution)/shard_map/pallas_call | solution.py:570
  19.5 1.2 %collective-permute-done.5 = f32[64,128]{1,0:T(8,128)S(1)} collective-permute-done((f32[64,128]{1,0:T(8,128)S(1)}, f32[64,128]{1,0:T(8,128)S(1)}, u32[]{:S(2)}, u32[]{:S(2)}) %collective-permute-start.5) | collective-permute-done | bytes 32800 | tf_op jit(solution)/shard_map/ppermute | solution.py:553
  21.8 2.4 %collective-permute-start.8 = (f32[64,128]{1,0:T(8,128)S(1)}, f32[64,128]{1,0:T(8,128)S(1)}, u32[]{:S(2)}, u32[]{:S(2)}) collective-permute-start(f32[64,128]{1,0:T(8,128)S(1)} %add.10.refs_0_), channel_id=1, source_target_pairs={{0,24},{4,28},{8,16},{12,20},{16,8},{20,12},{24,0},{28,4},{1,25},{... | collective-permute-start | bytes 98312 | tf_op jit(solution)/shard_map/ppermute | solution.py:553
  24.6 0.9 %collective-permute-done.7.refs_2_ = f32[64,128]{1,0:T(8,128)S(1)} collective-permute-done((f32[64,128]{1,0:T(8,128)S(1)}, f32[64,128]{1,0:T(8,128)S(1)}, u32[]{:S(2)}, u32[]{:S(2)}) %collective-permute-start.7) | collective-permute-done | bytes 32800 | tf_op jit(solution)/shard_map/ppermute | solution.py:553
  25.5 1.1 %collective-permute-done.8.refs_3_ = f32[64,128]{1,0:T(8,128)S(1)} collective-permute-done((f32[64,128]{1,0:T(8,128)S(1)}, f32[64,128]{1,0:T(8,128)S(1)}, u32[]{:S(2)}, u32[]{:S(2)}) %collective-permute-start.8) | collective-permute-done | bytes 32800 | tf_op jit(solution)/shard_map/ppermute | solution.py:553
  26.6 1.2 %shard_map.20 = (f32[256,128]{1,0:T(8,128)S(1)}, f32[256,128]{1,0:T(8,128)S(1)}) custom-call(f32[256,128]{1,0:T(8,128)S(1)} %get-tuple-element.30.even_ref, f32[256,128]{1,0:T(8,128)S(1)} %get-tuple-element.31.odd_ref, f32[64,128]{1,0:T(8,128)S(1)} %add.10.refs_0_, f32[64,128]{1,0:T(8,128)S(1)} %collective-permute-done.6.refs_1_, ...), custom_call_target="tpu_custom_call" | custom-call | tf_op jit(solution)/shard_map/pallas_call | solution.py:570
  27.8 3.4 %collective-permute-start.10 = (f32[256,128]{1,0:T(8,128)S(1)}, f32[256,128]{1,0:T(8,128)S(1)}, u32[]{:S(2)}, u32[]{:S(2)}) collective-permute-start(f32[256,128]{1,0:T(8,128)S(1)} %get-tuple-element.33.kept_ref), channel_id=1, source_target_pairs={{1,0},{0,2},{3,1},{2,3},{5,4},{4,6},{7,5},{6,7},{9,8},{8,10},{11,9... | collective-permute-start | bytes 393224 | tf_op jit(solution)/shard_map/ppermute | solution.py:597
  31.2 2.9 %collective-permute-done.10.came1_ref = f32[256,128]{1,0:T(8,128)S(1)} collective-permute-done((f32[256,128]{1,0:T(8,128)S(1)}, f32[256,128]{1,0:T(8,128)S(1)}, u32[]{:S(2)}, u32[]{:S(2)}) %collective-permute-start.10) | collective-permute-done | bytes 131104 | tf_op jit(solution)/shard_map/ppermute | solution.py:597
  34.1 3.2 %collective-permute-done.9.came0_ref = f32[256,128]{1,0:T(8,128)S(1)} collective-permute-done((f32[256,128]{1,0:T(8,128)S(1)}, f32[256,128]{1,0:T(8,128)S(1)}, u32[]{:S(2)}, u32[]{:S(2)}) %collective-permute-start.9) | collective-permute-done | bytes 131104 | tf_op jit(solution)/shard_map/ppermute | solution.py:597
  37.3 1.2 %shard_map.21 = (f32[256,128]{1,0:T(8,128)S(1)}, f32[256,128]{1,0:T(8,128)S(1)}, f32[256,128]{1,0:T(8,128)S(1)}, f32[256,128]{1,0:T(8,128)S(1)}, f32[16,128]{1,0:T(8,128)S(1)}, /*index=5*/f32[144,128]{1,0:T(8,128)S(1)}) custom-call(f32[256,128]{1,0:T(8,128)S(1)} %get-tuple-element.33.kept_ref, f32[256,128]{1,0:T(8,128)S(1)} %get-tuple-element.34.sent_ref, ...), custom_call_target="tpu_custom_call" | custom-call | tf_op jit(solution)/shard_map/pallas_call | solution.py:570
  38.5 0.7 %shard_map.22 = f32[144,128]{1,0:T(8,128)S(1)} custom-call(f32[256,128]{1,0:T(8,128)S(1)} %get-tuple-element.35.even_ref, f32[256,128]{1,0:T(8,128)S(1)} %get-tuple-element.36.odd_ref, f32[16,128]{1,0:T(8,128)S(1)} %get-tuple-element.37.corner_ref), custom_call_target="tpu_custom_call" | custom-call | tf_op jit(solution)/shard_map/pallas_call | solution.py:570
  39.8 1.6 %collective-permute-start.12 = (f32[144,128]{1,0:T(8,128)S(1)}, f32[144,128]{1,0:T(8,128)S(1)}, u32[]{:S(2)}, u32[]{:S(2)}) collective-permute-start(f32[144,128]{1,0:T(8,128)S(1)} %add.11.refs_0_), channel_id=1, source_target_pairs={{0,8},{4,12},{8,0},{12,4},{16,24},{20,28},{24,16},{28,20},{1,9},{5... | collective-permute-start | bytes 221192 | tf_op jit(solution)/shard_map/ppermute | solution.py:553
  41.3 1.5 %collective-permute-start.13 = (f32[144,128]{1,0:T(8,128)S(1)}, f32[144,128]{1,0:T(8,128)S(1)}, u32[]{:S(2)}, u32[]{:S(2)}) collective-permute-start(f32[144,128]{1,0:T(8,128)S(1)} %add.11.refs_0_), channel_id=1, source_target_pairs={{0,16},{4,20},{8,24},{12,28},{16,0},{20,4},{24,8},{28,12},{1,17},{... | collective-permute-start | bytes 221192 | tf_op jit(solution)/shard_map/ppermute | solution.py:553
  43.3 0.9 %collective-permute-done.12.refs_1_ = f32[144,128]{1,0:T(8,128)S(1)} collective-permute-done((f32[144,128]{1,0:T(8,128)S(1)}, f32[144,128]{1,0:T(8,128)S(1)}, u32[]{:S(2)}, u32[]{:S(2)}) %collective-permute-start.12) | collective-permute-done | bytes 73760 | tf_op jit(solution)/shard_map/ppermute | solution.py:553
  44.2 1.5 %collective-permute-done.13.refs_2_ = f32[144,128]{1,0:T(8,128)S(1)} collective-permute-done((f32[144,128]{1,0:T(8,128)S(1)}, f32[144,128]{1,0:T(8,128)S(1)}, u32[]{:S(2)}, u32[]{:S(2)}) %collective-permute-start.13) | collective-permute-done | bytes 73760 | tf_op jit(solution)/shard_map/ppermute | solution.py:553
  45.7 2.4 %collective-permute-done.14.refs_3_ = f32[144,128]{1,0:T(8,128)S(1)} collective-permute-done((f32[144,128]{1,0:T(8,128)S(1)}, f32[144,128]{1,0:T(8,128)S(1)}, u32[]{:S(2)}, u32[]{:S(2)}) %collective-permute-start.14) | collective-permute-done | bytes 73760 | tf_op jit(solution)/shard_map/ppermute | solution.py:553
  48.0 1.3 %shard_map.23.found_ref.refs_4_ = f32[96,128]{1,0:T(8,128)S(1)} custom-call(f32[144,128]{1,0:T(8,128)S(1)} %add.11.refs_0_, f32[144,128]{1,0:T(8,128)S(1)} %collective-permute-done.12.refs_1_, f32[144,128]{1,0:T(8,128)S(1)} %collective-permute-done.13.refs_2_, f32[144,128]{1,0:T(8,128)S(1)} %collective-permute-done.14.refs_3_), custom_call_target="tpu_custom_call" | custom-call | tf_op jit(solution)/shard_map/pallas_call | solution.py:570
  49.4 0.7 %shard_map.24 = (f32[256,128]{1,0:T(8,128)S(1)}, f32[256,128]{1,0:T(8,128)S(1)}) custom-call(f32[256,128]{1,0:T(8,128)S(1)} %get-tuple-element.35.even_ref, f32[256,128]{1,0:T(8,128)S(1)} %get-tuple-element.36.odd_ref, f32[96,128]{1,0:T(8,128)S(1)} %shard_map.23.found_ref.refs_4_), custom_call_target="tpu_custom_call" | custom-call | tf_op jit(solution)/shard_map/pallas_call | solution.py:570
  50.6 2.7 %shard_map.25 = (f32[256,128]{1,0:T(8,128)S(1)}, f32[256,128]{1,0:T(8,128)S(1)}) custom-call(f32[256,128]{1,0:T(8,128)S(1)} %get-tuple-element.39.refs_0_, f32[256,128]{1,0:T(8,128)S(1)} %get-tuple-element.40.refs_1_, f32[256,128]{1,0:T(8,128)S(1)} %get-tuple-element.41.refs_2_, f32[256,128]{1,0:T(8,128)S(1)} %get-tuple-element.42.refs_3_, ...), custom_call_target="tpu_custom_call" | custom-call | tf_op jit(solution)/shard_map/pallas_call | solution.py:570
  53.4 0.7 %collective-permute-start.16 = (f32[256,128]{1,0:T(8,128)S(1)}, f32[256,128]{1,0:T(8,128)S(1)}, u32[]{:S(2)}, u32[]{:S(2)}) collective-permute-start(f32[256,128]{1,0:T(8,128)S(1)} %get-tuple-element.43), channel_id=1, source_target_pairs={{2,0},{0,1},{3,2},{1,3},{6,4},{4,5},{7,6},{5,7},{10,8},{8,9},{11,1... | collective-permute-start | bytes 393224 | tf_op jit(solution)/shard_map/ppermute | solution.py:616
  54.1 5.8 %collective-permute-done.16 = f32[256,128]{1,0:T(8,128)S(1)} collective-permute-done((f32[256,128]{1,0:T(8,128)S(1)}, f32[256,128]{1,0:T(8,128)S(1)}, u32[]{:S(2)}, u32[]{:S(2)}) %collective-permute-start.16) | collective-permute-done | bytes 131104 | tf_op jit(solution)/shard_map/ppermute | solution.py:616
  59.9 0.7 %pad_maximum_fusion = f32[256,256]{1,0:T(8,128)} fusion(f32[256,128]{1,0:T(8,128)S(1)} %get-tuple-element.46, f32[256,128]{1,0:T(8,128)S(1)} %get-tuple-element.45), kind=kLoop, calls=%fused_computation | loop fusion | flops 65536 | bytes 524288 | tf_op jit(solution)/shard_map/concatenate | solution.py:620
  (18 shorter events, 4.1 us)
Async XLA Ops:
  0.0 0.9 %copy-start = (f32[256,256]{1,0:T(8,128)S(1)}, f32[256,256]{1,0:T(8,128)}, u32[]{:S(2)}) copy-start(f32[256,256]{1,0:T(8,128)} %basis_ref.1) | copy-start | bytes 786436
  1.8 1.4 %collective-permute-start = (f32[64,128]{1,0:T(8,128)S(1)}, f32[64,128]{1,0:T(8,128)S(1)}, u32[]{:S(2)}, u32[]{:S(2)}) collective-permute-start(f32[64,128]{1,0:T(8,128)S(1)} %get-tuple-element.27), channel_id=1, source_target_pairs={{0,4},{4,0},{8,12},{12,8},{16,20},{20,16},{24,28},{28,24},{1,5},{5... | collective-permute-start | bytes 98312 | tf_op jit(solution)/shard_map/ppermute | solution.py:553
  3.2 4.7 %collective-permute-start.1 = (f32[64,128]{1,0:T(8,128)S(1)}, f32[64,128]{1,0:T(8,128)S(1)}, u32[]{:S(2)}, u32[]{:S(2)}) collective-permute-start(f32[64,128]{1,0:T(8,128)S(1)} %add.9.refs_0_), channel_id=1, source_target_pairs={{0,8},{4,12},{8,0},{12,4},{16,24},{20,28},{24,16},{28,20},{1,9},{5... | collective-permute-start | bytes 98312 | tf_op jit(solution)/shard_map/ppermute | solution.py:553
  6.0 3.9 %collective-permute-start.2 = (f32[64,128]{1,0:T(8,128)S(1)}, f32[64,128]{1,0:T(8,128)S(1)}, u32[]{:S(2)}, u32[]{:S(2)}) collective-permute-start(f32[64,128]{1,0:T(8,128)S(1)} %add.9.refs_0_), channel_id=1, source_target_pairs={{0,16},{4,20},{8,24},{12,28},{16,0},{20,4},{24,8},{28,12},{1,17},{... | collective-permute-start | bytes 98312 | tf_op jit(solution)/shard_map/ppermute | solution.py:553
  7.5 4.8 %collective-permute-start.3 = (f32[64,128]{1,0:T(8,128)S(1)}, f32[64,128]{1,0:T(8,128)S(1)}, u32[]{:S(2)}, u32[]{:S(2)}) collective-permute-start(f32[64,128]{1,0:T(8,128)S(1)} %add.9.refs_0_), channel_id=1, source_target_pairs={{0,24},{4,28},{8,16},{12,20},{16,8},{20,12},{24,0},{28,4},{1,25},{... | collective-permute-start | bytes 98312 | tf_op jit(solution)/shard_map/ppermute | solution.py:553
  13.5 5.2 %collective-permute-start.4 = (f32[256,128]{1,0:T(8,128)S(1)}, f32[256,128]{1,0:T(8,128)S(1)}, u32[]{:S(2)}, u32[]{:S(2)}) collective-permute-start(f32[256,128]{1,0:T(8,128)S(1)} %get-tuple-element.29), channel_id=1, source_target_pairs={{1,0},{0,2},{3,1},{2,3},{5,4},{4,6},{7,5},{6,7},{9,8},{8,10},{11,9... | collective-permute-start | bytes 393224 | tf_op jit(solution)/shard_map/ppermute | solution.py:594
  19.4 1.3 %collective-permute-start.5 = (f32[64,128]{1,0:T(8,128)S(1)}, f32[64,128]{1,0:T(8,128)S(1)}, u32[]{:S(2)}, u32[]{:S(2)}) collective-permute-start(f32[64,128]{1,0:T(8,128)S(1)} %get-tuple-element.32), channel_id=1, source_target_pairs={{0,4},{4,0},{8,12},{12,8},{16,20},{20,16},{24,28},{28,24},{1,5},{5... | collective-permute-start | bytes 98312 | tf_op jit(solution)/shard_map/ppermute | solution.py:553
  20.7 3.9 %collective-permute-start.6 = (f32[64,128]{1,0:T(8,128)S(1)}, f32[64,128]{1,0:T(8,128)S(1)}, u32[]{:S(2)}, u32[]{:S(2)}) collective-permute-start(f32[64,128]{1,0:T(8,128)S(1)} %add.10.refs_0_), channel_id=1, source_target_pairs={{0,8},{4,12},{8,0},{12,4},{16,24},{20,28},{24,16},{28,20},{1,9},{5... | collective-permute-start | bytes 98312 | tf_op jit(solution)/shard_map/ppermute | solution.py:553
  21.2 4.3 %collective-permute-start.7 = (f32[64,128]{1,0:T(8,128)S(1)}, f32[64,128]{1,0:T(8,128)S(1)}, u32[]{:S(2)}, u32[]{:S(2)}) collective-permute-start(f32[64,128]{1,0:T(8,128)S(1)} %add.10.refs_0_), channel_id=1, source_target_pairs={{0,16},{4,20},{8,24},{12,28},{16,0},{20,4},{24,8},{28,12},{1,17},{... | collective-permute-start | bytes 98312 | tf_op jit(solution)/shard_map/ppermute | solution.py:553
  21.8 4.8 %collective-permute-start.8 = (f32[64,128]{1,0:T(8,128)S(1)}, f32[64,128]{1,0:T(8,128)S(1)}, u32[]{:S(2)}, u32[]{:S(2)}) collective-permute-start(f32[64,128]{1,0:T(8,128)S(1)} %add.10.refs_0_), channel_id=1, source_target_pairs={{0,24},{4,28},{8,16},{12,20},{16,8},{20,12},{24,0},{28,4},{1,25},{... | collective-permute-start | bytes 98312 | tf_op jit(solution)/shard_map/ppermute | solution.py:553
  27.8 6.3 %collective-permute-start.10 = (f32[256,128]{1,0:T(8,128)S(1)}, f32[256,128]{1,0:T(8,128)S(1)}, u32[]{:S(2)}, u32[]{:S(2)}) collective-permute-start(f32[256,128]{1,0:T(8,128)S(1)} %get-tuple-element.33.kept_ref), channel_id=1, source_target_pairs={{1,0},{0,2},{3,1},{2,3},{5,4},{4,6},{7,5},{6,7},{9,8},{8,10},{11,9... | collective-permute-start | bytes 393224 | tf_op jit(solution)/shard_map/ppermute | solution.py:597
  31.2 6.1 %collective-permute-start.9 = (f32[256,128]{1,0:T(8,128)S(1)}, f32[256,128]{1,0:T(8,128)S(1)}, u32[]{:S(2)}, u32[]{:S(2)}) collective-permute-start(f32[256,128]{1,0:T(8,128)S(1)} %get-tuple-element.34.sent_ref), channel_id=1, source_target_pairs={{2,0},{3,2},{0,1},{1,3},{6,4},{7,6},{4,5},{5,7},{10,8},{11,10},{8,... | collective-permute-start | bytes 393224 | tf_op jit(solution)/shard_map/ppermute | solution.py:597
  38.4 1.3 %collective-permute-start.11 = (f32[144,128]{1,0:T(8,128)S(1)}, f32[144,128]{1,0:T(8,128)S(1)}, u32[]{:S(2)}, u32[]{:S(2)}) collective-permute-start(f32[144,128]{1,0:T(8,128)S(1)} %get-tuple-element.38), channel_id=1, source_target_pairs={{0,4},{4,0},{8,12},{12,8},{16,20},{20,16},{24,28},{28,24},{1,5},{5... | collective-permute-start | bytes 221192 | tf_op jit(solution)/shard_map/ppermute | solution.py:553
  39.8 4.4 %collective-permute-start.12 = (f32[144,128]{1,0:T(8,128)S(1)}, f32[144,128]{1,0:T(8,128)S(1)}, u32[]{:S(2)}, u32[]{:S(2)}) collective-permute-start(f32[144,128]{1,0:T(8,128)S(1)} %add.11.refs_0_), channel_id=1, source_target_pairs={{0,8},{4,12},{8,0},{12,4},{16,24},{20,28},{24,16},{28,20},{1,9},{5... | collective-permute-start | bytes 221192 | tf_op jit(solution)/shard_map/ppermute | solution.py:553
  41.3 4.4 %collective-permute-start.13 = (f32[144,128]{1,0:T(8,128)S(1)}, f32[144,128]{1,0:T(8,128)S(1)}, u32[]{:S(2)}, u32[]{:S(2)}) collective-permute-start(f32[144,128]{1,0:T(8,128)S(1)} %add.11.refs_0_), channel_id=1, source_target_pairs={{0,16},{4,20},{8,24},{12,28},{16,0},{20,4},{24,8},{28,12},{1,17},{... | collective-permute-start | bytes 221192 | tf_op jit(solution)/shard_map/ppermute | solution.py:553
  42.8 5.3 %collective-permute-start.14 = (f32[144,128]{1,0:T(8,128)S(1)}, f32[144,128]{1,0:T(8,128)S(1)}, u32[]{:S(2)}, u32[]{:S(2)}) collective-permute-start(f32[144,128]{1,0:T(8,128)S(1)} %add.11.refs_0_), channel_id=1, source_target_pairs={{0,24},{4,28},{8,16},{12,20},{16,8},{20,12},{24,0},{28,4},{1,25},{... | collective-permute-start | bytes 221192 | tf_op jit(solution)/shard_map/ppermute | solution.py:553
  49.4 1.3 %collective-permute-start.15 = (f32[96,128]{1,0:T(8,128)S(1)}, f32[96,128]{1,0:T(8,128)S(1)}, u32[]{:S(2)}, u32[]{:S(2)}) collective-permute-start(f32[96,128]{1,0:T(8,128)S(1)} %shard_map.23.found_ref.refs_4_), channel_id=1, source_target_pairs={{0,4},{4,0},{8,12},{12,8},{16,20},{20,16},{24,28},{28,24},{1,5},{5... | collective-permute-start | bytes 147464 | tf_op jit(solution)/shard_map/ppermute | solution.py:553
  53.4 6.5 %collective-permute-start.16 = (f32[256,128]{1,0:T(8,128)S(1)}, f32[256,128]{1,0:T(8,128)S(1)}, u32[]{:S(2)}, u32[]{:S(2)}) collective-permute-start(f32[256,128]{1,0:T(8,128)S(1)} %get-tuple-element.43), channel_id=1, source_target_pairs={{2,0},{0,1},{3,2},{1,3},{6,4},{4,5},{7,6},{5,7},{10,8},{8,9},{11,1... | collective-permute-start | bytes 393224 | tf_op jit(solution)/shard_map/ppermute | solution.py:616

commit v6 on v5

--- a/solution.py
+++ b/solution.py
@@ -15,6 +15,7 @@
 FAR_DIAGS = 32
 WINDOW = 32
 NEAR = 16
+STRIP = 16
 
 
 def tournament_order(pair_count):
@@ -35,26 +36,45 @@
     return min(pair + 1, pair_total - 1) if pair % 2 else pair - 1
 
 
-def moves(pair_total):
+def last_moves(pair_total):
     ordering = tournament_order(pair_total)
-    plans = []
-    for round_index in range(ROUNDS):
-        sends, sends_first, gets_first = [], set(), set()
-        for pair in range(pair_total):
-            target = host_of(pair, pair_total, round_index + 1)
-            for place in (0, 1):
-                old = int(ordering[2 * pair + place])
-                source = host_of(old // 2, pair_total, round_index)
-                if source == target:
-                    continue
-                sends.append((source, target))
-                if old % 2 == 0:
-                    sends_first.add(source)
-                if place == 0:
-                    gets_first.add(target)
-        assert len({s for s, _ in sends}) == len(sends) == len({t for _, t in sends})
-        plans.append((sends, sends_first, gets_first))
-    return plans
+    sends, sends_first, gets_first = [], set(), set()
+    for pair in range(pair_total):
+        target = host_of(pair, pair_total, ROUNDS)
+        for place in (0, 1):
+            old = int(ordering[2 * pair + place])
+            source = host_of(old // 2, pair_total, ROUNDS - 1)
+            if source == target:
+                continue
+            sends.append((source, target))
+            if old % 2 == 0:
+                sends_first.add(source)
+            if place == 0:
+                gets_first.add(target)
+    assert len({s for s, _ in sends}) == len(sends) == len({t for _, t in sends})
+    return sends, sends_first, gets_first
+
+
+def first_moves(pair_total):
+    ordering = tournament_order(pair_total)
+    sends, sends_second, gets_second, own_second = [], set(), set(), set()
+    seconds = (set(), set())
+    for pair in range(pair_total):
+        here = host_of(pair, pair_total, 1)
+        for place in (0, 1):
+            old = int(ordering[2 * pair + place])
+            if old % 2:
+                seconds[place].add(here)
+            if old // 2 == here:
+                if place:
+                    own_second.add(here)
+                continue
+            sends.append((old // 2, here))
+            if old % 2:
+                sends_second.add(old // 2)
+                gets_second.add(here)
+    assert len({s for s, _ in sends}) == len(sends) == len({t for _, t in sends})
+    return sends, sends_second, gets_second, own_second, seconds
 
 
 def fused_moves(pair_total):
@@ -198,21 +218,39 @@
         band_ref[q * diags : (q + 1) * diags, :] = band
 
 
-def open_kernel(basis_ref, even_ref, odd_ref, band_ref):
-    width = basis_ref.shape[1] // 2
+def open_kernel(sends_second, basis_ref, even_ref, odd_ref, payload_ref):
+    rows, cols = basis_ref.shape
+    width = cols // 2
+    half = width // 2
     even, odd = separate(basis_ref[:, :width], basis_ref[:, width:])
     even_ref[...] = even
     odd_ref[...] = odd
-    store_bands(even, odd, band_ref, DIAGS)
-
-
-def pair_kernel(gets_first, kept_ref, came_ref, even_ref, odd_ref, band_ref):
-    flag = among(gets_first)
-    kept, came = kept_ref[...], came_ref[...]
-    even, odd = split_pair(jnp.where(flag, came, kept), jnp.where(flag, kept, came))
-    even_ref[...] = even
-    odd_ref[...] = odd
-    store_bands(even, odd, band_ref, DIAGS)
+    flag = among(sends_second)
+    even, odd = (jnp.where(flag, left(x, half - STRIP), x) for x in (even, odd))
+    payload_ref[:rows] = jnp.where(line_lanes(even) < half, even, right(odd, half))
+    group = rows * 2 * STRIP // width
+    strips = jnp.zeros((group, width), jnp.float32)
+    for i in range(rows // group):
+        for j, x in enumerate((even, odd)):
+            start = (2 * i + j) * STRIP
+            lane = line_lanes(x)
+            here = jnp.logical_and(lane >= start, lane < start + STRIP)
+            strips = jnp.where(here, left(x[i * group : (i + 1) * group], half - start), strips)
+    payload_ref[rows:] = strips
+
+
+def unpacked(payload, rows, second):
+    width = payload.shape[1]
+    half = width // 2
+    lane = line_lanes(payload)
+    main, strips = payload[:rows], payload[rows:]
+    group = strips.shape[0]
+    columns = []
+    for j, x in enumerate((main, left(main, half))):
+        ends = [right(strips, half - (2 * i + j) * STRIP) for i in range(rows // group)]
+        x = jnp.where(lane < half, x, jnp.where(lane < half + STRIP, jnp.concatenate(ends), 0.0))
+        columns.append(jnp.where(second, right(x, half - STRIP), x))
+    return columns
 
 
 def jacobi_angle(diag_even, diag_odd, coupling):
@@ -372,18 +410,6 @@
 
 def turn_columns(even, odd, angles, shifted=None):
     return columns_home(*turned(even, odd, angles), shifted)
-
-
-def turn_kernel(sends_first, even_ref, odd_ref, *refs):
-    *band_refs, kept_ref, sent_ref = refs
-    bands = [ref[...] for ref in band_refs]
-    band = pair_sums(bands)
-    bands = [band[q * DIAGS : (q + 1) * DIAGS] for q in range(4)]
-    angles, _ = angles_of(bands, False)
-    first, second = join_pair(*turn_columns(even_ref[...], odd_ref[...], angles))
-    flag = among(sends_first)
-    kept_ref[...] = jnp.where(flag, second, first)
-    sent_ref[...] = jnp.where(flag, first, second)
 
 
 def near_starts(width):
@@ -445,6 +471,10 @@
     return bands
 
 
+def either(flag, one, other):
+    return jnp.logical_or(jnp.logical_and(flag, one), jnp.logical_and(jnp.logical_not(flag), other))
+
+
 def halves_swapped(is_second):
     return among(is_second[0]), jnp.logical_not(among(is_second[1]))
 
@@ -453,31 +483,95 @@
     return lax.axis_index("row") % 2 == 1
 
 
-def fused_open(picks, is_second, kept_ref, sent_ref, came0_ref, came1_ref, *refs):
-    *column_refs, corner_ref, other_ref = refs
-    arrays = [ref[...] for ref in (sent_ref, kept_ref, came0_ref, came1_ref)]
-    blocks = [choose(pick, arrays) for pick in picks]
-    x, y = split_pair(*blocks[:2]), split_pair(*blocks[2:])
-    corner = cross_partial(*x, *y, among(is_second[0]), among(is_second[1]))
+def far_starts(width):
+    return REACH - 1, width // 2
+
+
+def pack_far(bands, flag):
+    width = bands[0].shape[1]
+    half, count = width // 2, (FAR_DIAGS - DIAGS) // 2
+    lane = line_lanes(bands[0])
+    packed = []
+    for band in bands:
+        one, two = band[DIAGS : DIAGS + count], band[DIAGS + count :]
+        one, two = (
+            jnp.where(flag, left(x, far_starts(width)[1] - at), left(x, far_starts(width)[0] - at))
+            for x, at in ((one, 0), (two, half))
+        )
+        packed.append(jnp.concatenate((band[:DIAGS], jnp.where(lane < half, one, two)), axis=0))
+    return packed
+
+
+def unpack_far(packed, flag):
+    width = packed.shape[1]
+    half = width // 2
+    parts = [packed[:DIAGS]]
+    for at in (0, half):
+        starts = [start - at for start in far_starts(width)]
+        x = packed[DIAGS:]
+        parts.append(jnp.where(flag, right(x, starts[1]), right(x, starts[0])))
+    return jnp.concatenate(parts, axis=0)
+
+
+PACKED = DIAGS + (FAR_DIAGS - DIAGS) // 2
+
+
+def store_part(even, odd, corner, flag, part_ref):
+    bands = pack_far(dense_bands(even, odd, FAR_DIAGS), flag)
+    for q, band in enumerate(bands):
+        part_ref[q * PACKED : (q + 1) * PACKED, :] = band
+    part_ref[4 * PACKED :, :] = corner
+
+
+def open_pairs(is_second, x, y, column_refs, corner_ref, other_ref):
+    x_second, y_second = among(is_second[0]), among(is_second[1])
+    corner = cross_partial(*x, *y, x_second, y_second)
     flag = on_odd_core()
     mine = [jnp.where(flag, b, a) for a, b in zip(x, y)]
     theirs = [jnp.where(flag, a, b) for a, b in zip(x, y)]
     for ref, value in zip(column_refs, mine + theirs):
         ref[...] = value
     corner_ref[...] = jnp.where(flag, corner[NEAR:], corner[:NEAR])
-    store_bands(*theirs, other_ref, FAR_DIAGS)
-    other_ref[4 * FAR_DIAGS :, :] = jnp.where(flag, corner[:NEAR], corner[NEAR:])
-
-
-def bands_kernel(even_ref, odd_ref, corner_ref, part_ref):
-    store_bands(even_ref[...], odd_ref[...], part_ref, FAR_DIAGS)
-    part_ref[4 * FAR_DIAGS :, :] = corner_ref[...]
-
-
-def angles_kernel(*refs):
+    store_part(
+        *theirs,
+        jnp.where(flag, corner[:NEAR], corner[NEAR:]),
+        either(flag, x_second, y_second),
+        other_ref,
+    )
+
+
+def first_open(own_second, gets_second, is_second, even_ref, odd_ref, payload_ref, *refs):
+    *column_refs, corner_ref, other_ref = refs
+    own = even_ref[...], odd_ref[...]
+    came = unpacked(payload_ref[...], own[0].shape[0], among(gets_second))
+    flag = among(own_second)
+    x = [jnp.where(flag, b, a) for a, b in zip(own, came)]
+    y = [jnp.where(flag, a, b) for a, b in zip(own, came)]
+    open_pairs(is_second, x, y, column_refs, corner_ref, other_ref)
+
+
+def fused_open(picks, is_second, kept_ref, sent_ref, came0_ref, came1_ref, *refs):
+    *column_refs, corner_ref, other_ref = refs
+    arrays = [ref[...] for ref in (sent_ref, kept_ref, came0_ref, came1_ref)]
+    blocks = [choose(pick, arrays) for pick in picks]
+    x, y = split_pair(*blocks[:2]), split_pair(*blocks[2:])
+    open_pairs(is_second, x, y, column_refs, corner_ref, other_ref)
+
+
+def own_second_flag(is_second):
+    return either(on_odd_core(), among(is_second[1]), among(is_second[0]))
+
+
+def bands_kernel(is_second, even_ref, odd_ref, corner_ref, part_ref):
+    flag = own_second_flag(is_second)
+    store_part(even_ref[...], odd_ref[...], corner_ref[...], flag, part_ref)
+
+
+def angles_kernel(is_second, *refs):
     *part_refs, found_ref = refs
     part = pair_sums([ref[...] for ref in part_refs])
-    quadrants = [part[q * FAR_DIAGS : (q + 1) * FAR_DIAGS] for q in range(4)]
+    flag = own_second_flag(is_second)
+    quadrants = [unpack_far(part[q * PACKED : (q + 1) * PACKED], flag) for q in range(4)]
     angles, bands = angles_of(quadrants, True)
     for step, pair in enumerate(angles):
         for i in (0, 1):
@@ -486,7 +580,7 @@
     found_ref[2 * JSTEPS : NEAR, :] = jnp.zeros((spare, part.shape[1]), jnp.float32)
     for q in range(4):
         found_ref[NEAR + q * DIAGS : NEAR + (q + 1) * DIAGS, :] = bands[q][:DIAGS]
-    found_ref[NEAR + 4 * DIAGS :, :] = part[4 * FAR_DIAGS :]
+    found_ref[NEAR + 4 * DIAGS :, :] = part[4 * PACKED :]
 
 
 def angles_in(found):
@@ -495,16 +589,13 @@
 
 def columns_kernel(is_second, even_ref, odd_ref, found_ref, *out_refs):
     x_swapped, y_swapped = halves_swapped(is_second)
-    flag = on_odd_core()
-    swapped = jnp.logical_or(
-        jnp.logical_and(flag, y_swapped), jnp.logical_and(jnp.logical_not(flag), x_swapped)
-    )
+    swapped = either(on_odd_core(), y_swapped, x_swapped)
     columns = turn_columns(even_ref[...], odd_ref[...], angles_in(found_ref[...]), swapped)
     for ref, value in zip(out_refs, columns):
         ref[...] = value
 
 
-def last_bands(x_found, y_found, x_second, y_second):
+def next_bands(x_found, y_found, x_second, y_second):
     corner = jnp.concatenate((x_found[NEAR + 4 * DIAGS :], y_found[NEAR + 4 * DIAGS :]), axis=0)
     middle = cross_bands(corner, angles_in(x_found), angles_in(y_found), x_second, y_second)
     half = corner.shape[1] // 2
@@ -521,23 +612,22 @@
     return bands
 
 
-def last_kernel(is_second, sends_first, *refs):
+def next_kernel(is_second, sends_first, in_order, *refs):
     mine_even, mine_odd, even_ref, odd_ref, found_ref, other_ref, kept_ref, sent_ref = refs
     found, other = found_ref[...], other_ref[...]
     flag = on_odd_core()
     x_found, y_found = jnp.where(flag, other, found), jnp.where(flag, found, other)
-    bands = last_bands(x_found, y_found, among(is_second[0]), among(is_second[1]))
+    bands = next_bands(x_found, y_found, among(is_second[0]), among(is_second[1]))
     x_swapped, y_swapped = halves_swapped(is_second)
-    swapped = jnp.logical_or(
-        jnp.logical_and(flag, x_swapped), jnp.logical_and(jnp.logical_not(flag), y_swapped)
-    )
+    swapped = either(flag, x_swapped, y_swapped)
     theirs = turn_columns(even_ref[...], odd_ref[...], angles_in(other), swapped)
     low = line_lanes(found) < found.shape[1] // 2
     from_mine = jnp.logical_xor(low, flag)
     even = jnp.where(from_mine, mine_even[...], theirs[0])
     odd = jnp.where(from_mine, mine_odd[...], theirs[1])
     angles, _ = angles_of(bands, False)
-    first, second = blocks_home(*turned(even, odd, angles))
+    even, odd = turned(even, odd, angles)
+    first, second = blocks_home(even, odd) if in_order else join_pair(*columns_home(even, odd))
     flag = among(sends_first)
     kept_ref[...] = jnp.where(flag, second, first)
     sent_ref[...] = jnp.where(flag, first, second)
@@ -574,45 +664,47 @@
     )(*args)
 
 
+def two_rounds(opened, is_second, sends_first, in_order):
+    *columns, corner, other = opened
+    column, width = columns[0].shape, columns[0].shape[1]
+    other = swap(other, "row", 1)
+    bands = functools.partial(bands_kernel, is_second)
+    (mine,) = call(bands, (other.shape,), *columns[:2], corner)
+    (found,) = call(
+        functools.partial(angles_kernel, is_second),
+        ((2 * NEAR + 4 * DIAGS, width),),
+        *exchange_groups(mine + other, "row", 1),
+    )
+    other = swap(found, "row", 1)
+    turn = functools.partial(columns_kernel, is_second)
+    columns[:2] = call(turn, (column, column), *columns[:2], found)
+    turn = functools.partial(next_kernel, is_second, sends_first, in_order)
+    return call(turn, (column, column), *columns, found, other)
+
+
 def per_device(basis):
     rows, cols = basis.shape
     width = cols // 2
     pair_total = lax.axis_size("pair")
     column = (rows, width)
-    band = (4 * DIAGS, width)
-    part = (4 * FAR_DIAGS + NEAR, width)
-    plans = moves(pair_total)
-    fused_sends, fused_first, picks, is_second = fused_moves(pair_total)
-    even, odd, partial = call(open_kernel, (column, column, band), basis)
-    for round_index in range(ROUNDS - 2):
-        sends, sends_first, gets_first = plans[round_index]
-        ahead = round_index == ROUNDS - 3
-        arrays = exchange_groups(partial, "row")
-        turn = functools.partial(turn_kernel, fused_first if ahead else sends_first)
-        kept, sent = call(turn, (column, column), even, odd, *arrays)
-        if not ahead:
-            came = lax.ppermute(sent, "pair", sends)
-            opening = functools.partial(pair_kernel, gets_first)
-            even, odd, partial = call(opening, (column, column, band), kept, came)
-    came = [lax.ppermute(x, "pair", s) for x, s in zip((sent, kept), fused_sends)]
-    *columns, corner, other = call(
-        functools.partial(fused_open, picks, is_second),
-        (column,) * 4 + ((NEAR, width), part),
-        kept,
-        sent,
-        *came,
-    )
-    other = swap(other, "row", 1)
-    (mine,) = call(bands_kernel, (part,), *columns[:2], corner)
-    (found,) = call(
-        angles_kernel, ((2 * NEAR + 4 * DIAGS, width),), *exchange_groups(mine + other, "row", 1)
-    )
-    other = swap(found, "row", 1)
-    turn = functools.partial(columns_kernel, is_second)
-    columns[:2] = call(turn, (column, column), *columns[:2], found)
-    sends, sends_first, gets_first = plans[-1]
-    last = functools.partial(last_kernel, is_second, sends_first)
-    kept, sent = call(last, (column, column), *columns, found, other)
+    opened = (column,) * 4 + ((NEAR, width), (4 * PACKED + NEAR, width))
+    payload = (rows + rows * 2 * STRIP // width, width)
+
+    sends, sends_second, gets_second, own_second, is_second = first_moves(pair_total)
+    opening = functools.partial(open_kernel, sends_second)
+    even, odd, sent = call(opening, (column, column, payload), basis)
+    came = lax.ppermute(sent, "pair", sends)
+    opening = functools.partial(first_open, own_second, gets_second, is_second)
+    arrays = call(opening, opened, even, odd, came)
+    sends, sends_first, picks, next_second = fused_moves(pair_total)
+    kept, sent = two_rounds(arrays, is_second, sends_first, False)
+
+    came = [lax.ppermute(x, "pair", s) for x, s in zip((sent, kept), sends)]
+    opening = functools.partial(fused_open, picks, next_second)
+    arrays = call(opening, opened, kept, sent, *came)
+    sends, sends_first, gets_first = last_moves(pair_total)
+    kept, sent = two_rounds(arrays, next_second, sends_first, True)
+
     came = lax.ppermute(sent, "pair", sends)
     flag = among(gets_first)
     first = jnp.where(flag, came, kept)

time: 60.8 us -> 56.8 us (0.934)
  waiting for transfers between devices: 29.4 us -> 24.2 us
  Pallas kernels: 10.6 us -> 13.9 us
  starting transfers between devices: 18.8 us -> 16.7 us
    ppermute x13 -> x10, waiting for transfers between devices: 15 us -> 9.42 us  [swap(): lax.ppermute(x, axis, [(i, i ^ mask) for i in range(lax.axis_size(axis))])]
    ppermute x13 -> x10, starting transfers between devices: 12.1 us -> 7.35 us  [swap(): lax.ppermute(x, axis, [(i, i ^ mask) for i in range(lax.axis_size(axis))])]
    pallas_call x9 -> x11, Pallas kernels: 10.6 us -> 13.9 us  [call(): pl.pallas_call(kernel, out_shape=out, compiler_params=pltpu.CompilerParam...]
    ppermute x2, starting transfers between devices: 3.37 us -> 5.88 us  [per_device(): came = lax.ppermute(sent, 'pair', sends)]
  transfers between devices with their start and end apart: 17 -> 14, of which waited for: 17 -> 14; matrix products, arithmetic and copies ran while one was open for 0% -> 0% of each run, Pallas kernels for 2% -> 5%
where the time goes in v6:
time: 56.8 us; the launch traced here: 56.6 us
  waiting for transfers between devices  24.2 us (43%)
  starting transfers between devices  16.7 us (29%)
  Pallas kernels  13.9 us (24%)
  local copies, waits for them, and re-layouts  0.95 us (2%)
  other arithmetic  0.76 us (1%)
    pallas_call x11, Pallas kernels, call(): pl.pallas_call(kernel, out_shape=out, compiler_params=pltpu.CompilerParam...  13.9 us
    ppermute x10, waiting for transfers between devices, swap(): lax.ppermute(x, axis, [(i, i ^ mask) for i in range(lax.axis_size(axis))])  9.42 us
    ppermute x2, waiting for transfers between devices, per_device(): came = lax.ppermute(sent, 'pair', sends)  8.18 us
    ppermute x10, starting transfers between devices, swap(): lax.ppermute(x, axis, [(i, i ^ mask) for i in range(lax.axis_size(axis))])  7.35 us
    ppermute x2, waiting for transfers between devices, per_device(): came = [lax.ppermute(x, 'pair', s) for x, s in zip((sent, kept), sends)]  6.56 us
    ppermute x2, starting transfers between devices, per_device(): came = lax.ppermute(sent, 'pair', sends)  5.88 us
    ppermute x2, starting transfers between devices, per_device(): came = [lax.ppermute(x, 'pair', s) for x, s in zip((sent, kept), sends)]  3.5 us
  transfers between devices with their start and end apart: 14, of which 14 were waited for; matrix products, arithmetic and copies ran while one was open for 0% of the time, Pallas kernels for 5%

profile of v6, /device:TPU:0, one launch (start us, length us, event | category | flops | bytes accessed | tf_op | source)
XLA Modules:
  0.0 56.6 jit_solution(12882988510176618589)
XLA Ops:
  0.0 0.9 %copy-done = f32[256,256]{1,0:T(8,128)S(1)} copy-done((f32[256,256]{1,0:T(8,128)S(1)}, f32[256,256]{1,0:T(8,128)}, u32[]{:S(2)}) %copy-start) | copy-done | bytes 262168
  1.4 4.1 %collective-permute-start = (f32[320,128]{1,0:T(8,128)S(1)}, f32[320,128]{1,0:T(8,128)S(1)}, u32[]{:S(2)}, u32[]{:S(2)}) collective-permute-start(f32[320,128]{1,0:T(8,128)S(1)} %get-tuple-element.30), channel_id=1, source_target_pairs={{1,0},{0,2},{3,1},{2,3},{5,4},{4,6},{7,5},{6,7},{9,8},{8,10},{11,9... | collective-permute-start | bytes 491528 | tf_op jit(solution)/shard_map/ppermute | solution.py:696
  5.4 3.5 %collective-permute-done.payload_ref = f32[320,128]{1,0:T(8,128)S(1)} collective-permute-done((f32[320,128]{1,0:T(8,128)S(1)}, f32[320,128]{1,0:T(8,128)S(1)}, u32[]{:S(2)}, u32[]{:S(2)}) %collective-permute-start) | collective-permute-done | bytes 163872 | tf_op jit(solution)/shard_map/ppermute | solution.py:696
  8.9 1.3 %shard_map.18 = (f32[256,128]{1,0:T(8,128)S(1)}, f32[256,128]{1,0:T(8,128)S(1)}, f32[256,128]{1,0:T(8,128)S(1)}, f32[256,128]{1,0:T(8,128)S(1)}, f32[16,128]{1,0:T(8,128)S(1)}, /*index=5*/f32[112,128]{1,0:T(8,128)S(1)}) custom-call(f32[256,128]{1,0:T(8,128)S(1)} %get-tuple-element.28.even_ref, f32[256,128]{1,0:T(8,128)S(1)} %get-tuple-element.29.odd_ref, ...), custom_call_target="tpu_custom_call" | custom-call | tf_op jit(solution)/shard_map/pallas_call | solution.py:660
  10.3 0.7 %shard_map.19 = f32[112,128]{1,0:T(8,128)S(1)} custom-call(f32[256,128]{1,0:T(8,128)S(1)} %get-tuple-element.31.even_ref, f32[256,128]{1,0:T(8,128)S(1)} %get-tuple-element.32.odd_ref, f32[16,128]{1,0:T(8,128)S(1)} %get-tuple-element.33.corner_ref), custom_call_target="tpu_custom_call" | custom-call | tf_op jit(solution)/shard_map/pallas_call | solution.py:660
  11.0 0.5 collective-permute-done.1
  11.5 1.6 %collective-permute-start.2 = (f32[112,128]{1,0:T(8,128)S(1)}, f32[112,128]{1,0:T(8,128)S(1)}, u32[]{:S(2)}, u32[]{:S(2)}) collective-permute-start(f32[112,128]{1,0:T(8,128)S(1)} %add.6.refs_0_), channel_id=1, source_target_pairs={{0,8},{4,12},{8,0},{12,4},{16,24},{20,28},{24,16},{28,20},{1,9},{5... | collective-permute-start | bytes 172040 | tf_op jit(solution)/shard_map/ppermute | solution.py:643
  13.1 1.5 %collective-permute-start.3 = (f32[112,128]{1,0:T(8,128)S(1)}, f32[112,128]{1,0:T(8,128)S(1)}, u32[]{:S(2)}, u32[]{:S(2)}) collective-permute-start(f32[112,128]{1,0:T(8,128)S(1)} %add.6.refs_0_), channel_id=1, source_target_pairs={{0,16},{4,20},{8,24},{12,28},{16,0},{20,4},{24,8},{28,12},{1,17},{... | collective-permute-start | bytes 172040 | tf_op jit(solution)/shard_map/ppermute | solution.py:643
  15.1 0.7 %collective-permute-done.2.refs_1_ = f32[112,128]{1,0:T(8,128)S(1)} collective-permute-done((f32[112,128]{1,0:T(8,128)S(1)}, f32[112,128]{1,0:T(8,128)S(1)}, u32[]{:S(2)}, u32[]{:S(2)}) %collective-permute-start.2) | collective-permute-done | bytes 57376 | tf_op jit(solution)/shard_map/ppermute | solution.py:643
  15.8 1.5 %collective-permute-done.3.refs_2_ = f32[112,128]{1,0:T(8,128)S(1)} collective-permute-done((f32[112,128]{1,0:T(8,128)S(1)}, f32[112,128]{1,0:T(8,128)S(1)}, u32[]{:S(2)}, u32[]{:S(2)}) %collective-permute-start.3) | collective-permute-done | bytes 57376 | tf_op jit(solution)/shard_map/ppermute | solution.py:643
  17.2 2.4 %collective-permute-done.4.refs_3_ = f32[112,128]{1,0:T(8,128)S(1)} collective-permute-done((f32[112,128]{1,0:T(8,128)S(1)}, f32[112,128]{1,0:T(8,128)S(1)}, u32[]{:S(2)}, u32[]{:S(2)}) %collective-permute-start.4) | collective-permute-done | bytes 57376 | tf_op jit(solution)/shard_map/ppermute | solution.py:643
  19.7 1.3 %shard_map.20.found_ref.refs_4_ = f32[96,128]{1,0:T(8,128)S(1)} custom-call(f32[112,128]{1,0:T(8,128)S(1)} %add.6.refs_0_, f32[112,128]{1,0:T(8,128)S(1)} %collective-permute-done.2.refs_1_, f32[112,128]{1,0:T(8,128)S(1)} %collective-permute-done.3.refs_2_, f32[112,128]{1,0:T(8,128)S(1)} %collective-permute-done.4.refs_3_), custom_call_target="tpu_custom_call" | custom-call | tf_op jit(solution)/shard_map/pallas_call | solution.py:660
  21.1 0.7 %shard_map.21 = (f32[256,128]{1,0:T(8,128)S(1)}, f32[256,128]{1,0:T(8,128)S(1)}) custom-call(f32[256,128]{1,0:T(8,128)S(1)} %get-tuple-element.31.even_ref, f32[256,128]{1,0:T(8,128)S(1)} %get-tuple-element.32.odd_ref, f32[96,128]{1,0:T(8,128)S(1)} %shard_map.20.found_ref.refs_4_), custom_call_target="tpu_custom_call" | custom-call | tf_op jit(solution)/shard_map/pallas_call | solution.py:660
  22.3 2.7 %shard_map.22 = (f32[256,128]{1,0:T(8,128)S(1)}, f32[256,128]{1,0:T(8,128)S(1)}) custom-call(f32[256,128]{1,0:T(8,128)S(1)} %get-tuple-element.35.refs_0_, f32[256,128]{1,0:T(8,128)S(1)} %get-tuple-element.36.refs_1_, f32[256,128]{1,0:T(8,128)S(1)} %get-tuple-element.37.refs_2_, f32[256,128]{1,0:T(8,128)S(1)} %get-tuple-element.38.refs_3_, ...), custom_call_target="tpu_custom_call" | custom-call | tf_op jit(solution)/shard_map/pallas_call | solution.py:660
  25.0 2.4 %collective-permute-start.6 = (f32[256,128]{1,0:T(8,128)S(1)}, f32[256,128]{1,0:T(8,128)S(1)}, u32[]{:S(2)}, u32[]{:S(2)}) collective-permute-start(f32[256,128]{1,0:T(8,128)S(1)} %get-tuple-element.40.sent_ref), channel_id=1, source_target_pairs={{2,0},{3,2},{0,1},{1,3},{6,4},{7,6},{4,5},{5,7},{10,8},{11,10},{8,... | collective-permute-start | bytes 393224 | tf_op jit(solution)/shard_map/ppermute | solution.py:702
  27.4 1.1 %collective-permute-start.7 = (f32[256,128]{1,0:T(8,128)S(1)}, f32[256,128]{1,0:T(8,128)S(1)}, u32[]{:S(2)}, u32[]{:S(2)}) collective-permute-start(f32[256,128]{1,0:T(8,128)S(1)} %get-tuple-element.39.kept_ref), channel_id=1, source_target_pairs={{1,0},{0,2},{3,1},{2,3},{5,4},{4,6},{7,5},{6,7},{9,8},{8,10},{11,9... | collective-permute-start | bytes 393224 | tf_op jit(solution)/shard_map/ppermute | solution.py:702
  28.5 3.9 %collective-permute-done.6.came0_ref = f32[256,128]{1,0:T(8,128)S(1)} collective-permute-done((f32[256,128]{1,0:T(8,128)S(1)}, f32[256,128]{1,0:T(8,128)S(1)}, u32[]{:S(2)}, u32[]{:S(2)}) %collective-permute-start.6) | collective-permute-done | bytes 131104 | tf_op jit(solution)/shard_map/ppermute | solution.py:702
  32.4 2.7 %collective-permute-done.7.came1_ref = f32[256,128]{1,0:T(8,128)S(1)} collective-permute-done((f32[256,128]{1,0:T(8,128)S(1)}, f32[256,128]{1,0:T(8,128)S(1)}, u32[]{:S(2)}, u32[]{:S(2)}) %collective-permute-start.7) | collective-permute-done | bytes 131104 | tf_op jit(solution)/shard_map/ppermute | solution.py:702
  35.1 1.2 %shard_map.23 = (f32[256,128]{1,0:T(8,128)S(1)}, f32[256,128]{1,0:T(8,128)S(1)}, f32[256,128]{1,0:T(8,128)S(1)}, f32[256,128]{1,0:T(8,128)S(1)}, f32[16,128]{1,0:T(8,128)S(1)}, /*index=5*/f32[112,128]{1,0:T(8,128)S(1)}) custom-call(f32[256,128]{1,0:T(8,128)S(1)} %get-tuple-element.39.kept_ref, f32[256,128]{1,0:T(8,128)S(1)} %get-tuple-element.40.sent_ref, ...), custom_call_target="tpu_custom_call" | custom-call | tf_op jit(solution)/shard_map/pallas_call | solution.py:660
  36.4 0.7 %shard_map.24 = f32[112,128]{1,0:T(8,128)S(1)} custom-call(f32[256,128]{1,0:T(8,128)S(1)} %get-tuple-element.41.even_ref, f32[256,128]{1,0:T(8,128)S(1)} %get-tuple-element.42.odd_ref, f32[16,128]{1,0:T(8,128)S(1)} %get-tuple-element.43.corner_ref), custom_call_target="tpu_custom_call" | custom-call | tf_op jit(solution)/shard_map/pallas_call | solution.py:660
  37.6 0.6 %collective-permute-start.10 = (f32[112,128]{1,0:T(8,128)S(1)}, f32[112,128]{1,0:T(8,128)S(1)}, u32[]{:S(2)}, u32[]{:S(2)}) collective-permute-start(f32[112,128]{1,0:T(8,128)S(1)} %add.7.refs_0_), channel_id=1, source_target_pairs={{0,16},{4,20},{8,24},{12,28},{16,0},{20,4},{24,8},{28,12},{1,17},{... | collective-permute-start | bytes 172040 | tf_op jit(solution)/shard_map/ppermute | solution.py:643
  38.2 1.5 %collective-permute-start.11 = (f32[112,128]{1,0:T(8,128)S(1)}, f32[112,128]{1,0:T(8,128)S(1)}, u32[]{:S(2)}, u32[]{:S(2)}) collective-permute-start(f32[112,128]{1,0:T(8,128)S(1)} %add.7.refs_0_), channel_id=1, source_target_pairs={{0,24},{4,28},{8,16},{12,20},{16,8},{20,12},{24,0},{28,4},{1,25},{... | collective-permute-start | bytes 172040 | tf_op jit(solution)/shard_map/ppermute | solution.py:643
  39.7 1.5 %collective-permute-start.9 = (f32[112,128]{1,0:T(8,128)S(1)}, f32[112,128]{1,0:T(8,128)S(1)}, u32[]{:S(2)}, u32[]{:S(2)}) collective-permute-start(f32[112,128]{1,0:T(8,128)S(1)} %add.7.refs_0_), channel_id=1, source_target_pairs={{0,8},{4,12},{8,0},{12,4},{16,24},{20,28},{24,16},{28,20},{1,9},{5... | collective-permute-start | bytes 172040 | tf_op jit(solution)/shard_map/ppermute | solution.py:643
  41.2 1.3 %collective-permute-done.10.refs_2_ = f32[112,128]{1,0:T(8,128)S(1)} collective-permute-done((f32[112,128]{1,0:T(8,128)S(1)}, f32[112,128]{1,0:T(8,128)S(1)}, u32[]{:S(2)}, u32[]{:S(2)}) %collective-permute-start.10) | collective-permute-done | bytes 57376 | tf_op jit(solution)/shard_map/ppermute | solution.py:643
  42.5 0.9 %collective-permute-done.11.refs_3_ = f32[112,128]{1,0:T(8,128)S(1)} collective-permute-done((f32[112,128]{1,0:T(8,128)S(1)}, f32[112,128]{1,0:T(8,128)S(1)}, u32[]{:S(2)}, u32[]{:S(2)}) %collective-permute-start.11) | collective-permute-done | bytes 57376 | tf_op jit(solution)/shard_map/ppermute | solution.py:643
  43.4 0.7 %collective-permute-done.9.refs_1_ = f32[112,128]{1,0:T(8,128)S(1)} collective-permute-done((f32[112,128]{1,0:T(8,128)S(1)}, f32[112,128]{1,0:T(8,128)S(1)}, u32[]{:S(2)}, u32[]{:S(2)}) %collective-permute-start.9) | collective-permute-done | bytes 57376 | tf_op jit(solution)/shard_map/ppermute | solution.py:643
  44.0 1.3 %shard_map.25.found_ref.refs_4_ = f32[96,128]{1,0:T(8,128)S(1)} custom-call(f32[112,128]{1,0:T(8,128)S(1)} %add.7.refs_0_, f32[112,128]{1,0:T(8,128)S(1)} %collective-permute-done.9.refs_1_, f32[112,128]{1,0:T(8,128)S(1)} %collective-permute-done.10.refs_2_, f32[112,128]{1,0:T(8,128)S(1)} %collective-permute-done.11.refs_3_), custom_call_target="tpu_custom_call" | custom-call | tf_op jit(solution)/shard_map/pallas_call | solution.py:660
  45.4 0.7 %shard_map.26 = (f32[256,128]{1,0:T(8,128)S(1)}, f32[256,128]{1,0:T(8,128)S(1)}) custom-call(f32[256,128]{1,0:T(8,128)S(1)} %get-tuple-element.41.even_ref, f32[256,128]{1,0:T(8,128)S(1)} %get-tuple-element.42.odd_ref, f32[96,128]{1,0:T(8,128)S(1)} %shard_map.25.found_ref.refs_4_), custom_call_target="tpu_custom_call" | custom-call | tf_op jit(solution)/shard_map/pallas_call | solution.py:660
  46.6 2.7 %shard_map.27 = (f32[256,128]{1,0:T(8,128)S(1)}, f32[256,128]{1,0:T(8,128)S(1)}) custom-call(f32[256,128]{1,0:T(8,128)S(1)} %get-tuple-element.45.refs_0_, f32[256,128]{1,0:T(8,128)S(1)} %get-tuple-element.46.refs_1_, f32[256,128]{1,0:T(8,128)S(1)} %get-tuple-element.47.refs_2_, f32[256,128]{1,0:T(8,128)S(1)} %get-tuple-element.48.refs_3_, ...), custom_call_target="tpu_custom_call" | custom-call | tf_op jit(solution)/shard_map/pallas_call | solution.py:660
  49.4 1.8 %collective-permute-start.13 = (f32[256,128]{1,0:T(8,128)S(1)}, f32[256,128]{1,0:T(8,128)S(1)}, u32[]{:S(2)}, u32[]{:S(2)}) collective-permute-start(f32[256,128]{1,0:T(8,128)S(1)} %get-tuple-element.49), channel_id=1, source_target_pairs={{2,0},{0,1},{3,2},{1,3},{6,4},{4,5},{7,6},{5,7},{10,8},{8,9},{11,1... | collective-permute-start | bytes 393224 | tf_op jit(solution)/shard_map/ppermute | solution.py:708
  51.2 4.7 %collective-permute-done.13 = f32[256,128]{1,0:T(8,128)S(1)} collective-permute-done((f32[256,128]{1,0:T(8,128)S(1)}, f32[256,128]{1,0:T(8,128)S(1)}, u32[]{:S(2)}, u32[]{:S(2)}) %collective-permute-start.13) | collective-permute-done | bytes 131104 | tf_op jit(solution)/shard_map/ppermute | solution.py:708
  55.9 0.7 %pad_maximum_fusion = f32[256,256]{1,0:T(8,128)} fusion(f32[256,128]{1,0:T(8,128)S(1)} %get-tuple-element.52, f32[256,128]{1,0:T(8,128)S(1)} %get-tuple-element.51), kind=kLoop, calls=%fused_computation | loop fusion | flops 65536 | bytes 524288 | tf_op jit(solution)/shard_map/concatenate | solution.py:712
  (13 shorter events, 2.6 us)
Async XLA Ops:
  0.0 0.9 %copy-start = (f32[256,256]{1,0:T(8,128)S(1)}, f32[256,256]{1,0:T(8,128)}, u32[]{:S(2)}) copy-start(f32[256,256]{1,0:T(8,128)} %basis_ref.1) | copy-start | bytes 786436
  1.4 7.5 %collective-permute-start = (f32[320,128]{1,0:T(8,128)S(1)}, f32[320,128]{1,0:T(8,128)S(1)}, u32[]{:S(2)}, u32[]{:S(2)}) collective-permute-start(f32[320,128]{1,0:T(8,128)S(1)} %get-tuple-element.30), channel_id=1, source_target_pairs={{1,0},{0,2},{3,1},{2,3},{5,4},{4,6},{7,5},{6,7},{9,8},{8,10},{11,9... | collective-permute-start | bytes 491528 | tf_op jit(solution)/shard_map/ppermute | solution.py:696
  10.2 1.3 %collective-permute-start.1 = (f32[112,128]{1,0:T(8,128)S(1)}, f32[112,128]{1,0:T(8,128)S(1)}, u32[]{:S(2)}, u32[]{:S(2)}) collective-permute-start(f32[112,128]{1,0:T(8,128)S(1)} %get-tuple-element.34), channel_id=1, source_target_pairs={{0,4},{4,0},{8,12},{12,8},{16,20},{20,16},{24,28},{28,24},{1,5},{5... | collective-permute-start | bytes 172040 | tf_op jit(solution)/shard_map/ppermute | solution.py:643
  11.5 4.2 %collective-permute-start.2 = (f32[112,128]{1,0:T(8,128)S(1)}, f32[112,128]{1,0:T(8,128)S(1)}, u32[]{:S(2)}, u32[]{:S(2)}) collective-permute-start(f32[112,128]{1,0:T(8,128)S(1)} %add.6.refs_0_), channel_id=1, source_target_pairs={{0,8},{4,12},{8,0},{12,4},{16,24},{20,28},{24,16},{28,20},{1,9},{5... | collective-permute-start | bytes 172040 | tf_op jit(solution)/shard_map/ppermute | solution.py:643
  13.1 4.2 %collective-permute-start.3 = (f32[112,128]{1,0:T(8,128)S(1)}, f32[112,128]{1,0:T(8,128)S(1)}, u32[]{:S(2)}, u32[]{:S(2)}) collective-permute-start(f32[112,128]{1,0:T(8,128)S(1)} %add.6.refs_0_), channel_id=1, source_target_pairs={{0,16},{4,20},{8,24},{12,28},{16,0},{20,4},{24,8},{28,12},{1,17},{... | collective-permute-start | bytes 172040 | tf_op jit(solution)/shard_map/ppermute | solution.py:643
  14.6 5.1 %collective-permute-start.4 = (f32[112,128]{1,0:T(8,128)S(1)}, f32[112,128]{1,0:T(8,128)S(1)}, u32[]{:S(2)}, u32[]{:S(2)}) collective-permute-start(f32[112,128]{1,0:T(8,128)S(1)} %add.6.refs_0_), channel_id=1, source_target_pairs={{0,24},{4,28},{8,16},{12,20},{16,8},{20,12},{24,0},{28,4},{1,25},{... | collective-permute-start | bytes 172040 | tf_op jit(solution)/shard_map/ppermute | solution.py:643
  21.0 1.3 %collective-permute-start.5 = (f32[96,128]{1,0:T(8,128)S(1)}, f32[96,128]{1,0:T(8,128)S(1)}, u32[]{:S(2)}, u32[]{:S(2)}) collective-permute-start(f32[96,128]{1,0:T(8,128)S(1)} %shard_map.20.found_ref.refs_4_), channel_id=1, source_target_pairs={{0,4},{4,0},{8,12},{12,8},{16,20},{20,16},{24,28},{28,24},{1,5},{5... | collective-permute-start | bytes 147464 | tf_op jit(solution)/shard_map/ppermute | solution.py:643
  25.0 7.4 %collective-permute-start.6 = (f32[256,128]{1,0:T(8,128)S(1)}, f32[256,128]{1,0:T(8,128)S(1)}, u32[]{:S(2)}, u32[]{:S(2)}) collective-permute-start(f32[256,128]{1,0:T(8,128)S(1)} %get-tuple-element.40.sent_ref), channel_id=1, source_target_pairs={{2,0},{3,2},{0,1},{1,3},{6,4},{7,6},{4,5},{5,7},{10,8},{11,10},{8,... | collective-permute-start | bytes 393224 | tf_op jit(solution)/shard_map/ppermute | solution.py:702
  27.4 7.6 %collective-permute-start.7 = (f32[256,128]{1,0:T(8,128)S(1)}, f32[256,128]{1,0:T(8,128)S(1)}, u32[]{:S(2)}, u32[]{:S(2)}) collective-permute-start(f32[256,128]{1,0:T(8,128)S(1)} %get-tuple-element.39.kept_ref), channel_id=1, source_target_pairs={{1,0},{0,2},{3,1},{2,3},{5,4},{4,6},{7,5},{6,7},{9,8},{8,10},{11,9... | collective-permute-start | bytes 393224 | tf_op jit(solution)/shard_map/ppermute | solution.py:702
  36.3 1.3 %collective-permute-start.8 = (f32[112,128]{1,0:T(8,128)S(1)}, f32[112,128]{1,0:T(8,128)S(1)}, u32[]{:S(2)}, u32[]{:S(2)}) collective-permute-start(f32[112,128]{1,0:T(8,128)S(1)} %get-tuple-element.44), channel_id=1, source_target_pairs={{0,4},{4,0},{8,12},{12,8},{16,20},{20,16},{24,28},{28,24},{1,5},{5... | collective-permute-start | bytes 172040 | tf_op jit(solution)/shard_map/ppermute | solution.py:643
  37.6 4.9 %collective-permute-start.10 = (f32[112,128]{1,0:T(8,128)S(1)}, f32[112,128]{1,0:T(8,128)S(1)}, u32[]{:S(2)}, u32[]{:S(2)}) collective-permute-start(f32[112,128]{1,0:T(8,128)S(1)} %add.7.refs_0_), channel_id=1, source_target_pairs={{0,16},{4,20},{8,24},{12,28},{16,0},{20,4},{24,8},{28,12},{1,17},{... | collective-permute-start | bytes 172040 | tf_op jit(solution)/shard_map/ppermute | solution.py:643
  38.2 5.2 %collective-permute-start.11 = (f32[112,128]{1,0:T(8,128)S(1)}, f32[112,128]{1,0:T(8,128)S(1)}, u32[]{:S(2)}, u32[]{:S(2)}) collective-permute-start(f32[112,128]{1,0:T(8,128)S(1)} %add.7.refs_0_), channel_id=1, source_target_pairs={{0,24},{4,28},{8,16},{12,20},{16,8},{20,12},{24,0},{28,4},{1,25},{... | collective-permute-start | bytes 172040 | tf_op jit(solution)/shard_map/ppermute | solution.py:643
  39.7 4.4 %collective-permute-start.9 = (f32[112,128]{1,0:T(8,128)S(1)}, f32[112,128]{1,0:T(8,128)S(1)}, u32[]{:S(2)}, u32[]{:S(2)}) collective-permute-start(f32[112,128]{1,0:T(8,128)S(1)} %add.7.refs_0_), channel_id=1, source_target_pairs={{0,8},{4,12},{8,0},{12,4},{16,24},{20,28},{24,16},{28,20},{1,9},{5... | collective-permute-start | bytes 172040 | tf_op jit(solution)/shard_map/ppermute | solution.py:643
  45.4 1.3 %collective-permute-start.12 = (f32[96,128]{1,0:T(8,128)S(1)}, f32[96,128]{1,0:T(8,128)S(1)}, u32[]{:S(2)}, u32[]{:S(2)}) collective-permute-start(f32[96,128]{1,0:T(8,128)S(1)} %shard_map.25.found_ref.refs_4_), channel_id=1, source_target_pairs={{0,4},{4,0},{8,12},{12,8},{16,20},{20,16},{24,28},{28,24},{1,5},{5... | collective-permute-start | bytes 147464 | tf_op jit(solution)/shard_map/ppermute | solution.py:643
  49.4 6.5 %collective-permute-start.13 = (f32[256,128]{1,0:T(8,128)S(1)}, f32[256,128]{1,0:T(8,128)S(1)}, u32[]{:S(2)}, u32[]{:S(2)}) collective-permute-start(f32[256,128]{1,0:T(8,128)S(1)} %get-tuple-element.49), channel_id=1, source_target_pairs={{2,0},{0,1},{3,2},{1,3},{6,4},{4,5},{7,6},{5,7},{10,8},{8,9},{11,1... | collective-permute-start | bytes 393224 | tf_op jit(solution)/shard_map/ppermute | solution.py:708

commit v7 on v6

--- a/solution.py
+++ b/solution.py
@@ -439,28 +439,33 @@
     return jnp.where(low, corner[:WINDOW], right(corner[WINDOW : 2 * WINDOW], 2 * WINDOW))
 
 
-def spread(packed, place, flag, starts):
-    at = place * WINDOW
-    return jnp.where(flag, right(packed, starts[1] - at), right(packed, starts[0] - at))
-
-
-def cross_bands(corner, x_angles, y_angles, x_second, y_second):
-    width = corner.shape[1]
+def own_rotation(angles, second, swapped, first_pair):
+    width = angles[0][0].shape[1]
     half = width // 2
     x_starts, y_starts = near_starts(width)
-    even = jnp.concatenate([spread(corner, p, x_second, x_starts) for p in (0, 2)], axis=0)
-    odd = jnp.concatenate([spread(corner, p, x_second, x_starts) for p in (1, 3)], axis=0)
-    even, odd = turn_columns(even, odd, x_angles)
-    stacked = jnp.concatenate((even, odd), axis=0)
-    ends = jnp.where(x_second, left(stacked, width - NEAR), left(stacked, half - NEAR))
-    ends = jnp.transpose(ends)[:NEAR]
-    even = jnp.concatenate([spread(ends, p, y_second, y_starts) for p in (0, 2)], axis=0)
-    odd = jnp.concatenate([spread(ends, p, y_second, y_starts) for p in (1, 3)], axis=0)
-    even, odd = turn_columns(even, odd, y_angles)
-    even = jnp.where(y_second, even, right(even, half))
-    odd = jnp.where(y_second, odd, right(odd, half))
-    quadrants = (even[:NEAR], odd[:NEAR], even[NEAR:], odd[NEAR:])
-    offset = lanes_of(ends) - lax.broadcasted_iota(jnp.int32, ends.shape, 0) - (half - NEAR)
+    starts = [jnp.where(first_pair, x, y) for x, y in zip(x_starts, y_starts)]
+    shape = (2 * WINDOW, width)
+    row = lax.broadcasted_iota(jnp.int32, shape, 0)
+    lane = lax.broadcasted_iota(jnp.int32, shape, 1) - jnp.where(second, starts[1], starts[0])
+    even, odd = (
+        jnp.where(jnp.logical_and(row == lane + at, row // WINDOW == at // WINDOW), 1.0, 0.0)
+        for at in (0, WINDOW)
+    )
+    even, odd = turn_columns(even, odd, angles, swapped)
+    low = lax.broadcasted_iota(jnp.int32, shape, 1) < half
+    return jnp.where(jnp.logical_xor(low, first_pair), right(odd, half), even)
+
+
+def cross_bands(packed, x_rotation, y_rotation):
+    width = packed.shape[1]
+    half = width // 2
+    corner = jnp.concatenate((packed[:, :half], right(packed, half)[:, :half]), axis=0)
+    highest = dict(precision=lax.Precision.HIGHEST, preferred_element_type=jnp.float32)
+    turned_x = jnp.dot(corner, x_rotation, **highest)
+    ends = lax.dot_general(turned_x, y_rotation, (((0,), (0,)), ((), ())), **highest)
+    even, odd = ends[half - NEAR : half], ends[width - NEAR :]
+    quadrants = (even, right(even, half), odd, right(odd, half))
+    offset = lanes_of(even) - lax.broadcasted_iota(jnp.int32, even.shape, 0) - (half - NEAR)
     diag = lax.broadcasted_iota(jnp.int32, (DIAGS, width), 0)
     bands = [jnp.zeros((DIAGS, width), jnp.float32) for _ in quadrants]
     for d in range(1, REACH):
@@ -558,6 +563,11 @@
     open_pairs(is_second, x, y, column_refs, corner_ref, other_ref)
 
 
+def swapped_flag(is_second):
+    x_swapped, y_swapped = halves_swapped(is_second)
+    return either(on_odd_core(), y_swapped, x_swapped)
+
+
 def own_second_flag(is_second):
     return either(on_odd_core(), among(is_second[1]), among(is_second[0]))
 
@@ -580,7 +590,14 @@
     found_ref[2 * JSTEPS : NEAR, :] = jnp.zeros((spare, part.shape[1]), jnp.float32)
     for q in range(4):
         found_ref[NEAR + q * DIAGS : NEAR + (q + 1) * DIAGS, :] = bands[q][:DIAGS]
-    found_ref[NEAR + 4 * DIAGS :, :] = part[4 * PACKED :]
+    found_ref[CORNER:ROTATION, :] = part[4 * PACKED :]
+    first_pair = jnp.logical_not(on_odd_core())
+    found_ref[ROTATION:, :] = own_rotation(angles, flag, swapped_flag(is_second), first_pair)
+
+
+CORNER = NEAR + 4 * DIAGS
+ROTATION = CORNER + NEAR
+FOUND = ROTATION + 2 * WINDOW
 
 
 def angles_in(found):
@@ -588,16 +605,15 @@
 
 
 def columns_kernel(is_second, even_ref, odd_ref, found_ref, *out_refs):
-    x_swapped, y_swapped = halves_swapped(is_second)
-    swapped = either(on_odd_core(), y_swapped, x_swapped)
-    columns = turn_columns(even_ref[...], odd_ref[...], angles_in(found_ref[...]), swapped)
+    angles = angles_in(found_ref[...])
+    columns = turn_columns(even_ref[...], odd_ref[...], angles, swapped_flag(is_second))
     for ref, value in zip(out_refs, columns):
         ref[...] = value
 
 
 def next_bands(x_found, y_found, x_second, y_second):
-    corner = jnp.concatenate((x_found[NEAR + 4 * DIAGS :], y_found[NEAR + 4 * DIAGS :]), axis=0)
-    middle = cross_bands(corner, angles_in(x_found), angles_in(y_found), x_second, y_second)
+    corner = jnp.concatenate((x_found[CORNER:ROTATION], y_found[CORNER:ROTATION]), axis=0)
+    middle = cross_bands(corner, x_found[ROTATION:], y_found[ROTATION:])
     half = corner.shape[1] // 2
     lane = lanes_of(middle[0])
     diag = lax.broadcasted_iota(jnp.int32, middle[0].shape, 0)
@@ -672,7 +688,7 @@
     (mine,) = call(bands, (other.shape,), *columns[:2], corner)
     (found,) = call(
         functools.partial(angles_kernel, is_second),
-        ((2 * NEAR + 4 * DIAGS, width),),
+        ((FOUND, width),),
         *exchange_groups(mine + other, "row", 1),
     )
     other = swap(found, "row", 1)

time: 56.8 us -> 55.6 us (0.979)
  Pallas kernels: 13.9 us -> 12.6 us
    pallas_call x11, Pallas kernels: 13.9 us -> 12.6 us  [call(): pl.pallas_call(kernel, out_shape=out, compiler_params=pltpu.CompilerParam...]
where the time goes in v7:
time: 55.6 us; the launch traced here: 55.5 us
  waiting for transfers between devices  24.2 us (44%)
  starting transfers between devices  16.8 us (30%)
  Pallas kernels  12.6 us (23%)
  local copies, waits for them, and re-layouts  0.95 us (2%)
  other arithmetic  0.76 us (1%)
    pallas_call x11, Pallas kernels, call(): pl.pallas_call(kernel, out_shape=out, compiler_params=pltpu.CompilerParam...  12.6 us
    ppermute x10, waiting for transfers between devices, swap(): lax.ppermute(x, axis, [(i, i ^ mask) for i in range(lax.axis_size(axis))])  9.51 us
    ppermute x2, waiting for transfers between devices, per_device(): came = lax.ppermute(sent, 'pair', sends)  8.18 us
    ppermute x10, starting transfers between devices, swap(): lax.ppermute(x, axis, [(i, i ^ mask) for i in range(lax.axis_size(axis))])  7.4 us
    ppermute x2, waiting for transfers between devices, per_device(): came = [lax.ppermute(x, 'pair', s) for x, s in zip((sent, kept), sends)]  6.56 us
    ppermute x2, starting transfers between devices, per_device(): came = lax.ppermute(sent, 'pair', sends)  5.88 us
    ppermute x2, starting transfers between devices, per_device(): came = [lax.ppermute(x, 'pair', s) for x, s in zip((sent, kept), sends)]  3.5 us
  transfers between devices with their start and end apart: 14, of which 14 were waited for; matrix products, arithmetic and copies ran while one was open for 0% of the time, Pallas kernels for 5%

profile of v7, /device:TPU:0, one launch (start us, length us, event | category | flops | bytes accessed | tf_op | source)
XLA Modules:
  0.0 55.5 jit_solution(4987667574908193005)
XLA Ops:
  0.0 0.9 %copy-done = f32[256,256]{1,0:T(8,128)S(1)} copy-done((f32[256,256]{1,0:T(8,128)S(1)}, f32[256,256]{1,0:T(8,128)}, u32[]{:S(2)}) %copy-start) | copy-done | bytes 262168
  1.4 4.1 %collective-permute-start = (f32[320,128]{1,0:T(8,128)S(1)}, f32[320,128]{1,0:T(8,128)S(1)}, u32[]{:S(2)}, u32[]{:S(2)}) collective-permute-start(f32[320,128]{1,0:T(8,128)S(1)} %get-tuple-element.30), channel_id=1, source_target_pairs={{1,0},{0,2},{3,1},{2,3},{5,4},{4,6},{7,5},{6,7},{9,8},{8,10},{11,9... | collective-permute-start | bytes 491528 | tf_op jit(solution)/shard_map/ppermute | solution.py:712
  5.4 3.5 %collective-permute-done.payload_ref = f32[320,128]{1,0:T(8,128)S(1)} collective-permute-done((f32[320,128]{1,0:T(8,128)S(1)}, f32[320,128]{1,0:T(8,128)S(1)}, u32[]{:S(2)}, u32[]{:S(2)}) %collective-permute-start) | collective-permute-done | bytes 163872 | tf_op jit(solution)/shard_map/ppermute | solution.py:712
  8.9 1.3 %shard_map.18 = (f32[256,128]{1,0:T(8,128)S(1)}, f32[256,128]{1,0:T(8,128)S(1)}, f32[256,128]{1,0:T(8,128)S(1)}, f32[256,128]{1,0:T(8,128)S(1)}, f32[16,128]{1,0:T(8,128)S(1)}, /*index=5*/f32[112,128]{1,0:T(8,128)S(1)}) custom-call(f32[256,128]{1,0:T(8,128)S(1)} %get-tuple-element.28.even_ref, f32[256,128]{1,0:T(8,128)S(1)} %get-tuple-element.29.odd_ref, ...), custom_call_target="tpu_custom_call" | custom-call | tf_op jit(solution)/shard_map/pallas_call | solution.py:676
  10.3 0.7 %shard_map.19 = f32[112,128]{1,0:T(8,128)S(1)} custom-call(f32[256,128]{1,0:T(8,128)S(1)} %get-tuple-element.31.even_ref, f32[256,128]{1,0:T(8,128)S(1)} %get-tuple-element.32.odd_ref, f32[16,128]{1,0:T(8,128)S(1)} %get-tuple-element.33.corner_ref), custom_call_target="tpu_custom_call" | custom-call | tf_op jit(solution)/shard_map/pallas_call | solution.py:676
  11.5 1.6 %collective-permute-start.2 = (f32[112,128]{1,0:T(8,128)S(1)}, f32[112,128]{1,0:T(8,128)S(1)}, u32[]{:S(2)}, u32[]{:S(2)}) collective-permute-start(f32[112,128]{1,0:T(8,128)S(1)} %add.6.refs_0_), channel_id=1, source_target_pairs={{0,8},{4,12},{8,0},{12,4},{16,24},{20,28},{24,16},{28,20},{1,9},{5... | collective-permute-start | bytes 172040 | tf_op jit(solution)/shard_map/ppermute | solution.py:659
  13.1 1.5 %collective-permute-start.3 = (f32[112,128]{1,0:T(8,128)S(1)}, f32[112,128]{1,0:T(8,128)S(1)}, u32[]{:S(2)}, u32[]{:S(2)}) collective-permute-start(f32[112,128]{1,0:T(8,128)S(1)} %add.6.refs_0_), channel_id=1, source_target_pairs={{0,16},{4,20},{8,24},{12,28},{16,0},{20,4},{24,8},{28,12},{1,17},{... | collective-permute-start | bytes 172040 | tf_op jit(solution)/shard_map/ppermute | solution.py:659
  15.1 0.7 %collective-permute-done.2.refs_1_ = f32[112,128]{1,0:T(8,128)S(1)} collective-permute-done((f32[112,128]{1,0:T(8,128)S(1)}, f32[112,128]{1,0:T(8,128)S(1)}, u32[]{:S(2)}, u32[]{:S(2)}) %collective-permute-start.2) | collective-permute-done | bytes 57376 | tf_op jit(solution)/shard_map/ppermute | solution.py:659
  15.8 1.5 %collective-permute-done.3.refs_2_ = f32[112,128]{1,0:T(8,128)S(1)} collective-permute-done((f32[112,128]{1,0:T(8,128)S(1)}, f32[112,128]{1,0:T(8,128)S(1)}, u32[]{:S(2)}, u32[]{:S(2)}) %collective-permute-start.3) | collective-permute-done | bytes 57376 | tf_op jit(solution)/shard_map/ppermute | solution.py:659
  17.2 2.4 %collective-permute-done.4.refs_3_ = f32[112,128]{1,0:T(8,128)S(1)} collective-permute-done((f32[112,128]{1,0:T(8,128)S(1)}, f32[112,128]{1,0:T(8,128)S(1)}, u32[]{:S(2)}, u32[]{:S(2)}) %collective-permute-start.4) | collective-permute-done | bytes 57376 | tf_op jit(solution)/shard_map/ppermute | solution.py:659
  19.7 1.4 %shard_map.20.found_ref.refs_4_ = f32[160,128]{1,0:T(8,128)S(1)} custom-call(f32[112,128]{1,0:T(8,128)S(1)} %add.6.refs_0_, f32[112,128]{1,0:T(8,128)S(1)} %collective-permute-done.2.refs_1_, f32[112,128]{1,0:T(8,128)S(1)} %collective-permute-done.3.refs_2_, f32[112,128]{1,0:T(8,128)S(1)} %collective-permute-done.4.refs_3_), custom_call_target="tpu_custom_call" | custom-call | tf_op jit(solution)/shard_map/pallas_call | solution.py:676
  21.1 0.7 %shard_map.21 = (f32[256,128]{1,0:T(8,128)S(1)}, f32[256,128]{1,0:T(8,128)S(1)}) custom-call(f32[256,128]{1,0:T(8,128)S(1)} %get-tuple-element.31.even_ref, f32[256,128]{1,0:T(8,128)S(1)} %get-tuple-element.32.odd_ref, f32[160,128]{1,0:T(8,128)S(1)} %shard_map.20.found_ref.refs_4_), custom_call_target="tpu_custom_call" | custom-call | tf_op jit(solution)/shard_map/pallas_call | solution.py:676
  21.9 0.5 collective-permute-done.5.refs_5_
  22.4 2.0 %shard_map.22 = (f32[256,128]{1,0:T(8,128)S(1)}, f32[256,128]{1,0:T(8,128)S(1)}) custom-call(f32[256,128]{1,0:T(8,128)S(1)} %get-tuple-element.35.refs_0_, f32[256,128]{1,0:T(8,128)S(1)} %get-tuple-element.36.refs_1_, f32[256,128]{1,0:T(8,128)S(1)} %get-tuple-element.37.refs_2_, f32[256,128]{1,0:T(8,128)S(1)} %get-tuple-element.38.refs_3_, ...), custom_call_target="tpu_custom_call" | custom-call | tf_op jit(solution)/shard_map/pallas_call | solution.py:676
  24.4 2.4 %collective-permute-start.6 = (f32[256,128]{1,0:T(8,128)S(1)}, f32[256,128]{1,0:T(8,128)S(1)}, u32[]{:S(2)}, u32[]{:S(2)}) collective-permute-start(f32[256,128]{1,0:T(8,128)S(1)} %get-tuple-element.40.sent_ref), channel_id=1, source_target_pairs={{2,0},{3,2},{0,1},{1,3},{6,4},{7,6},{4,5},{5,7},{10,8},{11,10},{8,... | collective-permute-start | bytes 393224 | tf_op jit(solution)/shard_map/ppermute | solution.py:718
  26.9 1.1 %collective-permute-start.7 = (f32[256,128]{1,0:T(8,128)S(1)}, f32[256,128]{1,0:T(8,128)S(1)}, u32[]{:S(2)}, u32[]{:S(2)}) collective-permute-start(f32[256,128]{1,0:T(8,128)S(1)} %get-tuple-element.39.kept_ref), channel_id=1, source_target_pairs={{1,0},{0,2},{3,1},{2,3},{5,4},{4,6},{7,5},{6,7},{9,8},{8,10},{11,9... | collective-permute-start | bytes 393224 | tf_op jit(solution)/shard_map/ppermute | solution.py:718
  28.0 3.9 %collective-permute-done.6.came0_ref = f32[256,128]{1,0:T(8,128)S(1)} collective-permute-done((f32[256,128]{1,0:T(8,128)S(1)}, f32[256,128]{1,0:T(8,128)S(1)}, u32[]{:S(2)}, u32[]{:S(2)}) %collective-permute-start.6) | collective-permute-done | bytes 131104 | tf_op jit(solution)/shard_map/ppermute | solution.py:718
  31.8 2.7 %collective-permute-done.7.came1_ref = f32[256,128]{1,0:T(8,128)S(1)} collective-permute-done((f32[256,128]{1,0:T(8,128)S(1)}, f32[256,128]{1,0:T(8,128)S(1)}, u32[]{:S(2)}, u32[]{:S(2)}) %collective-permute-start.7) | collective-permute-done | bytes 131104 | tf_op jit(solution)/shard_map/ppermute | solution.py:718
  34.5 1.2 %shard_map.23 = (f32[256,128]{1,0:T(8,128)S(1)}, f32[256,128]{1,0:T(8,128)S(1)}, f32[256,128]{1,0:T(8,128)S(1)}, f32[256,128]{1,0:T(8,128)S(1)}, f32[16,128]{1,0:T(8,128)S(1)}, /*index=5*/f32[112,128]{1,0:T(8,128)S(1)}) custom-call(f32[256,128]{1,0:T(8,128)S(1)} %get-tuple-element.39.kept_ref, f32[256,128]{1,0:T(8,128)S(1)} %get-tuple-element.40.sent_ref, ...), custom_call_target="tpu_custom_call" | custom-call | tf_op jit(solution)/shard_map/pallas_call | solution.py:676
  35.8 0.7 %shard_map.24 = f32[112,128]{1,0:T(8,128)S(1)} custom-call(f32[256,128]{1,0:T(8,128)S(1)} %get-tuple-element.41.even_ref, f32[256,128]{1,0:T(8,128)S(1)} %get-tuple-element.42.odd_ref, f32[16,128]{1,0:T(8,128)S(1)} %get-tuple-element.43.corner_ref), custom_call_target="tpu_custom_call" | custom-call | tf_op jit(solution)/shard_map/pallas_call | solution.py:676
  37.0 0.6 %collective-permute-start.10 = (f32[112,128]{1,0:T(8,128)S(1)}, f32[112,128]{1,0:T(8,128)S(1)}, u32[]{:S(2)}, u32[]{:S(2)}) collective-permute-start(f32[112,128]{1,0:T(8,128)S(1)} %add.7.refs_0_), channel_id=1, source_target_pairs={{0,16},{4,20},{8,24},{12,28},{16,0},{20,4},{24,8},{28,12},{1,17},{... | collective-permute-start | bytes 172040 | tf_op jit(solution)/shard_map/ppermute | solution.py:659
  37.6 1.5 %collective-permute-start.11 = (f32[112,128]{1,0:T(8,128)S(1)}, f32[112,128]{1,0:T(8,128)S(1)}, u32[]{:S(2)}, u32[]{:S(2)}) collective-permute-start(f32[112,128]{1,0:T(8,128)S(1)} %add.7.refs_0_), channel_id=1, source_target_pairs={{0,24},{4,28},{8,16},{12,20},{16,8},{20,12},{24,0},{28,4},{1,25},{... | collective-permute-start | bytes 172040 | tf_op jit(solution)/shard_map/ppermute | solution.py:659
  39.1 1.5 %collective-permute-start.9 = (f32[112,128]{1,0:T(8,128)S(1)}, f32[112,128]{1,0:T(8,128)S(1)}, u32[]{:S(2)}, u32[]{:S(2)}) collective-permute-start(f32[112,128]{1,0:T(8,128)S(1)} %add.7.refs_0_), channel_id=1, source_target_pairs={{0,8},{4,12},{8,0},{12,4},{16,24},{20,28},{24,16},{28,20},{1,9},{5... | collective-permute-start | bytes 172040 | tf_op jit(solution)/shard_map/ppermute | solution.py:659
  40.6 1.3 %collective-permute-done.10.refs_2_ = f32[112,128]{1,0:T(8,128)S(1)} collective-permute-done((f32[112,128]{1,0:T(8,128)S(1)}, f32[112,128]{1,0:T(8,128)S(1)}, u32[]{:S(2)}, u32[]{:S(2)}) %collective-permute-start.10) | collective-permute-done | bytes 57376 | tf_op jit(solution)/shard_map/ppermute | solution.py:659
  41.9 0.9 %collective-permute-done.11.refs_3_ = f32[112,128]{1,0:T(8,128)S(1)} collective-permute-done((f32[112,128]{1,0:T(8,128)S(1)}, f32[112,128]{1,0:T(8,128)S(1)}, u32[]{:S(2)}, u32[]{:S(2)}) %collective-permute-start.11) | collective-permute-done | bytes 57376 | tf_op jit(solution)/shard_map/ppermute | solution.py:659
  42.8 0.7 %collective-permute-done.9.refs_1_ = f32[112,128]{1,0:T(8,128)S(1)} collective-permute-done((f32[112,128]{1,0:T(8,128)S(1)}, f32[112,128]{1,0:T(8,128)S(1)}, u32[]{:S(2)}, u32[]{:S(2)}) %collective-permute-start.9) | collective-permute-done | bytes 57376 | tf_op jit(solution)/shard_map/ppermute | solution.py:659
  43.5 1.4 %shard_map.25.found_ref.refs_4_ = f32[160,128]{1,0:T(8,128)S(1)} custom-call(f32[112,128]{1,0:T(8,128)S(1)} %add.7.refs_0_, f32[112,128]{1,0:T(8,128)S(1)} %collective-permute-done.9.refs_1_, f32[112,128]{1,0:T(8,128)S(1)} %collective-permute-done.10.refs_2_, f32[112,128]{1,0:T(8,128)S(1)} %collective-permute-done.11.refs_3_), custom_call_target="tpu_custom_call" | custom-call | tf_op jit(solution)/shard_map/pallas_call | solution.py:676
  44.9 0.7 %shard_map.26 = (f32[256,128]{1,0:T(8,128)S(1)}, f32[256,128]{1,0:T(8,128)S(1)}) custom-call(f32[256,128]{1,0:T(8,128)S(1)} %get-tuple-element.41.even_ref, f32[256,128]{1,0:T(8,128)S(1)} %get-tuple-element.42.odd_ref, f32[160,128]{1,0:T(8,128)S(1)} %shard_map.25.found_ref.refs_4_), custom_call_target="tpu_custom_call" | custom-call | tf_op jit(solution)/shard_map/pallas_call | solution.py:676
  46.2 2.0 %shard_map.27 = (f32[256,128]{1,0:T(8,128)S(1)}, f32[256,128]{1,0:T(8,128)S(1)}) custom-call(f32[256,128]{1,0:T(8,128)S(1)} %get-tuple-element.45.refs_0_, f32[256,128]{1,0:T(8,128)S(1)} %get-tuple-element.46.refs_1_, f32[256,128]{1,0:T(8,128)S(1)} %get-tuple-element.47.refs_2_, f32[256,128]{1,0:T(8,128)S(1)} %get-tuple-element.48.refs_3_, ...), custom_call_target="tpu_custom_call" | custom-call | tf_op jit(solution)/shard_map/pallas_call | solution.py:676
  48.2 1.8 %collective-permute-start.13 = (f32[256,128]{1,0:T(8,128)S(1)}, f32[256,128]{1,0:T(8,128)S(1)}, u32[]{:S(2)}, u32[]{:S(2)}) collective-permute-start(f32[256,128]{1,0:T(8,128)S(1)} %get-tuple-element.49), channel_id=1, source_target_pairs={{2,0},{0,1},{3,2},{1,3},{6,4},{4,5},{7,6},{5,7},{10,8},{8,9},{11,1... | collective-permute-start | bytes 393224 | tf_op jit(solution)/shard_map/ppermute | solution.py:724
  50.0 4.7 %collective-permute-done.13 = f32[256,128]{1,0:T(8,128)S(1)} collective-permute-done((f32[256,128]{1,0:T(8,128)S(1)}, f32[256,128]{1,0:T(8,128)S(1)}, u32[]{:S(2)}, u32[]{:S(2)}) %collective-permute-start.13) | collective-permute-done | bytes 131104 | tf_op jit(solution)/shard_map/ppermute | solution.py:724
  54.8 0.7 %pad_maximum_fusion = f32[256,256]{1,0:T(8,128)} fusion(f32[256,128]{1,0:T(8,128)S(1)} %get-tuple-element.52, f32[256,128]{1,0:T(8,128)S(1)} %get-tuple-element.51), kind=kLoop, calls=%fused_computation | loop fusion | flops 65536 | bytes 524288 | tf_op jit(solution)/shard_map/concatenate | solution.py:728
  (13 shorter events, 2.7 us)
Async XLA Ops:
  0.0 0.9 %copy-start = (f32[256,256]{1,0:T(8,128)S(1)}, f32[256,256]{1,0:T(8,128)}, u32[]{:S(2)}) copy-start(f32[256,256]{1,0:T(8,128)} %basis_ref.1) | copy-start | bytes 786436
  1.4 7.5 %collective-permute-start = (f32[320,128]{1,0:T(8,128)S(1)}, f32[320,128]{1,0:T(8,128)S(1)}, u32[]{:S(2)}, u32[]{:S(2)}) collective-permute-start(f32[320,128]{1,0:T(8,128)S(1)} %get-tuple-element.30), channel_id=1, source_target_pairs={{1,0},{0,2},{3,1},{2,3},{5,4},{4,6},{7,5},{6,7},{9,8},{8,10},{11,9... | collective-permute-start | bytes 491528 | tf_op jit(solution)/shard_map/ppermute | solution.py:712
  10.2 1.3 %collective-permute-start.1 = (f32[112,128]{1,0:T(8,128)S(1)}, f32[112,128]{1,0:T(8,128)S(1)}, u32[]{:S(2)}, u32[]{:S(2)}) collective-permute-start(f32[112,128]{1,0:T(8,128)S(1)} %get-tuple-element.34), channel_id=1, source_target_pairs={{0,4},{4,0},{8,12},{12,8},{16,20},{20,16},{24,28},{28,24},{1,5},{5... | collective-permute-start | bytes 172040 | tf_op jit(solution)/shard_map/ppermute | solution.py:659
  11.5 4.2 %collective-permute-start.2 = (f32[112,128]{1,0:T(8,128)S(1)}, f32[112,128]{1,0:T(8,128)S(1)}, u32[]{:S(2)}, u32[]{:S(2)}) collective-permute-start(f32[112,128]{1,0:T(8,128)S(1)} %add.6.refs_0_), channel_id=1, source_target_pairs={{0,8},{4,12},{8,0},{12,4},{16,24},{20,28},{24,16},{28,20},{1,9},{5... | collective-permute-start | bytes 172040 | tf_op jit(solution)/shard_map/ppermute | solution.py:659
  13.1 4.2 %collective-permute-start.3 = (f32[112,128]{1,0:T(8,128)S(1)}, f32[112,128]{1,0:T(8,128)S(1)}, u32[]{:S(2)}, u32[]{:S(2)}) collective-permute-start(f32[112,128]{1,0:T(8,128)S(1)} %add.6.refs_0_), channel_id=1, source_target_pairs={{0,16},{4,20},{8,24},{12,28},{16,0},{20,4},{24,8},{28,12},{1,17},{... | collective-permute-start | bytes 172040 | tf_op jit(solution)/shard_map/ppermute | solution.py:659
  14.6 5.1 %collective-permute-start.4 = (f32[112,128]{1,0:T(8,128)S(1)}, f32[112,128]{1,0:T(8,128)S(1)}, u32[]{:S(2)}, u32[]{:S(2)}) collective-permute-start(f32[112,128]{1,0:T(8,128)S(1)} %add.6.refs_0_), channel_id=1, source_target_pairs={{0,24},{4,28},{8,16},{12,20},{16,8},{20,12},{24,0},{28,4},{1,25},{... | collective-permute-start | bytes 172040 | tf_op jit(solution)/shard_map/ppermute | solution.py:659
  21.1 1.3 %collective-permute-start.5 = (f32[160,128]{1,0:T(8,128)S(1)}, f32[160,128]{1,0:T(8,128)S(1)}, u32[]{:S(2)}, u32[]{:S(2)}) collective-permute-start(f32[160,128]{1,0:T(8,128)S(1)} %shard_map.20.found_ref.refs_4_), channel_id=1, source_target_pairs={{0,4},{4,0},{8,12},{12,8},{16,20},{20,16},{24,28},{28,24},{1,5},{5... | collective-permute-start | bytes 245768 | tf_op jit(solution)/shard_map/ppermute | solution.py:659
  24.4 7.4 %collective-permute-start.6 = (f32[256,128]{1,0:T(8,128)S(1)}, f32[256,128]{1,0:T(8,128)S(1)}, u32[]{:S(2)}, u32[]{:S(2)}) collective-permute-start(f32[256,128]{1,0:T(8,128)S(1)} %get-tuple-element.40.sent_ref), channel_id=1, source_target_pairs={{2,0},{3,2},{0,1},{1,3},{6,4},{7,6},{4,5},{5,7},{10,8},{11,10},{8,... | collective-permute-start | bytes 393224 | tf_op jit(solution)/shard_map/ppermute | solution.py:718
  26.9 7.6 %collective-permute-start.7 = (f32[256,128]{1,0:T(8,128)S(1)}, f32[256,128]{1,0:T(8,128)S(1)}, u32[]{:S(2)}, u32[]{:S(2)}) collective-permute-start(f32[256,128]{1,0:T(8,128)S(1)} %get-tuple-element.39.kept_ref), channel_id=1, source_target_pairs={{1,0},{0,2},{3,1},{2,3},{5,4},{4,6},{7,5},{6,7},{9,8},{8,10},{11,9... | collective-permute-start | bytes 393224 | tf_op jit(solution)/shard_map/ppermute | solution.py:718
  35.7 1.3 %collective-permute-start.8 = (f32[112,128]{1,0:T(8,128)S(1)}, f32[112,128]{1,0:T(8,128)S(1)}, u32[]{:S(2)}, u32[]{:S(2)}) collective-permute-start(f32[112,128]{1,0:T(8,128)S(1)} %get-tuple-element.44), channel_id=1, source_target_pairs={{0,4},{4,0},{8,12},{12,8},{16,20},{20,16},{24,28},{28,24},{1,5},{5... | collective-permute-start | bytes 172040 | tf_op jit(solution)/shard_map/ppermute | solution.py:659
  37.0 4.9 %collective-permute-start.10 = (f32[112,128]{1,0:T(8,128)S(1)}, f32[112,128]{1,0:T(8,128)S(1)}, u32[]{:S(2)}, u32[]{:S(2)}) collective-permute-start(f32[112,128]{1,0:T(8,128)S(1)} %add.7.refs_0_), channel_id=1, source_target_pairs={{0,16},{4,20},{8,24},{12,28},{16,0},{20,4},{24,8},{28,12},{1,17},{... | collective-permute-start | bytes 172040 | tf_op jit(solution)/shard_map/ppermute | solution.py:659
  37.6 5.2 %collective-permute-start.11 = (f32[112,128]{1,0:T(8,128)S(1)}, f32[112,128]{1,0:T(8,128)S(1)}, u32[]{:S(2)}, u32[]{:S(2)}) collective-permute-start(f32[112,128]{1,0:T(8,128)S(1)} %add.7.refs_0_), channel_id=1, source_target_pairs={{0,24},{4,28},{8,16},{12,20},{16,8},{20,12},{24,0},{28,4},{1,25},{... | collective-permute-start | bytes 172040 | tf_op jit(solution)/shard_map/ppermute | solution.py:659
  39.1 4.4 %collective-permute-start.9 = (f32[112,128]{1,0:T(8,128)S(1)}, f32[112,128]{1,0:T(8,128)S(1)}, u32[]{:S(2)}, u32[]{:S(2)}) collective-permute-start(f32[112,128]{1,0:T(8,128)S(1)} %add.7.refs_0_), channel_id=1, source_target_pairs={{0,8},{4,12},{8,0},{12,4},{16,24},{20,28},{24,16},{28,20},{1,9},{5... | collective-permute-start | bytes 172040 | tf_op jit(solution)/shard_map/ppermute | solution.py:659
  44.9 1.3 %collective-permute-start.12 = (f32[160,128]{1,0:T(8,128)S(1)}, f32[160,128]{1,0:T(8,128)S(1)}, u32[]{:S(2)}, u32[]{:S(2)}) collective-permute-start(f32[160,128]{1,0:T(8,128)S(1)} %shard_map.25.found_ref.refs_4_), channel_id=1, source_target_pairs={{0,4},{4,0},{8,12},{12,8},{16,20},{20,16},{24,28},{28,24},{1,5},{5... | collective-permute-start | bytes 245768 | tf_op jit(solution)/shard_map/ppermute | solution.py:659
  48.2 6.5 %collective-permute-start.13 = (f32[256,128]{1,0:T(8,128)S(1)}, f32[256,128]{1,0:T(8,128)S(1)}, u32[]{:S(2)}, u32[]{:S(2)}) collective-permute-start(f32[256,128]{1,0:T(8,128)S(1)} %get-tuple-element.49), channel_id=1, source_target_pairs={{2,0},{0,1},{3,2},{1,3},{6,4},{4,5},{7,6},{5,7},{10,8},{8,9},{11,1... | collective-permute-start | bytes 393224 | tf_op jit(solution)/shard_map/ppermute | solution.py:724

commit v8 on v7

--- a/solution.py
+++ b/solution.py
@@ -166,13 +166,9 @@
     return even, odd
 
 
-def join_pair(even, odd):
-    half = even.shape[1] // 2
-    low = lanes_of(even) < half
-    return jnp.where(low, even, right(odd, half)), jnp.where(low, right(even, half), odd)
-
-
 def take_lanes(x, source):
+    if x.shape[0] == 1:
+        return take_lanes(jnp.broadcast_to(x, (8, x.shape[1])), source)[:1]
     return jnp.take_along_axis(x, jnp.broadcast_to(source, x.shape), axis=1)
 
 
@@ -279,6 +275,51 @@
     return ee, eo, oe, oo
 
 
+def step_bands(ee, eo, oe, oo, cosine, sine):
+    lane = lanes_of(ee)
+    diag = lax.broadcasted_iota(jnp.int32, ee.shape, 0)
+    last = lane == ee.shape[1] - 1
+    on, next_on = diag == 0, diag == 1
+
+    def slanted(x, by):
+        if by >= 0:
+            return pltpu.roll(x, by, 1, stride=1, stride_axis=0)
+        return jnp.where(on, left(x, -by), down(slanted(x, 0), -by))
+
+    def rotated(by, wanted):
+        cl, sl = (jnp.broadcast_to(x, ee.shape) for x in (cosine, sine))
+        ck, sk = (slanted(x, by) for x in (cl, sl))
+        cl, sl, a, b, c, d = (right(x, by) for x in (cl, sl, ee, eo, oe, oo))
+        a, c = ck * a + sk * c, ck * c - sk * a
+        b, d = ck * b + sk * d, ck * d - sk * b
+        found = {"ee": (a, b), "eo": (b, a), "oe": (c, d), "oo": (d, c)}
+        return [
+            cl * one + sl * two if name in ("ee", "oe") else cl * one - sl * two
+            for name, (one, two) in found.items()
+            if name in wanted
+        ]
+
+    ee_0, eo_0, oe_0, oo_0 = rotated(0, ("ee", "eo", "oe", "oo"))
+    ee_r, eo_r, oe_r, oo_r = rotated(1, ("ee", "eo", "oe", "oo"))
+    eo_l, oo_l = rotated(-1, ("eo", "oo"))
+
+    near = down(jnp.where(on, eo_r, ee_r), 1)
+    turned = jnp.where(on, oo_r, oe_r)
+    ee_new = jnp.where(lane == diag + 1, turned, jnp.where(lane == diag, near, ee_r))
+    ee_new = jnp.where(jnp.logical_and(on, lane == 0), ee_0, ee_new)
+
+    eo_new = down(jnp.where(lane == diag - 1, oo_l, eo_l), -2)
+    eo_new = jnp.where(lane == diag, down(eo_l, -1), eo_new)
+    eo_new = jnp.where(last, down(ee_0, -1), eo_new)
+
+    oo_new = jnp.where(last, jnp.where(on, ee_0, down(oe_0, 1)), oo_l)
+
+    oe_new = down(oe_r, 2)
+    oe_new = jnp.where(next_on, jnp.where(lane == diag, oo_0, eo_0), oe_new)
+    oe_new = jnp.where(on, eo_new, oe_new)
+    return ee_new, eo_new, oe_new, oo_new
+
+
 def move_bands(ee, eo, oe, oo):
     lane = lanes_of(ee)
     diag = lax.broadcasted_iota(jnp.int32, ee.shape, 0)
@@ -338,42 +379,45 @@
     return even_new, odd_new
 
 
-def home_sources(even, odd):
-    lane = line_lanes(even)
-    by, end = JSTEPS - 1, even.shape[1] - 1
-    entered = jnp.logical_and(lane >= 1, lane <= by)
-    mixed_even = jnp.where(entered, right(odd, by + 1), even)
-    mixed_odd = jnp.where(lane > end - by, left(even, by + 1), odd)
-
-    def even_source(place):
-        moved = jnp.where(place <= end - by, place + by, end + 1 - place)
-        return jnp.where(place == 0, 0, moved)
-
-    def odd_source(place):
-        return jnp.where(place >= by, place - by, end - place)
-
-    return (mixed_even, even_source), (mixed_odd, odd_source)
-
-
-def columns_home(even, odd, shifted=None):
+def in_pair(even, shifted=None):
     lane = line_lanes(even)
     if shifted is not None:
         half = even.shape[1] // 2
         lane = jnp.where(shifted, jnp.where(lane < half, lane + half, lane - half), lane)
-    return tuple(take_lanes(x, source(lane)) for x, source in home_sources(even, odd))
-
-
-def blocks_home(even, odd):
-    lane = line_lanes(even)
-    (even, even_source), (odd, odd_source) = home_sources(even, odd)
-    blocks = []
-    for block in (0, 1):
-        place = block * (even.shape[1] // 2) + lane // 2
-        from_even, from_odd = (
-            take_lanes(x, source(place)) for x, source in ((even, even_source), (odd, odd_source))
+    return (lane < 0, lane), (lane >= 0, lane)
+
+
+def in_blocks(even):
+    lane, half = line_lanes(even), even.shape[1] // 2
+    place = jnp.where(lane < half, lane, lane - half)
+    return (lane >= half, place), (lane >= half, place + half)
+
+
+def in_order(even):
+    lane, half = line_lanes(even), even.shape[1] // 2
+    return (lane % 2 == 1, lane // 2), (lane % 2 == 1, lane // 2 + half)
+
+
+def turn_to(layout, even, odd, angles):
+    for cosine, sine in angles[:-1]:
+        even, odd = cosine * even + sine * odd, cosine * odd - sine * even
+        even, odd = move_columns(even, odd)
+    by, end = JSTEPS - 1, even.shape[1] - 1
+    results = []
+    for is_odd, place in layout:
+        stayed = place <= end - by
+        from_even = jnp.where(stayed, place + by, 2 * end + 1 - by - place)
+        from_even = jnp.where(place == 0, 0, from_even)
+        source = jnp.where(is_odd, jnp.abs(place - by), from_even)
+        is_even = jnp.logical_or(
+            jnp.logical_and(is_odd, place < by),
+            jnp.logical_and(jnp.logical_not(is_odd), stayed),
         )
-        blocks.append(jnp.where(lane % 2 == 0, from_even, from_odd))
-    return blocks
+        cosine, sine = (take_lanes(x, source) for x in angles[-1])
+        by_even = jnp.where(is_even, cosine, -sine)
+        by_odd = jnp.where(is_even, sine, cosine)
+        results.append(by_even * take_lanes(even, source) + by_odd * take_lanes(odd, source))
+    return results
 
 
 def trim(bands, reach):
@@ -381,35 +425,25 @@
     return [band[:rows] for band in bands]
 
 
-def angles_of(bands, carried):
+def angles_of(bands):
     angles = []
+    for step in range(JSTEPS):
+        ee, eo, oe, oo = bands = trim(bands, 2 * (JSTEPS - 1 - step))
+        angles.append(jacobi_angle(ee[0:1], oo[0:1], eo[0:1]))
+        if step < JSTEPS - 1:
+            bands = step_bands(*bands, *angles[-1])
+    return angles
+
+
+def carried(bands, angles):
     ahead = 2 * (JSTEPS - 1)
-    kept = 2 * ahead if carried else 0
-    for step in range(JSTEPS):
-        ee, eo, oe, oo = trim(bands, kept + ahead - 2 * step)
-        cosine, sine = jacobi_angle(ee[0:1], oo[0:1], eo[0:1])
-        angles.append((cosine, sine))
-        bands = ee, eo, oe, oo
-        if carried or step < JSTEPS - 1:
-            bands = turn_bands(ee, eo, oe, oo, cosine, sine)
+    for step, (cosine, sine) in enumerate(angles):
+        bands = turn_bands(*trim(bands, 3 * ahead - 2 * step), cosine, sine)
         if step < JSTEPS - 1:
             bands = move_bands(*bands)
-    if carried:
-        for step in range(JSTEPS - 1):
-            bands = move_bands_back(*trim(bands, kept - 2 * step))
-    return angles, bands
-
-
-def turned(even, odd, angles):
-    for step, (cosine, sine) in enumerate(angles):
-        even, odd = cosine * even + sine * odd, cosine * odd - sine * even
-        if step < JSTEPS - 1:
-            even, odd = move_columns(even, odd)
-    return even, odd
-
-
-def turn_columns(even, odd, angles, shifted=None):
-    return columns_home(*turned(even, odd, angles), shifted)
+    for step in range(JSTEPS - 1):
+        bands = move_bands_back(*trim(bands, 2 * (ahead - step)))
+    return bands
 
 
 def near_starts(width):
@@ -424,8 +458,9 @@
     lane = lanes_of(x_even)
 
     def window(even, odd, flag, starts):
-        at_zero = jnp.where(flag, left(even, starts[1]), left(even, starts[0]))
-        at_next = jnp.where(flag, left(odd, starts[1] - WINDOW), left(odd, starts[0] - WINDOW))
+        start = jnp.where(flag, starts[1], starts[0])
+        at_zero = pltpu.roll(even, width - start, 1)
+        at_next = pltpu.roll(odd, (width - start + WINDOW) % width, 1)
         return jnp.where(lane < WINDOW, at_zero, jnp.where(lane < 2 * WINDOW, at_next, 0.0))
 
     corner = lax.dot_general(
@@ -451,7 +486,7 @@
         jnp.where(jnp.logical_and(row == lane + at, row // WINDOW == at // WINDOW), 1.0, 0.0)
         for at in (0, WINDOW)
     )
-    even, odd = turn_columns(even, odd, angles, swapped)
+    even, odd = turn_to(in_pair(even, swapped), even, odd, angles)
     low = lax.broadcasted_iota(jnp.int32, shape, 1) < half
     return jnp.where(jnp.logical_xor(low, first_pair), right(odd, half), even)
 
@@ -582,7 +617,8 @@
     part = pair_sums([ref[...] for ref in part_refs])
     flag = own_second_flag(is_second)
     quadrants = [unpack_far(part[q * PACKED : (q + 1) * PACKED], flag) for q in range(4)]
-    angles, bands = angles_of(quadrants, True)
+    angles = angles_of(quadrants)
+    bands = carried(quadrants, angles)
     for step, pair in enumerate(angles):
         for i in (0, 1):
             found_ref[2 * step + i : 2 * step + i + 1, :] = pair[i]
@@ -606,7 +642,8 @@
 
 def columns_kernel(is_second, even_ref, odd_ref, found_ref, *out_refs):
     angles = angles_in(found_ref[...])
-    columns = turn_columns(even_ref[...], odd_ref[...], angles, swapped_flag(is_second))
+    layout = in_pair(even_ref, swapped_flag(is_second))
+    columns = turn_to(layout, even_ref[...], odd_ref[...], angles)
     for ref, value in zip(out_refs, columns):
         ref[...] = value
 
@@ -628,7 +665,7 @@
     return bands
 
 
-def next_kernel(is_second, sends_first, in_order, *refs):
+def next_kernel(is_second, sends_first, layout_of, *refs):
     mine_even, mine_odd, even_ref, odd_ref, found_ref, other_ref, kept_ref, sent_ref = refs
     found, other = found_ref[...], other_ref[...]
     flag = on_odd_core()
@@ -636,14 +673,14 @@
     bands = next_bands(x_found, y_found, among(is_second[0]), among(is_second[1]))
     x_swapped, y_swapped = halves_swapped(is_second)
     swapped = either(flag, x_swapped, y_swapped)
-    theirs = turn_columns(even_ref[...], odd_ref[...], angles_in(other), swapped)
+    layout = in_pair(even_ref, swapped)
+    theirs = turn_to(layout, even_ref[...], odd_ref[...], angles_in(other))
     low = line_lanes(found) < found.shape[1] // 2
     from_mine = jnp.logical_xor(low, flag)
     even = jnp.where(from_mine, mine_even[...], theirs[0])
     odd = jnp.where(from_mine, mine_odd[...], theirs[1])
-    angles, _ = angles_of(bands, False)
-    even, odd = turned(even, odd, angles)
-    first, second = blocks_home(even, odd) if in_order else join_pair(*columns_home(even, odd))
+    angles = angles_of(bands)
+    first, second = turn_to(layout_of(even), even, odd, angles)
     flag = among(sends_first)
     kept_ref[...] = jnp.where(flag, second, first)
     sent_ref[...] = jnp.where(flag, first, second)
@@ -680,7 +717,7 @@
     )(*args)
 
 
-def two_rounds(opened, is_second, sends_first, in_order):
+def two_rounds(opened, is_second, sends_first, layout_of):
     *columns, corner, other = opened
     column, width = columns[0].shape, columns[0].shape[1]
     other = swap(other, "row", 1)
@@ -694,7 +731,7 @@
     other = swap(found, "row", 1)
     turn = functools.partial(columns_kernel, is_second)
     columns[:2] = call(turn, (column, column), *columns[:2], found)
-    turn = functools.partial(next_kernel, is_second, sends_first, in_order)
+    turn = functools.partial(next_kernel, is_second, sends_first, layout_of)
     return call(turn, (column, column), *columns, found, other)
 
 
@@ -713,13 +750,13 @@
     opening = functools.partial(first_open, own_second, gets_second, is_second)
     arrays = call(opening, opened, even, odd, came)
     sends, sends_first, picks, next_second = fused_moves(pair_total)
-    kept, sent = two_rounds(arrays, is_second, sends_first, False)
+    kept, sent = two_rounds(arrays, is_second, sends_first, in_blocks)
 
     came = [lax.ppermute(x, "pair", s) for x, s in zip((sent, kept), sends)]
     opening = functools.partial(fused_open, picks, next_second)
     arrays = call(opening, opened, kept, sent, *came)
     sends, sends_first, gets_first = last_moves(pair_total)
-    kept, sent = two_rounds(arrays, next_second, sends_first, True)
+    kept, sent = two_rounds(arrays, next_second, sends_first, in_order)
 
     came = lax.ppermute(sent, "pair", sends)
     flag = among(gets_first)

time: 55.6 us -> 54.3 us (0.977)
  Pallas kernels: 12.6 us -> 11.2 us
    pallas_call x11, Pallas kernels: 12.6 us -> 11.2 us  [call(): pl.pallas_call(kernel, out_shape=out, compiler_params=pltpu.CompilerParam...]
where the time goes in v8:
time: 54.3 us; the launch traced here: 54.1 us
  waiting for transfers between devices  24.3 us (45%)
  starting transfers between devices  16.8 us (31%)
  Pallas kernels  11.2 us (21%)
  local copies, waits for them, and re-layouts  0.95 us (2%)
  other arithmetic  0.76 us (1%)
    pallas_call x11, Pallas kernels, call(): pl.pallas_call(kernel, out_shape=out, compiler_params=pltpu.CompilerParam...  11.2 us
    ppermute x10, waiting for transfers between devices, swap(): lax.ppermute(x, axis, [(i, i ^ mask) for i in range(lax.axis_size(axis))])  9.57 us
    ppermute x2, waiting for transfers between devices, per_device(): came = lax.ppermute(sent, 'pair', sends)  8.17 us
    ppermute x10, starting transfers between devices, swap(): lax.ppermute(x, axis, [(i, i ^ mask) for i in range(lax.axis_size(axis))])  7.4 us
    ppermute x2, waiting for transfers between devices, per_device(): came = [lax.ppermute(x, 'pair', s) for x, s in zip((sent, kept), sends)]  6.56 us
    ppermute x2, starting transfers between devices, per_device(): came = lax.ppermute(sent, 'pair', sends)  5.88 us
    ppermute x2, starting transfers between devices, per_device(): came = [lax.ppermute(x, 'pair', s) for x, s in zip((sent, kept), sends)]  3.5 us
  transfers between devices with their start and end apart: 14, of which 14 were waited for; matrix products, arithmetic and copies ran while one was open for 0% of the time, Pallas kernels for 5%

profile of v8, /device:TPU:0, one launch (start us, length us, event | category | flops | bytes accessed | tf_op | source)
XLA Modules:
  0.0 54.1 jit_solution(15304697494770953021)
XLA Ops:
  0.0 0.9 %copy-done = f32[256,256]{1,0:T(8,128)S(1)} copy-done((f32[256,256]{1,0:T(8,128)S(1)}, f32[256,256]{1,0:T(8,128)}, u32[]{:S(2)}) %copy-start) | copy-done | bytes 262168
  1.4 4.1 %collective-permute-start = (f32[320,128]{1,0:T(8,128)S(1)}, f32[320,128]{1,0:T(8,128)S(1)}, u32[]{:S(2)}, u32[]{:S(2)}) collective-permute-start(f32[320,128]{1,0:T(8,128)S(1)} %get-tuple-element.30), channel_id=1, source_target_pairs={{1,0},{0,2},{3,1},{2,3},{5,4},{4,6},{7,5},{6,7},{9,8},{8,10},{11,9... | collective-permute-start | bytes 491528 | tf_op jit(solution)/shard_map/ppermute | solution.py:749
  5.4 3.5 %collective-permute-done.payload_ref = f32[320,128]{1,0:T(8,128)S(1)} collective-permute-done((f32[320,128]{1,0:T(8,128)S(1)}, f32[320,128]{1,0:T(8,128)S(1)}, u32[]{:S(2)}, u32[]{:S(2)}) %collective-permute-start) | collective-permute-done | bytes 163872 | tf_op jit(solution)/shard_map/ppermute | solution.py:749
  8.9 1.2 %shard_map.18 = (f32[256,128]{1,0:T(8,128)S(1)}, f32[256,128]{1,0:T(8,128)S(1)}, f32[256,128]{1,0:T(8,128)S(1)}, f32[256,128]{1,0:T(8,128)S(1)}, f32[16,128]{1,0:T(8,128)S(1)}, /*index=5*/f32[112,128]{1,0:T(8,128)S(1)}) custom-call(f32[256,128]{1,0:T(8,128)S(1)} %get-tuple-element.28.even_ref, f32[256,128]{1,0:T(8,128)S(1)} %get-tuple-element.29.odd_ref, ...), custom_call_target="tpu_custom_call" | custom-call | tf_op jit(solution)/shard_map/pallas_call | solution.py:713
  10.2 0.7 %shard_map.19 = f32[112,128]{1,0:T(8,128)S(1)} custom-call(f32[256,128]{1,0:T(8,128)S(1)} %get-tuple-element.31.even_ref, f32[256,128]{1,0:T(8,128)S(1)} %get-tuple-element.32.odd_ref, f32[16,128]{1,0:T(8,128)S(1)} %get-tuple-element.33.corner_ref), custom_call_target="tpu_custom_call" | custom-call | tf_op jit(solution)/shard_map/pallas_call | solution.py:713
  11.4 1.6 %collective-permute-start.2 = (f32[112,128]{1,0:T(8,128)S(1)}, f32[112,128]{1,0:T(8,128)S(1)}, u32[]{:S(2)}, u32[]{:S(2)}) collective-permute-start(f32[112,128]{1,0:T(8,128)S(1)} %add.6.refs_0_), channel_id=1, source_target_pairs={{0,8},{4,12},{8,0},{12,4},{16,24},{20,28},{24,16},{28,20},{1,9},{5... | collective-permute-start | bytes 172040 | tf_op jit(solution)/shard_map/ppermute | solution.py:696
  13.0 1.5 %collective-permute-start.3 = (f32[112,128]{1,0:T(8,128)S(1)}, f32[112,128]{1,0:T(8,128)S(1)}, u32[]{:S(2)}, u32[]{:S(2)}) collective-permute-start(f32[112,128]{1,0:T(8,128)S(1)} %add.6.refs_0_), channel_id=1, source_target_pairs={{0,16},{4,20},{8,24},{12,28},{16,0},{20,4},{24,8},{28,12},{1,17},{... | collective-permute-start | bytes 172040 | tf_op jit(solution)/shard_map/ppermute | solution.py:696
  15.0 0.7 %collective-permute-done.2.refs_1_ = f32[112,128]{1,0:T(8,128)S(1)} collective-permute-done((f32[112,128]{1,0:T(8,128)S(1)}, f32[112,128]{1,0:T(8,128)S(1)}, u32[]{:S(2)}, u32[]{:S(2)}) %collective-permute-start.2) | collective-permute-done | bytes 57376 | tf_op jit(solution)/shard_map/ppermute | solution.py:696
  15.7 1.5 %collective-permute-done.3.refs_2_ = f32[112,128]{1,0:T(8,128)S(1)} collective-permute-done((f32[112,128]{1,0:T(8,128)S(1)}, f32[112,128]{1,0:T(8,128)S(1)}, u32[]{:S(2)}, u32[]{:S(2)}) %collective-permute-start.3) | collective-permute-done | bytes 57376 | tf_op jit(solution)/shard_map/ppermute | solution.py:696
  17.2 2.4 %collective-permute-done.4.refs_3_ = f32[112,128]{1,0:T(8,128)S(1)} collective-permute-done((f32[112,128]{1,0:T(8,128)S(1)}, f32[112,128]{1,0:T(8,128)S(1)}, u32[]{:S(2)}, u32[]{:S(2)}) %collective-permute-start.4) | collective-permute-done | bytes 57376 | tf_op jit(solution)/shard_map/ppermute | solution.py:696
  19.6 1.2 %shard_map.20.found_ref.refs_4_ = f32[160,128]{1,0:T(8,128)S(1)} custom-call(f32[112,128]{1,0:T(8,128)S(1)} %add.6.refs_0_, f32[112,128]{1,0:T(8,128)S(1)} %collective-permute-done.2.refs_1_, f32[112,128]{1,0:T(8,128)S(1)} %collective-permute-done.3.refs_2_, f32[112,128]{1,0:T(8,128)S(1)} %collective-permute-done.4.refs_3_), custom_call_target="tpu_custom_call" | custom-call | tf_op jit(solution)/shard_map/pallas_call | solution.py:713
  20.9 0.7 %shard_map.21 = (f32[256,128]{1,0:T(8,128)S(1)}, f32[256,128]{1,0:T(8,128)S(1)}) custom-call(f32[256,128]{1,0:T(8,128)S(1)} %get-tuple-element.31.even_ref, f32[256,128]{1,0:T(8,128)S(1)} %get-tuple-element.32.odd_ref, f32[160,128]{1,0:T(8,128)S(1)} %shard_map.20.found_ref.refs_4_), custom_call_target="tpu_custom_call" | custom-call | tf_op jit(solution)/shard_map/pallas_call | solution.py:713
  22.2 1.6 %shard_map.22 = (f32[256,128]{1,0:T(8,128)S(1)}, f32[256,128]{1,0:T(8,128)S(1)}) custom-call(f32[256,128]{1,0:T(8,128)S(1)} %get-tuple-element.35.refs_0_, f32[256,128]{1,0:T(8,128)S(1)} %get-tuple-element.36.refs_1_, f32[256,128]{1,0:T(8,128)S(1)} %get-tuple-element.37.refs_2_, f32[256,128]{1,0:T(8,128)S(1)} %get-tuple-element.38.refs_3_, ...), custom_call_target="tpu_custom_call" | custom-call | tf_op jit(solution)/shard_map/pallas_call | solution.py:713
  23.8 2.4 %collective-permute-start.6 = (f32[256,128]{1,0:T(8,128)S(1)}, f32[256,128]{1,0:T(8,128)S(1)}, u32[]{:S(2)}, u32[]{:S(2)}) collective-permute-start(f32[256,128]{1,0:T(8,128)S(1)} %get-tuple-element.40.sent_ref), channel_id=1, source_target_pairs={{2,0},{3,2},{0,1},{1,3},{6,4},{7,6},{4,5},{5,7},{10,8},{11,10},{8,... | collective-permute-start | bytes 393224 | tf_op jit(solution)/shard_map/ppermute | solution.py:755
  26.2 1.1 %collective-permute-start.7 = (f32[256,128]{1,0:T(8,128)S(1)}, f32[256,128]{1,0:T(8,128)S(1)}, u32[]{:S(2)}, u32[]{:S(2)}) collective-permute-start(f32[256,128]{1,0:T(8,128)S(1)} %get-tuple-element.39.kept_ref), channel_id=1, source_target_pairs={{1,0},{0,2},{3,1},{2,3},{5,4},{4,6},{7,5},{6,7},{9,8},{8,10},{11,9... | collective-permute-start | bytes 393224 | tf_op jit(solution)/shard_map/ppermute | solution.py:755
  27.3 3.9 %collective-permute-done.6.came0_ref = f32[256,128]{1,0:T(8,128)S(1)} collective-permute-done((f32[256,128]{1,0:T(8,128)S(1)}, f32[256,128]{1,0:T(8,128)S(1)}, u32[]{:S(2)}, u32[]{:S(2)}) %collective-permute-start.6) | collective-permute-done | bytes 131104 | tf_op jit(solution)/shard_map/ppermute | solution.py:755
  31.1 2.7 %collective-permute-done.7.came1_ref = f32[256,128]{1,0:T(8,128)S(1)} collective-permute-done((f32[256,128]{1,0:T(8,128)S(1)}, f32[256,128]{1,0:T(8,128)S(1)}, u32[]{:S(2)}, u32[]{:S(2)}) %collective-permute-start.7) | collective-permute-done | bytes 131104 | tf_op jit(solution)/shard_map/ppermute | solution.py:755
  33.8 1.1 %shard_map.23 = (f32[256,128]{1,0:T(8,128)S(1)}, f32[256,128]{1,0:T(8,128)S(1)}, f32[256,128]{1,0:T(8,128)S(1)}, f32[256,128]{1,0:T(8,128)S(1)}, f32[16,128]{1,0:T(8,128)S(1)}, /*index=5*/f32[112,128]{1,0:T(8,128)S(1)}) custom-call(f32[256,128]{1,0:T(8,128)S(1)} %get-tuple-element.39.kept_ref, f32[256,128]{1,0:T(8,128)S(1)} %get-tuple-element.40.sent_ref, ...), custom_call_target="tpu_custom_call" | custom-call | tf_op jit(solution)/shard_map/pallas_call | solution.py:713
  35.1 0.7 %shard_map.24 = f32[112,128]{1,0:T(8,128)S(1)} custom-call(f32[256,128]{1,0:T(8,128)S(1)} %get-tuple-element.41.even_ref, f32[256,128]{1,0:T(8,128)S(1)} %get-tuple-element.42.odd_ref, f32[16,128]{1,0:T(8,128)S(1)} %get-tuple-element.43.corner_ref), custom_call_target="tpu_custom_call" | custom-call | tf_op jit(solution)/shard_map/pallas_call | solution.py:713
  36.3 0.6 %collective-permute-start.10 = (f32[112,128]{1,0:T(8,128)S(1)}, f32[112,128]{1,0:T(8,128)S(1)}, u32[]{:S(2)}, u32[]{:S(2)}) collective-permute-start(f32[112,128]{1,0:T(8,128)S(1)} %add.7.refs_0_), channel_id=1, source_target_pairs={{0,16},{4,20},{8,24},{12,28},{16,0},{20,4},{24,8},{28,12},{1,17},{... | collective-permute-start | bytes 172040 | tf_op jit(solution)/shard_map/ppermute | solution.py:696
  36.9 1.5 %collective-permute-start.11 = (f32[112,128]{1,0:T(8,128)S(1)}, f32[112,128]{1,0:T(8,128)S(1)}, u32[]{:S(2)}, u32[]{:S(2)}) collective-permute-start(f32[112,128]{1,0:T(8,128)S(1)} %add.7.refs_0_), channel_id=1, source_target_pairs={{0,24},{4,28},{8,16},{12,20},{16,8},{20,12},{24,0},{28,4},{1,25},{... | collective-permute-start | bytes 172040 | tf_op jit(solution)/shard_map/ppermute | solution.py:696
  38.4 1.5 %collective-permute-start.9 = (f32[112,128]{1,0:T(8,128)S(1)}, f32[112,128]{1,0:T(8,128)S(1)}, u32[]{:S(2)}, u32[]{:S(2)}) collective-permute-start(f32[112,128]{1,0:T(8,128)S(1)} %add.7.refs_0_), channel_id=1, source_target_pairs={{0,8},{4,12},{8,0},{12,4},{16,24},{20,28},{24,16},{28,20},{1,9},{5... | collective-permute-start | bytes 172040 | tf_op jit(solution)/shard_map/ppermute | solution.py:696
  39.8 1.3 %collective-permute-done.10.refs_2_ = f32[112,128]{1,0:T(8,128)S(1)} collective-permute-done((f32[112,128]{1,0:T(8,128)S(1)}, f32[112,128]{1,0:T(8,128)S(1)}, u32[]{:S(2)}, u32[]{:S(2)}) %collective-permute-start.10) | collective-permute-done | bytes 57376 | tf_op jit(solution)/shard_map/ppermute | solution.py:696
  41.1 0.9 %collective-permute-done.11.refs_3_ = f32[112,128]{1,0:T(8,128)S(1)} collective-permute-done((f32[112,128]{1,0:T(8,128)S(1)}, f32[112,128]{1,0:T(8,128)S(1)}, u32[]{:S(2)}, u32[]{:S(2)}) %collective-permute-start.11) | collective-permute-done | bytes 57376 | tf_op jit(solution)/shard_map/ppermute | solution.py:696
  42.0 0.7 %collective-permute-done.9.refs_1_ = f32[112,128]{1,0:T(8,128)S(1)} collective-permute-done((f32[112,128]{1,0:T(8,128)S(1)}, f32[112,128]{1,0:T(8,128)S(1)}, u32[]{:S(2)}, u32[]{:S(2)}) %collective-permute-start.9) | collective-permute-done | bytes 57376 | tf_op jit(solution)/shard_map/ppermute | solution.py:696
  42.7 1.2 %shard_map.25.found_ref.refs_4_ = f32[160,128]{1,0:T(8,128)S(1)} custom-call(f32[112,128]{1,0:T(8,128)S(1)} %add.7.refs_0_, f32[112,128]{1,0:T(8,128)S(1)} %collective-permute-done.9.refs_1_, f32[112,128]{1,0:T(8,128)S(1)} %collective-permute-done.10.refs_2_, f32[112,128]{1,0:T(8,128)S(1)} %collective-permute-done.11.refs_3_), custom_call_target="tpu_custom_call" | custom-call | tf_op jit(solution)/shard_map/pallas_call | solution.py:713
  44.0 0.7 %shard_map.26 = (f32[256,128]{1,0:T(8,128)S(1)}, f32[256,128]{1,0:T(8,128)S(1)}) custom-call(f32[256,128]{1,0:T(8,128)S(1)} %get-tuple-element.41.even_ref, f32[256,128]{1,0:T(8,128)S(1)} %get-tuple-element.42.odd_ref, f32[160,128]{1,0:T(8,128)S(1)} %shard_map.25.found_ref.refs_4_), custom_call_target="tpu_custom_call" | custom-call | tf_op jit(solution)/shard_map/pallas_call | solution.py:713
  44.7 0.6 %collective-permute-done.12.refs_5_ = f32[160,128]{1,0:T(8,128)S(1)} collective-permute-done((f32[160,128]{1,0:T(8,128)S(1)}, f32[160,128]{1,0:T(8,128)S(1)}, u32[]{:S(2)}, u32[]{:S(2)}) %collective-permute-start.12) | collective-permute-done | bytes 81952 | tf_op jit(solution)/shard_map/ppermute | solution.py:696
  45.3 1.6 %shard_map.27 = (f32[256,128]{1,0:T(8,128)S(1)}, f32[256,128]{1,0:T(8,128)S(1)}) custom-call(f32[256,128]{1,0:T(8,128)S(1)} %get-tuple-element.45.refs_0_, f32[256,128]{1,0:T(8,128)S(1)} %get-tuple-element.46.refs_1_, f32[256,128]{1,0:T(8,128)S(1)} %get-tuple-element.47.refs_2_, f32[256,128]{1,0:T(8,128)S(1)} %get-tuple-element.48.refs_3_, ...), custom_call_target="tpu_custom_call" | custom-call | tf_op jit(solution)/shard_map/pallas_call | solution.py:713
  46.9 1.8 %collective-permute-start.13 = (f32[256,128]{1,0:T(8,128)S(1)}, f32[256,128]{1,0:T(8,128)S(1)}, u32[]{:S(2)}, u32[]{:S(2)}) collective-permute-start(f32[256,128]{1,0:T(8,128)S(1)} %get-tuple-element.49), channel_id=1, source_target_pairs={{2,0},{0,1},{3,2},{1,3},{6,4},{4,5},{7,6},{5,7},{10,8},{8,9},{11,1... | collective-permute-start | bytes 393224 | tf_op jit(solution)/shard_map/ppermute | solution.py:761
  48.7 4.7 %collective-permute-done.13 = f32[256,128]{1,0:T(8,128)S(1)} collective-permute-done((f32[256,128]{1,0:T(8,128)S(1)}, f32[256,128]{1,0:T(8,128)S(1)}, u32[]{:S(2)}, u32[]{:S(2)}) %collective-permute-start.13) | collective-permute-done | bytes 131104 | tf_op jit(solution)/shard_map/ppermute | solution.py:761
  53.4 0.7 %pad_maximum_fusion = f32[256,256]{1,0:T(8,128)} fusion(f32[256,128]{1,0:T(8,128)S(1)} %get-tuple-element.52, f32[256,128]{1,0:T(8,128)S(1)} %get-tuple-element.51), kind=kLoop, calls=%fused_computation | loop fusion | flops 65536 | bytes 524288 | tf_op jit(solution)/shard_map/concatenate | solution.py:765
  (13 shorter events, 2.8 us)
Async XLA Ops:
  0.0 0.9 %copy-start = (f32[256,256]{1,0:T(8,128)S(1)}, f32[256,256]{1,0:T(8,128)}, u32[]{:S(2)}) copy-start(f32[256,256]{1,0:T(8,128)} %basis_ref.1) | copy-start | bytes 786436
  1.4 7.5 %collective-permute-start = (f32[320,128]{1,0:T(8,128)S(1)}, f32[320,128]{1,0:T(8,128)S(1)}, u32[]{:S(2)}, u32[]{:S(2)}) collective-permute-start(f32[320,128]{1,0:T(8,128)S(1)} %get-tuple-element.30), channel_id=1, source_target_pairs={{1,0},{0,2},{3,1},{2,3},{5,4},{4,6},{7,5},{6,7},{9,8},{8,10},{11,9... | collective-permute-start | bytes 491528 | tf_op jit(solution)/shard_map/ppermute | solution.py:749
  10.1 1.3 %collective-permute-start.1 = (f32[112,128]{1,0:T(8,128)S(1)}, f32[112,128]{1,0:T(8,128)S(1)}, u32[]{:S(2)}, u32[]{:S(2)}) collective-permute-start(f32[112,128]{1,0:T(8,128)S(1)} %get-tuple-element.34), channel_id=1, source_target_pairs={{0,4},{4,0},{8,12},{12,8},{16,20},{20,16},{24,28},{28,24},{1,5},{5... | collective-permute-start | bytes 172040 | tf_op jit(solution)/shard_map/ppermute | solution.py:696
  11.4 4.2 %collective-permute-start.2 = (f32[112,128]{1,0:T(8,128)S(1)}, f32[112,128]{1,0:T(8,128)S(1)}, u32[]{:S(2)}, u32[]{:S(2)}) collective-permute-start(f32[112,128]{1,0:T(8,128)S(1)} %add.6.refs_0_), channel_id=1, source_target_pairs={{0,8},{4,12},{8,0},{12,4},{16,24},{20,28},{24,16},{28,20},{1,9},{5... | collective-permute-start | bytes 172040 | tf_op jit(solution)/shard_map/ppermute | solution.py:696
  13.0 4.2 %collective-permute-start.3 = (f32[112,128]{1,0:T(8,128)S(1)}, f32[112,128]{1,0:T(8,128)S(1)}, u32[]{:S(2)}, u32[]{:S(2)}) collective-permute-start(f32[112,128]{1,0:T(8,128)S(1)} %add.6.refs_0_), channel_id=1, source_target_pairs={{0,16},{4,20},{8,24},{12,28},{16,0},{20,4},{24,8},{28,12},{1,17},{... | collective-permute-start | bytes 172040 | tf_op jit(solution)/shard_map/ppermute | solution.py:696
  14.5 5.1 %collective-permute-start.4 = (f32[112,128]{1,0:T(8,128)S(1)}, f32[112,128]{1,0:T(8,128)S(1)}, u32[]{:S(2)}, u32[]{:S(2)}) collective-permute-start(f32[112,128]{1,0:T(8,128)S(1)} %add.6.refs_0_), channel_id=1, source_target_pairs={{0,24},{4,28},{8,16},{12,20},{16,8},{20,12},{24,0},{28,4},{1,25},{... | collective-permute-start | bytes 172040 | tf_op jit(solution)/shard_map/ppermute | solution.py:696
  20.8 1.3 %collective-permute-start.5 = (f32[160,128]{1,0:T(8,128)S(1)}, f32[160,128]{1,0:T(8,128)S(1)}, u32[]{:S(2)}, u32[]{:S(2)}) collective-permute-start(f32[160,128]{1,0:T(8,128)S(1)} %shard_map.20.found_ref.refs_4_), channel_id=1, source_target_pairs={{0,4},{4,0},{8,12},{12,8},{16,20},{20,16},{24,28},{28,24},{1,5},{5... | collective-permute-start | bytes 245768 | tf_op jit(solution)/shard_map/ppermute | solution.py:696
  23.8 7.4 %collective-permute-start.6 = (f32[256,128]{1,0:T(8,128)S(1)}, f32[256,128]{1,0:T(8,128)S(1)}, u32[]{:S(2)}, u32[]{:S(2)}) collective-permute-start(f32[256,128]{1,0:T(8,128)S(1)} %get-tuple-element.40.sent_ref), channel_id=1, source_target_pairs={{2,0},{3,2},{0,1},{1,3},{6,4},{7,6},{4,5},{5,7},{10,8},{11,10},{8,... | collective-permute-start | bytes 393224 | tf_op jit(solution)/shard_map/ppermute | solution.py:755
  26.2 7.6 %collective-permute-start.7 = (f32[256,128]{1,0:T(8,128)S(1)}, f32[256,128]{1,0:T(8,128)S(1)}, u32[]{:S(2)}, u32[]{:S(2)}) collective-permute-start(f32[256,128]{1,0:T(8,128)S(1)} %get-tuple-element.39.kept_ref), channel_id=1, source_target_pairs={{1,0},{0,2},{3,1},{2,3},{5,4},{4,6},{7,5},{6,7},{9,8},{8,10},{11,9... | collective-permute-start | bytes 393224 | tf_op jit(solution)/shard_map/ppermute | solution.py:755
  35.0 1.3 %collective-permute-start.8 = (f32[112,128]{1,0:T(8,128)S(1)}, f32[112,128]{1,0:T(8,128)S(1)}, u32[]{:S(2)}, u32[]{:S(2)}) collective-permute-start(f32[112,128]{1,0:T(8,128)S(1)} %get-tuple-element.44), channel_id=1, source_target_pairs={{0,4},{4,0},{8,12},{12,8},{16,20},{20,16},{24,28},{28,24},{1,5},{5... | collective-permute-start | bytes 172040 | tf_op jit(solution)/shard_map/ppermute | solution.py:696
  36.3 4.9 %collective-permute-start.10 = (f32[112,128]{1,0:T(8,128)S(1)}, f32[112,128]{1,0:T(8,128)S(1)}, u32[]{:S(2)}, u32[]{:S(2)}) collective-permute-start(f32[112,128]{1,0:T(8,128)S(1)} %add.7.refs_0_), channel_id=1, source_target_pairs={{0,16},{4,20},{8,24},{12,28},{16,0},{20,4},{24,8},{28,12},{1,17},{... | collective-permute-start | bytes 172040 | tf_op jit(solution)/shard_map/ppermute | solution.py:696
  36.9 5.2 %collective-permute-start.11 = (f32[112,128]{1,0:T(8,128)S(1)}, f32[112,128]{1,0:T(8,128)S(1)}, u32[]{:S(2)}, u32[]{:S(2)}) collective-permute-start(f32[112,128]{1,0:T(8,128)S(1)} %add.7.refs_0_), channel_id=1, source_target_pairs={{0,24},{4,28},{8,16},{12,20},{16,8},{20,12},{24,0},{28,4},{1,25},{... | collective-permute-start | bytes 172040 | tf_op jit(solution)/shard_map/ppermute | solution.py:696
  38.4 4.4 %collective-permute-start.9 = (f32[112,128]{1,0:T(8,128)S(1)}, f32[112,128]{1,0:T(8,128)S(1)}, u32[]{:S(2)}, u32[]{:S(2)}) collective-permute-start(f32[112,128]{1,0:T(8,128)S(1)} %add.7.refs_0_), channel_id=1, source_target_pairs={{0,8},{4,12},{8,0},{12,4},{16,24},{20,28},{24,16},{28,20},{1,9},{5... | collective-permute-start | bytes 172040 | tf_op jit(solution)/shard_map/ppermute | solution.py:696
  43.9 1.3 %collective-permute-start.12 = (f32[160,128]{1,0:T(8,128)S(1)}, f32[160,128]{1,0:T(8,128)S(1)}, u32[]{:S(2)}, u32[]{:S(2)}) collective-permute-start(f32[160,128]{1,0:T(8,128)S(1)} %shard_map.25.found_ref.refs_4_), channel_id=1, source_target_pairs={{0,4},{4,0},{8,12},{12,8},{16,20},{20,16},{24,28},{28,24},{1,5},{5... | collective-permute-start | bytes 245768 | tf_op jit(solution)/shard_map/ppermute | solution.py:696
  46.9 6.5 %collective-permute-start.13 = (f32[256,128]{1,0:T(8,128)S(1)}, f32[256,128]{1,0:T(8,128)S(1)}, u32[]{:S(2)}, u32[]{:S(2)}) collective-permute-start(f32[256,128]{1,0:T(8,128)S(1)} %get-tuple-element.49), channel_id=1, source_target_pairs={{2,0},{0,1},{3,2},{1,3},{6,4},{4,5},{7,6},{5,7},{10,8},{8,9},{11,1... | collective-permute-start | bytes 393224 | tf_op jit(solution)/shard_map/ppermute | solution.py:761

commit v9 on v8

--- a/solution.py
+++ b/solution.py
@@ -95,17 +95,17 @@
                     edges.append((there, old % 2, here))
     turn, left_over = {}, list(edges)
     while left_over:
-        source, _, target = left_over[0]
-        start = source
+        start = source = min(e[0] for e in left_over)
+        target, number = min(e[2] for e in left_over if e[0] == source), 0
         while True:
-            for number, one, other in ((0, source, target), (1, target, source)):
+            for one, other in ((source, target), (target, source)):
                 edge = next(e for e in left_over if (e[0], e[2]) == (one, other))
                 turn[edge] = number
                 left_over.remove(edge)
             if target == start:
                 break
-            ahead = [e[2] for e in left_over if e[0] == target]
-            source, target = target, ahead[0]
+            source, number = target, 1 - number
+            target = next(e[2] for e in left_over if e[0] == source)
     sends = [[(e[0], e[2]) for e in edges if turn[e] == i] for i in (0, 1)]
     for chosen in sends:
         assert len({a for a, _ in chosen}) == len({b for _, b in chosen}) == pair_total

time: 54.3 us -> 55.7 us (1.026)
  waiting for transfers between devices: 24.3 us -> 26.4 us
  starting transfers between devices: 16.8 us -> 16.1 us
    ppermute x2, waiting for transfers between devices: 8.17 us -> 9.46 us  [per_device(): came = lax.ppermute(sent, 'pair', sends)]
    ppermute x2, starting transfers between devices: 5.88 us -> 4.59 us  [per_device(): came = lax.ppermute(sent, 'pair', sends)]
    ppermute x2, waiting for transfers between devices: 6.56 us -> 7.34 us  [per_device(): came = [lax.ppermute(x, 'pair', s) for x, s in zip((sent, kept), sends)]]
    ppermute x2, starting transfers between devices: 3.5 us -> 4.12 us  [per_device(): came = [lax.ppermute(x, 'pair', s) for x, s in zip((sent, kept), sends)]]
where the time goes in v9:
time: 55.7 us; the launch traced here: 55.6 us
  waiting for transfers between devices  26.4 us (47%)
  starting transfers between devices  16.1 us (29%)
  Pallas kernels  11.2 us (20%)
  local copies, waits for them, and re-layouts  0.95 us (2%)
  other arithmetic  0.76 us (1%)
    pallas_call x11, Pallas kernels, call(): pl.pallas_call(kernel, out_shape=out, compiler_params=pltpu.CompilerParam...  11.2 us
    ppermute x10, waiting for transfers between devices, swap(): lax.ppermute(x, axis, [(i, i ^ mask) for i in range(lax.axis_size(axis))])  9.57 us
    ppermute x2, waiting for transfers between devices, per_device(): came = lax.ppermute(sent, 'pair', sends)  9.46 us
    ppermute x10, starting transfers between devices, swap(): lax.ppermute(x, axis, [(i, i ^ mask) for i in range(lax.axis_size(axis))])  7.39 us
    ppermute x2, waiting for transfers between devices, per_device(): came = [lax.ppermute(x, 'pair', s) for x, s in zip((sent, kept), sends)]  7.34 us
    ppermute x2, starting transfers between devices, per_device(): came = lax.ppermute(sent, 'pair', sends)  4.59 us
    ppermute x2, starting transfers between devices, per_device(): came = [lax.ppermute(x, 'pair', s) for x, s in zip((sent, kept), sends)]  4.12 us
  transfers between devices with their start and end apart: 14, of which 14 were waited for; matrix products, arithmetic and copies ran while one was open for 0% of the time, Pallas kernels for 5%

profile of v9, /device:TPU:0, one launch (start us, length us, event | category | flops | bytes accessed | tf_op | source)
XLA Modules:
  0.0 55.6 jit_solution(815031281006648841)
XLA Ops:
  0.0 0.9 %copy-done = f32[256,256]{1,0:T(8,128)S(1)} copy-done((f32[256,256]{1,0:T(8,128)S(1)}, f32[256,256]{1,0:T(8,128)}, u32[]{:S(2)}) %copy-start) | copy-done | bytes 262168
  1.4 4.1 %collective-permute-start = (f32[320,128]{1,0:T(8,128)S(1)}, f32[320,128]{1,0:T(8,128)S(1)}, u32[]{:S(2)}, u32[]{:S(2)}) collective-permute-start(f32[320,128]{1,0:T(8,128)S(1)} %get-tuple-element.30), channel_id=1, source_target_pairs={{1,0},{0,2},{3,1},{2,3},{5,4},{4,6},{7,5},{6,7},{9,8},{8,10},{11,9... | collective-permute-start | bytes 491528 | tf_op jit(solution)/shard_map/ppermute | solution.py:749
  5.4 3.5 %collective-permute-done.payload_ref = f32[320,128]{1,0:T(8,128)S(1)} collective-permute-done((f32[320,128]{1,0:T(8,128)S(1)}, f32[320,128]{1,0:T(8,128)S(1)}, u32[]{:S(2)}, u32[]{:S(2)}) %collective-permute-start) | collective-permute-done | bytes 163872 | tf_op jit(solution)/shard_map/ppermute | solution.py:749
  8.9 1.2 %shard_map.18 = (f32[256,128]{1,0:T(8,128)S(1)}, f32[256,128]{1,0:T(8,128)S(1)}, f32[256,128]{1,0:T(8,128)S(1)}, f32[256,128]{1,0:T(8,128)S(1)}, f32[16,128]{1,0:T(8,128)S(1)}, /*index=5*/f32[112,128]{1,0:T(8,128)S(1)}) custom-call(f32[256,128]{1,0:T(8,128)S(1)} %get-tuple-element.28.even_ref, f32[256,128]{1,0:T(8,128)S(1)} %get-tuple-element.29.odd_ref, ...), custom_call_target="tpu_custom_call" | custom-call | tf_op jit(solution)/shard_map/pallas_call | solution.py:713
  10.2 0.7 %shard_map.19 = f32[112,128]{1,0:T(8,128)S(1)} custom-call(f32[256,128]{1,0:T(8,128)S(1)} %get-tuple-element.31.even_ref, f32[256,128]{1,0:T(8,128)S(1)} %get-tuple-element.32.odd_ref, f32[16,128]{1,0:T(8,128)S(1)} %get-tuple-element.33.corner_ref), custom_call_target="tpu_custom_call" | custom-call | tf_op jit(solution)/shard_map/pallas_call | solution.py:713
  11.4 1.6 %collective-permute-start.2 = (f32[112,128]{1,0:T(8,128)S(1)}, f32[112,128]{1,0:T(8,128)S(1)}, u32[]{:S(2)}, u32[]{:S(2)}) collective-permute-start(f32[112,128]{1,0:T(8,128)S(1)} %add.6.refs_0_), channel_id=1, source_target_pairs={{0,8},{4,12},{8,0},{12,4},{16,24},{20,28},{24,16},{28,20},{1,9},{5... | collective-permute-start | bytes 172040 | tf_op jit(solution)/shard_map/ppermute | solution.py:696
  13.0 1.5 %collective-permute-start.3 = (f32[112,128]{1,0:T(8,128)S(1)}, f32[112,128]{1,0:T(8,128)S(1)}, u32[]{:S(2)}, u32[]{:S(2)}) collective-permute-start(f32[112,128]{1,0:T(8,128)S(1)} %add.6.refs_0_), channel_id=1, source_target_pairs={{0,16},{4,20},{8,24},{12,28},{16,0},{20,4},{24,8},{28,12},{1,17},{... | collective-permute-start | bytes 172040 | tf_op jit(solution)/shard_map/ppermute | solution.py:696
  15.0 0.7 %collective-permute-done.2.refs_1_ = f32[112,128]{1,0:T(8,128)S(1)} collective-permute-done((f32[112,128]{1,0:T(8,128)S(1)}, f32[112,128]{1,0:T(8,128)S(1)}, u32[]{:S(2)}, u32[]{:S(2)}) %collective-permute-start.2) | collective-permute-done | bytes 57376 | tf_op jit(solution)/shard_map/ppermute | solution.py:696
  15.7 1.5 %collective-permute-done.3.refs_2_ = f32[112,128]{1,0:T(8,128)S(1)} collective-permute-done((f32[112,128]{1,0:T(8,128)S(1)}, f32[112,128]{1,0:T(8,128)S(1)}, u32[]{:S(2)}, u32[]{:S(2)}) %collective-permute-start.3) | collective-permute-done | bytes 57376 | tf_op jit(solution)/shard_map/ppermute | solution.py:696
  17.2 2.4 %collective-permute-done.4.refs_3_ = f32[112,128]{1,0:T(8,128)S(1)} collective-permute-done((f32[112,128]{1,0:T(8,128)S(1)}, f32[112,128]{1,0:T(8,128)S(1)}, u32[]{:S(2)}, u32[]{:S(2)}) %collective-permute-start.4) | collective-permute-done | bytes 57376 | tf_op jit(solution)/shard_map/ppermute | solution.py:696
  19.6 1.2 %shard_map.20.found_ref.refs_4_ = f32[160,128]{1,0:T(8,128)S(1)} custom-call(f32[112,128]{1,0:T(8,128)S(1)} %add.6.refs_0_, f32[112,128]{1,0:T(8,128)S(1)} %collective-permute-done.2.refs_1_, f32[112,128]{1,0:T(8,128)S(1)} %collective-permute-done.3.refs_2_, f32[112,128]{1,0:T(8,128)S(1)} %collective-permute-done.4.refs_3_), custom_call_target="tpu_custom_call" | custom-call | tf_op jit(solution)/shard_map/pallas_call | solution.py:713
  20.9 0.7 %shard_map.21 = (f32[256,128]{1,0:T(8,128)S(1)}, f32[256,128]{1,0:T(8,128)S(1)}) custom-call(f32[256,128]{1,0:T(8,128)S(1)} %get-tuple-element.31.even_ref, f32[256,128]{1,0:T(8,128)S(1)} %get-tuple-element.32.odd_ref, f32[160,128]{1,0:T(8,128)S(1)} %shard_map.20.found_ref.refs_4_), custom_call_target="tpu_custom_call" | custom-call | tf_op jit(solution)/shard_map/pallas_call | solution.py:713
  21.6 0.6 collective-permute-done.5.refs_5_
  22.2 1.6 %shard_map.22 = (f32[256,128]{1,0:T(8,128)S(1)}, f32[256,128]{1,0:T(8,128)S(1)}) custom-call(f32[256,128]{1,0:T(8,128)S(1)} %get-tuple-element.35.refs_0_, f32[256,128]{1,0:T(8,128)S(1)} %get-tuple-element.36.refs_1_, f32[256,128]{1,0:T(8,128)S(1)} %get-tuple-element.37.refs_2_, f32[256,128]{1,0:T(8,128)S(1)} %get-tuple-element.38.refs_3_, ...), custom_call_target="tpu_custom_call" | custom-call | tf_op jit(solution)/shard_map/pallas_call | solution.py:713
  23.8 2.4 %collective-permute-start.6 = (f32[256,128]{1,0:T(8,128)S(1)}, f32[256,128]{1,0:T(8,128)S(1)}, u32[]{:S(2)}, u32[]{:S(2)}) collective-permute-start(f32[256,128]{1,0:T(8,128)S(1)} %get-tuple-element.40.sent_ref), channel_id=1, source_target_pairs={{1,0},{3,2},{0,1},{2,3},{5,4},{7,6},{4,5},{6,7},{9,8},{11,10},{8,9... | collective-permute-start | bytes 393224 | tf_op jit(solution)/shard_map/ppermute | solution.py:755
  26.2 1.7 %collective-permute-start.7 = (f32[256,128]{1,0:T(8,128)S(1)}, f32[256,128]{1,0:T(8,128)S(1)}, u32[]{:S(2)}, u32[]{:S(2)}) collective-permute-start(f32[256,128]{1,0:T(8,128)S(1)} %get-tuple-element.39.kept_ref), channel_id=1, source_target_pairs={{2,0},{0,2},{3,1},{1,3},{6,4},{4,6},{7,5},{5,7},{10,8},{8,10},{11,... | collective-permute-start | bytes 393224 | tf_op jit(solution)/shard_map/ppermute | solution.py:755
  27.9 4.3 %collective-permute-done.6.came0_ref = f32[256,128]{1,0:T(8,128)S(1)} collective-permute-done((f32[256,128]{1,0:T(8,128)S(1)}, f32[256,128]{1,0:T(8,128)S(1)}, u32[]{:S(2)}, u32[]{:S(2)}) %collective-permute-start.6) | collective-permute-done | bytes 131104 | tf_op jit(solution)/shard_map/ppermute | solution.py:755
  32.2 3.0 %collective-permute-done.7.came1_ref = f32[256,128]{1,0:T(8,128)S(1)} collective-permute-done((f32[256,128]{1,0:T(8,128)S(1)}, f32[256,128]{1,0:T(8,128)S(1)}, u32[]{:S(2)}, u32[]{:S(2)}) %collective-permute-start.7) | collective-permute-done | bytes 131104 | tf_op jit(solution)/shard_map/ppermute | solution.py:755
  35.3 1.1 %shard_map.23 = (f32[256,128]{1,0:T(8,128)S(1)}, f32[256,128]{1,0:T(8,128)S(1)}, f32[256,128]{1,0:T(8,128)S(1)}, f32[256,128]{1,0:T(8,128)S(1)}, f32[16,128]{1,0:T(8,128)S(1)}, /*index=5*/f32[112,128]{1,0:T(8,128)S(1)}) custom-call(f32[256,128]{1,0:T(8,128)S(1)} %get-tuple-element.39.kept_ref, f32[256,128]{1,0:T(8,128)S(1)} %get-tuple-element.40.sent_ref, ...), custom_call_target="tpu_custom_call" | custom-call | tf_op jit(solution)/shard_map/pallas_call | solution.py:713
  36.5 0.7 %shard_map.24 = f32[112,128]{1,0:T(8,128)S(1)} custom-call(f32[256,128]{1,0:T(8,128)S(1)} %get-tuple-element.41.even_ref, f32[256,128]{1,0:T(8,128)S(1)} %get-tuple-element.42.odd_ref, f32[16,128]{1,0:T(8,128)S(1)} %get-tuple-element.43.corner_ref), custom_call_target="tpu_custom_call" | custom-call | tf_op jit(solution)/shard_map/pallas_call | solution.py:713
  37.7 0.6 %collective-permute-start.10 = (f32[112,128]{1,0:T(8,128)S(1)}, f32[112,128]{1,0:T(8,128)S(1)}, u32[]{:S(2)}, u32[]{:S(2)}) collective-permute-start(f32[112,128]{1,0:T(8,128)S(1)} %add.7.refs_0_), channel_id=1, source_target_pairs={{0,16},{4,20},{8,24},{12,28},{16,0},{20,4},{24,8},{28,12},{1,17},{... | collective-permute-start | bytes 172040 | tf_op jit(solution)/shard_map/ppermute | solution.py:696
  38.3 1.5 %collective-permute-start.11 = (f32[112,128]{1,0:T(8,128)S(1)}, f32[112,128]{1,0:T(8,128)S(1)}, u32[]{:S(2)}, u32[]{:S(2)}) collective-permute-start(f32[112,128]{1,0:T(8,128)S(1)} %add.7.refs_0_), channel_id=1, source_target_pairs={{0,24},{4,28},{8,16},{12,20},{16,8},{20,12},{24,0},{28,4},{1,25},{... | collective-permute-start | bytes 172040 | tf_op jit(solution)/shard_map/ppermute | solution.py:696
  39.8 1.5 %collective-permute-start.9 = (f32[112,128]{1,0:T(8,128)S(1)}, f32[112,128]{1,0:T(8,128)S(1)}, u32[]{:S(2)}, u32[]{:S(2)}) collective-permute-start(f32[112,128]{1,0:T(8,128)S(1)} %add.7.refs_0_), channel_id=1, source_target_pairs={{0,8},{4,12},{8,0},{12,4},{16,24},{20,28},{24,16},{28,20},{1,9},{5... | collective-permute-start | bytes 172040 | tf_op jit(solution)/shard_map/ppermute | solution.py:696
  41.3 1.3 %collective-permute-done.10.refs_2_ = f32[112,128]{1,0:T(8,128)S(1)} collective-permute-done((f32[112,128]{1,0:T(8,128)S(1)}, f32[112,128]{1,0:T(8,128)S(1)}, u32[]{:S(2)}, u32[]{:S(2)}) %collective-permute-start.10) | collective-permute-done | bytes 57376 | tf_op jit(solution)/shard_map/ppermute | solution.py:696
  42.6 0.9 %collective-permute-done.11.refs_3_ = f32[112,128]{1,0:T(8,128)S(1)} collective-permute-done((f32[112,128]{1,0:T(8,128)S(1)}, f32[112,128]{1,0:T(8,128)S(1)}, u32[]{:S(2)}, u32[]{:S(2)}) %collective-permute-start.11) | collective-permute-done | bytes 57376 | tf_op jit(solution)/shard_map/ppermute | solution.py:696
  43.5 0.7 %collective-permute-done.9.refs_1_ = f32[112,128]{1,0:T(8,128)S(1)} collective-permute-done((f32[112,128]{1,0:T(8,128)S(1)}, f32[112,128]{1,0:T(8,128)S(1)}, u32[]{:S(2)}, u32[]{:S(2)}) %collective-permute-start.9) | collective-permute-done | bytes 57376 | tf_op jit(solution)/shard_map/ppermute | solution.py:696
  44.1 1.2 %shard_map.25.found_ref.refs_4_ = f32[160,128]{1,0:T(8,128)S(1)} custom-call(f32[112,128]{1,0:T(8,128)S(1)} %add.7.refs_0_, f32[112,128]{1,0:T(8,128)S(1)} %collective-permute-done.9.refs_1_, f32[112,128]{1,0:T(8,128)S(1)} %collective-permute-done.10.refs_2_, f32[112,128]{1,0:T(8,128)S(1)} %collective-permute-done.11.refs_3_), custom_call_target="tpu_custom_call" | custom-call | tf_op jit(solution)/shard_map/pallas_call | solution.py:713
  45.4 0.7 %shard_map.26 = (f32[256,128]{1,0:T(8,128)S(1)}, f32[256,128]{1,0:T(8,128)S(1)}) custom-call(f32[256,128]{1,0:T(8,128)S(1)} %get-tuple-element.41.even_ref, f32[256,128]{1,0:T(8,128)S(1)} %get-tuple-element.42.odd_ref, f32[160,128]{1,0:T(8,128)S(1)} %shard_map.25.found_ref.refs_4_), custom_call_target="tpu_custom_call" | custom-call | tf_op jit(solution)/shard_map/pallas_call | solution.py:713
  46.2 0.6 collective-permute-done.12.refs_5_
  46.7 1.6 %shard_map.27 = (f32[256,128]{1,0:T(8,128)S(1)}, f32[256,128]{1,0:T(8,128)S(1)}) custom-call(f32[256,128]{1,0:T(8,128)S(1)} %get-tuple-element.45.refs_0_, f32[256,128]{1,0:T(8,128)S(1)} %get-tuple-element.46.refs_1_, f32[256,128]{1,0:T(8,128)S(1)} %get-tuple-element.47.refs_2_, f32[256,128]{1,0:T(8,128)S(1)} %get-tuple-element.48.refs_3_, ...), custom_call_target="tpu_custom_call" | custom-call | tf_op jit(solution)/shard_map/pallas_call | solution.py:713
  48.8 6.0 %collective-permute-done.13 = f32[256,128]{1,0:T(8,128)S(1)} collective-permute-done((f32[256,128]{1,0:T(8,128)S(1)}, f32[256,128]{1,0:T(8,128)S(1)}, u32[]{:S(2)}, u32[]{:S(2)}) %collective-permute-start.13) | collective-permute-done | bytes 131104 | tf_op jit(solution)/shard_map/ppermute | solution.py:761
  54.8 0.7 %pad_maximum_fusion = f32[256,256]{1,0:T(8,128)} fusion(f32[256,128]{1,0:T(8,128)S(1)} %get-tuple-element.52, f32[256,128]{1,0:T(8,128)S(1)} %get-tuple-element.51), kind=kLoop, calls=%fused_computation | loop fusion | flops 65536 | bytes 524288 | tf_op jit(solution)/shard_map/concatenate | solution.py:765
  (13 shorter events, 2.7 us)
Async XLA Ops:
  0.0 0.9 %copy-start = (f32[256,256]{1,0:T(8,128)S(1)}, f32[256,256]{1,0:T(8,128)}, u32[]{:S(2)}) copy-start(f32[256,256]{1,0:T(8,128)} %basis_ref.1) | copy-start | bytes 786436
  1.4 7.5 %collective-permute-start = (f32[320,128]{1,0:T(8,128)S(1)}, f32[320,128]{1,0:T(8,128)S(1)}, u32[]{:S(2)}, u32[]{:S(2)}) collective-permute-start(f32[320,128]{1,0:T(8,128)S(1)} %get-tuple-element.30), channel_id=1, source_target_pairs={{1,0},{0,2},{3,1},{2,3},{5,4},{4,6},{7,5},{6,7},{9,8},{8,10},{11,9... | collective-permute-start | bytes 491528 | tf_op jit(solution)/shard_map/ppermute | solution.py:749
  10.1 1.3 %collective-permute-start.1 = (f32[112,128]{1,0:T(8,128)S(1)}, f32[112,128]{1,0:T(8,128)S(1)}, u32[]{:S(2)}, u32[]{:S(2)}) collective-permute-start(f32[112,128]{1,0:T(8,128)S(1)} %get-tuple-element.34), channel_id=1, source_target_pairs={{0,4},{4,0},{8,12},{12,8},{16,20},{20,16},{24,28},{28,24},{1,5},{5... | collective-permute-start | bytes 172040 | tf_op jit(solution)/shard_map/ppermute | solution.py:696
  11.4 4.2 %collective-permute-start.2 = (f32[112,128]{1,0:T(8,128)S(1)}, f32[112,128]{1,0:T(8,128)S(1)}, u32[]{:S(2)}, u32[]{:S(2)}) collective-permute-start(f32[112,128]{1,0:T(8,128)S(1)} %add.6.refs_0_), channel_id=1, source_target_pairs={{0,8},{4,12},{8,0},{12,4},{16,24},{20,28},{24,16},{28,20},{1,9},{5... | collective-permute-start | bytes 172040 | tf_op jit(solution)/shard_map/ppermute | solution.py:696
  13.0 4.2 %collective-permute-start.3 = (f32[112,128]{1,0:T(8,128)S(1)}, f32[112,128]{1,0:T(8,128)S(1)}, u32[]{:S(2)}, u32[]{:S(2)}) collective-permute-start(f32[112,128]{1,0:T(8,128)S(1)} %add.6.refs_0_), channel_id=1, source_target_pairs={{0,16},{4,20},{8,24},{12,28},{16,0},{20,4},{24,8},{28,12},{1,17},{... | collective-permute-start | bytes 172040 | tf_op jit(solution)/shard_map/ppermute | solution.py:696
  14.5 5.1 %collective-permute-start.4 = (f32[112,128]{1,0:T(8,128)S(1)}, f32[112,128]{1,0:T(8,128)S(1)}, u32[]{:S(2)}, u32[]{:S(2)}) collective-permute-start(f32[112,128]{1,0:T(8,128)S(1)} %add.6.refs_0_), channel_id=1, source_target_pairs={{0,24},{4,28},{8,16},{12,20},{16,8},{20,12},{24,0},{28,4},{1,25},{... | collective-permute-start | bytes 172040 | tf_op jit(solution)/shard_map/ppermute | solution.py:696
  20.8 1.3 %collective-permute-start.5 = (f32[160,128]{1,0:T(8,128)S(1)}, f32[160,128]{1,0:T(8,128)S(1)}, u32[]{:S(2)}, u32[]{:S(2)}) collective-permute-start(f32[160,128]{1,0:T(8,128)S(1)} %shard_map.20.found_ref.refs_4_), channel_id=1, source_target_pairs={{0,4},{4,0},{8,12},{12,8},{16,20},{20,16},{24,28},{28,24},{1,5},{5... | collective-permute-start | bytes 245768 | tf_op jit(solution)/shard_map/ppermute | solution.py:696
  23.8 8.5 %collective-permute-start.6 = (f32[256,128]{1,0:T(8,128)S(1)}, f32[256,128]{1,0:T(8,128)S(1)}, u32[]{:S(2)}, u32[]{:S(2)}) collective-permute-start(f32[256,128]{1,0:T(8,128)S(1)} %get-tuple-element.40.sent_ref), channel_id=1, source_target_pairs={{1,0},{3,2},{0,1},{2,3},{5,4},{7,6},{4,5},{6,7},{9,8},{11,10},{8,9... | collective-permute-start | bytes 393224 | tf_op jit(solution)/shard_map/ppermute | solution.py:755
  26.2 9.0 %collective-permute-start.7 = (f32[256,128]{1,0:T(8,128)S(1)}, f32[256,128]{1,0:T(8,128)S(1)}, u32[]{:S(2)}, u32[]{:S(2)}) collective-permute-start(f32[256,128]{1,0:T(8,128)S(1)} %get-tuple-element.39.kept_ref), channel_id=1, source_target_pairs={{2,0},{0,2},{3,1},{1,3},{6,4},{4,6},{7,5},{5,7},{10,8},{8,10},{11,... | collective-permute-start | bytes 393224 | tf_op jit(solution)/shard_map/ppermute | solution.py:755
  36.4 1.3 %collective-permute-start.8 = (f32[112,128]{1,0:T(8,128)S(1)}, f32[112,128]{1,0:T(8,128)S(1)}, u32[]{:S(2)}, u32[]{:S(2)}) collective-permute-start(f32[112,128]{1,0:T(8,128)S(1)} %get-tuple-element.44), channel_id=1, source_target_pairs={{0,4},{4,0},{8,12},{12,8},{16,20},{20,16},{24,28},{28,24},{1,5},{5... | collective-permute-start | bytes 172040 | tf_op jit(solution)/shard_map/ppermute | solution.py:696
  37.7 4.9 %collective-permute-start.10 = (f32[112,128]{1,0:T(8,128)S(1)}, f32[112,128]{1,0:T(8,128)S(1)}, u32[]{:S(2)}, u32[]{:S(2)}) collective-permute-start(f32[112,128]{1,0:T(8,128)S(1)} %add.7.refs_0_), channel_id=1, source_target_pairs={{0,16},{4,20},{8,24},{12,28},{16,0},{20,4},{24,8},{28,12},{1,17},{... | collective-permute-start | bytes 172040 | tf_op jit(solution)/shard_map/ppermute | solution.py:696
  38.3 5.2 %collective-permute-start.11 = (f32[112,128]{1,0:T(8,128)S(1)}, f32[112,128]{1,0:T(8,128)S(1)}, u32[]{:S(2)}, u32[]{:S(2)}) collective-permute-start(f32[112,128]{1,0:T(8,128)S(1)} %add.7.refs_0_), channel_id=1, source_target_pairs={{0,24},{4,28},{8,16},{12,20},{16,8},{20,12},{24,0},{28,4},{1,25},{... | collective-permute-start | bytes 172040 | tf_op jit(solution)/shard_map/ppermute | solution.py:696
  39.8 4.4 %collective-permute-start.9 = (f32[112,128]{1,0:T(8,128)S(1)}, f32[112,128]{1,0:T(8,128)S(1)}, u32[]{:S(2)}, u32[]{:S(2)}) collective-permute-start(f32[112,128]{1,0:T(8,128)S(1)} %add.7.refs_0_), channel_id=1, source_target_pairs={{0,8},{4,12},{8,0},{12,4},{16,24},{20,28},{24,16},{28,20},{1,9},{5... | collective-permute-start | bytes 172040 | tf_op jit(solution)/shard_map/ppermute | solution.py:696
  45.4 1.3 %collective-permute-start.12 = (f32[160,128]{1,0:T(8,128)S(1)}, f32[160,128]{1,0:T(8,128)S(1)}, u32[]{:S(2)}, u32[]{:S(2)}) collective-permute-start(f32[160,128]{1,0:T(8,128)S(1)} %shard_map.25.found_ref.refs_4_), channel_id=1, source_target_pairs={{0,4},{4,0},{8,12},{12,8},{16,20},{20,16},{24,28},{28,24},{1,5},{5... | collective-permute-start | bytes 245768 | tf_op jit(solution)/shard_map/ppermute | solution.py:696
  48.3 6.5 %collective-permute-start.13 = (f32[256,128]{1,0:T(8,128)S(1)}, f32[256,128]{1,0:T(8,128)S(1)}, u32[]{:S(2)}, u32[]{:S(2)}) collective-permute-start(f32[256,128]{1,0:T(8,128)S(1)} %get-tuple-element.49), channel_id=1, source_target_pairs={{2,0},{0,1},{3,2},{1,3},{6,4},{4,5},{7,6},{5,7},{10,8},{8,9},{11,1... | collective-permute-start | bytes 393224 | tf_op jit(solution)/shard_map/ppermute | solution.py:761

commit v10 on v8

--- a/solution.py
+++ b/solution.py
@@ -98,7 +98,7 @@
         source, _, target = left_over[0]
         start = source
         while True:
-            for number, one, other in ((0, source, target), (1, target, source)):
+            for number, one, other in ((1, source, target), (0, target, source)):
                 edge = next(e for e in left_over if (e[0], e[2]) == (one, other))
                 turn[edge] = number
                 left_over.remove(edge)

time: 54.3 us -> 55.3 us (1.018)
  waiting for transfers between devices: 24.3 us -> 26.4 us
  starting transfers between devices: 16.8 us -> 15.7 us
    ppermute x2, waiting for transfers between devices: 6.56 us -> 7.68 us  [per_device(): came = [lax.ppermute(x, 'pair', s) for x, s in zip((sent, kept), sends)]]
    ppermute x2, starting transfers between devices: 5.88 us -> 4.86 us  [per_device(): came = lax.ppermute(sent, 'pair', sends)]
    ppermute x2, waiting for transfers between devices: 8.17 us -> 9.19 us  [per_device(): came = lax.ppermute(sent, 'pair', sends)]
where the time goes in v10:
time: 55.3 us; the launch traced here: 55.2 us
  waiting for transfers between devices  26.4 us (48%)
  starting transfers between devices  15.7 us (28%)
  Pallas kernels  11.2 us (20%)
  local copies, waits for them, and re-layouts  0.95 us (2%)
  other arithmetic  0.76 us (1%)
    pallas_call x11, Pallas kernels, call(): pl.pallas_call(kernel, out_shape=out, compiler_params=pltpu.CompilerParam...  11.2 us
    ppermute x10, waiting for transfers between devices, swap(): lax.ppermute(x, axis, [(i, i ^ mask) for i in range(lax.axis_size(axis))])  9.57 us
    ppermute x2, waiting for transfers between devices, per_device(): came = lax.ppermute(sent, 'pair', sends)  9.19 us
    ppermute x2, waiting for transfers between devices, per_device(): came = [lax.ppermute(x, 'pair', s) for x, s in zip((sent, kept), sends)]  7.68 us
    ppermute x10, starting transfers between devices, swap(): lax.ppermute(x, axis, [(i, i ^ mask) for i in range(lax.axis_size(axis))])  7.39 us
    ppermute x2, starting transfers between devices, per_device(): came = lax.ppermute(sent, 'pair', sends)  4.86 us
    ppermute x2, starting transfers between devices, per_device(): came = [lax.ppermute(x, 'pair', s) for x, s in zip((sent, kept), sends)]  3.44 us
  transfers between devices with their start and end apart: 14, of which 14 were waited for; matrix products, arithmetic and copies ran while one was open for 0% of the time, Pallas kernels for 5%

profile of v10, /device:TPU:0, one launch (start us, length us, event | category | flops | bytes accessed | tf_op | source)
XLA Modules:
  0.0 55.2 jit_solution(7026863180069049263)
XLA Ops:
  0.0 0.9 %copy-done = f32[256,256]{1,0:T(8,128)S(1)} copy-done((f32[256,256]{1,0:T(8,128)S(1)}, f32[256,256]{1,0:T(8,128)}, u32[]{:S(2)}) %copy-start) | copy-done | bytes 262168
  1.4 4.1 %collective-permute-start = (f32[320,128]{1,0:T(8,128)S(1)}, f32[320,128]{1,0:T(8,128)S(1)}, u32[]{:S(2)}, u32[]{:S(2)}) collective-permute-start(f32[320,128]{1,0:T(8,128)S(1)} %get-tuple-element.30), channel_id=1, source_target_pairs={{1,0},{0,2},{3,1},{2,3},{5,4},{4,6},{7,5},{6,7},{9,8},{8,10},{11,9... | collective-permute-start | bytes 491528 | tf_op jit(solution)/shard_map/ppermute | solution.py:749
  5.4 3.5 %collective-permute-done.payload_ref = f32[320,128]{1,0:T(8,128)S(1)} collective-permute-done((f32[320,128]{1,0:T(8,128)S(1)}, f32[320,128]{1,0:T(8,128)S(1)}, u32[]{:S(2)}, u32[]{:S(2)}) %collective-permute-start) | collective-permute-done | bytes 163872 | tf_op jit(solution)/shard_map/ppermute | solution.py:749
  8.9 1.2 %shard_map.18 = (f32[256,128]{1,0:T(8,128)S(1)}, f32[256,128]{1,0:T(8,128)S(1)}, f32[256,128]{1,0:T(8,128)S(1)}, f32[256,128]{1,0:T(8,128)S(1)}, f32[16,128]{1,0:T(8,128)S(1)}, /*index=5*/f32[112,128]{1,0:T(8,128)S(1)}) custom-call(f32[256,128]{1,0:T(8,128)S(1)} %get-tuple-element.28.even_ref, f32[256,128]{1,0:T(8,128)S(1)} %get-tuple-element.29.odd_ref, ...), custom_call_target="tpu_custom_call" | custom-call | tf_op jit(solution)/shard_map/pallas_call | solution.py:713
  10.2 0.7 %shard_map.19 = f32[112,128]{1,0:T(8,128)S(1)} custom-call(f32[256,128]{1,0:T(8,128)S(1)} %get-tuple-element.31.even_ref, f32[256,128]{1,0:T(8,128)S(1)} %get-tuple-element.32.odd_ref, f32[16,128]{1,0:T(8,128)S(1)} %get-tuple-element.33.corner_ref), custom_call_target="tpu_custom_call" | custom-call | tf_op jit(solution)/shard_map/pallas_call | solution.py:713
  11.4 1.6 %collective-permute-start.2 = (f32[112,128]{1,0:T(8,128)S(1)}, f32[112,128]{1,0:T(8,128)S(1)}, u32[]{:S(2)}, u32[]{:S(2)}) collective-permute-start(f32[112,128]{1,0:T(8,128)S(1)} %add.6.refs_0_), channel_id=1, source_target_pairs={{0,8},{4,12},{8,0},{12,4},{16,24},{20,28},{24,16},{28,20},{1,9},{5... | collective-permute-start | bytes 172040 | tf_op jit(solution)/shard_map/ppermute | solution.py:696
  13.0 1.5 %collective-permute-start.3 = (f32[112,128]{1,0:T(8,128)S(1)}, f32[112,128]{1,0:T(8,128)S(1)}, u32[]{:S(2)}, u32[]{:S(2)}) collective-permute-start(f32[112,128]{1,0:T(8,128)S(1)} %add.6.refs_0_), channel_id=1, source_target_pairs={{0,16},{4,20},{8,24},{12,28},{16,0},{20,4},{24,8},{28,12},{1,17},{... | collective-permute-start | bytes 172040 | tf_op jit(solution)/shard_map/ppermute | solution.py:696
  15.0 0.7 %collective-permute-done.2.refs_1_ = f32[112,128]{1,0:T(8,128)S(1)} collective-permute-done((f32[112,128]{1,0:T(8,128)S(1)}, f32[112,128]{1,0:T(8,128)S(1)}, u32[]{:S(2)}, u32[]{:S(2)}) %collective-permute-start.2) | collective-permute-done | bytes 57376 | tf_op jit(solution)/shard_map/ppermute | solution.py:696
  15.7 1.5 %collective-permute-done.3.refs_2_ = f32[112,128]{1,0:T(8,128)S(1)} collective-permute-done((f32[112,128]{1,0:T(8,128)S(1)}, f32[112,128]{1,0:T(8,128)S(1)}, u32[]{:S(2)}, u32[]{:S(2)}) %collective-permute-start.3) | collective-permute-done | bytes 57376 | tf_op jit(solution)/shard_map/ppermute | solution.py:696
  17.2 2.4 %collective-permute-done.4.refs_3_ = f32[112,128]{1,0:T(8,128)S(1)} collective-permute-done((f32[112,128]{1,0:T(8,128)S(1)}, f32[112,128]{1,0:T(8,128)S(1)}, u32[]{:S(2)}, u32[]{:S(2)}) %collective-permute-start.4) | collective-permute-done | bytes 57376 | tf_op jit(solution)/shard_map/ppermute | solution.py:696
  19.6 1.2 %shard_map.20.found_ref.refs_4_ = f32[160,128]{1,0:T(8,128)S(1)} custom-call(f32[112,128]{1,0:T(8,128)S(1)} %add.6.refs_0_, f32[112,128]{1,0:T(8,128)S(1)} %collective-permute-done.2.refs_1_, f32[112,128]{1,0:T(8,128)S(1)} %collective-permute-done.3.refs_2_, f32[112,128]{1,0:T(8,128)S(1)} %collective-permute-done.4.refs_3_), custom_call_target="tpu_custom_call" | custom-call | tf_op jit(solution)/shard_map/pallas_call | solution.py:713
  20.9 0.7 %shard_map.21 = (f32[256,128]{1,0:T(8,128)S(1)}, f32[256,128]{1,0:T(8,128)S(1)}) custom-call(f32[256,128]{1,0:T(8,128)S(1)} %get-tuple-element.31.even_ref, f32[256,128]{1,0:T(8,128)S(1)} %get-tuple-element.32.odd_ref, f32[160,128]{1,0:T(8,128)S(1)} %shard_map.20.found_ref.refs_4_), custom_call_target="tpu_custom_call" | custom-call | tf_op jit(solution)/shard_map/pallas_call | solution.py:713
  21.6 0.6 %collective-permute-done.5.refs_5_ = f32[160,128]{1,0:T(8,128)S(1)} collective-permute-done((f32[160,128]{1,0:T(8,128)S(1)}, f32[160,128]{1,0:T(8,128)S(1)}, u32[]{:S(2)}, u32[]{:S(2)}) %collective-permute-start.5) | collective-permute-done | bytes 81952 | tf_op jit(solution)/shard_map/ppermute | solution.py:696
  22.2 1.6 %shard_map.22 = (f32[256,128]{1,0:T(8,128)S(1)}, f32[256,128]{1,0:T(8,128)S(1)}) custom-call(f32[256,128]{1,0:T(8,128)S(1)} %get-tuple-element.35.refs_0_, f32[256,128]{1,0:T(8,128)S(1)} %get-tuple-element.36.refs_1_, f32[256,128]{1,0:T(8,128)S(1)} %get-tuple-element.37.refs_2_, f32[256,128]{1,0:T(8,128)S(1)} %get-tuple-element.38.refs_3_, ...), custom_call_target="tpu_custom_call" | custom-call | tf_op jit(solution)/shard_map/pallas_call | solution.py:713
  23.8 3.4 %collective-permute-start.6 = (f32[256,128]{1,0:T(8,128)S(1)}, f32[256,128]{1,0:T(8,128)S(1)}, u32[]{:S(2)}, u32[]{:S(2)}) collective-permute-start(f32[256,128]{1,0:T(8,128)S(1)} %get-tuple-element.40.sent_ref), channel_id=1, source_target_pairs={{1,0},{0,2},{3,1},{2,3},{5,4},{4,6},{7,5},{6,7},{9,8},{8,10},{11,9... | collective-permute-start | bytes 393224 | tf_op jit(solution)/shard_map/ppermute | solution.py:755
  27.2 3.9 %collective-permute-done.6.came0_ref = f32[256,128]{1,0:T(8,128)S(1)} collective-permute-done((f32[256,128]{1,0:T(8,128)S(1)}, f32[256,128]{1,0:T(8,128)S(1)}, u32[]{:S(2)}, u32[]{:S(2)}) %collective-permute-start.6) | collective-permute-done | bytes 131104 | tf_op jit(solution)/shard_map/ppermute | solution.py:755
  31.1 3.8 %collective-permute-done.7.came1_ref = f32[256,128]{1,0:T(8,128)S(1)} collective-permute-done((f32[256,128]{1,0:T(8,128)S(1)}, f32[256,128]{1,0:T(8,128)S(1)}, u32[]{:S(2)}, u32[]{:S(2)}) %collective-permute-start.7) | collective-permute-done | bytes 131104 | tf_op jit(solution)/shard_map/ppermute | solution.py:755
  34.9 1.1 %shard_map.23 = (f32[256,128]{1,0:T(8,128)S(1)}, f32[256,128]{1,0:T(8,128)S(1)}, f32[256,128]{1,0:T(8,128)S(1)}, f32[256,128]{1,0:T(8,128)S(1)}, f32[16,128]{1,0:T(8,128)S(1)}, /*index=5*/f32[112,128]{1,0:T(8,128)S(1)}) custom-call(f32[256,128]{1,0:T(8,128)S(1)} %get-tuple-element.39.kept_ref, f32[256,128]{1,0:T(8,128)S(1)} %get-tuple-element.40.sent_ref, ...), custom_call_target="tpu_custom_call" | custom-call | tf_op jit(solution)/shard_map/pallas_call | solution.py:713
  36.1 0.7 %shard_map.24 = f32[112,128]{1,0:T(8,128)S(1)} custom-call(f32[256,128]{1,0:T(8,128)S(1)} %get-tuple-element.41.even_ref, f32[256,128]{1,0:T(8,128)S(1)} %get-tuple-element.42.odd_ref, f32[16,128]{1,0:T(8,128)S(1)} %get-tuple-element.43.corner_ref), custom_call_target="tpu_custom_call" | custom-call | tf_op jit(solution)/shard_map/pallas_call | solution.py:713
  37.3 0.6 %collective-permute-start.10 = (f32[112,128]{1,0:T(8,128)S(1)}, f32[112,128]{1,0:T(8,128)S(1)}, u32[]{:S(2)}, u32[]{:S(2)}) collective-permute-start(f32[112,128]{1,0:T(8,128)S(1)} %add.7.refs_0_), channel_id=1, source_target_pairs={{0,16},{4,20},{8,24},{12,28},{16,0},{20,4},{24,8},{28,12},{1,17},{... | collective-permute-start | bytes 172040 | tf_op jit(solution)/shard_map/ppermute | solution.py:696
  37.9 1.5 %collective-permute-start.11 = (f32[112,128]{1,0:T(8,128)S(1)}, f32[112,128]{1,0:T(8,128)S(1)}, u32[]{:S(2)}, u32[]{:S(2)}) collective-permute-start(f32[112,128]{1,0:T(8,128)S(1)} %add.7.refs_0_), channel_id=1, source_target_pairs={{0,24},{4,28},{8,16},{12,20},{16,8},{20,12},{24,0},{28,4},{1,25},{... | collective-permute-start | bytes 172040 | tf_op jit(solution)/shard_map/ppermute | solution.py:696
  39.4 1.5 %collective-permute-start.9 = (f32[112,128]{1,0:T(8,128)S(1)}, f32[112,128]{1,0:T(8,128)S(1)}, u32[]{:S(2)}, u32[]{:S(2)}) collective-permute-start(f32[112,128]{1,0:T(8,128)S(1)} %add.7.refs_0_), channel_id=1, source_target_pairs={{0,8},{4,12},{8,0},{12,4},{16,24},{20,28},{24,16},{28,20},{1,9},{5... | collective-permute-start | bytes 172040 | tf_op jit(solution)/shard_map/ppermute | solution.py:696
  40.9 1.3 %collective-permute-done.10.refs_2_ = f32[112,128]{1,0:T(8,128)S(1)} collective-permute-done((f32[112,128]{1,0:T(8,128)S(1)}, f32[112,128]{1,0:T(8,128)S(1)}, u32[]{:S(2)}, u32[]{:S(2)}) %collective-permute-start.10) | collective-permute-done | bytes 57376 | tf_op jit(solution)/shard_map/ppermute | solution.py:696
  42.2 0.9 %collective-permute-done.11.refs_3_ = f32[112,128]{1,0:T(8,128)S(1)} collective-permute-done((f32[112,128]{1,0:T(8,128)S(1)}, f32[112,128]{1,0:T(8,128)S(1)}, u32[]{:S(2)}, u32[]{:S(2)}) %collective-permute-start.11) | collective-permute-done | bytes 57376 | tf_op jit(solution)/shard_map/ppermute | solution.py:696
  43.1 0.7 %collective-permute-done.9.refs_1_ = f32[112,128]{1,0:T(8,128)S(1)} collective-permute-done((f32[112,128]{1,0:T(8,128)S(1)}, f32[112,128]{1,0:T(8,128)S(1)}, u32[]{:S(2)}, u32[]{:S(2)}) %collective-permute-start.9) | collective-permute-done | bytes 57376 | tf_op jit(solution)/shard_map/ppermute | solution.py:696
  43.8 1.2 %shard_map.25.found_ref.refs_4_ = f32[160,128]{1,0:T(8,128)S(1)} custom-call(f32[112,128]{1,0:T(8,128)S(1)} %add.7.refs_0_, f32[112,128]{1,0:T(8,128)S(1)} %collective-permute-done.9.refs_1_, f32[112,128]{1,0:T(8,128)S(1)} %collective-permute-done.10.refs_2_, f32[112,128]{1,0:T(8,128)S(1)} %collective-permute-done.11.refs_3_), custom_call_target="tpu_custom_call" | custom-call | tf_op jit(solution)/shard_map/pallas_call | solution.py:713
  45.1 0.7 %shard_map.26 = (f32[256,128]{1,0:T(8,128)S(1)}, f32[256,128]{1,0:T(8,128)S(1)}) custom-call(f32[256,128]{1,0:T(8,128)S(1)} %get-tuple-element.41.even_ref, f32[256,128]{1,0:T(8,128)S(1)} %get-tuple-element.42.odd_ref, f32[160,128]{1,0:T(8,128)S(1)} %shard_map.25.found_ref.refs_4_), custom_call_target="tpu_custom_call" | custom-call | tf_op jit(solution)/shard_map/pallas_call | solution.py:713
  45.8 0.6 %collective-permute-done.12.refs_5_ = f32[160,128]{1,0:T(8,128)S(1)} collective-permute-done((f32[160,128]{1,0:T(8,128)S(1)}, f32[160,128]{1,0:T(8,128)S(1)}, u32[]{:S(2)}, u32[]{:S(2)}) %collective-permute-start.12) | collective-permute-done | bytes 81952 | tf_op jit(solution)/shard_map/ppermute | solution.py:696
  46.4 1.6 %shard_map.27 = (f32[256,128]{1,0:T(8,128)S(1)}, f32[256,128]{1,0:T(8,128)S(1)}) custom-call(f32[256,128]{1,0:T(8,128)S(1)} %get-tuple-element.45.refs_0_, f32[256,128]{1,0:T(8,128)S(1)} %get-tuple-element.46.refs_1_, f32[256,128]{1,0:T(8,128)S(1)} %get-tuple-element.47.refs_2_, f32[256,128]{1,0:T(8,128)S(1)} %get-tuple-element.48.refs_3_, ...), custom_call_target="tpu_custom_call" | custom-call | tf_op jit(solution)/shard_map/pallas_call | solution.py:713
  48.0 0.8 %collective-permute-start.13 = (f32[256,128]{1,0:T(8,128)S(1)}, f32[256,128]{1,0:T(8,128)S(1)}, u32[]{:S(2)}, u32[]{:S(2)}) collective-permute-start(f32[256,128]{1,0:T(8,128)S(1)} %get-tuple-element.49), channel_id=1, source_target_pairs={{2,0},{0,1},{3,2},{1,3},{6,4},{4,5},{7,6},{5,7},{10,8},{8,9},{11,1... | collective-permute-start | bytes 393224 | tf_op jit(solution)/shard_map/ppermute | solution.py:761
  48.7 5.7 %collective-permute-done.13 = f32[256,128]{1,0:T(8,128)S(1)} collective-permute-done((f32[256,128]{1,0:T(8,128)S(1)}, f32[256,128]{1,0:T(8,128)S(1)}, u32[]{:S(2)}, u32[]{:S(2)}) %collective-permute-start.13) | collective-permute-done | bytes 131104 | tf_op jit(solution)/shard_map/ppermute | solution.py:761
  54.5 0.7 %pad_maximum_fusion = f32[256,256]{1,0:T(8,128)} fusion(f32[256,128]{1,0:T(8,128)S(1)} %get-tuple-element.52, f32[256,128]{1,0:T(8,128)S(1)} %get-tuple-element.51), kind=kLoop, calls=%fused_computation | loop fusion | flops 65536 | bytes 524288 | tf_op jit(solution)/shard_map/concatenate | solution.py:765
  (13 shorter events, 2.2 us)
Async XLA Ops:
  0.0 0.9 %copy-start = (f32[256,256]{1,0:T(8,128)S(1)}, f32[256,256]{1,0:T(8,128)}, u32[]{:S(2)}) copy-start(f32[256,256]{1,0:T(8,128)} %basis_ref.1) | copy-start | bytes 786436
  1.4 7.5 %collective-permute-start = (f32[320,128]{1,0:T(8,128)S(1)}, f32[320,128]{1,0:T(8,128)S(1)}, u32[]{:S(2)}, u32[]{:S(2)}) collective-permute-start(f32[320,128]{1,0:T(8,128)S(1)} %get-tuple-element.30), channel_id=1, source_target_pairs={{1,0},{0,2},{3,1},{2,3},{5,4},{4,6},{7,5},{6,7},{9,8},{8,10},{11,9... | collective-permute-start | bytes 491528 | tf_op jit(solution)/shard_map/ppermute | solution.py:749
  10.1 1.3 %collective-permute-start.1 = (f32[112,128]{1,0:T(8,128)S(1)}, f32[112,128]{1,0:T(8,128)S(1)}, u32[]{:S(2)}, u32[]{:S(2)}) collective-permute-start(f32[112,128]{1,0:T(8,128)S(1)} %get-tuple-element.34), channel_id=1, source_target_pairs={{0,4},{4,0},{8,12},{12,8},{16,20},{20,16},{24,28},{28,24},{1,5},{5... | collective-permute-start | bytes 172040 | tf_op jit(solution)/shard_map/ppermute | solution.py:696
  11.4 4.2 %collective-permute-start.2 = (f32[112,128]{1,0:T(8,128)S(1)}, f32[112,128]{1,0:T(8,128)S(1)}, u32[]{:S(2)}, u32[]{:S(2)}) collective-permute-start(f32[112,128]{1,0:T(8,128)S(1)} %add.6.refs_0_), channel_id=1, source_target_pairs={{0,8},{4,12},{8,0},{12,4},{16,24},{20,28},{24,16},{28,20},{1,9},{5... | collective-permute-start | bytes 172040 | tf_op jit(solution)/shard_map/ppermute | solution.py:696
  13.0 4.2 %collective-permute-start.3 = (f32[112,128]{1,0:T(8,128)S(1)}, f32[112,128]{1,0:T(8,128)S(1)}, u32[]{:S(2)}, u32[]{:S(2)}) collective-permute-start(f32[112,128]{1,0:T(8,128)S(1)} %add.6.refs_0_), channel_id=1, source_target_pairs={{0,16},{4,20},{8,24},{12,28},{16,0},{20,4},{24,8},{28,12},{1,17},{... | collective-permute-start | bytes 172040 | tf_op jit(solution)/shard_map/ppermute | solution.py:696
  14.5 5.1 %collective-permute-start.4 = (f32[112,128]{1,0:T(8,128)S(1)}, f32[112,128]{1,0:T(8,128)S(1)}, u32[]{:S(2)}, u32[]{:S(2)}) collective-permute-start(f32[112,128]{1,0:T(8,128)S(1)} %add.6.refs_0_), channel_id=1, source_target_pairs={{0,24},{4,28},{8,16},{12,20},{16,8},{20,12},{24,0},{28,4},{1,25},{... | collective-permute-start | bytes 172040 | tf_op jit(solution)/shard_map/ppermute | solution.py:696
  20.8 1.3 %collective-permute-start.5 = (f32[160,128]{1,0:T(8,128)S(1)}, f32[160,128]{1,0:T(8,128)S(1)}, u32[]{:S(2)}, u32[]{:S(2)}) collective-permute-start(f32[160,128]{1,0:T(8,128)S(1)} %shard_map.20.found_ref.refs_4_), channel_id=1, source_target_pairs={{0,4},{4,0},{8,12},{12,8},{16,20},{20,16},{24,28},{28,24},{1,5},{5... | collective-permute-start | bytes 245768 | tf_op jit(solution)/shard_map/ppermute | solution.py:696
  23.8 7.3 %collective-permute-start.6 = (f32[256,128]{1,0:T(8,128)S(1)}, f32[256,128]{1,0:T(8,128)S(1)}, u32[]{:S(2)}, u32[]{:S(2)}) collective-permute-start(f32[256,128]{1,0:T(8,128)S(1)} %get-tuple-element.40.sent_ref), channel_id=1, source_target_pairs={{1,0},{0,2},{3,1},{2,3},{5,4},{4,6},{7,5},{6,7},{9,8},{8,10},{11,9... | collective-permute-start | bytes 393224 | tf_op jit(solution)/shard_map/ppermute | solution.py:755
  27.2 7.7 %collective-permute-start.7 = (f32[256,128]{1,0:T(8,128)S(1)}, f32[256,128]{1,0:T(8,128)S(1)}, u32[]{:S(2)}, u32[]{:S(2)}) collective-permute-start(f32[256,128]{1,0:T(8,128)S(1)} %get-tuple-element.39.kept_ref), channel_id=1, source_target_pairs={{2,0},{3,2},{0,1},{1,3},{6,4},{7,6},{4,5},{5,7},{10,8},{11,10},{8,... | collective-permute-start | bytes 393224 | tf_op jit(solution)/shard_map/ppermute | solution.py:755
  36.0 1.3 %collective-permute-start.8 = (f32[112,128]{1,0:T(8,128)S(1)}, f32[112,128]{1,0:T(8,128)S(1)}, u32[]{:S(2)}, u32[]{:S(2)}) collective-permute-start(f32[112,128]{1,0:T(8,128)S(1)} %get-tuple-element.44), channel_id=1, source_target_pairs={{0,4},{4,0},{8,12},{12,8},{16,20},{20,16},{24,28},{28,24},{1,5},{5... | collective-permute-start | bytes 172040 | tf_op jit(solution)/shard_map/ppermute | solution.py:696
  37.3 4.9 %collective-permute-start.10 = (f32[112,128]{1,0:T(8,128)S(1)}, f32[112,128]{1,0:T(8,128)S(1)}, u32[]{:S(2)}, u32[]{:S(2)}) collective-permute-start(f32[112,128]{1,0:T(8,128)S(1)} %add.7.refs_0_), channel_id=1, source_target_pairs={{0,16},{4,20},{8,24},{12,28},{16,0},{20,4},{24,8},{28,12},{1,17},{... | collective-permute-start | bytes 172040 | tf_op jit(solution)/shard_map/ppermute | solution.py:696
  37.9 5.2 %collective-permute-start.11 = (f32[112,128]{1,0:T(8,128)S(1)}, f32[112,128]{1,0:T(8,128)S(1)}, u32[]{:S(2)}, u32[]{:S(2)}) collective-permute-start(f32[112,128]{1,0:T(8,128)S(1)} %add.7.refs_0_), channel_id=1, source_target_pairs={{0,24},{4,28},{8,16},{12,20},{16,8},{20,12},{24,0},{28,4},{1,25},{... | collective-permute-start | bytes 172040 | tf_op jit(solution)/shard_map/ppermute | solution.py:696
  39.4 4.4 %collective-permute-start.9 = (f32[112,128]{1,0:T(8,128)S(1)}, f32[112,128]{1,0:T(8,128)S(1)}, u32[]{:S(2)}, u32[]{:S(2)}) collective-permute-start(f32[112,128]{1,0:T(8,128)S(1)} %add.7.refs_0_), channel_id=1, source_target_pairs={{0,8},{4,12},{8,0},{12,4},{16,24},{20,28},{24,16},{28,20},{1,9},{5... | collective-permute-start | bytes 172040 | tf_op jit(solution)/shard_map/ppermute | solution.py:696
  45.0 1.3 %collective-permute-start.12 = (f32[160,128]{1,0:T(8,128)S(1)}, f32[160,128]{1,0:T(8,128)S(1)}, u32[]{:S(2)}, u32[]{:S(2)}) collective-permute-start(f32[160,128]{1,0:T(8,128)S(1)} %shard_map.25.found_ref.refs_4_), channel_id=1, source_target_pairs={{0,4},{4,0},{8,12},{12,8},{16,20},{20,16},{24,28},{28,24},{1,5},{5... | collective-permute-start | bytes 245768 | tf_op jit(solution)/shard_map/ppermute | solution.py:696
  48.0 6.5 %collective-permute-start.13 = (f32[256,128]{1,0:T(8,128)S(1)}, f32[256,128]{1,0:T(8,128)S(1)}, u32[]{:S(2)}, u32[]{:S(2)}) collective-permute-start(f32[256,128]{1,0:T(8,128)S(1)} %get-tuple-element.49), channel_id=1, source_target_pairs={{2,0},{0,1},{3,2},{1,3},{6,4},{4,5},{7,6},{5,7},{10,8},{8,9},{11,1... | collective-permute-start | bytes 393224 | tf_op jit(solution)/shard_map/ppermute | solution.py:761

commit v11 on v8

--- a/solution.py
+++ b/solution.py
@@ -16,6 +16,7 @@
 WINDOW = 32
 NEAR = 16
 STRIP = 16
+BACK = 3
 
 
 def tournament_order(pair_count):
@@ -344,31 +345,41 @@
     return ee_new, eo_new, oe_new, oo_new
 
 
-def move_bands_back(ee, eo, oe, oo):
-    lane = lanes_of(ee)
+def move_bands_back(views, by):
+    ee, eo, oe, oo = views[by]
+    ee_left, _, oe_left, _ = views[by - 1]
+    _, eo_right, _, oo_right = views[by + 1]
+    width = ee.shape[1]
+    lane = lanes_of(ee) - by
+    lane = jnp.where(lane < 0, lane + width, jnp.where(lane >= width, lane - width, lane))
     diag = lax.broadcasted_iota(jnp.int32, ee.shape, 0)
-    last, first = lane == ee.shape[1] - 1, lane == diag
+    last, first = lane == width - 1, lane == diag
     on, next_on = diag == 0, diag == 1
-    ahead, behind = lane == diag + 1, lane == diag - 1
-    eo_down, oo_up = down(eo, 1), down(oo, -1)
-    eo_twice = down(eo, 2)
-
-    ee_left = left(jnp.where(ahead, down(ee, -1), ee), 1)
-    ee_old = jnp.where(jnp.logical_and(first, on), ee, ee_left)
-    ee_old = jnp.where(last, jnp.where(on, oo, eo_down), ee_old)
-
-    oe_left = left(jnp.where(jnp.logical_and(ahead, diag > 0), ee, down(oe, -2)), 1)
-    eo_far = right(jnp.where(behind, eo_down, eo_twice), 1)
-    eo_old = jnp.where(on, jnp.where(last, oo_up, oe_left), eo_far)
+    oo_up, eo_twice = down(oo, -1), down(eo_right, 2)
+
+    far = jnp.where(first, down(ee_left, -1), ee_left)
+    ee_old = jnp.where(jnp.logical_and(first, on), ee, far)
+    ee_old = jnp.where(last, jnp.where(on, oo, down(eo, 1)), ee_old)
+
+    near = jnp.where(jnp.logical_and(first, diag > 0), ee_left, down(oe_left, -2))
+    eo_old = jnp.where(first, down(eo_right, 1), eo_twice)
+    eo_old = jnp.where(on, jnp.where(last, oo_up, near), eo_old)
     eo_old = jnp.where(jnp.logical_and(next_on, lane > 1), oe, eo_old)
-    eo_old = jnp.where(jnp.logical_and(on, first), ee_left, eo_old)
-
-    oe_old = jnp.where(on, eo_old, jnp.where(last, oo_up, oe_left))
-
-    oo_old = right(jnp.where(behind, eo_twice, oo), 1)
+    eo_old = jnp.where(jnp.logical_and(on, first), far, eo_old)
+
+    oe_old = jnp.where(on, eo_old, jnp.where(last, oo_up, near))
+
+    oo_old = jnp.where(first, eo_twice, oo_right)
     oo_old = jnp.where(jnp.logical_and(next_on, first), oe, oo_old)
-    oo_old = jnp.where(jnp.logical_and(on, first), left(ee, 1), oo_old)
+    oo_old = jnp.where(jnp.logical_and(on, first), ee_left, oo_old)
     return ee_old, eo_old, oe_old, oo_old
+
+
+def bands_back(bands, count):
+    views = {by: [right(x, by) for x in bands] for by in range(-count, count + 1)}
+    for reach in reversed(range(count)):
+        views = {by: move_bands_back(views, by) for by in range(-reach, reach + 1)}
+    return views[0]
 
 
 def move_columns(even, odd):
@@ -441,8 +452,11 @@
         bands = turn_bands(*trim(bands, 3 * ahead - 2 * step), cosine, sine)
         if step < JSTEPS - 1:
             bands = move_bands(*bands)
-    for step in range(JSTEPS - 1):
-        bands = move_bands_back(*trim(bands, 2 * (ahead - step)))
+    done = 0
+    while done < JSTEPS - 1:
+        count = min(BACK, JSTEPS - 1 - done)
+        bands = bands_back(trim(bands, 2 * (ahead - done)), count)
+        done += count
     return bands
 
 
@@ -556,46 +570,38 @@
 PACKED = DIAGS + (FAR_DIAGS - DIAGS) // 2
 
 
-def store_part(even, odd, corner, flag, part_ref):
+def store_part(even, odd, flag, part_ref):
     bands = pack_far(dense_bands(even, odd, FAR_DIAGS), flag)
     for q, band in enumerate(bands):
         part_ref[q * PACKED : (q + 1) * PACKED, :] = band
-    part_ref[4 * PACKED :, :] = corner
-
-
-def open_pairs(is_second, x, y, column_refs, corner_ref, other_ref):
-    x_second, y_second = among(is_second[0]), among(is_second[1])
-    corner = cross_partial(*x, *y, x_second, y_second)
+
+
+def open_pairs(is_second, x, y, column_refs, other_ref):
     flag = on_odd_core()
     mine = [jnp.where(flag, b, a) for a, b in zip(x, y)]
     theirs = [jnp.where(flag, a, b) for a, b in zip(x, y)]
     for ref, value in zip(column_refs, mine + theirs):
         ref[...] = value
-    corner_ref[...] = jnp.where(flag, corner[NEAR:], corner[:NEAR])
-    store_part(
-        *theirs,
-        jnp.where(flag, corner[:NEAR], corner[NEAR:]),
-        either(flag, x_second, y_second),
-        other_ref,
-    )
+    store_part(*theirs, either(flag, among(is_second[0]), among(is_second[1])), other_ref)
+    other_ref[4 * PACKED :, :] = jnp.zeros((WINDOW, theirs[0].shape[1]), jnp.float32)
 
 
 def first_open(own_second, gets_second, is_second, even_ref, odd_ref, payload_ref, *refs):
-    *column_refs, corner_ref, other_ref = refs
+    *column_refs, other_ref = refs
     own = even_ref[...], odd_ref[...]
     came = unpacked(payload_ref[...], own[0].shape[0], among(gets_second))
     flag = among(own_second)
     x = [jnp.where(flag, b, a) for a, b in zip(own, came)]
     y = [jnp.where(flag, a, b) for a, b in zip(own, came)]
-    open_pairs(is_second, x, y, column_refs, corner_ref, other_ref)
+    open_pairs(is_second, x, y, column_refs, other_ref)
 
 
 def fused_open(picks, is_second, kept_ref, sent_ref, came0_ref, came1_ref, *refs):
-    *column_refs, corner_ref, other_ref = refs
+    *column_refs, other_ref = refs
     arrays = [ref[...] for ref in (sent_ref, kept_ref, came0_ref, came1_ref)]
     blocks = [choose(pick, arrays) for pick in picks]
     x, y = split_pair(*blocks[:2]), split_pair(*blocks[2:])
-    open_pairs(is_second, x, y, column_refs, corner_ref, other_ref)
+    open_pairs(is_second, x, y, column_refs, other_ref)
 
 
 def swapped_flag(is_second):
@@ -607,9 +613,15 @@
     return either(on_odd_core(), among(is_second[1]), among(is_second[0]))
 
 
-def bands_kernel(is_second, even_ref, odd_ref, corner_ref, part_ref):
-    flag = own_second_flag(is_second)
-    store_part(even_ref[...], odd_ref[...], corner_ref[...], flag, part_ref)
+def bands_kernel(is_second, *refs):
+    *column_refs, part_ref = refs
+    columns = [ref[...] for ref in column_refs]
+    store_part(*columns[:2], own_second_flag(is_second), part_ref)
+    flag = on_odd_core()
+    x = [jnp.where(flag, b, a) for a, b in zip(columns[:2], columns[2:])]
+    y = [jnp.where(flag, a, b) for a, b in zip(columns[:2], columns[2:])]
+    corner = cross_partial(*x, *y, among(is_second[0]), among(is_second[1]))
+    part_ref[4 * PACKED :, :] = corner
 
 
 def angles_kernel(is_second, *refs):
@@ -632,7 +644,7 @@
 
 
 CORNER = NEAR + 4 * DIAGS
-ROTATION = CORNER + NEAR
+ROTATION = CORNER + WINDOW
 FOUND = ROTATION + 2 * WINDOW
 
 
@@ -649,7 +661,7 @@
 
 
 def next_bands(x_found, y_found, x_second, y_second):
-    corner = jnp.concatenate((x_found[CORNER:ROTATION], y_found[CORNER:ROTATION]), axis=0)
+    corner = x_found[CORNER:ROTATION] + y_found[CORNER:ROTATION]
     middle = cross_bands(corner, x_found[ROTATION:], y_found[ROTATION:])
     half = corner.shape[1] // 2
     lane = lanes_of(middle[0])
@@ -718,11 +730,11 @@
 
 
 def two_rounds(opened, is_second, sends_first, layout_of):
-    *columns, corner, other = opened
+    *columns, other = opened
     column, width = columns[0].shape, columns[0].shape[1]
     other = swap(other, "row", 1)
     bands = functools.partial(bands_kernel, is_second)
-    (mine,) = call(bands, (other.shape,), *columns[:2], corner)
+    (mine,) = call(bands, (other.shape,), *columns)
     (found,) = call(
         functools.partial(angles_kernel, is_second),
         ((FOUND, width),),
@@ -740,7 +752,7 @@
     width = cols // 2
     pair_total = lax.axis_size("pair")
     column = (rows, width)
-    opened = (column,) * 4 + ((NEAR, width), (4 * PACKED + NEAR, width))
+    opened = (column,) * 4 + ((4 * PACKED + WINDOW, width),)
     payload = (rows + rows * 2 * STRIP // width, width)
 
     sends, sends_second, gets_second, own_second, is_second = first_moves(pair_total)

time: 54.3 us -> 53.9 us (level)
  transfers between devices with their start and end apart: 14 -> 14, of which waited for: 14 -> 14; matrix products, arithmetic and copies ran while one was open for 0% -> 0% of each run, Pallas kernels for 5% -> 6%
where the time goes in v11:
time: 53.9 us; the launch traced here: 53.7 us
  waiting for transfers between devices  24.4 us (45%)
  starting transfers between devices  16.8 us (31%)
  Pallas kernels  10.7 us (20%)
  local copies, waits for them, and re-layouts  0.95 us (2%)
  other arithmetic  0.76 us (1%)
    pallas_call x11, Pallas kernels, call(): pl.pallas_call(kernel, out_shape=out, compiler_params=pltpu.CompilerParam...  10.7 us
    ppermute x10, waiting for transfers between devices, swap(): lax.ppermute(x, axis, [(i, i ^ mask) for i in range(lax.axis_size(axis))])  9.69 us
    ppermute x2, waiting for transfers between devices, per_device(): came = lax.ppermute(sent, 'pair', sends)  8.18 us
    ppermute x10, starting transfers between devices, swap(): lax.ppermute(x, axis, [(i, i ^ mask) for i in range(lax.axis_size(axis))])  7.4 us
    ppermute x2, waiting for transfers between devices, per_device(): came = [lax.ppermute(x, 'pair', s) for x, s in zip((sent, kept), sends)]  6.56 us
    ppermute x2, starting transfers between devices, per_device(): came = lax.ppermute(sent, 'pair', sends)  5.88 us
    ppermute x2, starting transfers between devices, per_device(): came = [lax.ppermute(x, 'pair', s) for x, s in zip((sent, kept), sends)]  3.5 us
  transfers between devices with their start and end apart: 14, of which 14 were waited for; matrix products, arithmetic and copies ran while one was open for 0% of the time, Pallas kernels for 6%

profile of v11, /device:TPU:0, one launch (start us, length us, event | category | flops | bytes accessed | tf_op | source)
XLA Modules:
  0.0 53.7 jit_solution(22033866519062715)
XLA Ops:
  0.0 0.9 %copy-done = f32[256,256]{1,0:T(8,128)S(1)} copy-done((f32[256,256]{1,0:T(8,128)S(1)}, f32[256,256]{1,0:T(8,128)}, u32[]{:S(2)}) %copy-start) | copy-done | bytes 262168
  1.4 4.1 %collective-permute-start = (f32[320,128]{1,0:T(8,128)S(1)}, f32[320,128]{1,0:T(8,128)S(1)}, u32[]{:S(2)}, u32[]{:S(2)}) collective-permute-start(f32[320,128]{1,0:T(8,128)S(1)} %get-tuple-element.28), channel_id=1, source_target_pairs={{1,0},{0,2},{3,1},{2,3},{5,4},{4,6},{7,5},{6,7},{9,8},{8,10},{11,9... | collective-permute-start | bytes 491528 | tf_op jit(solution)/shard_map/ppermute | solution.py:761
  5.4 3.5 %collective-permute-done.payload_ref = f32[320,128]{1,0:T(8,128)S(1)} collective-permute-done((f32[320,128]{1,0:T(8,128)S(1)}, f32[320,128]{1,0:T(8,128)S(1)}, u32[]{:S(2)}, u32[]{:S(2)}) %collective-permute-start) | collective-permute-done | bytes 163872 | tf_op jit(solution)/shard_map/ppermute | solution.py:761
  8.9 0.9 %shard_map.18 = (f32[256,128]{1,0:T(8,128)S(1)}, f32[256,128]{1,0:T(8,128)S(1)}, f32[256,128]{1,0:T(8,128)S(1)}, f32[256,128]{1,0:T(8,128)S(1)}, f32[128,128]{1,0:T(8,128)S(1)}) custom-call(f32[256,128]{1,0:T(8,128)S(1)} %get-tuple-element.26.even_ref, f32[256,128]{1,0:T(8,128)S(1)} %get-tuple-element.27.odd_ref, f32[320,128]{1,0:T(8,128)S(1)} %collective-permute-done.payload_ref), custom_call_target="tpu_custom_call" | custom-call | tf_op jit(solution)/shard_map/pallas_call | solution.py:725
  9.9 1.0 %shard_map.19 = f32[128,128]{1,0:T(8,128)S(1)} custom-call(f32[256,128]{1,0:T(8,128)S(1)} %get-tuple-element.29.refs_0_.even_ref, f32[256,128]{1,0:T(8,128)S(1)} %get-tuple-element.30.refs_1_.odd_ref, f32[256,128]{1,0:T(8,128)S(1)} %get-tuple-element.31.refs_2_, f32[256,128]{1,0:T(8,128)S(1)} %get-tuple-element.32.refs_3_), custom_call_target="tpu_custom_call" | custom-call | tf_op jit(solution)/shard_map/pallas_call | solution.py:725
  11.2 1.6 %collective-permute-start.2 = (f32[128,128]{1,0:T(8,128)S(1)}, f32[128,128]{1,0:T(8,128)S(1)}, u32[]{:S(2)}, u32[]{:S(2)}) collective-permute-start(f32[128,128]{1,0:T(8,128)S(1)} %add.6.refs_0_), channel_id=1, source_target_pairs={{0,8},{4,12},{8,0},{12,4},{16,24},{20,28},{24,16},{28,20},{1,9},{5... | collective-permute-start | bytes 196616 | tf_op jit(solution)/shard_map/ppermute | solution.py:708
  12.7 1.5 %collective-permute-start.3 = (f32[128,128]{1,0:T(8,128)S(1)}, f32[128,128]{1,0:T(8,128)S(1)}, u32[]{:S(2)}, u32[]{:S(2)}) collective-permute-start(f32[128,128]{1,0:T(8,128)S(1)} %add.6.refs_0_), channel_id=1, source_target_pairs={{0,16},{4,20},{8,24},{12,28},{16,0},{20,4},{24,8},{28,12},{1,17},{... | collective-permute-start | bytes 196616 | tf_op jit(solution)/shard_map/ppermute | solution.py:708
  14.7 0.8 %collective-permute-done.2.refs_1_ = f32[128,128]{1,0:T(8,128)S(1)} collective-permute-done((f32[128,128]{1,0:T(8,128)S(1)}, f32[128,128]{1,0:T(8,128)S(1)}, u32[]{:S(2)}, u32[]{:S(2)}) %collective-permute-start.2) | collective-permute-done | bytes 65568 | tf_op jit(solution)/shard_map/ppermute | solution.py:708
  15.5 1.5 %collective-permute-done.3.refs_2_ = f32[128,128]{1,0:T(8,128)S(1)} collective-permute-done((f32[128,128]{1,0:T(8,128)S(1)}, f32[128,128]{1,0:T(8,128)S(1)}, u32[]{:S(2)}, u32[]{:S(2)}) %collective-permute-start.3) | collective-permute-done | bytes 65568 | tf_op jit(solution)/shard_map/ppermute | solution.py:708
  17.0 2.4 %collective-permute-done.4.refs_3_ = f32[128,128]{1,0:T(8,128)S(1)} collective-permute-done((f32[128,128]{1,0:T(8,128)S(1)}, f32[128,128]{1,0:T(8,128)S(1)}, u32[]{:S(2)}, u32[]{:S(2)}) %collective-permute-start.4) | collective-permute-done | bytes 65568 | tf_op jit(solution)/shard_map/ppermute | solution.py:708
  19.4 1.0 %shard_map.20.found_ref.refs_4_ = f32[176,128]{1,0:T(8,128)S(1)} custom-call(f32[128,128]{1,0:T(8,128)S(1)} %add.6.refs_0_, f32[128,128]{1,0:T(8,128)S(1)} %collective-permute-done.2.refs_1_, f32[128,128]{1,0:T(8,128)S(1)} %collective-permute-done.3.refs_2_, f32[128,128]{1,0:T(8,128)S(1)} %collective-permute-done.4.refs_3_), custom_call_target="tpu_custom_call" | custom-call | tf_op jit(solution)/shard_map/pallas_call | solution.py:725
  20.5 0.7 %shard_map.21 = (f32[256,128]{1,0:T(8,128)S(1)}, f32[256,128]{1,0:T(8,128)S(1)}) custom-call(f32[256,128]{1,0:T(8,128)S(1)} %get-tuple-element.29.refs_0_.even_ref, f32[256,128]{1,0:T(8,128)S(1)} %get-tuple-element.30.refs_1_.odd_ref, f32[176,128]{1,0:T(8,128)S(1)} %shard_map.20.found_ref.refs_4_), custom_call_target="tpu_custom_call" | custom-call | tf_op jit(solution)/shard_map/pallas_call | solution.py:725
  21.2 0.6 %collective-permute-done.5.refs_5_ = f32[176,128]{1,0:T(8,128)S(1)} collective-permute-done((f32[176,128]{1,0:T(8,128)S(1)}, f32[176,128]{1,0:T(8,128)S(1)}, u32[]{:S(2)}, u32[]{:S(2)}) %collective-permute-start.5) | collective-permute-done | bytes 90144 | tf_op jit(solution)/shard_map/ppermute | solution.py:708
  21.8 1.6 %shard_map.22 = (f32[256,128]{1,0:T(8,128)S(1)}, f32[256,128]{1,0:T(8,128)S(1)}) custom-call(f32[256,128]{1,0:T(8,128)S(1)} %get-tuple-element.34.refs_0_, f32[256,128]{1,0:T(8,128)S(1)} %get-tuple-element.35.refs_1_, f32[256,128]{1,0:T(8,128)S(1)} %get-tuple-element.31.refs_2_, f32[256,128]{1,0:T(8,128)S(1)} %get-tuple-element.32.refs_3_, ...), custom_call_target="tpu_custom_call" | custom-call | tf_op jit(solution)/shard_map/pallas_call | solution.py:725
  23.3 2.4 %collective-permute-start.6 = (f32[256,128]{1,0:T(8,128)S(1)}, f32[256,128]{1,0:T(8,128)S(1)}, u32[]{:S(2)}, u32[]{:S(2)}) collective-permute-start(f32[256,128]{1,0:T(8,128)S(1)} %get-tuple-element.37.sent_ref), channel_id=1, source_target_pairs={{2,0},{3,2},{0,1},{1,3},{6,4},{7,6},{4,5},{5,7},{10,8},{11,10},{8,... | collective-permute-start | bytes 393224 | tf_op jit(solution)/shard_map/ppermute | solution.py:767
  25.8 1.1 %collective-permute-start.7 = (f32[256,128]{1,0:T(8,128)S(1)}, f32[256,128]{1,0:T(8,128)S(1)}, u32[]{:S(2)}, u32[]{:S(2)}) collective-permute-start(f32[256,128]{1,0:T(8,128)S(1)} %get-tuple-element.36.kept_ref), channel_id=1, source_target_pairs={{1,0},{0,2},{3,1},{2,3},{5,4},{4,6},{7,5},{6,7},{9,8},{8,10},{11,9... | collective-permute-start | bytes 393224 | tf_op jit(solution)/shard_map/ppermute | solution.py:767
  26.8 3.9 %collective-permute-done.6.came0_ref = f32[256,128]{1,0:T(8,128)S(1)} collective-permute-done((f32[256,128]{1,0:T(8,128)S(1)}, f32[256,128]{1,0:T(8,128)S(1)}, u32[]{:S(2)}, u32[]{:S(2)}) %collective-permute-start.6) | collective-permute-done | bytes 131104 | tf_op jit(solution)/shard_map/ppermute | solution.py:767
  30.7 2.7 %collective-permute-done.7.came1_ref = f32[256,128]{1,0:T(8,128)S(1)} collective-permute-done((f32[256,128]{1,0:T(8,128)S(1)}, f32[256,128]{1,0:T(8,128)S(1)}, u32[]{:S(2)}, u32[]{:S(2)}) %collective-permute-start.7) | collective-permute-done | bytes 131104 | tf_op jit(solution)/shard_map/ppermute | solution.py:767
  33.4 0.9 %shard_map.23 = (f32[256,128]{1,0:T(8,128)S(1)}, f32[256,128]{1,0:T(8,128)S(1)}, f32[256,128]{1,0:T(8,128)S(1)}, f32[256,128]{1,0:T(8,128)S(1)}, f32[128,128]{1,0:T(8,128)S(1)}) custom-call(f32[256,128]{1,0:T(8,128)S(1)} %get-tuple-element.36.kept_ref, f32[256,128]{1,0:T(8,128)S(1)} %get-tuple-element.37.sent_ref, ...), custom_call_target="tpu_custom_call" | custom-call | tf_op jit(solution)/shard_map/pallas_call | solution.py:725
  34.4 1.0 %shard_map.24 = f32[128,128]{1,0:T(8,128)S(1)} custom-call(f32[256,128]{1,0:T(8,128)S(1)} %get-tuple-element.38.refs_0_.even_ref, f32[256,128]{1,0:T(8,128)S(1)} %get-tuple-element.39.refs_1_.odd_ref, f32[256,128]{1,0:T(8,128)S(1)} %get-tuple-element.40.refs_2_, f32[256,128]{1,0:T(8,128)S(1)} %get-tuple-element.41.refs_3_), custom_call_target="tpu_custom_call" | custom-call | tf_op jit(solution)/shard_map/pallas_call | solution.py:725
  35.6 0.6 %collective-permute-start.10 = (f32[128,128]{1,0:T(8,128)S(1)}, f32[128,128]{1,0:T(8,128)S(1)}, u32[]{:S(2)}, u32[]{:S(2)}) collective-permute-start(f32[128,128]{1,0:T(8,128)S(1)} %add.7.refs_0_), channel_id=1, source_target_pairs={{0,16},{4,20},{8,24},{12,28},{16,0},{20,4},{24,8},{28,12},{1,17},{... | collective-permute-start | bytes 196616 | tf_op jit(solution)/shard_map/ppermute | solution.py:708
  36.2 1.5 %collective-permute-start.11 = (f32[128,128]{1,0:T(8,128)S(1)}, f32[128,128]{1,0:T(8,128)S(1)}, u32[]{:S(2)}, u32[]{:S(2)}) collective-permute-start(f32[128,128]{1,0:T(8,128)S(1)} %add.7.refs_0_), channel_id=1, source_target_pairs={{0,24},{4,28},{8,16},{12,20},{16,8},{20,12},{24,0},{28,4},{1,25},{... | collective-permute-start | bytes 196616 | tf_op jit(solution)/shard_map/ppermute | solution.py:708
  37.7 1.5 %collective-permute-start.9 = (f32[128,128]{1,0:T(8,128)S(1)}, f32[128,128]{1,0:T(8,128)S(1)}, u32[]{:S(2)}, u32[]{:S(2)}) collective-permute-start(f32[128,128]{1,0:T(8,128)S(1)} %add.7.refs_0_), channel_id=1, source_target_pairs={{0,8},{4,12},{8,0},{12,4},{16,24},{20,28},{24,16},{28,20},{1,9},{5... | collective-permute-start | bytes 196616 | tf_op jit(solution)/shard_map/ppermute | solution.py:708
  39.2 1.5 %collective-permute-done.10.refs_2_ = f32[128,128]{1,0:T(8,128)S(1)} collective-permute-done((f32[128,128]{1,0:T(8,128)S(1)}, f32[128,128]{1,0:T(8,128)S(1)}, u32[]{:S(2)}, u32[]{:S(2)}) %collective-permute-start.10) | collective-permute-done | bytes 65568 | tf_op jit(solution)/shard_map/ppermute | solution.py:708
  40.7 1.1 %collective-permute-done.11.refs_3_ = f32[128,128]{1,0:T(8,128)S(1)} collective-permute-done((f32[128,128]{1,0:T(8,128)S(1)}, f32[128,128]{1,0:T(8,128)S(1)}, u32[]{:S(2)}, u32[]{:S(2)}) %collective-permute-start.11) | collective-permute-done | bytes 65568 | tf_op jit(solution)/shard_map/ppermute | solution.py:708
  41.8 0.8 %collective-permute-done.9.refs_1_ = f32[128,128]{1,0:T(8,128)S(1)} collective-permute-done((f32[128,128]{1,0:T(8,128)S(1)}, f32[128,128]{1,0:T(8,128)S(1)}, u32[]{:S(2)}, u32[]{:S(2)}) %collective-permute-start.9) | collective-permute-done | bytes 65568 | tf_op jit(solution)/shard_map/ppermute | solution.py:708
  42.5 1.0 %shard_map.25.found_ref.refs_4_ = f32[176,128]{1,0:T(8,128)S(1)} custom-call(f32[128,128]{1,0:T(8,128)S(1)} %add.7.refs_0_, f32[128,128]{1,0:T(8,128)S(1)} %collective-permute-done.9.refs_1_, f32[128,128]{1,0:T(8,128)S(1)} %collective-permute-done.10.refs_2_, f32[128,128]{1,0:T(8,128)S(1)} %collective-permute-done.11.refs_3_), custom_call_target="tpu_custom_call" | custom-call | tf_op jit(solution)/shard_map/pallas_call | solution.py:725
  43.6 0.7 %shard_map.26 = (f32[256,128]{1,0:T(8,128)S(1)}, f32[256,128]{1,0:T(8,128)S(1)}) custom-call(f32[256,128]{1,0:T(8,128)S(1)} %get-tuple-element.38.refs_0_.even_ref, f32[256,128]{1,0:T(8,128)S(1)} %get-tuple-element.39.refs_1_.odd_ref, f32[176,128]{1,0:T(8,128)S(1)} %shard_map.25.found_ref.refs_4_), custom_call_target="tpu_custom_call" | custom-call | tf_op jit(solution)/shard_map/pallas_call | solution.py:725
  44.9 1.6 %shard_map.27 = (f32[256,128]{1,0:T(8,128)S(1)}, f32[256,128]{1,0:T(8,128)S(1)}) custom-call(f32[256,128]{1,0:T(8,128)S(1)} %get-tuple-element.43.refs_0_, f32[256,128]{1,0:T(8,128)S(1)} %get-tuple-element.44.refs_1_, f32[256,128]{1,0:T(8,128)S(1)} %get-tuple-element.40.refs_2_, f32[256,128]{1,0:T(8,128)S(1)} %get-tuple-element.41.refs_3_, ...), custom_call_target="tpu_custom_call" | custom-call | tf_op jit(solution)/shard_map/pallas_call | solution.py:725
  46.5 1.8 %collective-permute-start.13 = (f32[256,128]{1,0:T(8,128)S(1)}, f32[256,128]{1,0:T(8,128)S(1)}, u32[]{:S(2)}, u32[]{:S(2)}) collective-permute-start(f32[256,128]{1,0:T(8,128)S(1)} %get-tuple-element.45), channel_id=1, source_target_pairs={{2,0},{0,1},{3,2},{1,3},{6,4},{4,5},{7,6},{5,7},{10,8},{8,9},{11,1... | collective-permute-start | bytes 393224 | tf_op jit(solution)/shard_map/ppermute | solution.py:773
  48.3 4.7 %collective-permute-done.13 = f32[256,128]{1,0:T(8,128)S(1)} collective-permute-done((f32[256,128]{1,0:T(8,128)S(1)}, f32[256,128]{1,0:T(8,128)S(1)}, u32[]{:S(2)}, u32[]{:S(2)}) %collective-permute-start.13) | collective-permute-done | bytes 131104 | tf_op jit(solution)/shard_map/ppermute | solution.py:773
  53.0 0.7 %pad_maximum_fusion = f32[256,256]{1,0:T(8,128)} fusion(f32[256,128]{1,0:T(8,128)S(1)} %get-tuple-element.48, f32[256,128]{1,0:T(8,128)S(1)} %get-tuple-element.47), kind=kLoop, calls=%fused_computation | loop fusion | flops 65536 | bytes 524288 | tf_op jit(solution)/shard_map/concatenate | solution.py:777
  (13 shorter events, 2.3 us)
Async XLA Ops:
  0.0 0.9 %copy-start = (f32[256,256]{1,0:T(8,128)S(1)}, f32[256,256]{1,0:T(8,128)}, u32[]{:S(2)}) copy-start(f32[256,256]{1,0:T(8,128)} %basis_ref.1) | copy-start | bytes 786436
  1.4 7.5 %collective-permute-start = (f32[320,128]{1,0:T(8,128)S(1)}, f32[320,128]{1,0:T(8,128)S(1)}, u32[]{:S(2)}, u32[]{:S(2)}) collective-permute-start(f32[320,128]{1,0:T(8,128)S(1)} %get-tuple-element.28), channel_id=1, source_target_pairs={{1,0},{0,2},{3,1},{2,3},{5,4},{4,6},{7,5},{6,7},{9,8},{8,10},{11,9... | collective-permute-start | bytes 491528 | tf_op jit(solution)/shard_map/ppermute | solution.py:761
  9.8 1.3 %collective-permute-start.1 = (f32[128,128]{1,0:T(8,128)S(1)}, f32[128,128]{1,0:T(8,128)S(1)}, u32[]{:S(2)}, u32[]{:S(2)}) collective-permute-start(f32[128,128]{1,0:T(8,128)S(1)} %get-tuple-element.33), channel_id=1, source_target_pairs={{0,4},{4,0},{8,12},{12,8},{16,20},{20,16},{24,28},{28,24},{1,5},{5... | collective-permute-start | bytes 196616 | tf_op jit(solution)/shard_map/ppermute | solution.py:708
  11.2 4.3 %collective-permute-start.2 = (f32[128,128]{1,0:T(8,128)S(1)}, f32[128,128]{1,0:T(8,128)S(1)}, u32[]{:S(2)}, u32[]{:S(2)}) collective-permute-start(f32[128,128]{1,0:T(8,128)S(1)} %add.6.refs_0_), channel_id=1, source_target_pairs={{0,8},{4,12},{8,0},{12,4},{16,24},{20,28},{24,16},{28,20},{1,9},{5... | collective-permute-start | bytes 196616 | tf_op jit(solution)/shard_map/ppermute | solution.py:708
  12.7 4.3 %collective-permute-start.3 = (f32[128,128]{1,0:T(8,128)S(1)}, f32[128,128]{1,0:T(8,128)S(1)}, u32[]{:S(2)}, u32[]{:S(2)}) collective-permute-start(f32[128,128]{1,0:T(8,128)S(1)} %add.6.refs_0_), channel_id=1, source_target_pairs={{0,16},{4,20},{8,24},{12,28},{16,0},{20,4},{24,8},{28,12},{1,17},{... | collective-permute-start | bytes 196616 | tf_op jit(solution)/shard_map/ppermute | solution.py:708
  14.2 5.2 %collective-permute-start.4 = (f32[128,128]{1,0:T(8,128)S(1)}, f32[128,128]{1,0:T(8,128)S(1)}, u32[]{:S(2)}, u32[]{:S(2)}) collective-permute-start(f32[128,128]{1,0:T(8,128)S(1)} %add.6.refs_0_), channel_id=1, source_target_pairs={{0,24},{4,28},{8,16},{12,20},{16,8},{20,12},{24,0},{28,4},{1,25},{... | collective-permute-start | bytes 196616 | tf_op jit(solution)/shard_map/ppermute | solution.py:708
  20.4 1.4 %collective-permute-start.5 = (f32[176,128]{1,0:T(8,128)S(1)}, f32[176,128]{1,0:T(8,128)S(1)}, u32[]{:S(2)}, u32[]{:S(2)}) collective-permute-start(f32[176,128]{1,0:T(8,128)S(1)} %shard_map.20.found_ref.refs_4_), channel_id=1, source_target_pairs={{0,4},{4,0},{8,12},{12,8},{16,20},{20,16},{24,28},{28,24},{1,5},{5... | collective-permute-start | bytes 270344 | tf_op jit(solution)/shard_map/ppermute | solution.py:708
  23.3 7.4 %collective-permute-start.6 = (f32[256,128]{1,0:T(8,128)S(1)}, f32[256,128]{1,0:T(8,128)S(1)}, u32[]{:S(2)}, u32[]{:S(2)}) collective-permute-start(f32[256,128]{1,0:T(8,128)S(1)} %get-tuple-element.37.sent_ref), channel_id=1, source_target_pairs={{2,0},{3,2},{0,1},{1,3},{6,4},{7,6},{4,5},{5,7},{10,8},{11,10},{8,... | collective-permute-start | bytes 393224 | tf_op jit(solution)/shard_map/ppermute | solution.py:767
  25.8 7.6 %collective-permute-start.7 = (f32[256,128]{1,0:T(8,128)S(1)}, f32[256,128]{1,0:T(8,128)S(1)}, u32[]{:S(2)}, u32[]{:S(2)}) collective-permute-start(f32[256,128]{1,0:T(8,128)S(1)} %get-tuple-element.36.kept_ref), channel_id=1, source_target_pairs={{1,0},{0,2},{3,1},{2,3},{5,4},{4,6},{7,5},{6,7},{9,8},{8,10},{11,9... | collective-permute-start | bytes 393224 | tf_op jit(solution)/shard_map/ppermute | solution.py:767
  34.3 1.3 %collective-permute-start.8 = (f32[128,128]{1,0:T(8,128)S(1)}, f32[128,128]{1,0:T(8,128)S(1)}, u32[]{:S(2)}, u32[]{:S(2)}) collective-permute-start(f32[128,128]{1,0:T(8,128)S(1)} %get-tuple-element.42), channel_id=1, source_target_pairs={{0,4},{4,0},{8,12},{12,8},{16,20},{20,16},{24,28},{28,24},{1,5},{5... | collective-permute-start | bytes 196616 | tf_op jit(solution)/shard_map/ppermute | solution.py:708
  35.6 5.0 %collective-permute-start.10 = (f32[128,128]{1,0:T(8,128)S(1)}, f32[128,128]{1,0:T(8,128)S(1)}, u32[]{:S(2)}, u32[]{:S(2)}) collective-permute-start(f32[128,128]{1,0:T(8,128)S(1)} %add.7.refs_0_), channel_id=1, source_target_pairs={{0,16},{4,20},{8,24},{12,28},{16,0},{20,4},{24,8},{28,12},{1,17},{... | collective-permute-start | bytes 196616 | tf_op jit(solution)/shard_map/ppermute | solution.py:708
  36.2 5.6 %collective-permute-start.11 = (f32[128,128]{1,0:T(8,128)S(1)}, f32[128,128]{1,0:T(8,128)S(1)}, u32[]{:S(2)}, u32[]{:S(2)}) collective-permute-start(f32[128,128]{1,0:T(8,128)S(1)} %add.7.refs_0_), channel_id=1, source_target_pairs={{0,24},{4,28},{8,16},{12,20},{16,8},{20,12},{24,0},{28,4},{1,25},{... | collective-permute-start | bytes 196616 | tf_op jit(solution)/shard_map/ppermute | solution.py:708
  37.7 4.8 %collective-permute-start.9 = (f32[128,128]{1,0:T(8,128)S(1)}, f32[128,128]{1,0:T(8,128)S(1)}, u32[]{:S(2)}, u32[]{:S(2)}) collective-permute-start(f32[128,128]{1,0:T(8,128)S(1)} %add.7.refs_0_), channel_id=1, source_target_pairs={{0,8},{4,12},{8,0},{12,4},{16,24},{20,28},{24,16},{28,20},{1,9},{5... | collective-permute-start | bytes 196616 | tf_op jit(solution)/shard_map/ppermute | solution.py:708
  43.6 1.4 %collective-permute-start.12 = (f32[176,128]{1,0:T(8,128)S(1)}, f32[176,128]{1,0:T(8,128)S(1)}, u32[]{:S(2)}, u32[]{:S(2)}) collective-permute-start(f32[176,128]{1,0:T(8,128)S(1)} %shard_map.25.found_ref.refs_4_), channel_id=1, source_target_pairs={{0,4},{4,0},{8,12},{12,8},{16,20},{20,16},{24,28},{28,24},{1,5},{5... | collective-permute-start | bytes 270344 | tf_op jit(solution)/shard_map/ppermute | solution.py:708
  46.5 6.5 %collective-permute-start.13 = (f32[256,128]{1,0:T(8,128)S(1)}, f32[256,128]{1,0:T(8,128)S(1)}, u32[]{:S(2)}, u32[]{:S(2)}) collective-permute-start(f32[256,128]{1,0:T(8,128)S(1)} %get-tuple-element.45), channel_id=1, source_target_pairs={{2,0},{0,1},{3,2},{1,3},{6,4},{4,5},{7,6},{5,7},{10,8},{8,9},{11,1... | collective-permute-start | bytes 393224 | tf_op jit(solution)/shard_map/ppermute | solution.py:773

commit v12 on v11

--- a/solution.py
+++ b/solution.py
@@ -537,37 +537,56 @@
     return lax.axis_index("row") % 2 == 1
 
 
-def far_starts(width):
-    return REACH - 1, width // 2
+PLACES = (
+    (((16, 16, 80), (60, 16, 108)), ((16, 28, 21), (44, 30, 80))),
+    (((68, 16, 24), (112, 16, 0)), ((70, 29, 84), (99, 29, 10))),
+)
+MIDDLES = (44, 99)
+
+
+def pick_by(flag, one, other):
+    return jnp.where(flag, other, one)
 
 
 def pack_far(bands, flag):
     width = bands[0].shape[1]
-    half, count = width // 2, (FAR_DIAGS - DIAGS) // 2
-    lane = line_lanes(bands[0])
+    lane = lax.broadcasted_iota(jnp.int32, (DIAGS, width), 1)
+    odd_row = lax.broadcasted_iota(jnp.int32, (DIAGS, width), 0) % 2 == 1
+    moves = []
+    for parity in (0, 1):
+        for part in (0, 1):
+            one, other = PLACES[0][parity][part], PLACES[1][parity][part]
+            shift = pick_by(flag, (one[2] - one[0]) % width, (other[2] - other[0]) % width)
+            start = pick_by(flag, one[2], other[2])
+            count = pick_by(flag, one[1], other[1])
+            here = jnp.logical_and(lane >= start, lane < start + count)
+            moves.append((shift, jnp.logical_and(here, odd_row == (parity == 1))))
     packed = []
     for band in bands:
-        one, two = band[DIAGS : DIAGS + count], band[DIAGS + count :]
-        one, two = (
-            jnp.where(flag, left(x, far_starts(width)[1] - at), left(x, far_starts(width)[0] - at))
-            for x, at in ((one, 0), (two, half))
-        )
-        packed.append(jnp.concatenate((band[:DIAGS], jnp.where(lane < half, one, two)), axis=0))
+        near, far = band[:DIAGS], down(band[DIAGS:], -1)
+        for shift, here in moves:
+            near = jnp.where(here, pltpu.roll(far, shift, 1), near)
+        packed.append(near)
     return packed
 
 
 def unpack_far(packed, flag):
     width = packed.shape[1]
-    half = width // 2
-    parts = [packed[:DIAGS]]
-    for at in (0, half):
-        starts = [start - at for start in far_starts(width)]
-        x = packed[DIAGS:]
-        parts.append(jnp.where(flag, right(x, starts[1]), right(x, starts[0])))
-    return jnp.concatenate(parts, axis=0)
-
-
-PACKED = DIAGS + (FAR_DIAGS - DIAGS) // 2
+    lane = lanes_of(packed)
+    odd_row = lax.broadcasted_iota(jnp.int32, packed.shape, 0) % 2 == 1
+    parts = []
+    for part in (0, 1):
+        rolled = []
+        for parity in (0, 1):
+            one, other = PLACES[0][parity][part], PLACES[1][parity][part]
+            shift = pick_by(flag, (one[0] - one[2]) % width, (other[0] - other[2]) % width)
+            rolled.append(pltpu.roll(packed, shift, 1))
+        parts.append(jnp.where(odd_row, rolled[1], rolled[0]))
+    far = jnp.where(lane < pick_by(flag, *MIDDLES), *parts)
+    return jnp.concatenate((packed, down(far, 1)), axis=0)
+
+
+PACKED = DIAGS
 
 
 def store_part(even, odd, flag, part_ref):

time: 53.9 us -> 53.1 us (0.985)
  waiting for transfers between devices: 24.4 us -> 23.5 us
    ppermute x10, waiting for transfers between devices: 9.69 us -> 8.81 us  [swap(): lax.ppermute(x, axis, [(i, i ^ mask) for i in range(lax.axis_size(axis))])]
where the time goes in v12:
time: 53.1 us; the launch traced here: 53 us
  waiting for transfers between devices  23.5 us (44%)
  starting transfers between devices  16.8 us (32%)
  Pallas kernels  10.8 us (20%)
  local copies, waits for them, and re-layouts  0.95 us (2%)
  other arithmetic  0.75 us (1%)
    pallas_call x11, Pallas kernels, call(): pl.pallas_call(kernel, out_shape=out, compiler_params=pltpu.CompilerParam...  10.8 us
    ppermute x10, waiting for transfers between devices, swap(): lax.ppermute(x, axis, [(i, i ^ mask) for i in range(lax.axis_size(axis))])  8.81 us
    ppermute x2, waiting for transfers between devices, per_device(): came = lax.ppermute(sent, 'pair', sends)  8.17 us
    ppermute x10, starting transfers between devices, swap(): lax.ppermute(x, axis, [(i, i ^ mask) for i in range(lax.axis_size(axis))])  7.38 us
    ppermute x2, waiting for transfers between devices, per_device(): came = [lax.ppermute(x, 'pair', s) for x, s in zip((sent, kept), sends)]  6.56 us
    ppermute x2, starting transfers between devices, per_device(): came = lax.ppermute(sent, 'pair', sends)  5.88 us
    ppermute x2, starting transfers between devices, per_device(): came = [lax.ppermute(x, 'pair', s) for x, s in zip((sent, kept), sends)]  3.5 us
  transfers between devices with their start and end apart: 14, of which 14 were waited for; matrix products, arithmetic and copies ran while one was open for 0% of the time, Pallas kernels for 6%

profile of v12, /device:TPU:0, one launch (start us, length us, event | category | flops | bytes accessed | tf_op | source)
XLA Modules:
  0.0 53.0 jit_solution(17583275478275166714)
XLA Ops:
  0.0 0.9 %copy-done = f32[256,256]{1,0:T(8,128)S(1)} copy-done((f32[256,256]{1,0:T(8,128)S(1)}, f32[256,256]{1,0:T(8,128)}, u32[]{:S(2)}) %copy-start) | copy-done | bytes 262168
  1.4 4.1 %collective-permute-start = (f32[320,128]{1,0:T(8,128)S(1)}, f32[320,128]{1,0:T(8,128)S(1)}, u32[]{:S(2)}, u32[]{:S(2)}) collective-permute-start(f32[320,128]{1,0:T(8,128)S(1)} %get-tuple-element.28), channel_id=1, source_target_pairs={{1,0},{0,2},{3,1},{2,3},{5,4},{4,6},{7,5},{6,7},{9,8},{8,10},{11,9... | collective-permute-start | bytes 491528 | tf_op jit(solution)/shard_map/ppermute | solution.py:780
  5.4 3.5 %collective-permute-done.payload_ref = f32[320,128]{1,0:T(8,128)S(1)} collective-permute-done((f32[320,128]{1,0:T(8,128)S(1)}, f32[320,128]{1,0:T(8,128)S(1)}, u32[]{:S(2)}, u32[]{:S(2)}) %collective-permute-start) | collective-permute-done | bytes 163872 | tf_op jit(solution)/shard_map/ppermute | solution.py:780
  8.9 1.0 %shard_map.18 = (f32[256,128]{1,0:T(8,128)S(1)}, f32[256,128]{1,0:T(8,128)S(1)}, f32[256,128]{1,0:T(8,128)S(1)}, f32[256,128]{1,0:T(8,128)S(1)}, f32[96,128]{1,0:T(8,128)S(1)}) custom-call(f32[256,128]{1,0:T(8,128)S(1)} %get-tuple-element.26.even_ref, f32[256,128]{1,0:T(8,128)S(1)} %get-tuple-element.27.odd_ref, f32[320,128]{1,0:T(8,128)S(1)} %collective-permute-done.payload_ref), custom_call_target="tpu_custom_call" | custom-call | tf_op jit(solution)/shard_map/pallas_call | solution.py:744
  10.0 0.9 %shard_map.19 = f32[96,128]{1,0:T(8,128)S(1)} custom-call(f32[256,128]{1,0:T(8,128)S(1)} %get-tuple-element.29.refs_0_.even_ref, f32[256,128]{1,0:T(8,128)S(1)} %get-tuple-element.30.refs_1_.odd_ref, f32[256,128]{1,0:T(8,128)S(1)} %get-tuple-element.31.refs_2_, f32[256,128]{1,0:T(8,128)S(1)} %get-tuple-element.32.refs_3_), custom_call_target="tpu_custom_call" | custom-call | tf_op jit(solution)/shard_map/pallas_call | solution.py:744
  11.2 1.6 %collective-permute-start.2 = (f32[96,128]{1,0:T(8,128)S(1)}, f32[96,128]{1,0:T(8,128)S(1)}, u32[]{:S(2)}, u32[]{:S(2)}) collective-permute-start(f32[96,128]{1,0:T(8,128)S(1)} %add.6.refs_0_), channel_id=1, source_target_pairs={{0,8},{4,12},{8,0},{12,4},{16,24},{20,28},{24,16},{28,20},{1,9},{5... | collective-permute-start | bytes 147464 | tf_op jit(solution)/shard_map/ppermute | solution.py:727
  12.8 1.5 %collective-permute-start.3 = (f32[96,128]{1,0:T(8,128)S(1)}, f32[96,128]{1,0:T(8,128)S(1)}, u32[]{:S(2)}, u32[]{:S(2)}) collective-permute-start(f32[96,128]{1,0:T(8,128)S(1)} %add.6.refs_0_), channel_id=1, source_target_pairs={{0,16},{4,20},{8,24},{12,28},{16,0},{20,4},{24,8},{28,12},{1,17},{... | collective-permute-start | bytes 147464 | tf_op jit(solution)/shard_map/ppermute | solution.py:727
  14.8 0.6 %collective-permute-done.2.refs_1_ = f32[96,128]{1,0:T(8,128)S(1)} collective-permute-done((f32[96,128]{1,0:T(8,128)S(1)}, f32[96,128]{1,0:T(8,128)S(1)}, u32[]{:S(2)}, u32[]{:S(2)}) %collective-permute-start.2) | collective-permute-done | bytes 49184 | tf_op jit(solution)/shard_map/ppermute | solution.py:727
  15.4 1.5 %collective-permute-done.3.refs_2_ = f32[96,128]{1,0:T(8,128)S(1)} collective-permute-done((f32[96,128]{1,0:T(8,128)S(1)}, f32[96,128]{1,0:T(8,128)S(1)}, u32[]{:S(2)}, u32[]{:S(2)}) %collective-permute-start.3) | collective-permute-done | bytes 49184 | tf_op jit(solution)/shard_map/ppermute | solution.py:727
  16.8 2.4 %collective-permute-done.4.refs_3_ = f32[96,128]{1,0:T(8,128)S(1)} collective-permute-done((f32[96,128]{1,0:T(8,128)S(1)}, f32[96,128]{1,0:T(8,128)S(1)}, u32[]{:S(2)}, u32[]{:S(2)}) %collective-permute-start.4) | collective-permute-done | bytes 49184 | tf_op jit(solution)/shard_map/ppermute | solution.py:727
  19.3 1.0 %shard_map.20.found_ref.refs_4_ = f32[176,128]{1,0:T(8,128)S(1)} custom-call(f32[96,128]{1,0:T(8,128)S(1)} %add.6.refs_0_, f32[96,128]{1,0:T(8,128)S(1)} %collective-permute-done.2.refs_1_, f32[96,128]{1,0:T(8,128)S(1)} %collective-permute-done.3.refs_2_, f32[96,128]{1,0:T(8,128)S(1)} %collective-permute-done.4.refs_3_), custom_call_target="tpu_custom_call" | custom-call | tf_op jit(solution)/shard_map/pallas_call | solution.py:744
  20.4 0.7 %shard_map.21 = (f32[256,128]{1,0:T(8,128)S(1)}, f32[256,128]{1,0:T(8,128)S(1)}) custom-call(f32[256,128]{1,0:T(8,128)S(1)} %get-tuple-element.29.refs_0_.even_ref, f32[256,128]{1,0:T(8,128)S(1)} %get-tuple-element.30.refs_1_.odd_ref, f32[176,128]{1,0:T(8,128)S(1)} %shard_map.20.found_ref.refs_4_), custom_call_target="tpu_custom_call" | custom-call | tf_op jit(solution)/shard_map/pallas_call | solution.py:744
  21.1 0.6 %collective-permute-done.5.refs_5_ = f32[176,128]{1,0:T(8,128)S(1)} collective-permute-done((f32[176,128]{1,0:T(8,128)S(1)}, f32[176,128]{1,0:T(8,128)S(1)}, u32[]{:S(2)}, u32[]{:S(2)}) %collective-permute-start.5) | collective-permute-done | bytes 90144 | tf_op jit(solution)/shard_map/ppermute | solution.py:727
  21.7 1.6 %shard_map.22 = (f32[256,128]{1,0:T(8,128)S(1)}, f32[256,128]{1,0:T(8,128)S(1)}) custom-call(f32[256,128]{1,0:T(8,128)S(1)} %get-tuple-element.34.refs_0_, f32[256,128]{1,0:T(8,128)S(1)} %get-tuple-element.35.refs_1_, f32[256,128]{1,0:T(8,128)S(1)} %get-tuple-element.31.refs_2_, f32[256,128]{1,0:T(8,128)S(1)} %get-tuple-element.32.refs_3_, ...), custom_call_target="tpu_custom_call" | custom-call | tf_op jit(solution)/shard_map/pallas_call | solution.py:744
  23.2 2.4 %collective-permute-start.6 = (f32[256,128]{1,0:T(8,128)S(1)}, f32[256,128]{1,0:T(8,128)S(1)}, u32[]{:S(2)}, u32[]{:S(2)}) collective-permute-start(f32[256,128]{1,0:T(8,128)S(1)} %get-tuple-element.37.sent_ref), channel_id=1, source_target_pairs={{2,0},{3,2},{0,1},{1,3},{6,4},{7,6},{4,5},{5,7},{10,8},{11,10},{8,... | collective-permute-start | bytes 393224 | tf_op jit(solution)/shard_map/ppermute | solution.py:786
  25.7 1.1 %collective-permute-start.7 = (f32[256,128]{1,0:T(8,128)S(1)}, f32[256,128]{1,0:T(8,128)S(1)}, u32[]{:S(2)}, u32[]{:S(2)}) collective-permute-start(f32[256,128]{1,0:T(8,128)S(1)} %get-tuple-element.36.kept_ref), channel_id=1, source_target_pairs={{1,0},{0,2},{3,1},{2,3},{5,4},{4,6},{7,5},{6,7},{9,8},{8,10},{11,9... | collective-permute-start | bytes 393224 | tf_op jit(solution)/shard_map/ppermute | solution.py:786
  26.7 3.9 %collective-permute-done.6.came0_ref = f32[256,128]{1,0:T(8,128)S(1)} collective-permute-done((f32[256,128]{1,0:T(8,128)S(1)}, f32[256,128]{1,0:T(8,128)S(1)}, u32[]{:S(2)}, u32[]{:S(2)}) %collective-permute-start.6) | collective-permute-done | bytes 131104 | tf_op jit(solution)/shard_map/ppermute | solution.py:786
  30.6 2.7 %collective-permute-done.7.came1_ref = f32[256,128]{1,0:T(8,128)S(1)} collective-permute-done((f32[256,128]{1,0:T(8,128)S(1)}, f32[256,128]{1,0:T(8,128)S(1)}, u32[]{:S(2)}, u32[]{:S(2)}) %collective-permute-start.7) | collective-permute-done | bytes 131104 | tf_op jit(solution)/shard_map/ppermute | solution.py:786
  33.3 0.9 %shard_map.23 = (f32[256,128]{1,0:T(8,128)S(1)}, f32[256,128]{1,0:T(8,128)S(1)}, f32[256,128]{1,0:T(8,128)S(1)}, f32[256,128]{1,0:T(8,128)S(1)}, f32[96,128]{1,0:T(8,128)S(1)}) custom-call(f32[256,128]{1,0:T(8,128)S(1)} %get-tuple-element.36.kept_ref, f32[256,128]{1,0:T(8,128)S(1)} %get-tuple-element.37.sent_ref, ...), custom_call_target="tpu_custom_call" | custom-call | tf_op jit(solution)/shard_map/pallas_call | solution.py:744
  34.3 0.9 %shard_map.24 = f32[96,128]{1,0:T(8,128)S(1)} custom-call(f32[256,128]{1,0:T(8,128)S(1)} %get-tuple-element.38.refs_0_.even_ref, f32[256,128]{1,0:T(8,128)S(1)} %get-tuple-element.39.refs_1_.odd_ref, f32[256,128]{1,0:T(8,128)S(1)} %get-tuple-element.40.refs_2_, f32[256,128]{1,0:T(8,128)S(1)} %get-tuple-element.41.refs_3_), custom_call_target="tpu_custom_call" | custom-call | tf_op jit(solution)/shard_map/pallas_call | solution.py:744
  35.5 0.6 %collective-permute-start.10 = (f32[96,128]{1,0:T(8,128)S(1)}, f32[96,128]{1,0:T(8,128)S(1)}, u32[]{:S(2)}, u32[]{:S(2)}) collective-permute-start(f32[96,128]{1,0:T(8,128)S(1)} %add.7.refs_0_), channel_id=1, source_target_pairs={{0,16},{4,20},{8,24},{12,28},{16,0},{20,4},{24,8},{28,12},{1,17},{... | collective-permute-start | bytes 147464 | tf_op jit(solution)/shard_map/ppermute | solution.py:727
  36.1 1.5 %collective-permute-start.11 = (f32[96,128]{1,0:T(8,128)S(1)}, f32[96,128]{1,0:T(8,128)S(1)}, u32[]{:S(2)}, u32[]{:S(2)}) collective-permute-start(f32[96,128]{1,0:T(8,128)S(1)} %add.7.refs_0_), channel_id=1, source_target_pairs={{0,24},{4,28},{8,16},{12,20},{16,8},{20,12},{24,0},{28,4},{1,25},{... | collective-permute-start | bytes 147464 | tf_op jit(solution)/shard_map/ppermute | solution.py:727
  37.6 1.5 %collective-permute-start.9 = (f32[96,128]{1,0:T(8,128)S(1)}, f32[96,128]{1,0:T(8,128)S(1)}, u32[]{:S(2)}, u32[]{:S(2)}) collective-permute-start(f32[96,128]{1,0:T(8,128)S(1)} %add.7.refs_0_), channel_id=1, source_target_pairs={{0,8},{4,12},{8,0},{12,4},{16,24},{20,28},{24,16},{28,20},{1,9},{5... | collective-permute-start | bytes 147464 | tf_op jit(solution)/shard_map/ppermute | solution.py:727
  39.1 1.1 %collective-permute-done.10.refs_2_ = f32[96,128]{1,0:T(8,128)S(1)} collective-permute-done((f32[96,128]{1,0:T(8,128)S(1)}, f32[96,128]{1,0:T(8,128)S(1)}, u32[]{:S(2)}, u32[]{:S(2)}) %collective-permute-start.10) | collective-permute-done | bytes 49184 | tf_op jit(solution)/shard_map/ppermute | solution.py:727
  40.2 0.9 %collective-permute-done.11.refs_3_ = f32[96,128]{1,0:T(8,128)S(1)} collective-permute-done((f32[96,128]{1,0:T(8,128)S(1)}, f32[96,128]{1,0:T(8,128)S(1)}, u32[]{:S(2)}, u32[]{:S(2)}) %collective-permute-start.11) | collective-permute-done | bytes 49184 | tf_op jit(solution)/shard_map/ppermute | solution.py:727
  41.2 0.6 %collective-permute-done.9.refs_1_ = f32[96,128]{1,0:T(8,128)S(1)} collective-permute-done((f32[96,128]{1,0:T(8,128)S(1)}, f32[96,128]{1,0:T(8,128)S(1)}, u32[]{:S(2)}, u32[]{:S(2)}) %collective-permute-start.9) | collective-permute-done | bytes 49184 | tf_op jit(solution)/shard_map/ppermute | solution.py:727
  41.7 1.0 %shard_map.25.found_ref.refs_4_ = f32[176,128]{1,0:T(8,128)S(1)} custom-call(f32[96,128]{1,0:T(8,128)S(1)} %add.7.refs_0_, f32[96,128]{1,0:T(8,128)S(1)} %collective-permute-done.9.refs_1_, f32[96,128]{1,0:T(8,128)S(1)} %collective-permute-done.10.refs_2_, f32[96,128]{1,0:T(8,128)S(1)} %collective-permute-done.11.refs_3_), custom_call_target="tpu_custom_call" | custom-call | tf_op jit(solution)/shard_map/pallas_call | solution.py:744
  42.9 0.7 %shard_map.26 = (f32[256,128]{1,0:T(8,128)S(1)}, f32[256,128]{1,0:T(8,128)S(1)}) custom-call(f32[256,128]{1,0:T(8,128)S(1)} %get-tuple-element.38.refs_0_.even_ref, f32[256,128]{1,0:T(8,128)S(1)} %get-tuple-element.39.refs_1_.odd_ref, f32[176,128]{1,0:T(8,128)S(1)} %shard_map.25.found_ref.refs_4_), custom_call_target="tpu_custom_call" | custom-call | tf_op jit(solution)/shard_map/pallas_call | solution.py:744
  44.1 1.6 %shard_map.27 = (f32[256,128]{1,0:T(8,128)S(1)}, f32[256,128]{1,0:T(8,128)S(1)}) custom-call(f32[256,128]{1,0:T(8,128)S(1)} %get-tuple-element.43.refs_0_, f32[256,128]{1,0:T(8,128)S(1)} %get-tuple-element.44.refs_1_, f32[256,128]{1,0:T(8,128)S(1)} %get-tuple-element.40.refs_2_, f32[256,128]{1,0:T(8,128)S(1)} %get-tuple-element.41.refs_3_, ...), custom_call_target="tpu_custom_call" | custom-call | tf_op jit(solution)/shard_map/pallas_call | solution.py:744
  45.7 1.8 %collective-permute-start.13 = (f32[256,128]{1,0:T(8,128)S(1)}, f32[256,128]{1,0:T(8,128)S(1)}, u32[]{:S(2)}, u32[]{:S(2)}) collective-permute-start(f32[256,128]{1,0:T(8,128)S(1)} %get-tuple-element.45), channel_id=1, source_target_pairs={{2,0},{0,1},{3,2},{1,3},{6,4},{4,5},{7,6},{5,7},{10,8},{8,9},{11,1... | collective-permute-start | bytes 393224 | tf_op jit(solution)/shard_map/ppermute | solution.py:792
  47.5 4.7 %collective-permute-done.13 = f32[256,128]{1,0:T(8,128)S(1)} collective-permute-done((f32[256,128]{1,0:T(8,128)S(1)}, f32[256,128]{1,0:T(8,128)S(1)}, u32[]{:S(2)}, u32[]{:S(2)}) %collective-permute-start.13) | collective-permute-done | bytes 131104 | tf_op jit(solution)/shard_map/ppermute | solution.py:792
  52.2 0.7 %pad_maximum_fusion = f32[256,256]{1,0:T(8,128)} fusion(f32[256,128]{1,0:T(8,128)S(1)} %get-tuple-element.48, f32[256,128]{1,0:T(8,128)S(1)} %get-tuple-element.47), kind=kLoop, calls=%fused_computation | loop fusion | flops 65536 | bytes 524288 | tf_op jit(solution)/shard_map/concatenate | solution.py:796
  (13 shorter events, 2.3 us)
Async XLA Ops:
  0.0 0.9 %copy-start = (f32[256,256]{1,0:T(8,128)S(1)}, f32[256,256]{1,0:T(8,128)}, u32[]{:S(2)}) copy-start(f32[256,256]{1,0:T(8,128)} %basis_ref.1) | copy-start | bytes 786436
  1.4 7.5 %collective-permute-start = (f32[320,128]{1,0:T(8,128)S(1)}, f32[320,128]{1,0:T(8,128)S(1)}, u32[]{:S(2)}, u32[]{:S(2)}) collective-permute-start(f32[320,128]{1,0:T(8,128)S(1)} %get-tuple-element.28), channel_id=1, source_target_pairs={{1,0},{0,2},{3,1},{2,3},{5,4},{4,6},{7,5},{6,7},{9,8},{8,10},{11,9... | collective-permute-start | bytes 491528 | tf_op jit(solution)/shard_map/ppermute | solution.py:780
  9.9 1.3 %collective-permute-start.1 = (f32[96,128]{1,0:T(8,128)S(1)}, f32[96,128]{1,0:T(8,128)S(1)}, u32[]{:S(2)}, u32[]{:S(2)}) collective-permute-start(f32[96,128]{1,0:T(8,128)S(1)} %get-tuple-element.33), channel_id=1, source_target_pairs={{0,4},{4,0},{8,12},{12,8},{16,20},{20,16},{24,28},{28,24},{1,5},{5... | collective-permute-start | bytes 147464 | tf_op jit(solution)/shard_map/ppermute | solution.py:727
  11.2 4.2 %collective-permute-start.2 = (f32[96,128]{1,0:T(8,128)S(1)}, f32[96,128]{1,0:T(8,128)S(1)}, u32[]{:S(2)}, u32[]{:S(2)}) collective-permute-start(f32[96,128]{1,0:T(8,128)S(1)} %add.6.refs_0_), channel_id=1, source_target_pairs={{0,8},{4,12},{8,0},{12,4},{16,24},{20,28},{24,16},{28,20},{1,9},{5... | collective-permute-start | bytes 147464 | tf_op jit(solution)/shard_map/ppermute | solution.py:727
  12.8 4.1 %collective-permute-start.3 = (f32[96,128]{1,0:T(8,128)S(1)}, f32[96,128]{1,0:T(8,128)S(1)}, u32[]{:S(2)}, u32[]{:S(2)}) collective-permute-start(f32[96,128]{1,0:T(8,128)S(1)} %add.6.refs_0_), channel_id=1, source_target_pairs={{0,16},{4,20},{8,24},{12,28},{16,0},{20,4},{24,8},{28,12},{1,17},{... | collective-permute-start | bytes 147464 | tf_op jit(solution)/shard_map/ppermute | solution.py:727
  14.3 5.0 %collective-permute-start.4 = (f32[96,128]{1,0:T(8,128)S(1)}, f32[96,128]{1,0:T(8,128)S(1)}, u32[]{:S(2)}, u32[]{:S(2)}) collective-permute-start(f32[96,128]{1,0:T(8,128)S(1)} %add.6.refs_0_), channel_id=1, source_target_pairs={{0,24},{4,28},{8,16},{12,20},{16,8},{20,12},{24,0},{28,4},{1,25},{... | collective-permute-start | bytes 147464 | tf_op jit(solution)/shard_map/ppermute | solution.py:727
  20.3 1.4 %collective-permute-start.5 = (f32[176,128]{1,0:T(8,128)S(1)}, f32[176,128]{1,0:T(8,128)S(1)}, u32[]{:S(2)}, u32[]{:S(2)}) collective-permute-start(f32[176,128]{1,0:T(8,128)S(1)} %shard_map.20.found_ref.refs_4_), channel_id=1, source_target_pairs={{0,4},{4,0},{8,12},{12,8},{16,20},{20,16},{24,28},{28,24},{1,5},{5... | collective-permute-start | bytes 270344 | tf_op jit(solution)/shard_map/ppermute | solution.py:727
  23.2 7.4 %collective-permute-start.6 = (f32[256,128]{1,0:T(8,128)S(1)}, f32[256,128]{1,0:T(8,128)S(1)}, u32[]{:S(2)}, u32[]{:S(2)}) collective-permute-start(f32[256,128]{1,0:T(8,128)S(1)} %get-tuple-element.37.sent_ref), channel_id=1, source_target_pairs={{2,0},{3,2},{0,1},{1,3},{6,4},{7,6},{4,5},{5,7},{10,8},{11,10},{8,... | collective-permute-start | bytes 393224 | tf_op jit(solution)/shard_map/ppermute | solution.py:786
  25.7 7.6 %collective-permute-start.7 = (f32[256,128]{1,0:T(8,128)S(1)}, f32[256,128]{1,0:T(8,128)S(1)}, u32[]{:S(2)}, u32[]{:S(2)}) collective-permute-start(f32[256,128]{1,0:T(8,128)S(1)} %get-tuple-element.36.kept_ref), channel_id=1, source_target_pairs={{1,0},{0,2},{3,1},{2,3},{5,4},{4,6},{7,5},{6,7},{9,8},{8,10},{11,9... | collective-permute-start | bytes 393224 | tf_op jit(solution)/shard_map/ppermute | solution.py:786
  34.2 1.3 %collective-permute-start.8 = (f32[96,128]{1,0:T(8,128)S(1)}, f32[96,128]{1,0:T(8,128)S(1)}, u32[]{:S(2)}, u32[]{:S(2)}) collective-permute-start(f32[96,128]{1,0:T(8,128)S(1)} %get-tuple-element.42), channel_id=1, source_target_pairs={{0,4},{4,0},{8,12},{12,8},{16,20},{20,16},{24,28},{28,24},{1,5},{5... | collective-permute-start | bytes 147464 | tf_op jit(solution)/shard_map/ppermute | solution.py:727
  35.5 4.7 %collective-permute-start.10 = (f32[96,128]{1,0:T(8,128)S(1)}, f32[96,128]{1,0:T(8,128)S(1)}, u32[]{:S(2)}, u32[]{:S(2)}) collective-permute-start(f32[96,128]{1,0:T(8,128)S(1)} %add.7.refs_0_), channel_id=1, source_target_pairs={{0,16},{4,20},{8,24},{12,28},{16,0},{20,4},{24,8},{28,12},{1,17},{... | collective-permute-start | bytes 147464 | tf_op jit(solution)/shard_map/ppermute | solution.py:727
  36.1 5.0 %collective-permute-start.11 = (f32[96,128]{1,0:T(8,128)S(1)}, f32[96,128]{1,0:T(8,128)S(1)}, u32[]{:S(2)}, u32[]{:S(2)}) collective-permute-start(f32[96,128]{1,0:T(8,128)S(1)} %add.7.refs_0_), channel_id=1, source_target_pairs={{0,24},{4,28},{8,16},{12,20},{16,8},{20,12},{24,0},{28,4},{1,25},{... | collective-permute-start | bytes 147464 | tf_op jit(solution)/shard_map/ppermute | solution.py:727
  37.6 4.1 %collective-permute-start.9 = (f32[96,128]{1,0:T(8,128)S(1)}, f32[96,128]{1,0:T(8,128)S(1)}, u32[]{:S(2)}, u32[]{:S(2)}) collective-permute-start(f32[96,128]{1,0:T(8,128)S(1)} %add.7.refs_0_), channel_id=1, source_target_pairs={{0,8},{4,12},{8,0},{12,4},{16,24},{20,28},{24,16},{28,20},{1,9},{5... | collective-permute-start | bytes 147464 | tf_op jit(solution)/shard_map/ppermute | solution.py:727
  42.8 1.4 %collective-permute-start.12 = (f32[176,128]{1,0:T(8,128)S(1)}, f32[176,128]{1,0:T(8,128)S(1)}, u32[]{:S(2)}, u32[]{:S(2)}) collective-permute-start(f32[176,128]{1,0:T(8,128)S(1)} %shard_map.25.found_ref.refs_4_), channel_id=1, source_target_pairs={{0,4},{4,0},{8,12},{12,8},{16,20},{20,16},{24,28},{28,24},{1,5},{5... | collective-permute-start | bytes 270344 | tf_op jit(solution)/shard_map/ppermute | solution.py:727
  45.7 6.5 %collective-permute-start.13 = (f32[256,128]{1,0:T(8,128)S(1)}, f32[256,128]{1,0:T(8,128)S(1)}, u32[]{:S(2)}, u32[]{:S(2)}) collective-permute-start(f32[256,128]{1,0:T(8,128)S(1)} %get-tuple-element.45), channel_id=1, source_target_pairs={{2,0},{0,1},{3,2},{1,3},{6,4},{4,5},{7,6},{5,7},{10,8},{8,9},{11,1... | collective-permute-start | bytes 393224 | tf_op jit(solution)/shard_map/ppermute | solution.py:792

commit v13 on v12

--- a/solution.py
+++ b/solution.py
@@ -215,25 +215,30 @@
         band_ref[q * diags : (q + 1) * diags, :] = band
 
 
-def open_kernel(sends_second, basis_ref, even_ref, odd_ref, payload_ref):
+def payload_kernel(sends_second, basis_ref, payload_ref):
     rows, cols = basis_ref.shape
     width = cols // 2
     half = width // 2
-    even, odd = separate(basis_ref[:, :width], basis_ref[:, width:])
-    even_ref[...] = even
-    odd_ref[...] = odd
-    flag = among(sends_second)
-    even, odd = (jnp.where(flag, left(x, half - STRIP), x) for x in (even, odd))
-    payload_ref[:rows] = jnp.where(line_lanes(even) < half, even, right(odd, half))
+    first, second = basis_ref[:, :width], basis_ref[:, width:]
+    lane = line_lanes(first)
+    start = jnp.where(among(sends_second), half - STRIP, 0)
+    place = start + jnp.where(lane < half, lane, lane - half)
+    odd = jnp.where(lane < half, 0, 1)
+    in_first = place < half
+    source = 2 * jnp.where(in_first, place, place - half) + odd
+    payload_ref[:rows] = jnp.where(in_first, take_lanes(first, source), take_lanes(second, source))
     group = rows * 2 * STRIP // width
+    source = 2 * (start + lane % STRIP) + lane // STRIP % 2
     strips = jnp.zeros((group, width), jnp.float32)
     for i in range(rows // group):
-        for j, x in enumerate((even, odd)):
-            start = (2 * i + j) * STRIP
-            lane = line_lanes(x)
-            here = jnp.logical_and(lane >= start, lane < start + STRIP)
-            strips = jnp.where(here, left(x[i * group : (i + 1) * group], half - start), strips)
+        here = lane // (2 * STRIP) == i
+        strips = jnp.where(here, take_lanes(second[i * group : (i + 1) * group], source), strips)
     payload_ref[rows:] = strips
+
+
+def open_kernel(basis_ref, even_ref, odd_ref):
+    width = basis_ref.shape[1] // 2
+    even_ref[...], odd_ref[...] = separate(basis_ref[:, :width], basis_ref[:, width:])
 
 
 def unpacked(payload, rows, second):
@@ -473,7 +478,7 @@
 
     def window(even, odd, flag, starts):
         start = jnp.where(flag, starts[1], starts[0])
-        at_zero = pltpu.roll(even, width - start, 1)
+        at_zero = pltpu.roll(even, (width - start) % width, 1)
         at_next = pltpu.roll(odd, (width - start + WINDOW) % width, 1)
         return jnp.where(lane < WINDOW, at_zero, jnp.where(lane < 2 * WINDOW, at_next, 0.0))
 
@@ -775,9 +780,9 @@
     payload = (rows + rows * 2 * STRIP // width, width)
 
     sends, sends_second, gets_second, own_second, is_second = first_moves(pair_total)
-    opening = functools.partial(open_kernel, sends_second)
-    even, odd, sent = call(opening, (column, column, payload), basis)
+    (sent,) = call(functools.partial(payload_kernel, sends_second), (payload,), basis)
     came = lax.ppermute(sent, "pair", sends)
+    even, odd = call(open_kernel, (column, column), basis)
     opening = functools.partial(first_open, own_second, gets_second, is_second)
     arrays = call(opening, opened, even, odd, came)
     sends, sends_first, picks, next_second = fused_moves(pair_total)

time: 53.1 us -> 52.9 us (level)
    pallas_call x11 -> x12, Pallas kernels: 10.8 us -> 10.8 us  [call(): pl.pallas_call(kernel, out_shape=out, compiler_params=pltpu.CompilerParam...]
  transfers between devices with their start and end apart: 14 -> 14, of which waited for: 14 -> 14; matrix products, arithmetic and copies ran while one was open for 0% -> 0% of each run, Pallas kernels for 6% -> 7%
where the time goes in v13:
time: 52.9 us; the launch traced here: 52.7 us
  waiting for transfers between devices  23.3 us (44%)
  starting transfers between devices  16.8 us (32%)
  Pallas kernels  10.8 us (20%)
  local copies, waits for them, and re-layouts  0.95 us (2%)
  other arithmetic  0.75 us (1%)
    pallas_call x12, Pallas kernels, call(): pl.pallas_call(kernel, out_shape=out, compiler_params=pltpu.CompilerParam...  10.8 us
    ppermute x10, waiting for transfers between devices, swap(): lax.ppermute(x, axis, [(i, i ^ mask) for i in range(lax.axis_size(axis))])  8.81 us
    ppermute x2, waiting for transfers between devices, per_device(): came = lax.ppermute(sent, 'pair', sends)  7.96 us
    ppermute x10, starting transfers between devices, swap(): lax.ppermute(x, axis, [(i, i ^ mask) for i in range(lax.axis_size(axis))])  7.38 us
    ppermute x2, waiting for transfers between devices, per_device(): came = [lax.ppermute(x, 'pair', s) for x, s in zip((sent, kept), sends)]  6.56 us
    ppermute x2, starting transfers between devices, per_device(): came = lax.ppermute(sent, 'pair', sends)  5.88 us
    ppermute x2, starting transfers between devices, per_device(): came = [lax.ppermute(x, 'pair', s) for x, s in zip((sent, kept), sends)]  3.5 us
  transfers between devices with their start and end apart: 14, of which 14 were waited for; matrix products, arithmetic and copies ran while one was open for 0% of the time, Pallas kernels for 7%

profile of v13, /device:TPU:0, one launch (start us, length us, event | category | flops | bytes accessed | tf_op | source)
XLA Modules:
  0.0 52.7 jit_solution(8793939953521223725)
XLA Ops:
  0.0 0.9 %copy-done = f32[256,256]{1,0:T(8,128)S(1)} copy-done((f32[256,256]{1,0:T(8,128)S(1)}, f32[256,256]{1,0:T(8,128)}, u32[]{:S(2)}) %copy-start) | copy-done | bytes 262168
  1.1 4.1 %collective-permute-start = (f32[320,128]{1,0:T(8,128)S(1)}, f32[320,128]{1,0:T(8,128)S(1)}, u32[]{:S(2)}, u32[]{:S(2)}) collective-permute-start(f32[320,128]{1,0:T(8,128)S(1)} %shard_map.18), channel_id=1, source_target_pairs={{1,0},{0,2},{3,1},{2,3},{5,4},{4,6},{7,5},{6,7},{9,8},{8,10},{11,9... | collective-permute-start | bytes 491528 | tf_op jit(solution)/shard_map/ppermute | solution.py:784
  5.4 3.2 %collective-permute-done.payload_ref = f32[320,128]{1,0:T(8,128)S(1)} collective-permute-done((f32[320,128]{1,0:T(8,128)S(1)}, f32[320,128]{1,0:T(8,128)S(1)}, u32[]{:S(2)}, u32[]{:S(2)}) %collective-permute-start) | collective-permute-done | bytes 163872 | tf_op jit(solution)/shard_map/ppermute | solution.py:784
  8.7 1.0 %shard_map.19 = (f32[256,128]{1,0:T(8,128)S(1)}, f32[256,128]{1,0:T(8,128)S(1)}, f32[256,128]{1,0:T(8,128)S(1)}, f32[256,128]{1,0:T(8,128)S(1)}, f32[96,128]{1,0:T(8,128)S(1)}) custom-call(f32[256,128]{1,0:T(8,128)S(1)} %get-tuple-element.25.even_ref, f32[256,128]{1,0:T(8,128)S(1)} %get-tuple-element.26.odd_ref, f32[320,128]{1,0:T(8,128)S(1)} %collective-permute-done.payload_ref), custom_call_target="tpu_custom_call" | custom-call | tf_op jit(solution)/shard_map/pallas_call | solution.py:749
  9.8 0.9 %shard_map.20 = f32[96,128]{1,0:T(8,128)S(1)} custom-call(f32[256,128]{1,0:T(8,128)S(1)} %get-tuple-element.27.refs_0_.even_ref, f32[256,128]{1,0:T(8,128)S(1)} %get-tuple-element.28.refs_1_.odd_ref, f32[256,128]{1,0:T(8,128)S(1)} %get-tuple-element.29.refs_2_, f32[256,128]{1,0:T(8,128)S(1)} %get-tuple-element.30.refs_3_), custom_call_target="tpu_custom_call" | custom-call | tf_op jit(solution)/shard_map/pallas_call | solution.py:749
  11.0 1.6 %collective-permute-start.2 = (f32[96,128]{1,0:T(8,128)S(1)}, f32[96,128]{1,0:T(8,128)S(1)}, u32[]{:S(2)}, u32[]{:S(2)}) collective-permute-start(f32[96,128]{1,0:T(8,128)S(1)} %add.6.refs_0_), channel_id=1, source_target_pairs={{0,8},{4,12},{8,0},{12,4},{16,24},{20,28},{24,16},{28,20},{1,9},{5... | collective-permute-start | bytes 147464 | tf_op jit(solution)/shard_map/ppermute | solution.py:732
  12.5 1.5 %collective-permute-start.3 = (f32[96,128]{1,0:T(8,128)S(1)}, f32[96,128]{1,0:T(8,128)S(1)}, u32[]{:S(2)}, u32[]{:S(2)}) collective-permute-start(f32[96,128]{1,0:T(8,128)S(1)} %add.6.refs_0_), channel_id=1, source_target_pairs={{0,16},{4,20},{8,24},{12,28},{16,0},{20,4},{24,8},{28,12},{1,17},{... | collective-permute-start | bytes 147464 | tf_op jit(solution)/shard_map/ppermute | solution.py:732
  14.5 0.6 %collective-permute-done.2.refs_1_ = f32[96,128]{1,0:T(8,128)S(1)} collective-permute-done((f32[96,128]{1,0:T(8,128)S(1)}, f32[96,128]{1,0:T(8,128)S(1)}, u32[]{:S(2)}, u32[]{:S(2)}) %collective-permute-start.2) | collective-permute-done | bytes 49184 | tf_op jit(solution)/shard_map/ppermute | solution.py:732
  15.1 1.5 %collective-permute-done.3.refs_2_ = f32[96,128]{1,0:T(8,128)S(1)} collective-permute-done((f32[96,128]{1,0:T(8,128)S(1)}, f32[96,128]{1,0:T(8,128)S(1)}, u32[]{:S(2)}, u32[]{:S(2)}) %collective-permute-start.3) | collective-permute-done | bytes 49184 | tf_op jit(solution)/shard_map/ppermute | solution.py:732
  16.6 2.4 %collective-permute-done.4.refs_3_ = f32[96,128]{1,0:T(8,128)S(1)} collective-permute-done((f32[96,128]{1,0:T(8,128)S(1)}, f32[96,128]{1,0:T(8,128)S(1)}, u32[]{:S(2)}, u32[]{:S(2)}) %collective-permute-start.4) | collective-permute-done | bytes 49184 | tf_op jit(solution)/shard_map/ppermute | solution.py:732
  19.0 1.0 %shard_map.21.found_ref.refs_4_ = f32[176,128]{1,0:T(8,128)S(1)} custom-call(f32[96,128]{1,0:T(8,128)S(1)} %add.6.refs_0_, f32[96,128]{1,0:T(8,128)S(1)} %collective-permute-done.2.refs_1_, f32[96,128]{1,0:T(8,128)S(1)} %collective-permute-done.3.refs_2_, f32[96,128]{1,0:T(8,128)S(1)} %collective-permute-done.4.refs_3_), custom_call_target="tpu_custom_call" | custom-call | tf_op jit(solution)/shard_map/pallas_call | solution.py:749
  20.2 0.7 %shard_map.22 = (f32[256,128]{1,0:T(8,128)S(1)}, f32[256,128]{1,0:T(8,128)S(1)}) custom-call(f32[256,128]{1,0:T(8,128)S(1)} %get-tuple-element.27.refs_0_.even_ref, f32[256,128]{1,0:T(8,128)S(1)} %get-tuple-element.28.refs_1_.odd_ref, f32[176,128]{1,0:T(8,128)S(1)} %shard_map.21.found_ref.refs_4_), custom_call_target="tpu_custom_call" | custom-call | tf_op jit(solution)/shard_map/pallas_call | solution.py:749
  20.9 0.6 %collective-permute-done.5.refs_5_ = f32[176,128]{1,0:T(8,128)S(1)} collective-permute-done((f32[176,128]{1,0:T(8,128)S(1)}, f32[176,128]{1,0:T(8,128)S(1)}, u32[]{:S(2)}, u32[]{:S(2)}) %collective-permute-start.5) | collective-permute-done | bytes 90144 | tf_op jit(solution)/shard_map/ppermute | solution.py:732
  21.5 1.6 %shard_map.23 = (f32[256,128]{1,0:T(8,128)S(1)}, f32[256,128]{1,0:T(8,128)S(1)}) custom-call(f32[256,128]{1,0:T(8,128)S(1)} %get-tuple-element.32.refs_0_, f32[256,128]{1,0:T(8,128)S(1)} %get-tuple-element.33.refs_1_, f32[256,128]{1,0:T(8,128)S(1)} %get-tuple-element.29.refs_2_, f32[256,128]{1,0:T(8,128)S(1)} %get-tuple-element.30.refs_3_, ...), custom_call_target="tpu_custom_call" | custom-call | tf_op jit(solution)/shard_map/pallas_call | solution.py:749
  23.0 2.4 %collective-permute-start.6 = (f32[256,128]{1,0:T(8,128)S(1)}, f32[256,128]{1,0:T(8,128)S(1)}, u32[]{:S(2)}, u32[]{:S(2)}) collective-permute-start(f32[256,128]{1,0:T(8,128)S(1)} %get-tuple-element.35.sent_ref), channel_id=1, source_target_pairs={{2,0},{3,2},{0,1},{1,3},{6,4},{7,6},{4,5},{5,7},{10,8},{11,10},{8,... | collective-permute-start | bytes 393224 | tf_op jit(solution)/shard_map/ppermute | solution.py:791
  25.4 1.1 %collective-permute-start.7 = (f32[256,128]{1,0:T(8,128)S(1)}, f32[256,128]{1,0:T(8,128)S(1)}, u32[]{:S(2)}, u32[]{:S(2)}) collective-permute-start(f32[256,128]{1,0:T(8,128)S(1)} %get-tuple-element.34.kept_ref), channel_id=1, source_target_pairs={{1,0},{0,2},{3,1},{2,3},{5,4},{4,6},{7,5},{6,7},{9,8},{8,10},{11,9... | collective-permute-start | bytes 393224 | tf_op jit(solution)/shard_map/ppermute | solution.py:791
  26.5 3.9 %collective-permute-done.6.came0_ref = f32[256,128]{1,0:T(8,128)S(1)} collective-permute-done((f32[256,128]{1,0:T(8,128)S(1)}, f32[256,128]{1,0:T(8,128)S(1)}, u32[]{:S(2)}, u32[]{:S(2)}) %collective-permute-start.6) | collective-permute-done | bytes 131104 | tf_op jit(solution)/shard_map/ppermute | solution.py:791
  30.4 2.7 %collective-permute-done.7.came1_ref = f32[256,128]{1,0:T(8,128)S(1)} collective-permute-done((f32[256,128]{1,0:T(8,128)S(1)}, f32[256,128]{1,0:T(8,128)S(1)}, u32[]{:S(2)}, u32[]{:S(2)}) %collective-permute-start.7) | collective-permute-done | bytes 131104 | tf_op jit(solution)/shard_map/ppermute | solution.py:791
  33.1 0.9 %shard_map.24 = (f32[256,128]{1,0:T(8,128)S(1)}, f32[256,128]{1,0:T(8,128)S(1)}, f32[256,128]{1,0:T(8,128)S(1)}, f32[256,128]{1,0:T(8,128)S(1)}, f32[96,128]{1,0:T(8,128)S(1)}) custom-call(f32[256,128]{1,0:T(8,128)S(1)} %get-tuple-element.34.kept_ref, f32[256,128]{1,0:T(8,128)S(1)} %get-tuple-element.35.sent_ref, ...), custom_call_target="tpu_custom_call" | custom-call | tf_op jit(solution)/shard_map/pallas_call | solution.py:749
  34.1 0.9 %shard_map.25 = f32[96,128]{1,0:T(8,128)S(1)} custom-call(f32[256,128]{1,0:T(8,128)S(1)} %get-tuple-element.36.refs_0_.even_ref, f32[256,128]{1,0:T(8,128)S(1)} %get-tuple-element.37.refs_1_.odd_ref, f32[256,128]{1,0:T(8,128)S(1)} %get-tuple-element.38.refs_2_, f32[256,128]{1,0:T(8,128)S(1)} %get-tuple-element.39.refs_3_), custom_call_target="tpu_custom_call" | custom-call | tf_op jit(solution)/shard_map/pallas_call | solution.py:749
  35.3 0.6 %collective-permute-start.10 = (f32[96,128]{1,0:T(8,128)S(1)}, f32[96,128]{1,0:T(8,128)S(1)}, u32[]{:S(2)}, u32[]{:S(2)}) collective-permute-start(f32[96,128]{1,0:T(8,128)S(1)} %add.7.refs_0_), channel_id=1, source_target_pairs={{0,16},{4,20},{8,24},{12,28},{16,0},{20,4},{24,8},{28,12},{1,17},{... | collective-permute-start | bytes 147464 | tf_op jit(solution)/shard_map/ppermute | solution.py:732
  35.9 1.5 %collective-permute-start.11 = (f32[96,128]{1,0:T(8,128)S(1)}, f32[96,128]{1,0:T(8,128)S(1)}, u32[]{:S(2)}, u32[]{:S(2)}) collective-permute-start(f32[96,128]{1,0:T(8,128)S(1)} %add.7.refs_0_), channel_id=1, source_target_pairs={{0,24},{4,28},{8,16},{12,20},{16,8},{20,12},{24,0},{28,4},{1,25},{... | collective-permute-start | bytes 147464 | tf_op jit(solution)/shard_map/ppermute | solution.py:732
  37.4 1.5 %collective-permute-start.9 = (f32[96,128]{1,0:T(8,128)S(1)}, f32[96,128]{1,0:T(8,128)S(1)}, u32[]{:S(2)}, u32[]{:S(2)}) collective-permute-start(f32[96,128]{1,0:T(8,128)S(1)} %add.7.refs_0_), channel_id=1, source_target_pairs={{0,8},{4,12},{8,0},{12,4},{16,24},{20,28},{24,16},{28,20},{1,9},{5... | collective-permute-start | bytes 147464 | tf_op jit(solution)/shard_map/ppermute | solution.py:732
  38.9 1.1 %collective-permute-done.10.refs_2_ = f32[96,128]{1,0:T(8,128)S(1)} collective-permute-done((f32[96,128]{1,0:T(8,128)S(1)}, f32[96,128]{1,0:T(8,128)S(1)}, u32[]{:S(2)}, u32[]{:S(2)}) %collective-permute-start.10) | collective-permute-done | bytes 49184 | tf_op jit(solution)/shard_map/ppermute | solution.py:732
  40.0 0.9 %collective-permute-done.11.refs_3_ = f32[96,128]{1,0:T(8,128)S(1)} collective-permute-done((f32[96,128]{1,0:T(8,128)S(1)}, f32[96,128]{1,0:T(8,128)S(1)}, u32[]{:S(2)}, u32[]{:S(2)}) %collective-permute-start.11) | collective-permute-done | bytes 49184 | tf_op jit(solution)/shard_map/ppermute | solution.py:732
  40.9 0.6 %collective-permute-done.9.refs_1_ = f32[96,128]{1,0:T(8,128)S(1)} collective-permute-done((f32[96,128]{1,0:T(8,128)S(1)}, f32[96,128]{1,0:T(8,128)S(1)}, u32[]{:S(2)}, u32[]{:S(2)}) %collective-permute-start.9) | collective-permute-done | bytes 49184 | tf_op jit(solution)/shard_map/ppermute | solution.py:732
  41.5 1.0 %shard_map.26.found_ref.refs_4_ = f32[176,128]{1,0:T(8,128)S(1)} custom-call(f32[96,128]{1,0:T(8,128)S(1)} %add.7.refs_0_, f32[96,128]{1,0:T(8,128)S(1)} %collective-permute-done.9.refs_1_, f32[96,128]{1,0:T(8,128)S(1)} %collective-permute-done.10.refs_2_, f32[96,128]{1,0:T(8,128)S(1)} %collective-permute-done.11.refs_3_), custom_call_target="tpu_custom_call" | custom-call | tf_op jit(solution)/shard_map/pallas_call | solution.py:749
  42.7 0.7 %shard_map.27 = (f32[256,128]{1,0:T(8,128)S(1)}, f32[256,128]{1,0:T(8,128)S(1)}) custom-call(f32[256,128]{1,0:T(8,128)S(1)} %get-tuple-element.36.refs_0_.even_ref, f32[256,128]{1,0:T(8,128)S(1)} %get-tuple-element.37.refs_1_.odd_ref, f32[176,128]{1,0:T(8,128)S(1)} %shard_map.26.found_ref.refs_4_), custom_call_target="tpu_custom_call" | custom-call | tf_op jit(solution)/shard_map/pallas_call | solution.py:749
  43.9 1.6 %shard_map.28 = (f32[256,128]{1,0:T(8,128)S(1)}, f32[256,128]{1,0:T(8,128)S(1)}) custom-call(f32[256,128]{1,0:T(8,128)S(1)} %get-tuple-element.41.refs_0_, f32[256,128]{1,0:T(8,128)S(1)} %get-tuple-element.42.refs_1_, f32[256,128]{1,0:T(8,128)S(1)} %get-tuple-element.38.refs_2_, f32[256,128]{1,0:T(8,128)S(1)} %get-tuple-element.39.refs_3_, ...), custom_call_target="tpu_custom_call" | custom-call | tf_op jit(solution)/shard_map/pallas_call | solution.py:749
  45.5 1.8 %collective-permute-start.13 = (f32[256,128]{1,0:T(8,128)S(1)}, f32[256,128]{1,0:T(8,128)S(1)}, u32[]{:S(2)}, u32[]{:S(2)}) collective-permute-start(f32[256,128]{1,0:T(8,128)S(1)} %get-tuple-element.43), channel_id=1, source_target_pairs={{2,0},{0,1},{3,2},{1,3},{6,4},{4,5},{7,6},{5,7},{10,8},{8,9},{11,1... | collective-permute-start | bytes 393224 | tf_op jit(solution)/shard_map/ppermute | solution.py:797
  47.3 4.7 %collective-permute-done.13 = f32[256,128]{1,0:T(8,128)S(1)} collective-permute-done((f32[256,128]{1,0:T(8,128)S(1)}, f32[256,128]{1,0:T(8,128)S(1)}, u32[]{:S(2)}, u32[]{:S(2)}) %collective-permute-start.13) | collective-permute-done | bytes 131104 | tf_op jit(solution)/shard_map/ppermute | solution.py:797
  52.0 0.7 %pad_maximum_fusion = f32[256,256]{1,0:T(8,128)} fusion(f32[256,128]{1,0:T(8,128)S(1)} %get-tuple-element.46, f32[256,128]{1,0:T(8,128)S(1)} %get-tuple-element.45), kind=kLoop, calls=%fused_computation | loop fusion | flops 65536 | bytes 524288 | tf_op jit(solution)/shard_map/concatenate | solution.py:801
  (14 shorter events, 2.3 us)
Async XLA Ops:
  0.0 0.9 %copy-start = (f32[256,256]{1,0:T(8,128)S(1)}, f32[256,256]{1,0:T(8,128)}, u32[]{:S(2)}) copy-start(f32[256,256]{1,0:T(8,128)} %basis_ref.3) | copy-start | bytes 786436
  1.1 7.5 %collective-permute-start = (f32[320,128]{1,0:T(8,128)S(1)}, f32[320,128]{1,0:T(8,128)S(1)}, u32[]{:S(2)}, u32[]{:S(2)}) collective-permute-start(f32[320,128]{1,0:T(8,128)S(1)} %shard_map.18), channel_id=1, source_target_pairs={{1,0},{0,2},{3,1},{2,3},{5,4},{4,6},{7,5},{6,7},{9,8},{8,10},{11,9... | collective-permute-start | bytes 491528 | tf_op jit(solution)/shard_map/ppermute | solution.py:784
  9.7 1.3 %collective-permute-start.1 = (f32[96,128]{1,0:T(8,128)S(1)}, f32[96,128]{1,0:T(8,128)S(1)}, u32[]{:S(2)}, u32[]{:S(2)}) collective-permute-start(f32[96,128]{1,0:T(8,128)S(1)} %get-tuple-element.31), channel_id=1, source_target_pairs={{0,4},{4,0},{8,12},{12,8},{16,20},{20,16},{24,28},{28,24},{1,5},{5... | collective-permute-start | bytes 147464 | tf_op jit(solution)/shard_map/ppermute | solution.py:732
  11.0 4.2 %collective-permute-start.2 = (f32[96,128]{1,0:T(8,128)S(1)}, f32[96,128]{1,0:T(8,128)S(1)}, u32[]{:S(2)}, u32[]{:S(2)}) collective-permute-start(f32[96,128]{1,0:T(8,128)S(1)} %add.6.refs_0_), channel_id=1, source_target_pairs={{0,8},{4,12},{8,0},{12,4},{16,24},{20,28},{24,16},{28,20},{1,9},{5... | collective-permute-start | bytes 147464 | tf_op jit(solution)/shard_map/ppermute | solution.py:732
  12.5 4.1 %collective-permute-start.3 = (f32[96,128]{1,0:T(8,128)S(1)}, f32[96,128]{1,0:T(8,128)S(1)}, u32[]{:S(2)}, u32[]{:S(2)}) collective-permute-start(f32[96,128]{1,0:T(8,128)S(1)} %add.6.refs_0_), channel_id=1, source_target_pairs={{0,16},{4,20},{8,24},{12,28},{16,0},{20,4},{24,8},{28,12},{1,17},{... | collective-permute-start | bytes 147464 | tf_op jit(solution)/shard_map/ppermute | solution.py:732
  14.1 5.0 %collective-permute-start.4 = (f32[96,128]{1,0:T(8,128)S(1)}, f32[96,128]{1,0:T(8,128)S(1)}, u32[]{:S(2)}, u32[]{:S(2)}) collective-permute-start(f32[96,128]{1,0:T(8,128)S(1)} %add.6.refs_0_), channel_id=1, source_target_pairs={{0,24},{4,28},{8,16},{12,20},{16,8},{20,12},{24,0},{28,4},{1,25},{... | collective-permute-start | bytes 147464 | tf_op jit(solution)/shard_map/ppermute | solution.py:732
  20.1 1.4 %collective-permute-start.5 = (f32[176,128]{1,0:T(8,128)S(1)}, f32[176,128]{1,0:T(8,128)S(1)}, u32[]{:S(2)}, u32[]{:S(2)}) collective-permute-start(f32[176,128]{1,0:T(8,128)S(1)} %shard_map.21.found_ref.refs_4_), channel_id=1, source_target_pairs={{0,4},{4,0},{8,12},{12,8},{16,20},{20,16},{24,28},{28,24},{1,5},{5... | collective-permute-start | bytes 270344 | tf_op jit(solution)/shard_map/ppermute | solution.py:732
  23.0 7.4 %collective-permute-start.6 = (f32[256,128]{1,0:T(8,128)S(1)}, f32[256,128]{1,0:T(8,128)S(1)}, u32[]{:S(2)}, u32[]{:S(2)}) collective-permute-start(f32[256,128]{1,0:T(8,128)S(1)} %get-tuple-element.35.sent_ref), channel_id=1, source_target_pairs={{2,0},{3,2},{0,1},{1,3},{6,4},{7,6},{4,5},{5,7},{10,8},{11,10},{8,... | collective-permute-start | bytes 393224 | tf_op jit(solution)/shard_map/ppermute | solution.py:791
  25.4 7.6 %collective-permute-start.7 = (f32[256,128]{1,0:T(8,128)S(1)}, f32[256,128]{1,0:T(8,128)S(1)}, u32[]{:S(2)}, u32[]{:S(2)}) collective-permute-start(f32[256,128]{1,0:T(8,128)S(1)} %get-tuple-element.34.kept_ref), channel_id=1, source_target_pairs={{1,0},{0,2},{3,1},{2,3},{5,4},{4,6},{7,5},{6,7},{9,8},{8,10},{11,9... | collective-permute-start | bytes 393224 | tf_op jit(solution)/shard_map/ppermute | solution.py:791
  34.0 1.3 %collective-permute-start.8 = (f32[96,128]{1,0:T(8,128)S(1)}, f32[96,128]{1,0:T(8,128)S(1)}, u32[]{:S(2)}, u32[]{:S(2)}) collective-permute-start(f32[96,128]{1,0:T(8,128)S(1)} %get-tuple-element.40), channel_id=1, source_target_pairs={{0,4},{4,0},{8,12},{12,8},{16,20},{20,16},{24,28},{28,24},{1,5},{5... | collective-permute-start | bytes 147464 | tf_op jit(solution)/shard_map/ppermute | solution.py:732
  35.3 4.7 %collective-permute-start.10 = (f32[96,128]{1,0:T(8,128)S(1)}, f32[96,128]{1,0:T(8,128)S(1)}, u32[]{:S(2)}, u32[]{:S(2)}) collective-permute-start(f32[96,128]{1,0:T(8,128)S(1)} %add.7.refs_0_), channel_id=1, source_target_pairs={{0,16},{4,20},{8,24},{12,28},{16,0},{20,4},{24,8},{28,12},{1,17},{... | collective-permute-start | bytes 147464 | tf_op jit(solution)/shard_map/ppermute | solution.py:732
  35.9 5.0 %collective-permute-start.11 = (f32[96,128]{1,0:T(8,128)S(1)}, f32[96,128]{1,0:T(8,128)S(1)}, u32[]{:S(2)}, u32[]{:S(2)}) collective-permute-start(f32[96,128]{1,0:T(8,128)S(1)} %add.7.refs_0_), channel_id=1, source_target_pairs={{0,24},{4,28},{8,16},{12,20},{16,8},{20,12},{24,0},{28,4},{1,25},{... | collective-permute-start | bytes 147464 | tf_op jit(solution)/shard_map/ppermute | solution.py:732
  37.4 4.1 %collective-permute-start.9 = (f32[96,128]{1,0:T(8,128)S(1)}, f32[96,128]{1,0:T(8,128)S(1)}, u32[]{:S(2)}, u32[]{:S(2)}) collective-permute-start(f32[96,128]{1,0:T(8,128)S(1)} %add.7.refs_0_), channel_id=1, source_target_pairs={{0,8},{4,12},{8,0},{12,4},{16,24},{20,28},{24,16},{28,20},{1,9},{5... | collective-permute-start | bytes 147464 | tf_op jit(solution)/shard_map/ppermute | solution.py:732
  42.6 1.4 %collective-permute-start.12 = (f32[176,128]{1,0:T(8,128)S(1)}, f32[176,128]{1,0:T(8,128)S(1)}, u32[]{:S(2)}, u32[]{:S(2)}) collective-permute-start(f32[176,128]{1,0:T(8,128)S(1)} %shard_map.26.found_ref.refs_4_), channel_id=1, source_target_pairs={{0,4},{4,0},{8,12},{12,8},{16,20},{20,16},{24,28},{28,24},{1,5},{5... | collective-permute-start | bytes 270344 | tf_op jit(solution)/shard_map/ppermute | solution.py:732
  45.5 6.5 %collective-permute-start.13 = (f32[256,128]{1,0:T(8,128)S(1)}, f32[256,128]{1,0:T(8,128)S(1)}, u32[]{:S(2)}, u32[]{:S(2)}) collective-permute-start(f32[256,128]{1,0:T(8,128)S(1)} %get-tuple-element.43), channel_id=1, source_target_pairs={{2,0},{0,1},{3,2},{1,3},{6,4},{4,5},{7,6},{5,7},{10,8},{8,9},{11,1... | collective-permute-start | bytes 393224 | tf_op jit(solution)/shard_map/ppermute | solution.py:797

commit v14 on v13

--- a/solution.py
+++ b/solution.py
@@ -600,32 +600,34 @@
         part_ref[q * PACKED : (q + 1) * PACKED, :] = band
 
 
-def open_pairs(is_second, x, y, column_refs, other_ref):
+def open_pairs(is_second, x, y, column_refs, corner_ref, other_ref):
+    corner = cross_partial(*x, *y, among(is_second[0]), among(is_second[1]))
     flag = on_odd_core()
     mine = [jnp.where(flag, b, a) for a, b in zip(x, y)]
     theirs = [jnp.where(flag, a, b) for a, b in zip(x, y)]
     for ref, value in zip(column_refs, mine + theirs):
         ref[...] = value
     store_part(*theirs, either(flag, among(is_second[0]), among(is_second[1])), other_ref)
-    other_ref[4 * PACKED :, :] = jnp.zeros((WINDOW, theirs[0].shape[1]), jnp.float32)
+    corner_ref[...] = jnp.where(flag, corner[NEAR:], corner[:NEAR])
+    other_ref[4 * PACKED :, :] = jnp.where(flag, corner[:NEAR], corner[NEAR:])
 
 
 def first_open(own_second, gets_second, is_second, even_ref, odd_ref, payload_ref, *refs):
-    *column_refs, other_ref = refs
+    *column_refs, corner_ref, other_ref = refs
     own = even_ref[...], odd_ref[...]
     came = unpacked(payload_ref[...], own[0].shape[0], among(gets_second))
     flag = among(own_second)
     x = [jnp.where(flag, b, a) for a, b in zip(own, came)]
     y = [jnp.where(flag, a, b) for a, b in zip(own, came)]
-    open_pairs(is_second, x, y, column_refs, other_ref)
+    open_pairs(is_second, x, y, column_refs, corner_ref, other_ref)
 
 
 def fused_open(picks, is_second, kept_ref, sent_ref, came0_ref, came1_ref, *refs):
-    *column_refs, other_ref = refs
+    *column_refs, corner_ref, other_ref = refs
     arrays = [ref[...] for ref in (sent_ref, kept_ref, came0_ref, came1_ref)]
     blocks = [choose(pick, arrays) for pick in picks]
     x, y = split_pair(*blocks[:2]), split_pair(*blocks[2:])
-    open_pairs(is_second, x, y, column_refs, other_ref)
+    open_pairs(is_second, x, y, column_refs, corner_ref, other_ref)
 
 
 def swapped_flag(is_second):
@@ -637,15 +639,9 @@
     return either(on_odd_core(), among(is_second[1]), among(is_second[0]))
 
 
-def bands_kernel(is_second, *refs):
-    *column_refs, part_ref = refs
-    columns = [ref[...] for ref in column_refs]
-    store_part(*columns[:2], own_second_flag(is_second), part_ref)
-    flag = on_odd_core()
-    x = [jnp.where(flag, b, a) for a, b in zip(columns[:2], columns[2:])]
-    y = [jnp.where(flag, a, b) for a, b in zip(columns[:2], columns[2:])]
-    corner = cross_partial(*x, *y, among(is_second[0]), among(is_second[1]))
-    part_ref[4 * PACKED :, :] = corner
+def bands_kernel(is_second, even_ref, odd_ref, corner_ref, part_ref):
+    store_part(even_ref[...], odd_ref[...], own_second_flag(is_second), part_ref)
+    part_ref[4 * PACKED :, :] = corner_ref[...]
 
 
 def angles_kernel(is_second, *refs):
@@ -668,7 +664,7 @@
 
 
 CORNER = NEAR + 4 * DIAGS
-ROTATION = CORNER + WINDOW
+ROTATION = CORNER + NEAR
 FOUND = ROTATION + 2 * WINDOW
 
 
@@ -685,7 +681,7 @@
 
 
 def next_bands(x_found, y_found, x_second, y_second):
-    corner = x_found[CORNER:ROTATION] + y_found[CORNER:ROTATION]
+    corner = jnp.concatenate((x_found[CORNER:ROTATION], y_found[CORNER:ROTATION]), axis=0)
     middle = cross_bands(corner, x_found[ROTATION:], y_found[ROTATION:])
     half = corner.shape[1] // 2
     lane = lanes_of(middle[0])
@@ -754,11 +750,11 @@
 
 
 def two_rounds(opened, is_second, sends_first, layout_of):
-    *columns, other = opened
+    *columns, corner, other = opened
     column, width = columns[0].shape, columns[0].shape[1]
     other = swap(other, "row", 1)
     bands = functools.partial(bands_kernel, is_second)
-    (mine,) = call(bands, (other.shape,), *columns)
+    (mine,) = call(bands, (other.shape,), *columns[:2], corner)
     (found,) = call(
         functools.partial(angles_kernel, is_second),
         ((FOUND, width),),
@@ -776,7 +772,7 @@
     width = cols // 2
     pair_total = lax.axis_size("pair")
     column = (rows, width)
-    opened = (column,) * 4 + ((4 * PACKED + WINDOW, width),)
+    opened = (column,) * 4 + ((NEAR, width), (4 * PACKED + NEAR, width))
     payload = (rows + rows * 2 * STRIP // width, width)
 
     sends, sends_second, gets_second, own_second, is_second = first_moves(pair_total)

time: 52.9 us -> 53 us (level)
  transfers between devices with their start and end apart: 14 -> 14, of which waited for: 14 -> 14; matrix products, arithmetic and copies ran while one was open for 0% -> 0% of each run, Pallas kernels for 7% -> 6%
where the time goes in v14:
time: 53 us; the launch traced here: 52.9 us
  waiting for transfers between devices  23.4 us (44%)
  starting transfers between devices  16.6 us (31%)
  Pallas kernels  11 us (21%)
  local copies, waits for them, and re-layouts  0.95 us (2%)
  other arithmetic  0.75 us (1%)
    pallas_call x12, Pallas kernels, call(): pl.pallas_call(kernel, out_shape=out, compiler_params=pltpu.CompilerParam...  11 us
    ppermute x10, waiting for transfers between devices, swap(): lax.ppermute(x, axis, [(i, i ^ mask) for i in range(lax.axis_size(axis))])  8.91 us
    ppermute x2, waiting for transfers between devices, per_device(): came = lax.ppermute(sent, 'pair', sends)  7.96 us
    ppermute x10, starting transfers between devices, swap(): lax.ppermute(x, axis, [(i, i ^ mask) for i in range(lax.axis_size(axis))])  7.24 us
    ppermute x2, waiting for transfers between devices, per_device(): came = [lax.ppermute(x, 'pair', s) for x, s in zip((sent, kept), sends)]  6.56 us
    ppermute x2, starting transfers between devices, per_device(): came = lax.ppermute(sent, 'pair', sends)  5.88 us
    ppermute x2, starting transfers between devices, per_device(): came = [lax.ppermute(x, 'pair', s) for x, s in zip((sent, kept), sends)]  3.5 us
  transfers between devices with their start and end apart: 14, of which 14 were waited for; matrix products, arithmetic and copies ran while one was open for 0% of the time, Pallas kernels for 6%

profile of v14, /device:TPU:0, one launch (start us, length us, event | category | flops | bytes accessed | tf_op | source)
XLA Modules:
  0.0 52.9 jit_solution(3215907785435237279)
XLA Ops:
  0.0 0.9 %copy-done = f32[256,256]{1,0:T(8,128)S(1)} copy-done((f32[256,256]{1,0:T(8,128)S(1)}, f32[256,256]{1,0:T(8,128)}, u32[]{:S(2)}) %copy-start) | copy-done | bytes 262168
  1.1 4.1 %collective-permute-start = (f32[320,128]{1,0:T(8,128)S(1)}, f32[320,128]{1,0:T(8,128)S(1)}, u32[]{:S(2)}, u32[]{:S(2)}) collective-permute-start(f32[320,128]{1,0:T(8,128)S(1)} %shard_map.18), channel_id=1, source_target_pairs={{1,0},{0,2},{3,1},{2,3},{5,4},{4,6},{7,5},{6,7},{9,8},{8,10},{11,9... | collective-permute-start | bytes 491528 | tf_op jit(solution)/shard_map/ppermute | solution.py:780
  5.4 3.2 %collective-permute-done.payload_ref = f32[320,128]{1,0:T(8,128)S(1)} collective-permute-done((f32[320,128]{1,0:T(8,128)S(1)}, f32[320,128]{1,0:T(8,128)S(1)}, u32[]{:S(2)}, u32[]{:S(2)}) %collective-permute-start) | collective-permute-done | bytes 163872 | tf_op jit(solution)/shard_map/ppermute | solution.py:780
  8.7 1.2 %shard_map.19 = (f32[256,128]{1,0:T(8,128)S(1)}, f32[256,128]{1,0:T(8,128)S(1)}, f32[256,128]{1,0:T(8,128)S(1)}, f32[256,128]{1,0:T(8,128)S(1)}, f32[16,128]{1,0:T(8,128)S(1)}, /*index=5*/f32[80,128]{1,0:T(8,128)S(1)}) custom-call(f32[256,128]{1,0:T(8,128)S(1)} %get-tuple-element.27.even_ref, f32[256,128]{1,0:T(8,128)S(1)} %get-tuple-element.28.odd_ref, ...), custom_call_target="tpu_custom_call" | custom-call | tf_op jit(solution)/shard_map/pallas_call | solution.py:745
  10.0 0.8 %shard_map.20 = f32[80,128]{1,0:T(8,128)S(1)} custom-call(f32[256,128]{1,0:T(8,128)S(1)} %get-tuple-element.29.even_ref, f32[256,128]{1,0:T(8,128)S(1)} %get-tuple-element.30.odd_ref, f32[16,128]{1,0:T(8,128)S(1)} %get-tuple-element.31.corner_ref), custom_call_target="tpu_custom_call" | custom-call | tf_op jit(solution)/shard_map/pallas_call | solution.py:745
  11.2 1.5 %collective-permute-start.2 = (f32[80,128]{1,0:T(8,128)S(1)}, f32[80,128]{1,0:T(8,128)S(1)}, u32[]{:S(2)}, u32[]{:S(2)}) collective-permute-start(f32[80,128]{1,0:T(8,128)S(1)} %add.6.refs_0_), channel_id=1, source_target_pairs={{0,8},{4,12},{8,0},{12,4},{16,24},{20,28},{24,16},{28,20},{1,9},{5... | collective-permute-start | bytes 122888 | tf_op jit(solution)/shard_map/ppermute | solution.py:728
  12.7 1.5 %collective-permute-start.3 = (f32[80,128]{1,0:T(8,128)S(1)}, f32[80,128]{1,0:T(8,128)S(1)}, u32[]{:S(2)}, u32[]{:S(2)}) collective-permute-start(f32[80,128]{1,0:T(8,128)S(1)} %add.6.refs_0_), channel_id=1, source_target_pairs={{0,16},{4,20},{8,24},{12,28},{16,0},{20,4},{24,8},{28,12},{1,17},{... | collective-permute-start | bytes 122888 | tf_op jit(solution)/shard_map/ppermute | solution.py:728
  14.7 0.5 collective-permute-done.2.refs_1_
  15.2 1.5 %collective-permute-done.3.refs_2_ = f32[80,128]{1,0:T(8,128)S(1)} collective-permute-done((f32[80,128]{1,0:T(8,128)S(1)}, f32[80,128]{1,0:T(8,128)S(1)}, u32[]{:S(2)}, u32[]{:S(2)}) %collective-permute-start.3) | collective-permute-done | bytes 40992 | tf_op jit(solution)/shard_map/ppermute | solution.py:728
  16.7 2.4 %collective-permute-done.4.refs_3_ = f32[80,128]{1,0:T(8,128)S(1)} collective-permute-done((f32[80,128]{1,0:T(8,128)S(1)}, f32[80,128]{1,0:T(8,128)S(1)}, u32[]{:S(2)}, u32[]{:S(2)}) %collective-permute-start.4) | collective-permute-done | bytes 40992 | tf_op jit(solution)/shard_map/ppermute | solution.py:728
  19.1 1.0 %shard_map.21.found_ref.refs_4_ = f32[160,128]{1,0:T(8,128)S(1)} custom-call(f32[80,128]{1,0:T(8,128)S(1)} %add.6.refs_0_, f32[80,128]{1,0:T(8,128)S(1)} %collective-permute-done.2.refs_1_, f32[80,128]{1,0:T(8,128)S(1)} %collective-permute-done.3.refs_2_, f32[80,128]{1,0:T(8,128)S(1)} %collective-permute-done.4.refs_3_), custom_call_target="tpu_custom_call" | custom-call | tf_op jit(solution)/shard_map/pallas_call | solution.py:745
  20.2 0.7 %shard_map.22 = (f32[256,128]{1,0:T(8,128)S(1)}, f32[256,128]{1,0:T(8,128)S(1)}) custom-call(f32[256,128]{1,0:T(8,128)S(1)} %get-tuple-element.29.even_ref, f32[256,128]{1,0:T(8,128)S(1)} %get-tuple-element.30.odd_ref, f32[160,128]{1,0:T(8,128)S(1)} %shard_map.21.found_ref.refs_4_), custom_call_target="tpu_custom_call" | custom-call | tf_op jit(solution)/shard_map/pallas_call | solution.py:745
  21.0 0.6 %collective-permute-done.5.refs_5_ = f32[160,128]{1,0:T(8,128)S(1)} collective-permute-done((f32[160,128]{1,0:T(8,128)S(1)}, f32[160,128]{1,0:T(8,128)S(1)}, u32[]{:S(2)}, u32[]{:S(2)}) %collective-permute-start.5) | collective-permute-done | bytes 81952 | tf_op jit(solution)/shard_map/ppermute | solution.py:728
  21.5 1.6 %shard_map.23 = (f32[256,128]{1,0:T(8,128)S(1)}, f32[256,128]{1,0:T(8,128)S(1)}) custom-call(f32[256,128]{1,0:T(8,128)S(1)} %get-tuple-element.33.refs_0_, f32[256,128]{1,0:T(8,128)S(1)} %get-tuple-element.34.refs_1_, f32[256,128]{1,0:T(8,128)S(1)} %get-tuple-element.35.refs_2_, f32[256,128]{1,0:T(8,128)S(1)} %get-tuple-element.36.refs_3_, ...), custom_call_target="tpu_custom_call" | custom-call | tf_op jit(solution)/shard_map/pallas_call | solution.py:745
  23.1 2.4 %collective-permute-start.6 = (f32[256,128]{1,0:T(8,128)S(1)}, f32[256,128]{1,0:T(8,128)S(1)}, u32[]{:S(2)}, u32[]{:S(2)}) collective-permute-start(f32[256,128]{1,0:T(8,128)S(1)} %get-tuple-element.38.sent_ref), channel_id=1, source_target_pairs={{2,0},{3,2},{0,1},{1,3},{6,4},{7,6},{4,5},{5,7},{10,8},{11,10},{8,... | collective-permute-start | bytes 393224 | tf_op jit(solution)/shard_map/ppermute | solution.py:787
  25.5 1.1 %collective-permute-start.7 = (f32[256,128]{1,0:T(8,128)S(1)}, f32[256,128]{1,0:T(8,128)S(1)}, u32[]{:S(2)}, u32[]{:S(2)}) collective-permute-start(f32[256,128]{1,0:T(8,128)S(1)} %get-tuple-element.37.kept_ref), channel_id=1, source_target_pairs={{1,0},{0,2},{3,1},{2,3},{5,4},{4,6},{7,5},{6,7},{9,8},{8,10},{11,9... | collective-permute-start | bytes 393224 | tf_op jit(solution)/shard_map/ppermute | solution.py:787
  26.6 3.9 %collective-permute-done.6.came0_ref = f32[256,128]{1,0:T(8,128)S(1)} collective-permute-done((f32[256,128]{1,0:T(8,128)S(1)}, f32[256,128]{1,0:T(8,128)S(1)}, u32[]{:S(2)}, u32[]{:S(2)}) %collective-permute-start.6) | collective-permute-done | bytes 131104 | tf_op jit(solution)/shard_map/ppermute | solution.py:787
  30.5 2.7 %collective-permute-done.7.came1_ref = f32[256,128]{1,0:T(8,128)S(1)} collective-permute-done((f32[256,128]{1,0:T(8,128)S(1)}, f32[256,128]{1,0:T(8,128)S(1)}, u32[]{:S(2)}, u32[]{:S(2)}) %collective-permute-start.7) | collective-permute-done | bytes 131104 | tf_op jit(solution)/shard_map/ppermute | solution.py:787
  33.2 1.2 %shard_map.24 = (f32[256,128]{1,0:T(8,128)S(1)}, f32[256,128]{1,0:T(8,128)S(1)}, f32[256,128]{1,0:T(8,128)S(1)}, f32[256,128]{1,0:T(8,128)S(1)}, f32[16,128]{1,0:T(8,128)S(1)}, /*index=5*/f32[80,128]{1,0:T(8,128)S(1)}) custom-call(f32[256,128]{1,0:T(8,128)S(1)} %get-tuple-element.37.kept_ref, f32[256,128]{1,0:T(8,128)S(1)} %get-tuple-element.38.sent_ref, ...), custom_call_target="tpu_custom_call" | custom-call | tf_op jit(solution)/shard_map/pallas_call | solution.py:745
  34.4 0.8 %shard_map.25 = f32[80,128]{1,0:T(8,128)S(1)} custom-call(f32[256,128]{1,0:T(8,128)S(1)} %get-tuple-element.39.even_ref, f32[256,128]{1,0:T(8,128)S(1)} %get-tuple-element.40.odd_ref, f32[16,128]{1,0:T(8,128)S(1)} %get-tuple-element.41.corner_ref), custom_call_target="tpu_custom_call" | custom-call | tf_op jit(solution)/shard_map/pallas_call | solution.py:745
  36.1 1.5 %collective-permute-start.11 = (f32[80,128]{1,0:T(8,128)S(1)}, f32[80,128]{1,0:T(8,128)S(1)}, u32[]{:S(2)}, u32[]{:S(2)}) collective-permute-start(f32[80,128]{1,0:T(8,128)S(1)} %add.7.refs_0_), channel_id=1, source_target_pairs={{0,24},{4,28},{8,16},{12,20},{16,8},{20,12},{24,0},{28,4},{1,25},{... | collective-permute-start | bytes 122888 | tf_op jit(solution)/shard_map/ppermute | solution.py:728
  37.6 1.5 %collective-permute-start.9 = (f32[80,128]{1,0:T(8,128)S(1)}, f32[80,128]{1,0:T(8,128)S(1)}, u32[]{:S(2)}, u32[]{:S(2)}) collective-permute-start(f32[80,128]{1,0:T(8,128)S(1)} %add.7.refs_0_), channel_id=1, source_target_pairs={{0,8},{4,12},{8,0},{12,4},{16,24},{20,28},{24,16},{28,20},{1,9},{5... | collective-permute-start | bytes 122888 | tf_op jit(solution)/shard_map/ppermute | solution.py:728
  39.1 1.0 %collective-permute-done.10.refs_2_ = f32[80,128]{1,0:T(8,128)S(1)} collective-permute-done((f32[80,128]{1,0:T(8,128)S(1)}, f32[80,128]{1,0:T(8,128)S(1)}, u32[]{:S(2)}, u32[]{:S(2)}) %collective-permute-start.10) | collective-permute-done | bytes 40992 | tf_op jit(solution)/shard_map/ppermute | solution.py:728
  40.1 1.0 %collective-permute-done.11.refs_3_ = f32[80,128]{1,0:T(8,128)S(1)} collective-permute-done((f32[80,128]{1,0:T(8,128)S(1)}, f32[80,128]{1,0:T(8,128)S(1)}, u32[]{:S(2)}, u32[]{:S(2)}) %collective-permute-start.11) | collective-permute-done | bytes 40992 | tf_op jit(solution)/shard_map/ppermute | solution.py:728
  41.0 0.6 %collective-permute-done.9.refs_1_ = f32[80,128]{1,0:T(8,128)S(1)} collective-permute-done((f32[80,128]{1,0:T(8,128)S(1)}, f32[80,128]{1,0:T(8,128)S(1)}, u32[]{:S(2)}, u32[]{:S(2)}) %collective-permute-start.9) | collective-permute-done | bytes 40992 | tf_op jit(solution)/shard_map/ppermute | solution.py:728
  41.6 1.0 %shard_map.26.found_ref.refs_4_ = f32[160,128]{1,0:T(8,128)S(1)} custom-call(f32[80,128]{1,0:T(8,128)S(1)} %add.7.refs_0_, f32[80,128]{1,0:T(8,128)S(1)} %collective-permute-done.9.refs_1_, f32[80,128]{1,0:T(8,128)S(1)} %collective-permute-done.10.refs_2_, f32[80,128]{1,0:T(8,128)S(1)} %collective-permute-done.11.refs_3_), custom_call_target="tpu_custom_call" | custom-call | tf_op jit(solution)/shard_map/pallas_call | solution.py:745
  42.8 0.7 %shard_map.27 = (f32[256,128]{1,0:T(8,128)S(1)}, f32[256,128]{1,0:T(8,128)S(1)}) custom-call(f32[256,128]{1,0:T(8,128)S(1)} %get-tuple-element.39.even_ref, f32[256,128]{1,0:T(8,128)S(1)} %get-tuple-element.40.odd_ref, f32[160,128]{1,0:T(8,128)S(1)} %shard_map.26.found_ref.refs_4_), custom_call_target="tpu_custom_call" | custom-call | tf_op jit(solution)/shard_map/pallas_call | solution.py:745
  43.5 0.6 %collective-permute-done.12.refs_5_ = f32[160,128]{1,0:T(8,128)S(1)} collective-permute-done((f32[160,128]{1,0:T(8,128)S(1)}, f32[160,128]{1,0:T(8,128)S(1)}, u32[]{:S(2)}, u32[]{:S(2)}) %collective-permute-start.12) | collective-permute-done | bytes 81952 | tf_op jit(solution)/shard_map/ppermute | solution.py:728
  44.0 1.6 %shard_map.28 = (f32[256,128]{1,0:T(8,128)S(1)}, f32[256,128]{1,0:T(8,128)S(1)}) custom-call(f32[256,128]{1,0:T(8,128)S(1)} %get-tuple-element.43.refs_0_, f32[256,128]{1,0:T(8,128)S(1)} %get-tuple-element.44.refs_1_, f32[256,128]{1,0:T(8,128)S(1)} %get-tuple-element.45.refs_2_, f32[256,128]{1,0:T(8,128)S(1)} %get-tuple-element.46.refs_3_, ...), custom_call_target="tpu_custom_call" | custom-call | tf_op jit(solution)/shard_map/pallas_call | solution.py:745
  45.6 1.8 %collective-permute-start.13 = (f32[256,128]{1,0:T(8,128)S(1)}, f32[256,128]{1,0:T(8,128)S(1)}, u32[]{:S(2)}, u32[]{:S(2)}) collective-permute-start(f32[256,128]{1,0:T(8,128)S(1)} %get-tuple-element.47), channel_id=1, source_target_pairs={{2,0},{0,1},{3,2},{1,3},{6,4},{4,5},{7,6},{5,7},{10,8},{8,9},{11,1... | collective-permute-start | bytes 393224 | tf_op jit(solution)/shard_map/ppermute | solution.py:793
  47.4 4.7 %collective-permute-done.13 = f32[256,128]{1,0:T(8,128)S(1)} collective-permute-done((f32[256,128]{1,0:T(8,128)S(1)}, f32[256,128]{1,0:T(8,128)S(1)}, u32[]{:S(2)}, u32[]{:S(2)}) %collective-permute-start.13) | collective-permute-done | bytes 131104 | tf_op jit(solution)/shard_map/ppermute | solution.py:793
  52.2 0.7 %pad_maximum_fusion = f32[256,256]{1,0:T(8,128)} fusion(f32[256,128]{1,0:T(8,128)S(1)} %get-tuple-element.50, f32[256,128]{1,0:T(8,128)S(1)} %get-tuple-element.49), kind=kLoop, calls=%fused_computation | loop fusion | flops 65536 | bytes 524288 | tf_op jit(solution)/shard_map/concatenate | solution.py:797
  (14 shorter events, 2.5 us)
Async XLA Ops:
  0.0 0.9 %copy-start = (f32[256,256]{1,0:T(8,128)S(1)}, f32[256,256]{1,0:T(8,128)}, u32[]{:S(2)}) copy-start(f32[256,256]{1,0:T(8,128)} %basis_ref.3) | copy-start | bytes 786436
  1.1 7.5 %collective-permute-start = (f32[320,128]{1,0:T(8,128)S(1)}, f32[320,128]{1,0:T(8,128)S(1)}, u32[]{:S(2)}, u32[]{:S(2)}) collective-permute-start(f32[320,128]{1,0:T(8,128)S(1)} %shard_map.18), channel_id=1, source_target_pairs={{1,0},{0,2},{3,1},{2,3},{5,4},{4,6},{7,5},{6,7},{9,8},{8,10},{11,9... | collective-permute-start | bytes 491528 | tf_op jit(solution)/shard_map/ppermute | solution.py:780
  9.9 1.3 %collective-permute-start.1 = (f32[80,128]{1,0:T(8,128)S(1)}, f32[80,128]{1,0:T(8,128)S(1)}, u32[]{:S(2)}, u32[]{:S(2)}) collective-permute-start(f32[80,128]{1,0:T(8,128)S(1)} %get-tuple-element.32), channel_id=1, source_target_pairs={{0,4},{4,0},{8,12},{12,8},{16,20},{20,16},{24,28},{28,24},{1,5},{5... | collective-permute-start | bytes 122888 | tf_op jit(solution)/shard_map/ppermute | solution.py:728
  11.2 4.0 %collective-permute-start.2 = (f32[80,128]{1,0:T(8,128)S(1)}, f32[80,128]{1,0:T(8,128)S(1)}, u32[]{:S(2)}, u32[]{:S(2)}) collective-permute-start(f32[80,128]{1,0:T(8,128)S(1)} %add.6.refs_0_), channel_id=1, source_target_pairs={{0,8},{4,12},{8,0},{12,4},{16,24},{20,28},{24,16},{28,20},{1,9},{5... | collective-permute-start | bytes 122888 | tf_op jit(solution)/shard_map/ppermute | solution.py:728
  12.7 4.0 %collective-permute-start.3 = (f32[80,128]{1,0:T(8,128)S(1)}, f32[80,128]{1,0:T(8,128)S(1)}, u32[]{:S(2)}, u32[]{:S(2)}) collective-permute-start(f32[80,128]{1,0:T(8,128)S(1)} %add.6.refs_0_), channel_id=1, source_target_pairs={{0,16},{4,20},{8,24},{12,28},{16,0},{20,4},{24,8},{28,12},{1,17},{... | collective-permute-start | bytes 122888 | tf_op jit(solution)/shard_map/ppermute | solution.py:728
  14.2 4.9 %collective-permute-start.4 = (f32[80,128]{1,0:T(8,128)S(1)}, f32[80,128]{1,0:T(8,128)S(1)}, u32[]{:S(2)}, u32[]{:S(2)}) collective-permute-start(f32[80,128]{1,0:T(8,128)S(1)} %add.6.refs_0_), channel_id=1, source_target_pairs={{0,24},{4,28},{8,16},{12,20},{16,8},{20,12},{24,0},{28,4},{1,25},{... | collective-permute-start | bytes 122888 | tf_op jit(solution)/shard_map/ppermute | solution.py:728
  20.2 1.3 %collective-permute-start.5 = (f32[160,128]{1,0:T(8,128)S(1)}, f32[160,128]{1,0:T(8,128)S(1)}, u32[]{:S(2)}, u32[]{:S(2)}) collective-permute-start(f32[160,128]{1,0:T(8,128)S(1)} %shard_map.21.found_ref.refs_4_), channel_id=1, source_target_pairs={{0,4},{4,0},{8,12},{12,8},{16,20},{20,16},{24,28},{28,24},{1,5},{5... | collective-permute-start | bytes 245768 | tf_op jit(solution)/shard_map/ppermute | solution.py:728
  23.1 7.4 %collective-permute-start.6 = (f32[256,128]{1,0:T(8,128)S(1)}, f32[256,128]{1,0:T(8,128)S(1)}, u32[]{:S(2)}, u32[]{:S(2)}) collective-permute-start(f32[256,128]{1,0:T(8,128)S(1)} %get-tuple-element.38.sent_ref), channel_id=1, source_target_pairs={{2,0},{3,2},{0,1},{1,3},{6,4},{7,6},{4,5},{5,7},{10,8},{11,10},{8,... | collective-permute-start | bytes 393224 | tf_op jit(solution)/shard_map/ppermute | solution.py:787
  25.5 7.6 %collective-permute-start.7 = (f32[256,128]{1,0:T(8,128)S(1)}, f32[256,128]{1,0:T(8,128)S(1)}, u32[]{:S(2)}, u32[]{:S(2)}) collective-permute-start(f32[256,128]{1,0:T(8,128)S(1)} %get-tuple-element.37.kept_ref), channel_id=1, source_target_pairs={{1,0},{0,2},{3,1},{2,3},{5,4},{4,6},{7,5},{6,7},{9,8},{8,10},{11,9... | collective-permute-start | bytes 393224 | tf_op jit(solution)/shard_map/ppermute | solution.py:787
  34.3 1.3 %collective-permute-start.8 = (f32[80,128]{1,0:T(8,128)S(1)}, f32[80,128]{1,0:T(8,128)S(1)}, u32[]{:S(2)}, u32[]{:S(2)}) collective-permute-start(f32[80,128]{1,0:T(8,128)S(1)} %get-tuple-element.42), channel_id=1, source_target_pairs={{0,4},{4,0},{8,12},{12,8},{16,20},{20,16},{24,28},{28,24},{1,5},{5... | collective-permute-start | bytes 122888 | tf_op jit(solution)/shard_map/ppermute | solution.py:728
  35.6 4.4 %collective-permute-start.10 = (f32[80,128]{1,0:T(8,128)S(1)}, f32[80,128]{1,0:T(8,128)S(1)}, u32[]{:S(2)}, u32[]{:S(2)}) collective-permute-start(f32[80,128]{1,0:T(8,128)S(1)} %add.7.refs_0_), channel_id=1, source_target_pairs={{0,16},{4,20},{8,24},{12,28},{16,0},{20,4},{24,8},{28,12},{1,17},{... | collective-permute-start | bytes 122888 | tf_op jit(solution)/shard_map/ppermute | solution.py:728
  36.1 4.9 %collective-permute-start.11 = (f32[80,128]{1,0:T(8,128)S(1)}, f32[80,128]{1,0:T(8,128)S(1)}, u32[]{:S(2)}, u32[]{:S(2)}) collective-permute-start(f32[80,128]{1,0:T(8,128)S(1)} %add.7.refs_0_), channel_id=1, source_target_pairs={{0,24},{4,28},{8,16},{12,20},{16,8},{20,12},{24,0},{28,4},{1,25},{... | collective-permute-start | bytes 122888 | tf_op jit(solution)/shard_map/ppermute | solution.py:728
  37.6 4.0 %collective-permute-start.9 = (f32[80,128]{1,0:T(8,128)S(1)}, f32[80,128]{1,0:T(8,128)S(1)}, u32[]{:S(2)}, u32[]{:S(2)}) collective-permute-start(f32[80,128]{1,0:T(8,128)S(1)} %add.7.refs_0_), channel_id=1, source_target_pairs={{0,8},{4,12},{8,0},{12,4},{16,24},{20,28},{24,16},{28,20},{1,9},{5... | collective-permute-start | bytes 122888 | tf_op jit(solution)/shard_map/ppermute | solution.py:728
  42.7 1.3 %collective-permute-start.12 = (f32[160,128]{1,0:T(8,128)S(1)}, f32[160,128]{1,0:T(8,128)S(1)}, u32[]{:S(2)}, u32[]{:S(2)}) collective-permute-start(f32[160,128]{1,0:T(8,128)S(1)} %shard_map.26.found_ref.refs_4_), channel_id=1, source_target_pairs={{0,4},{4,0},{8,12},{12,8},{16,20},{20,16},{24,28},{28,24},{1,5},{5... | collective-permute-start | bytes 245768 | tf_op jit(solution)/shard_map/ppermute | solution.py:728
  45.6 6.5 %collective-permute-start.13 = (f32[256,128]{1,0:T(8,128)S(1)}, f32[256,128]{1,0:T(8,128)S(1)}, u32[]{:S(2)}, u32[]{:S(2)}) collective-permute-start(f32[256,128]{1,0:T(8,128)S(1)} %get-tuple-element.47), channel_id=1, source_target_pairs={{2,0},{0,1},{3,2},{1,3},{6,4},{4,5},{7,6},{5,7},{10,8},{8,9},{11,1... | collective-permute-start | bytes 393224 | tf_op jit(solution)/shard_map/ppermute | solution.py:793

commit v15 on v13

--- a/solution.py
+++ b/solution.py
@@ -96,17 +96,17 @@
                     edges.append((there, old % 2, here))
     turn, left_over = {}, list(edges)
     while left_over:
-        source, _, target = left_over[0]
-        start = source
+        start = source = min(e[0] for e in left_over)
+        target, number = min(e[2] for e in left_over if e[0] == source), 1
         while True:
-            for number, one, other in ((0, source, target), (1, target, source)):
+            for one, other in ((source, target), (target, source)):
                 edge = next(e for e in left_over if (e[0], e[2]) == (one, other))
                 turn[edge] = number
                 left_over.remove(edge)
             if target == start:
                 break
-            ahead = [e[2] for e in left_over if e[0] == target]
-            source, target = target, ahead[0]
+            source, number = target, 1 - number
+            target = next(e[2] for e in left_over if e[0] == source)
     sends = [[(e[0], e[2]) for e in edges if turn[e] == i] for i in (0, 1)]
     for chosen in sends:
         assert len({a for a, _ in chosen}) == len({b for _, b in chosen}) == pair_total

time: 52.9 us -> 53.2 us (level)
    ppermute x2, starting transfers between devices: 3.5 us -> 4.12 us  [per_device(): came = [lax.ppermute(x, 'pair', s) for x, s in zip((sent, kept), sends)]]
where the time goes in v15:
time: 53.2 us; the launch traced here: 53 us
  waiting for transfers between devices  23.3 us (44%)
  starting transfers between devices  17.1 us (32%)
  Pallas kernels  10.8 us (20%)
  local copies, waits for them, and re-layouts  0.95 us (2%)
  other arithmetic  0.75 us (1%)
    pallas_call x12, Pallas kernels, call(): pl.pallas_call(kernel, out_shape=out, compiler_params=pltpu.CompilerParam...  10.8 us
    ppermute x10, waiting for transfers between devices, swap(): lax.ppermute(x, axis, [(i, i ^ mask) for i in range(lax.axis_size(axis))])  8.81 us
    ppermute x2, waiting for transfers between devices, per_device(): came = lax.ppermute(sent, 'pair', sends)  8.22 us
    ppermute x10, starting transfers between devices, swap(): lax.ppermute(x, axis, [(i, i ^ mask) for i in range(lax.axis_size(axis))])  7.37 us
    ppermute x2, waiting for transfers between devices, per_device(): came = [lax.ppermute(x, 'pair', s) for x, s in zip((sent, kept), sends)]  6.24 us
    ppermute x2, starting transfers between devices, per_device(): came = lax.ppermute(sent, 'pair', sends)  5.63 us
    ppermute x2, starting transfers between devices, per_device(): came = [lax.ppermute(x, 'pair', s) for x, s in zip((sent, kept), sends)]  4.12 us
  transfers between devices with their start and end apart: 14, of which 14 were waited for; matrix products, arithmetic and copies ran while one was open for 0% of the time, Pallas kernels for 7%

profile of v15, /device:TPU:0, one launch (start us, length us, event | category | flops | bytes accessed | tf_op | source)
XLA Modules:
  0.0 53.0 jit_solution(860358842342574295)
XLA Ops:
  0.0 0.9 %copy-done = f32[256,256]{1,0:T(8,128)S(1)} copy-done((f32[256,256]{1,0:T(8,128)S(1)}, f32[256,256]{1,0:T(8,128)}, u32[]{:S(2)}) %copy-start) | copy-done | bytes 262168
  1.1 4.1 %collective-permute-start = (f32[320,128]{1,0:T(8,128)S(1)}, f32[320,128]{1,0:T(8,128)S(1)}, u32[]{:S(2)}, u32[]{:S(2)}) collective-permute-start(f32[320,128]{1,0:T(8,128)S(1)} %shard_map.18), channel_id=1, source_target_pairs={{1,0},{0,2},{3,1},{2,3},{5,4},{4,6},{7,5},{6,7},{9,8},{8,10},{11,9... | collective-permute-start | bytes 491528 | tf_op jit(solution)/shard_map/ppermute | solution.py:784
  5.4 3.2 %collective-permute-done.payload_ref = f32[320,128]{1,0:T(8,128)S(1)} collective-permute-done((f32[320,128]{1,0:T(8,128)S(1)}, f32[320,128]{1,0:T(8,128)S(1)}, u32[]{:S(2)}, u32[]{:S(2)}) %collective-permute-start) | collective-permute-done | bytes 163872 | tf_op jit(solution)/shard_map/ppermute | solution.py:784
  8.7 1.0 %shard_map.19 = (f32[256,128]{1,0:T(8,128)S(1)}, f32[256,128]{1,0:T(8,128)S(1)}, f32[256,128]{1,0:T(8,128)S(1)}, f32[256,128]{1,0:T(8,128)S(1)}, f32[96,128]{1,0:T(8,128)S(1)}) custom-call(f32[256,128]{1,0:T(8,128)S(1)} %get-tuple-element.25.even_ref, f32[256,128]{1,0:T(8,128)S(1)} %get-tuple-element.26.odd_ref, f32[320,128]{1,0:T(8,128)S(1)} %collective-permute-done.payload_ref), custom_call_target="tpu_custom_call" | custom-call | tf_op jit(solution)/shard_map/pallas_call | solution.py:749
  9.8 0.9 %shard_map.20 = f32[96,128]{1,0:T(8,128)S(1)} custom-call(f32[256,128]{1,0:T(8,128)S(1)} %get-tuple-element.27.refs_0_.even_ref, f32[256,128]{1,0:T(8,128)S(1)} %get-tuple-element.28.refs_1_.odd_ref, f32[256,128]{1,0:T(8,128)S(1)} %get-tuple-element.29.refs_2_, f32[256,128]{1,0:T(8,128)S(1)} %get-tuple-element.30.refs_3_), custom_call_target="tpu_custom_call" | custom-call | tf_op jit(solution)/shard_map/pallas_call | solution.py:749
  11.0 1.6 %collective-permute-start.2 = (f32[96,128]{1,0:T(8,128)S(1)}, f32[96,128]{1,0:T(8,128)S(1)}, u32[]{:S(2)}, u32[]{:S(2)}) collective-permute-start(f32[96,128]{1,0:T(8,128)S(1)} %add.6.refs_0_), channel_id=1, source_target_pairs={{0,8},{4,12},{8,0},{12,4},{16,24},{20,28},{24,16},{28,20},{1,9},{5... | collective-permute-start | bytes 147464 | tf_op jit(solution)/shard_map/ppermute | solution.py:732
  12.5 1.5 %collective-permute-start.3 = (f32[96,128]{1,0:T(8,128)S(1)}, f32[96,128]{1,0:T(8,128)S(1)}, u32[]{:S(2)}, u32[]{:S(2)}) collective-permute-start(f32[96,128]{1,0:T(8,128)S(1)} %add.6.refs_0_), channel_id=1, source_target_pairs={{0,16},{4,20},{8,24},{12,28},{16,0},{20,4},{24,8},{28,12},{1,17},{... | collective-permute-start | bytes 147464 | tf_op jit(solution)/shard_map/ppermute | solution.py:732
  14.5 0.6 %collective-permute-done.2.refs_1_ = f32[96,128]{1,0:T(8,128)S(1)} collective-permute-done((f32[96,128]{1,0:T(8,128)S(1)}, f32[96,128]{1,0:T(8,128)S(1)}, u32[]{:S(2)}, u32[]{:S(2)}) %collective-permute-start.2) | collective-permute-done | bytes 49184 | tf_op jit(solution)/shard_map/ppermute | solution.py:732
  15.1 1.5 %collective-permute-done.3.refs_2_ = f32[96,128]{1,0:T(8,128)S(1)} collective-permute-done((f32[96,128]{1,0:T(8,128)S(1)}, f32[96,128]{1,0:T(8,128)S(1)}, u32[]{:S(2)}, u32[]{:S(2)}) %collective-permute-start.3) | collective-permute-done | bytes 49184 | tf_op jit(solution)/shard_map/ppermute | solution.py:732
  16.6 2.4 %collective-permute-done.4.refs_3_ = f32[96,128]{1,0:T(8,128)S(1)} collective-permute-done((f32[96,128]{1,0:T(8,128)S(1)}, f32[96,128]{1,0:T(8,128)S(1)}, u32[]{:S(2)}, u32[]{:S(2)}) %collective-permute-start.4) | collective-permute-done | bytes 49184 | tf_op jit(solution)/shard_map/ppermute | solution.py:732
  19.0 1.0 %shard_map.21.found_ref.refs_4_ = f32[176,128]{1,0:T(8,128)S(1)} custom-call(f32[96,128]{1,0:T(8,128)S(1)} %add.6.refs_0_, f32[96,128]{1,0:T(8,128)S(1)} %collective-permute-done.2.refs_1_, f32[96,128]{1,0:T(8,128)S(1)} %collective-permute-done.3.refs_2_, f32[96,128]{1,0:T(8,128)S(1)} %collective-permute-done.4.refs_3_), custom_call_target="tpu_custom_call" | custom-call | tf_op jit(solution)/shard_map/pallas_call | solution.py:749
  20.2 0.7 %shard_map.22 = (f32[256,128]{1,0:T(8,128)S(1)}, f32[256,128]{1,0:T(8,128)S(1)}) custom-call(f32[256,128]{1,0:T(8,128)S(1)} %get-tuple-element.27.refs_0_.even_ref, f32[256,128]{1,0:T(8,128)S(1)} %get-tuple-element.28.refs_1_.odd_ref, f32[176,128]{1,0:T(8,128)S(1)} %shard_map.21.found_ref.refs_4_), custom_call_target="tpu_custom_call" | custom-call | tf_op jit(solution)/shard_map/pallas_call | solution.py:749
  20.9 0.6 %collective-permute-done.5.refs_5_ = f32[176,128]{1,0:T(8,128)S(1)} collective-permute-done((f32[176,128]{1,0:T(8,128)S(1)}, f32[176,128]{1,0:T(8,128)S(1)}, u32[]{:S(2)}, u32[]{:S(2)}) %collective-permute-start.5) | collective-permute-done | bytes 90144 | tf_op jit(solution)/shard_map/ppermute | solution.py:732
  21.5 1.6 %shard_map.23 = (f32[256,128]{1,0:T(8,128)S(1)}, f32[256,128]{1,0:T(8,128)S(1)}) custom-call(f32[256,128]{1,0:T(8,128)S(1)} %get-tuple-element.32.refs_0_, f32[256,128]{1,0:T(8,128)S(1)} %get-tuple-element.33.refs_1_, f32[256,128]{1,0:T(8,128)S(1)} %get-tuple-element.29.refs_2_, f32[256,128]{1,0:T(8,128)S(1)} %get-tuple-element.30.refs_3_, ...), custom_call_target="tpu_custom_call" | custom-call | tf_op jit(solution)/shard_map/pallas_call | solution.py:749
  23.0 3.4 %collective-permute-start.6 = (f32[256,128]{1,0:T(8,128)S(1)}, f32[256,128]{1,0:T(8,128)S(1)}, u32[]{:S(2)}, u32[]{:S(2)}) collective-permute-start(f32[256,128]{1,0:T(8,128)S(1)} %get-tuple-element.35.sent_ref), channel_id=1, source_target_pairs={{2,0},{0,2},{3,1},{1,3},{6,4},{4,6},{7,5},{5,7},{10,8},{8,10},{11,... | collective-permute-start | bytes 393224 | tf_op jit(solution)/shard_map/ppermute | solution.py:791
  26.5 0.7 %collective-permute-start.7 = (f32[256,128]{1,0:T(8,128)S(1)}, f32[256,128]{1,0:T(8,128)S(1)}, u32[]{:S(2)}, u32[]{:S(2)}) collective-permute-start(f32[256,128]{1,0:T(8,128)S(1)} %get-tuple-element.34.kept_ref), channel_id=1, source_target_pairs={{1,0},{3,2},{0,1},{2,3},{5,4},{7,6},{4,5},{6,7},{9,8},{11,10},{8,9... | collective-permute-start | bytes 393224 | tf_op jit(solution)/shard_map/ppermute | solution.py:791
  27.1 6.1 %collective-permute-done.6.came0_ref = f32[256,128]{1,0:T(8,128)S(1)} collective-permute-done((f32[256,128]{1,0:T(8,128)S(1)}, f32[256,128]{1,0:T(8,128)S(1)}, u32[]{:S(2)}, u32[]{:S(2)}) %collective-permute-start.6) | collective-permute-done | bytes 131104 | tf_op jit(solution)/shard_map/ppermute | solution.py:791
  33.4 0.9 %shard_map.24 = (f32[256,128]{1,0:T(8,128)S(1)}, f32[256,128]{1,0:T(8,128)S(1)}, f32[256,128]{1,0:T(8,128)S(1)}, f32[256,128]{1,0:T(8,128)S(1)}, f32[96,128]{1,0:T(8,128)S(1)}) custom-call(f32[256,128]{1,0:T(8,128)S(1)} %get-tuple-element.34.kept_ref, f32[256,128]{1,0:T(8,128)S(1)} %get-tuple-element.35.sent_ref, ...), custom_call_target="tpu_custom_call" | custom-call | tf_op jit(solution)/shard_map/pallas_call | solution.py:749
  34.4 0.9 %shard_map.25 = f32[96,128]{1,0:T(8,128)S(1)} custom-call(f32[256,128]{1,0:T(8,128)S(1)} %get-tuple-element.36.refs_0_.even_ref, f32[256,128]{1,0:T(8,128)S(1)} %get-tuple-element.37.refs_1_.odd_ref, f32[256,128]{1,0:T(8,128)S(1)} %get-tuple-element.38.refs_2_, f32[256,128]{1,0:T(8,128)S(1)} %get-tuple-element.39.refs_3_), custom_call_target="tpu_custom_call" | custom-call | tf_op jit(solution)/shard_map/pallas_call | solution.py:749
  35.6 0.6 %collective-permute-start.10 = (f32[96,128]{1,0:T(8,128)S(1)}, f32[96,128]{1,0:T(8,128)S(1)}, u32[]{:S(2)}, u32[]{:S(2)}) collective-permute-start(f32[96,128]{1,0:T(8,128)S(1)} %add.7.refs_0_), channel_id=1, source_target_pairs={{0,16},{4,20},{8,24},{12,28},{16,0},{20,4},{24,8},{28,12},{1,17},{... | collective-permute-start | bytes 147464 | tf_op jit(solution)/shard_map/ppermute | solution.py:732
  36.2 1.5 %collective-permute-start.11 = (f32[96,128]{1,0:T(8,128)S(1)}, f32[96,128]{1,0:T(8,128)S(1)}, u32[]{:S(2)}, u32[]{:S(2)}) collective-permute-start(f32[96,128]{1,0:T(8,128)S(1)} %add.7.refs_0_), channel_id=1, source_target_pairs={{0,24},{4,28},{8,16},{12,20},{16,8},{20,12},{24,0},{28,4},{1,25},{... | collective-permute-start | bytes 147464 | tf_op jit(solution)/shard_map/ppermute | solution.py:732
  37.7 1.5 %collective-permute-start.9 = (f32[96,128]{1,0:T(8,128)S(1)}, f32[96,128]{1,0:T(8,128)S(1)}, u32[]{:S(2)}, u32[]{:S(2)}) collective-permute-start(f32[96,128]{1,0:T(8,128)S(1)} %add.7.refs_0_), channel_id=1, source_target_pairs={{0,8},{4,12},{8,0},{12,4},{16,24},{20,28},{24,16},{28,20},{1,9},{5... | collective-permute-start | bytes 147464 | tf_op jit(solution)/shard_map/ppermute | solution.py:732
  39.2 1.1 %collective-permute-done.10.refs_2_ = f32[96,128]{1,0:T(8,128)S(1)} collective-permute-done((f32[96,128]{1,0:T(8,128)S(1)}, f32[96,128]{1,0:T(8,128)S(1)}, u32[]{:S(2)}, u32[]{:S(2)}) %collective-permute-start.10) | collective-permute-done | bytes 49184 | tf_op jit(solution)/shard_map/ppermute | solution.py:732
  40.3 0.9 %collective-permute-done.11.refs_3_ = f32[96,128]{1,0:T(8,128)S(1)} collective-permute-done((f32[96,128]{1,0:T(8,128)S(1)}, f32[96,128]{1,0:T(8,128)S(1)}, u32[]{:S(2)}, u32[]{:S(2)}) %collective-permute-start.11) | collective-permute-done | bytes 49184 | tf_op jit(solution)/shard_map/ppermute | solution.py:732
  41.2 0.6 %collective-permute-done.9.refs_1_ = f32[96,128]{1,0:T(8,128)S(1)} collective-permute-done((f32[96,128]{1,0:T(8,128)S(1)}, f32[96,128]{1,0:T(8,128)S(1)}, u32[]{:S(2)}, u32[]{:S(2)}) %collective-permute-start.9) | collective-permute-done | bytes 49184 | tf_op jit(solution)/shard_map/ppermute | solution.py:732
  41.8 1.0 %shard_map.26.found_ref.refs_4_ = f32[176,128]{1,0:T(8,128)S(1)} custom-call(f32[96,128]{1,0:T(8,128)S(1)} %add.7.refs_0_, f32[96,128]{1,0:T(8,128)S(1)} %collective-permute-done.9.refs_1_, f32[96,128]{1,0:T(8,128)S(1)} %collective-permute-done.10.refs_2_, f32[96,128]{1,0:T(8,128)S(1)} %collective-permute-done.11.refs_3_), custom_call_target="tpu_custom_call" | custom-call | tf_op jit(solution)/shard_map/pallas_call | solution.py:749
  42.9 0.7 %shard_map.27 = (f32[256,128]{1,0:T(8,128)S(1)}, f32[256,128]{1,0:T(8,128)S(1)}) custom-call(f32[256,128]{1,0:T(8,128)S(1)} %get-tuple-element.36.refs_0_.even_ref, f32[256,128]{1,0:T(8,128)S(1)} %get-tuple-element.37.refs_1_.odd_ref, f32[176,128]{1,0:T(8,128)S(1)} %shard_map.26.found_ref.refs_4_), custom_call_target="tpu_custom_call" | custom-call | tf_op jit(solution)/shard_map/pallas_call | solution.py:749
  43.7 0.6 %collective-permute-done.12.refs_5_ = f32[176,128]{1,0:T(8,128)S(1)} collective-permute-done((f32[176,128]{1,0:T(8,128)S(1)}, f32[176,128]{1,0:T(8,128)S(1)}, u32[]{:S(2)}, u32[]{:S(2)}) %collective-permute-start.12) | collective-permute-done | bytes 90144 | tf_op jit(solution)/shard_map/ppermute | solution.py:732
  44.2 1.6 %shard_map.28 = (f32[256,128]{1,0:T(8,128)S(1)}, f32[256,128]{1,0:T(8,128)S(1)}) custom-call(f32[256,128]{1,0:T(8,128)S(1)} %get-tuple-element.41.refs_0_, f32[256,128]{1,0:T(8,128)S(1)} %get-tuple-element.42.refs_1_, f32[256,128]{1,0:T(8,128)S(1)} %get-tuple-element.38.refs_2_, f32[256,128]{1,0:T(8,128)S(1)} %get-tuple-element.39.refs_3_, ...), custom_call_target="tpu_custom_call" | custom-call | tf_op jit(solution)/shard_map/pallas_call | solution.py:749
  45.8 1.5 %collective-permute-start.13 = (f32[256,128]{1,0:T(8,128)S(1)}, f32[256,128]{1,0:T(8,128)S(1)}, u32[]{:S(2)}, u32[]{:S(2)}) collective-permute-start(f32[256,128]{1,0:T(8,128)S(1)} %get-tuple-element.43), channel_id=1, source_target_pairs={{2,0},{0,1},{3,2},{1,3},{6,4},{4,5},{7,6},{5,7},{10,8},{8,9},{11,1... | collective-permute-start | bytes 393224 | tf_op jit(solution)/shard_map/ppermute | solution.py:797
  47.3 5.0 %collective-permute-done.13 = f32[256,128]{1,0:T(8,128)S(1)} collective-permute-done((f32[256,128]{1,0:T(8,128)S(1)}, f32[256,128]{1,0:T(8,128)S(1)}, u32[]{:S(2)}, u32[]{:S(2)}) %collective-permute-start.13) | collective-permute-done | bytes 131104 | tf_op jit(solution)/shard_map/ppermute | solution.py:797
  52.3 0.7 %pad_maximum_fusion = f32[256,256]{1,0:T(8,128)} fusion(f32[256,128]{1,0:T(8,128)S(1)} %get-tuple-element.46, f32[256,128]{1,0:T(8,128)S(1)} %get-tuple-element.45), kind=kLoop, calls=%fused_computation | loop fusion | flops 65536 | bytes 524288 | tf_op jit(solution)/shard_map/concatenate | solution.py:801
  (14 shorter events, 1.9 us)
Async XLA Ops:
  0.0 0.9 %copy-start = (f32[256,256]{1,0:T(8,128)S(1)}, f32[256,256]{1,0:T(8,128)}, u32[]{:S(2)}) copy-start(f32[256,256]{1,0:T(8,128)} %basis_ref.3) | copy-start | bytes 786436
  1.1 7.5 %collective-permute-start = (f32[320,128]{1,0:T(8,128)S(1)}, f32[320,128]{1,0:T(8,128)S(1)}, u32[]{:S(2)}, u32[]{:S(2)}) collective-permute-start(f32[320,128]{1,0:T(8,128)S(1)} %shard_map.18), channel_id=1, source_target_pairs={{1,0},{0,2},{3,1},{2,3},{5,4},{4,6},{7,5},{6,7},{9,8},{8,10},{11,9... | collective-permute-start | bytes 491528 | tf_op jit(solution)/shard_map/ppermute | solution.py:784
  9.7 1.3 %collective-permute-start.1 = (f32[96,128]{1,0:T(8,128)S(1)}, f32[96,128]{1,0:T(8,128)S(1)}, u32[]{:S(2)}, u32[]{:S(2)}) collective-permute-start(f32[96,128]{1,0:T(8,128)S(1)} %get-tuple-element.31), channel_id=1, source_target_pairs={{0,4},{4,0},{8,12},{12,8},{16,20},{20,16},{24,28},{28,24},{1,5},{5... | collective-permute-start | bytes 147464 | tf_op jit(solution)/shard_map/ppermute | solution.py:732
  11.0 4.2 %collective-permute-start.2 = (f32[96,128]{1,0:T(8,128)S(1)}, f32[96,128]{1,0:T(8,128)S(1)}, u32[]{:S(2)}, u32[]{:S(2)}) collective-permute-start(f32[96,128]{1,0:T(8,128)S(1)} %add.6.refs_0_), channel_id=1, source_target_pairs={{0,8},{4,12},{8,0},{12,4},{16,24},{20,28},{24,16},{28,20},{1,9},{5... | collective-permute-start | bytes 147464 | tf_op jit(solution)/shard_map/ppermute | solution.py:732
  12.5 4.1 %collective-permute-start.3 = (f32[96,128]{1,0:T(8,128)S(1)}, f32[96,128]{1,0:T(8,128)S(1)}, u32[]{:S(2)}, u32[]{:S(2)}) collective-permute-start(f32[96,128]{1,0:T(8,128)S(1)} %add.6.refs_0_), channel_id=1, source_target_pairs={{0,16},{4,20},{8,24},{12,28},{16,0},{20,4},{24,8},{28,12},{1,17},{... | collective-permute-start | bytes 147464 | tf_op jit(solution)/shard_map/ppermute | solution.py:732
  14.1 5.0 %collective-permute-start.4 = (f32[96,128]{1,0:T(8,128)S(1)}, f32[96,128]{1,0:T(8,128)S(1)}, u32[]{:S(2)}, u32[]{:S(2)}) collective-permute-start(f32[96,128]{1,0:T(8,128)S(1)} %add.6.refs_0_), channel_id=1, source_target_pairs={{0,24},{4,28},{8,16},{12,20},{16,8},{20,12},{24,0},{28,4},{1,25},{... | collective-permute-start | bytes 147464 | tf_op jit(solution)/shard_map/ppermute | solution.py:732
  20.1 1.4 %collective-permute-start.5 = (f32[176,128]{1,0:T(8,128)S(1)}, f32[176,128]{1,0:T(8,128)S(1)}, u32[]{:S(2)}, u32[]{:S(2)}) collective-permute-start(f32[176,128]{1,0:T(8,128)S(1)} %shard_map.21.found_ref.refs_4_), channel_id=1, source_target_pairs={{0,4},{4,0},{8,12},{12,8},{16,20},{20,16},{24,28},{28,24},{1,5},{5... | collective-permute-start | bytes 270344 | tf_op jit(solution)/shard_map/ppermute | solution.py:732
  23.0 10.2 %collective-permute-start.6 = (f32[256,128]{1,0:T(8,128)S(1)}, f32[256,128]{1,0:T(8,128)S(1)}, u32[]{:S(2)}, u32[]{:S(2)}) collective-permute-start(f32[256,128]{1,0:T(8,128)S(1)} %get-tuple-element.35.sent_ref), channel_id=1, source_target_pairs={{2,0},{0,2},{3,1},{1,3},{6,4},{4,6},{7,5},{5,7},{10,8},{8,10},{11,... | collective-permute-start | bytes 393224 | tf_op jit(solution)/shard_map/ppermute | solution.py:791
  26.5 6.9 %collective-permute-start.7 = (f32[256,128]{1,0:T(8,128)S(1)}, f32[256,128]{1,0:T(8,128)S(1)}, u32[]{:S(2)}, u32[]{:S(2)}) collective-permute-start(f32[256,128]{1,0:T(8,128)S(1)} %get-tuple-element.34.kept_ref), channel_id=1, source_target_pairs={{1,0},{3,2},{0,1},{2,3},{5,4},{7,6},{4,5},{6,7},{9,8},{11,10},{8,9... | collective-permute-start | bytes 393224 | tf_op jit(solution)/shard_map/ppermute | solution.py:791
  34.3 1.3 %collective-permute-start.8 = (f32[96,128]{1,0:T(8,128)S(1)}, f32[96,128]{1,0:T(8,128)S(1)}, u32[]{:S(2)}, u32[]{:S(2)}) collective-permute-start(f32[96,128]{1,0:T(8,128)S(1)} %get-tuple-element.40), channel_id=1, source_target_pairs={{0,4},{4,0},{8,12},{12,8},{16,20},{20,16},{24,28},{28,24},{1,5},{5... | collective-permute-start | bytes 147464 | tf_op jit(solution)/shard_map/ppermute | solution.py:732
  35.6 4.7 %collective-permute-start.10 = (f32[96,128]{1,0:T(8,128)S(1)}, f32[96,128]{1,0:T(8,128)S(1)}, u32[]{:S(2)}, u32[]{:S(2)}) collective-permute-start(f32[96,128]{1,0:T(8,128)S(1)} %add.7.refs_0_), channel_id=1, source_target_pairs={{0,16},{4,20},{8,24},{12,28},{16,0},{20,4},{24,8},{28,12},{1,17},{... | collective-permute-start | bytes 147464 | tf_op jit(solution)/shard_map/ppermute | solution.py:732
  36.2 5.0 %collective-permute-start.11 = (f32[96,128]{1,0:T(8,128)S(1)}, f32[96,128]{1,0:T(8,128)S(1)}, u32[]{:S(2)}, u32[]{:S(2)}) collective-permute-start(f32[96,128]{1,0:T(8,128)S(1)} %add.7.refs_0_), channel_id=1, source_target_pairs={{0,24},{4,28},{8,16},{12,20},{16,8},{20,12},{24,0},{28,4},{1,25},{... | collective-permute-start | bytes 147464 | tf_op jit(solution)/shard_map/ppermute | solution.py:732
  37.7 4.1 %collective-permute-start.9 = (f32[96,128]{1,0:T(8,128)S(1)}, f32[96,128]{1,0:T(8,128)S(1)}, u32[]{:S(2)}, u32[]{:S(2)}) collective-permute-start(f32[96,128]{1,0:T(8,128)S(1)} %add.7.refs_0_), channel_id=1, source_target_pairs={{0,8},{4,12},{8,0},{12,4},{16,24},{20,28},{24,16},{28,20},{1,9},{5... | collective-permute-start | bytes 147464 | tf_op jit(solution)/shard_map/ppermute | solution.py:732
  42.9 1.4 %collective-permute-start.12 = (f32[176,128]{1,0:T(8,128)S(1)}, f32[176,128]{1,0:T(8,128)S(1)}, u32[]{:S(2)}, u32[]{:S(2)}) collective-permute-start(f32[176,128]{1,0:T(8,128)S(1)} %shard_map.26.found_ref.refs_4_), channel_id=1, source_target_pairs={{0,4},{4,0},{8,12},{12,8},{16,20},{20,16},{24,28},{28,24},{1,5},{5... | collective-permute-start | bytes 270344 | tf_op jit(solution)/shard_map/ppermute | solution.py:732
  45.8 6.5 %collective-permute-start.13 = (f32[256,128]{1,0:T(8,128)S(1)}, f32[256,128]{1,0:T(8,128)S(1)}, u32[]{:S(2)}, u32[]{:S(2)}) collective-permute-start(f32[256,128]{1,0:T(8,128)S(1)} %get-tuple-element.43), channel_id=1, source_target_pairs={{2,0},{0,1},{3,2},{1,3},{6,4},{4,5},{7,6},{5,7},{10,8},{8,9},{11,1... | collective-permute-start | bytes 393224 | tf_op jit(solution)/shard_map/ppermute | solution.py:797

commit v16 on v13

--- a/solution.py
+++ b/solution.py
@@ -15,7 +15,7 @@
 FAR_DIAGS = 32
 WINDOW = 32
 NEAR = 16
-STRIP = 16
+STRIP = REACH - 1
 BACK = 3
 
 
@@ -215,6 +215,10 @@
         band_ref[q * diags : (q + 1) * diags, :] = band
 
 
+def strip_rows(rows, width):
+    return -(-rows // (8 * (width // (2 * STRIP)))) * 8
+
+
 def payload_kernel(sends_second, basis_ref, payload_ref):
     rows, cols = basis_ref.shape
     width = cols // 2
@@ -227,12 +231,19 @@
     in_first = place < half
     source = 2 * jnp.where(in_first, place, place - half) + odd
     payload_ref[:rows] = jnp.where(in_first, take_lanes(first, source), take_lanes(second, source))
-    group = rows * 2 * STRIP // width
-    source = 2 * (start + lane % STRIP) + lane // STRIP % 2
+    places = width // STRIP
+    place = lane - STRIP * sum(jnp.where(lane >= STRIP * i, 1, 0) for i in range(1, places))
+    odd = sum(jnp.where(lane >= STRIP * i, 1 if i % 2 else -1, 0) for i in range(1, places))
+    source = jnp.minimum(2 * (start + place) + odd, width - 1)
+    group = strip_rows(rows, width)
     strips = jnp.zeros((group, width), jnp.float32)
-    for i in range(rows // group):
-        here = lane // (2 * STRIP) == i
-        strips = jnp.where(here, take_lanes(second[i * group : (i + 1) * group], source), strips)
+    for i, at in enumerate(range(0, rows, group)):
+        here = jnp.logical_and(lane >= 2 * STRIP * i, lane < 2 * STRIP * (i + 1))
+        part = take_lanes(second[at : at + group], source)
+        if part.shape[0] < group:
+            spare = jnp.zeros((group - part.shape[0], width), jnp.float32)
+            part = jnp.concatenate((part, spare), axis=0)
+        strips = jnp.where(here, part, strips)
     payload_ref[rows:] = strips
 
 
@@ -249,8 +260,12 @@
     group = strips.shape[0]
     columns = []
     for j, x in enumerate((main, left(main, half))):
-        ends = [right(strips, half - (2 * i + j) * STRIP) for i in range(rows // group)]
-        x = jnp.where(lane < half, x, jnp.where(lane < half + STRIP, jnp.concatenate(ends), 0.0))
+        ends = [
+            right(strips, half - (2 * i + j) * STRIP)[: rows - at]
+            for i, at in enumerate(range(0, rows, group))
+        ]
+        ends = jnp.concatenate(ends, axis=0)
+        x = jnp.where(lane < half, x, jnp.where(lane < half + STRIP, ends, 0.0))
         columns.append(jnp.where(second, right(x, half - STRIP), x))
     return columns
 
@@ -777,7 +792,7 @@
     pair_total = lax.axis_size("pair")
     column = (rows, width)
     opened = (column,) * 4 + ((4 * PACKED + WINDOW, width),)
-    payload = (rows + rows * 2 * STRIP // width, width)
+    payload = (rows + strip_rows(rows, width), width)
 
     sends, sends_second, gets_second, own_second, is_second = first_moves(pair_total)
     (sent,) = call(functools.partial(payload_kernel, sends_second), (payload,), basis)

time: 52.9 us -> 52.7 us (level)
  no operation moved by 1% of the time
where the time goes in v16:
time: 52.7 us; the launch traced here: 52.6 us
  waiting for transfers between devices  23.1 us (44%)
  starting transfers between devices  16.8 us (32%)
  Pallas kernels  10.9 us (21%)
  local copies, waits for them, and re-layouts  0.95 us (2%)
  other arithmetic  0.76 us (1%)
    pallas_call x12, Pallas kernels, call(): pl.pallas_call(kernel, out_shape=out, compiler_params=pltpu.CompilerParam...  10.9 us
    ppermute x10, waiting for transfers between devices, swap(): lax.ppermute(x, axis, [(i, i ^ mask) for i in range(lax.axis_size(axis))])  8.8 us
    ppermute x2, waiting for transfers between devices, per_device(): came = lax.ppermute(sent, 'pair', sends)  7.79 us
    ppermute x10, starting transfers between devices, swap(): lax.ppermute(x, axis, [(i, i ^ mask) for i in range(lax.axis_size(axis))])  7.38 us
    ppermute x2, waiting for transfers between devices, per_device(): came = [lax.ppermute(x, 'pair', s) for x, s in zip((sent, kept), sends)]  6.56 us
    ppermute x2, starting transfers between devices, per_device(): came = lax.ppermute(sent, 'pair', sends)  5.88 us
    ppermute x2, starting transfers between devices, per_device(): came = [lax.ppermute(x, 'pair', s) for x, s in zip((sent, kept), sends)]  3.5 us
  transfers between devices with their start and end apart: 14, of which 14 were waited for; matrix products, arithmetic and copies ran while one was open for 0% of the time, Pallas kernels for 7%

profile of v16, /device:TPU:0, one launch (start us, length us, event | category | flops | bytes accessed | tf_op | source)
XLA Modules:
  0.0 52.6 jit_solution(3038259736211502528)
XLA Ops:
  0.0 0.9 %copy-done = f32[256,256]{1,0:T(8,128)S(1)} copy-done((f32[256,256]{1,0:T(8,128)S(1)}, f32[256,256]{1,0:T(8,128)}, u32[]{:S(2)}) %copy-start) | copy-done | bytes 262168
  1.1 4.1 %collective-permute-start = (f32[304,128]{1,0:T(8,128)S(1)}, f32[304,128]{1,0:T(8,128)S(1)}, u32[]{:S(2)}, u32[]{:S(2)}) collective-permute-start(f32[304,128]{1,0:T(8,128)S(1)} %shard_map.18), channel_id=1, source_target_pairs={{1,0},{0,2},{3,1},{2,3},{5,4},{4,6},{7,5},{6,7},{9,8},{8,10},{11,9... | collective-permute-start | bytes 466952 | tf_op jit(solution)/shard_map/ppermute | solution.py:799
  5.4 3.1 %collective-permute-done.payload_ref = f32[304,128]{1,0:T(8,128)S(1)} collective-permute-done((f32[304,128]{1,0:T(8,128)S(1)}, f32[304,128]{1,0:T(8,128)S(1)}, u32[]{:S(2)}, u32[]{:S(2)}) %collective-permute-start) | collective-permute-done | bytes 155680 | tf_op jit(solution)/shard_map/ppermute | solution.py:799
  8.5 1.0 %shard_map.19 = (f32[256,128]{1,0:T(8,128)S(1)}, f32[256,128]{1,0:T(8,128)S(1)}, f32[256,128]{1,0:T(8,128)S(1)}, f32[256,128]{1,0:T(8,128)S(1)}, f32[96,128]{1,0:T(8,128)S(1)}) custom-call(f32[256,128]{1,0:T(8,128)S(1)} %get-tuple-element.25.even_ref, f32[256,128]{1,0:T(8,128)S(1)} %get-tuple-element.26.odd_ref, f32[304,128]{1,0:T(8,128)S(1)} %collective-permute-done.payload_ref), custom_call_target="tpu_custom_call" | custom-call | tf_op jit(solution)/shard_map/pallas_call | solution.py:764
  9.6 1.0 %shard_map.20 = f32[96,128]{1,0:T(8,128)S(1)} custom-call(f32[256,128]{1,0:T(8,128)S(1)} %get-tuple-element.27.refs_0_.even_ref, f32[256,128]{1,0:T(8,128)S(1)} %get-tuple-element.28.refs_1_.odd_ref, f32[256,128]{1,0:T(8,128)S(1)} %get-tuple-element.29.refs_2_, f32[256,128]{1,0:T(8,128)S(1)} %get-tuple-element.30.refs_3_), custom_call_target="tpu_custom_call" | custom-call | tf_op jit(solution)/shard_map/pallas_call | solution.py:764
  10.8 1.6 %collective-permute-start.2 = (f32[96,128]{1,0:T(8,128)S(1)}, f32[96,128]{1,0:T(8,128)S(1)}, u32[]{:S(2)}, u32[]{:S(2)}) collective-permute-start(f32[96,128]{1,0:T(8,128)S(1)} %add.6.refs_0_), channel_id=1, source_target_pairs={{0,8},{4,12},{8,0},{12,4},{16,24},{20,28},{24,16},{28,20},{1,9},{5... | collective-permute-start | bytes 147464 | tf_op jit(solution)/shard_map/ppermute | solution.py:747
  12.4 1.5 %collective-permute-start.3 = (f32[96,128]{1,0:T(8,128)S(1)}, f32[96,128]{1,0:T(8,128)S(1)}, u32[]{:S(2)}, u32[]{:S(2)}) collective-permute-start(f32[96,128]{1,0:T(8,128)S(1)} %add.6.refs_0_), channel_id=1, source_target_pairs={{0,16},{4,20},{8,24},{12,28},{16,0},{20,4},{24,8},{28,12},{1,17},{... | collective-permute-start | bytes 147464 | tf_op jit(solution)/shard_map/ppermute | solution.py:747
  14.4 0.6 %collective-permute-done.2.refs_1_ = f32[96,128]{1,0:T(8,128)S(1)} collective-permute-done((f32[96,128]{1,0:T(8,128)S(1)}, f32[96,128]{1,0:T(8,128)S(1)}, u32[]{:S(2)}, u32[]{:S(2)}) %collective-permute-start.2) | collective-permute-done | bytes 49184 | tf_op jit(solution)/shard_map/ppermute | solution.py:747
  15.0 1.5 %collective-permute-done.3.refs_2_ = f32[96,128]{1,0:T(8,128)S(1)} collective-permute-done((f32[96,128]{1,0:T(8,128)S(1)}, f32[96,128]{1,0:T(8,128)S(1)}, u32[]{:S(2)}, u32[]{:S(2)}) %collective-permute-start.3) | collective-permute-done | bytes 49184 | tf_op jit(solution)/shard_map/ppermute | solution.py:747
  16.5 2.4 %collective-permute-done.4.refs_3_ = f32[96,128]{1,0:T(8,128)S(1)} collective-permute-done((f32[96,128]{1,0:T(8,128)S(1)}, f32[96,128]{1,0:T(8,128)S(1)}, u32[]{:S(2)}, u32[]{:S(2)}) %collective-permute-start.4) | collective-permute-done | bytes 49184 | tf_op jit(solution)/shard_map/ppermute | solution.py:747
  18.9 1.0 %shard_map.21.found_ref.refs_4_ = f32[176,128]{1,0:T(8,128)S(1)} custom-call(f32[96,128]{1,0:T(8,128)S(1)} %add.6.refs_0_, f32[96,128]{1,0:T(8,128)S(1)} %collective-permute-done.2.refs_1_, f32[96,128]{1,0:T(8,128)S(1)} %collective-permute-done.3.refs_2_, f32[96,128]{1,0:T(8,128)S(1)} %collective-permute-done.4.refs_3_), custom_call_target="tpu_custom_call" | custom-call | tf_op jit(solution)/shard_map/pallas_call | solution.py:764
  20.0 0.7 %shard_map.22 = (f32[256,128]{1,0:T(8,128)S(1)}, f32[256,128]{1,0:T(8,128)S(1)}) custom-call(f32[256,128]{1,0:T(8,128)S(1)} %get-tuple-element.27.refs_0_.even_ref, f32[256,128]{1,0:T(8,128)S(1)} %get-tuple-element.28.refs_1_.odd_ref, f32[176,128]{1,0:T(8,128)S(1)} %shard_map.21.found_ref.refs_4_), custom_call_target="tpu_custom_call" | custom-call | tf_op jit(solution)/shard_map/pallas_call | solution.py:764
  20.7 0.6 %collective-permute-done.5.refs_5_ = f32[176,128]{1,0:T(8,128)S(1)} collective-permute-done((f32[176,128]{1,0:T(8,128)S(1)}, f32[176,128]{1,0:T(8,128)S(1)}, u32[]{:S(2)}, u32[]{:S(2)}) %collective-permute-start.5) | collective-permute-done | bytes 90144 | tf_op jit(solution)/shard_map/ppermute | solution.py:747
  21.3 1.6 %shard_map.23 = (f32[256,128]{1,0:T(8,128)S(1)}, f32[256,128]{1,0:T(8,128)S(1)}) custom-call(f32[256,128]{1,0:T(8,128)S(1)} %get-tuple-element.32.refs_0_, f32[256,128]{1,0:T(8,128)S(1)} %get-tuple-element.33.refs_1_, f32[256,128]{1,0:T(8,128)S(1)} %get-tuple-element.29.refs_2_, f32[256,128]{1,0:T(8,128)S(1)} %get-tuple-element.30.refs_3_, ...), custom_call_target="tpu_custom_call" | custom-call | tf_op jit(solution)/shard_map/pallas_call | solution.py:764
  22.9 2.4 %collective-permute-start.6 = (f32[256,128]{1,0:T(8,128)S(1)}, f32[256,128]{1,0:T(8,128)S(1)}, u32[]{:S(2)}, u32[]{:S(2)}) collective-permute-start(f32[256,128]{1,0:T(8,128)S(1)} %get-tuple-element.35.sent_ref), channel_id=1, source_target_pairs={{2,0},{3,2},{0,1},{1,3},{6,4},{7,6},{4,5},{5,7},{10,8},{11,10},{8,... | collective-permute-start | bytes 393224 | tf_op jit(solution)/shard_map/ppermute | solution.py:806
  25.3 1.1 %collective-permute-start.7 = (f32[256,128]{1,0:T(8,128)S(1)}, f32[256,128]{1,0:T(8,128)S(1)}, u32[]{:S(2)}, u32[]{:S(2)}) collective-permute-start(f32[256,128]{1,0:T(8,128)S(1)} %get-tuple-element.34.kept_ref), channel_id=1, source_target_pairs={{1,0},{0,2},{3,1},{2,3},{5,4},{4,6},{7,5},{6,7},{9,8},{8,10},{11,9... | collective-permute-start | bytes 393224 | tf_op jit(solution)/shard_map/ppermute | solution.py:806
  26.4 3.9 %collective-permute-done.6.came0_ref = f32[256,128]{1,0:T(8,128)S(1)} collective-permute-done((f32[256,128]{1,0:T(8,128)S(1)}, f32[256,128]{1,0:T(8,128)S(1)}, u32[]{:S(2)}, u32[]{:S(2)}) %collective-permute-start.6) | collective-permute-done | bytes 131104 | tf_op jit(solution)/shard_map/ppermute | solution.py:806
  30.2 2.7 %collective-permute-done.7.came1_ref = f32[256,128]{1,0:T(8,128)S(1)} collective-permute-done((f32[256,128]{1,0:T(8,128)S(1)}, f32[256,128]{1,0:T(8,128)S(1)}, u32[]{:S(2)}, u32[]{:S(2)}) %collective-permute-start.7) | collective-permute-done | bytes 131104 | tf_op jit(solution)/shard_map/ppermute | solution.py:806
  32.9 0.9 %shard_map.24 = (f32[256,128]{1,0:T(8,128)S(1)}, f32[256,128]{1,0:T(8,128)S(1)}, f32[256,128]{1,0:T(8,128)S(1)}, f32[256,128]{1,0:T(8,128)S(1)}, f32[96,128]{1,0:T(8,128)S(1)}) custom-call(f32[256,128]{1,0:T(8,128)S(1)} %get-tuple-element.34.kept_ref, f32[256,128]{1,0:T(8,128)S(1)} %get-tuple-element.35.sent_ref, ...), custom_call_target="tpu_custom_call" | custom-call | tf_op jit(solution)/shard_map/pallas_call | solution.py:764
  33.9 0.9 %shard_map.25 = f32[96,128]{1,0:T(8,128)S(1)} custom-call(f32[256,128]{1,0:T(8,128)S(1)} %get-tuple-element.36.refs_0_.even_ref, f32[256,128]{1,0:T(8,128)S(1)} %get-tuple-element.37.refs_1_.odd_ref, f32[256,128]{1,0:T(8,128)S(1)} %get-tuple-element.38.refs_2_, f32[256,128]{1,0:T(8,128)S(1)} %get-tuple-element.39.refs_3_), custom_call_target="tpu_custom_call" | custom-call | tf_op jit(solution)/shard_map/pallas_call | solution.py:764
  35.2 0.6 %collective-permute-start.10 = (f32[96,128]{1,0:T(8,128)S(1)}, f32[96,128]{1,0:T(8,128)S(1)}, u32[]{:S(2)}, u32[]{:S(2)}) collective-permute-start(f32[96,128]{1,0:T(8,128)S(1)} %add.7.refs_0_), channel_id=1, source_target_pairs={{0,16},{4,20},{8,24},{12,28},{16,0},{20,4},{24,8},{28,12},{1,17},{... | collective-permute-start | bytes 147464 | tf_op jit(solution)/shard_map/ppermute | solution.py:747
  35.7 1.5 %collective-permute-start.11 = (f32[96,128]{1,0:T(8,128)S(1)}, f32[96,128]{1,0:T(8,128)S(1)}, u32[]{:S(2)}, u32[]{:S(2)}) collective-permute-start(f32[96,128]{1,0:T(8,128)S(1)} %add.7.refs_0_), channel_id=1, source_target_pairs={{0,24},{4,28},{8,16},{12,20},{16,8},{20,12},{24,0},{28,4},{1,25},{... | collective-permute-start | bytes 147464 | tf_op jit(solution)/shard_map/ppermute | solution.py:747
  37.2 1.5 %collective-permute-start.9 = (f32[96,128]{1,0:T(8,128)S(1)}, f32[96,128]{1,0:T(8,128)S(1)}, u32[]{:S(2)}, u32[]{:S(2)}) collective-permute-start(f32[96,128]{1,0:T(8,128)S(1)} %add.7.refs_0_), channel_id=1, source_target_pairs={{0,8},{4,12},{8,0},{12,4},{16,24},{20,28},{24,16},{28,20},{1,9},{5... | collective-permute-start | bytes 147464 | tf_op jit(solution)/shard_map/ppermute | solution.py:747
  38.7 1.1 %collective-permute-done.10.refs_2_ = f32[96,128]{1,0:T(8,128)S(1)} collective-permute-done((f32[96,128]{1,0:T(8,128)S(1)}, f32[96,128]{1,0:T(8,128)S(1)}, u32[]{:S(2)}, u32[]{:S(2)}) %collective-permute-start.10) | collective-permute-done | bytes 49184 | tf_op jit(solution)/shard_map/ppermute | solution.py:747
  39.8 0.9 %collective-permute-done.11.refs_3_ = f32[96,128]{1,0:T(8,128)S(1)} collective-permute-done((f32[96,128]{1,0:T(8,128)S(1)}, f32[96,128]{1,0:T(8,128)S(1)}, u32[]{:S(2)}, u32[]{:S(2)}) %collective-permute-start.11) | collective-permute-done | bytes 49184 | tf_op jit(solution)/shard_map/ppermute | solution.py:747
  40.8 0.6 %collective-permute-done.9.refs_1_ = f32[96,128]{1,0:T(8,128)S(1)} collective-permute-done((f32[96,128]{1,0:T(8,128)S(1)}, f32[96,128]{1,0:T(8,128)S(1)}, u32[]{:S(2)}, u32[]{:S(2)}) %collective-permute-start.9) | collective-permute-done | bytes 49184 | tf_op jit(solution)/shard_map/ppermute | solution.py:747
  41.4 1.0 %shard_map.26.found_ref.refs_4_ = f32[176,128]{1,0:T(8,128)S(1)} custom-call(f32[96,128]{1,0:T(8,128)S(1)} %add.7.refs_0_, f32[96,128]{1,0:T(8,128)S(1)} %collective-permute-done.9.refs_1_, f32[96,128]{1,0:T(8,128)S(1)} %collective-permute-done.10.refs_2_, f32[96,128]{1,0:T(8,128)S(1)} %collective-permute-done.11.refs_3_), custom_call_target="tpu_custom_call" | custom-call | tf_op jit(solution)/shard_map/pallas_call | solution.py:764
  42.5 0.7 %shard_map.27 = (f32[256,128]{1,0:T(8,128)S(1)}, f32[256,128]{1,0:T(8,128)S(1)}) custom-call(f32[256,128]{1,0:T(8,128)S(1)} %get-tuple-element.36.refs_0_.even_ref, f32[256,128]{1,0:T(8,128)S(1)} %get-tuple-element.37.refs_1_.odd_ref, f32[176,128]{1,0:T(8,128)S(1)} %shard_map.26.found_ref.refs_4_), custom_call_target="tpu_custom_call" | custom-call | tf_op jit(solution)/shard_map/pallas_call | solution.py:764
  43.8 1.6 %shard_map.28 = (f32[256,128]{1,0:T(8,128)S(1)}, f32[256,128]{1,0:T(8,128)S(1)}) custom-call(f32[256,128]{1,0:T(8,128)S(1)} %get-tuple-element.41.refs_0_, f32[256,128]{1,0:T(8,128)S(1)} %get-tuple-element.42.refs_1_, f32[256,128]{1,0:T(8,128)S(1)} %get-tuple-element.38.refs_2_, f32[256,128]{1,0:T(8,128)S(1)} %get-tuple-element.39.refs_3_, ...), custom_call_target="tpu_custom_call" | custom-call | tf_op jit(solution)/shard_map/pallas_call | solution.py:764
  45.3 1.8 %collective-permute-start.13 = (f32[256,128]{1,0:T(8,128)S(1)}, f32[256,128]{1,0:T(8,128)S(1)}, u32[]{:S(2)}, u32[]{:S(2)}) collective-permute-start(f32[256,128]{1,0:T(8,128)S(1)} %get-tuple-element.43), channel_id=1, source_target_pairs={{2,0},{0,1},{3,2},{1,3},{6,4},{4,5},{7,6},{5,7},{10,8},{8,9},{11,1... | collective-permute-start | bytes 393224 | tf_op jit(solution)/shard_map/ppermute | solution.py:812
  47.1 4.7 %collective-permute-done.13 = f32[256,128]{1,0:T(8,128)S(1)} collective-permute-done((f32[256,128]{1,0:T(8,128)S(1)}, f32[256,128]{1,0:T(8,128)S(1)}, u32[]{:S(2)}, u32[]{:S(2)}) %collective-permute-start.13) | collective-permute-done | bytes 131104 | tf_op jit(solution)/shard_map/ppermute | solution.py:812
  51.9 0.7 %pad_maximum_fusion = f32[256,256]{1,0:T(8,128)} fusion(f32[256,128]{1,0:T(8,128)S(1)} %get-tuple-element.46, f32[256,128]{1,0:T(8,128)S(1)} %get-tuple-element.45), kind=kLoop, calls=%fused_computation | loop fusion | flops 65536 | bytes 524288 | tf_op jit(solution)/shard_map/concatenate | solution.py:816
  (14 shorter events, 2.3 us)
Async XLA Ops:
  0.0 0.9 %copy-start = (f32[256,256]{1,0:T(8,128)S(1)}, f32[256,256]{1,0:T(8,128)}, u32[]{:S(2)}) copy-start(f32[256,256]{1,0:T(8,128)} %basis_ref.3) | copy-start | bytes 786436
  1.1 7.4 %collective-permute-start = (f32[304,128]{1,0:T(8,128)S(1)}, f32[304,128]{1,0:T(8,128)S(1)}, u32[]{:S(2)}, u32[]{:S(2)}) collective-permute-start(f32[304,128]{1,0:T(8,128)S(1)} %shard_map.18), channel_id=1, source_target_pairs={{1,0},{0,2},{3,1},{2,3},{5,4},{4,6},{7,5},{6,7},{9,8},{8,10},{11,9... | collective-permute-start | bytes 466952 | tf_op jit(solution)/shard_map/ppermute | solution.py:799
  9.5 1.3 %collective-permute-start.1 = (f32[96,128]{1,0:T(8,128)S(1)}, f32[96,128]{1,0:T(8,128)S(1)}, u32[]{:S(2)}, u32[]{:S(2)}) collective-permute-start(f32[96,128]{1,0:T(8,128)S(1)} %get-tuple-element.31), channel_id=1, source_target_pairs={{0,4},{4,0},{8,12},{12,8},{16,20},{20,16},{24,28},{28,24},{1,5},{5... | collective-permute-start | bytes 147464 | tf_op jit(solution)/shard_map/ppermute | solution.py:747
  10.8 4.1 %collective-permute-start.2 = (f32[96,128]{1,0:T(8,128)S(1)}, f32[96,128]{1,0:T(8,128)S(1)}, u32[]{:S(2)}, u32[]{:S(2)}) collective-permute-start(f32[96,128]{1,0:T(8,128)S(1)} %add.6.refs_0_), channel_id=1, source_target_pairs={{0,8},{4,12},{8,0},{12,4},{16,24},{20,28},{24,16},{28,20},{1,9},{5... | collective-permute-start | bytes 147464 | tf_op jit(solution)/shard_map/ppermute | solution.py:747
  12.4 4.1 %collective-permute-start.3 = (f32[96,128]{1,0:T(8,128)S(1)}, f32[96,128]{1,0:T(8,128)S(1)}, u32[]{:S(2)}, u32[]{:S(2)}) collective-permute-start(f32[96,128]{1,0:T(8,128)S(1)} %add.6.refs_0_), channel_id=1, source_target_pairs={{0,16},{4,20},{8,24},{12,28},{16,0},{20,4},{24,8},{28,12},{1,17},{... | collective-permute-start | bytes 147464 | tf_op jit(solution)/shard_map/ppermute | solution.py:747
  13.9 5.0 %collective-permute-start.4 = (f32[96,128]{1,0:T(8,128)S(1)}, f32[96,128]{1,0:T(8,128)S(1)}, u32[]{:S(2)}, u32[]{:S(2)}) collective-permute-start(f32[96,128]{1,0:T(8,128)S(1)} %add.6.refs_0_), channel_id=1, source_target_pairs={{0,24},{4,28},{8,16},{12,20},{16,8},{20,12},{24,0},{28,4},{1,25},{... | collective-permute-start | bytes 147464 | tf_op jit(solution)/shard_map/ppermute | solution.py:747
  19.9 1.4 %collective-permute-start.5 = (f32[176,128]{1,0:T(8,128)S(1)}, f32[176,128]{1,0:T(8,128)S(1)}, u32[]{:S(2)}, u32[]{:S(2)}) collective-permute-start(f32[176,128]{1,0:T(8,128)S(1)} %shard_map.21.found_ref.refs_4_), channel_id=1, source_target_pairs={{0,4},{4,0},{8,12},{12,8},{16,20},{20,16},{24,28},{28,24},{1,5},{5... | collective-permute-start | bytes 270344 | tf_op jit(solution)/shard_map/ppermute | solution.py:747
  22.9 7.4 %collective-permute-start.6 = (f32[256,128]{1,0:T(8,128)S(1)}, f32[256,128]{1,0:T(8,128)S(1)}, u32[]{:S(2)}, u32[]{:S(2)}) collective-permute-start(f32[256,128]{1,0:T(8,128)S(1)} %get-tuple-element.35.sent_ref), channel_id=1, source_target_pairs={{2,0},{3,2},{0,1},{1,3},{6,4},{7,6},{4,5},{5,7},{10,8},{11,10},{8,... | collective-permute-start | bytes 393224 | tf_op jit(solution)/shard_map/ppermute | solution.py:806
  25.3 7.6 %collective-permute-start.7 = (f32[256,128]{1,0:T(8,128)S(1)}, f32[256,128]{1,0:T(8,128)S(1)}, u32[]{:S(2)}, u32[]{:S(2)}) collective-permute-start(f32[256,128]{1,0:T(8,128)S(1)} %get-tuple-element.34.kept_ref), channel_id=1, source_target_pairs={{1,0},{0,2},{3,1},{2,3},{5,4},{4,6},{7,5},{6,7},{9,8},{8,10},{11,9... | collective-permute-start | bytes 393224 | tf_op jit(solution)/shard_map/ppermute | solution.py:806
  33.9 1.3 %collective-permute-start.8 = (f32[96,128]{1,0:T(8,128)S(1)}, f32[96,128]{1,0:T(8,128)S(1)}, u32[]{:S(2)}, u32[]{:S(2)}) collective-permute-start(f32[96,128]{1,0:T(8,128)S(1)} %get-tuple-element.40), channel_id=1, source_target_pairs={{0,4},{4,0},{8,12},{12,8},{16,20},{20,16},{24,28},{28,24},{1,5},{5... | collective-permute-start | bytes 147464 | tf_op jit(solution)/shard_map/ppermute | solution.py:747
  35.2 4.7 %collective-permute-start.10 = (f32[96,128]{1,0:T(8,128)S(1)}, f32[96,128]{1,0:T(8,128)S(1)}, u32[]{:S(2)}, u32[]{:S(2)}) collective-permute-start(f32[96,128]{1,0:T(8,128)S(1)} %add.7.refs_0_), channel_id=1, source_target_pairs={{0,16},{4,20},{8,24},{12,28},{16,0},{20,4},{24,8},{28,12},{1,17},{... | collective-permute-start | bytes 147464 | tf_op jit(solution)/shard_map/ppermute | solution.py:747
  35.7 5.0 %collective-permute-start.11 = (f32[96,128]{1,0:T(8,128)S(1)}, f32[96,128]{1,0:T(8,128)S(1)}, u32[]{:S(2)}, u32[]{:S(2)}) collective-permute-start(f32[96,128]{1,0:T(8,128)S(1)} %add.7.refs_0_), channel_id=1, source_target_pairs={{0,24},{4,28},{8,16},{12,20},{16,8},{20,12},{24,0},{28,4},{1,25},{... | collective-permute-start | bytes 147464 | tf_op jit(solution)/shard_map/ppermute | solution.py:747
  37.2 4.1 %collective-permute-start.9 = (f32[96,128]{1,0:T(8,128)S(1)}, f32[96,128]{1,0:T(8,128)S(1)}, u32[]{:S(2)}, u32[]{:S(2)}) collective-permute-start(f32[96,128]{1,0:T(8,128)S(1)} %add.7.refs_0_), channel_id=1, source_target_pairs={{0,8},{4,12},{8,0},{12,4},{16,24},{20,28},{24,16},{28,20},{1,9},{5... | collective-permute-start | bytes 147464 | tf_op jit(solution)/shard_map/ppermute | solution.py:747
  42.4 1.4 %collective-permute-start.12 = (f32[176,128]{1,0:T(8,128)S(1)}, f32[176,128]{1,0:T(8,128)S(1)}, u32[]{:S(2)}, u32[]{:S(2)}) collective-permute-start(f32[176,128]{1,0:T(8,128)S(1)} %shard_map.26.found_ref.refs_4_), channel_id=1, source_target_pairs={{0,4},{4,0},{8,12},{12,8},{16,20},{20,16},{24,28},{28,24},{1,5},{5... | collective-permute-start | bytes 270344 | tf_op jit(solution)/shard_map/ppermute | solution.py:747
  45.3 6.5 %collective-permute-start.13 = (f32[256,128]{1,0:T(8,128)S(1)}, f32[256,128]{1,0:T(8,128)S(1)}, u32[]{:S(2)}, u32[]{:S(2)}) collective-permute-start(f32[256,128]{1,0:T(8,128)S(1)} %get-tuple-element.43), channel_id=1, source_target_pairs={{2,0},{0,1},{3,2},{1,3},{6,4},{4,5},{7,6},{5,7},{10,8},{8,9},{11,1... | collective-permute-start | bytes 393224 | tf_op jit(solution)/shard_map/ppermute | solution.py:812

commit v17 on v14

--- a/solution.py
+++ b/solution.py
@@ -15,7 +15,7 @@
 FAR_DIAGS = 32
 WINDOW = 32
 NEAR = 16
-STRIP = 16
+STRIP = REACH - 1
 BACK = 3
 
 
@@ -215,6 +215,10 @@
         band_ref[q * diags : (q + 1) * diags, :] = band
 
 
+def strip_rows(rows, width):
+    return -(-rows // (8 * (width // (2 * STRIP)))) * 8
+
+
 def payload_kernel(sends_second, basis_ref, payload_ref):
     rows, cols = basis_ref.shape
     width = cols // 2
@@ -227,12 +231,19 @@
     in_first = place < half
     source = 2 * jnp.where(in_first, place, place - half) + odd
     payload_ref[:rows] = jnp.where(in_first, take_lanes(first, source), take_lanes(second, source))
-    group = rows * 2 * STRIP // width
-    source = 2 * (start + lane % STRIP) + lane // STRIP % 2
+    places = width // STRIP
+    place = lane - STRIP * sum(jnp.where(lane >= STRIP * i, 1, 0) for i in range(1, places))
+    odd = sum(jnp.where(lane >= STRIP * i, 1 if i % 2 else -1, 0) for i in range(1, places))
+    source = jnp.minimum(2 * (start + place) + odd, width - 1)
+    group = strip_rows(rows, width)
     strips = jnp.zeros((group, width), jnp.float32)
-    for i in range(rows // group):
-        here = lane // (2 * STRIP) == i
-        strips = jnp.where(here, take_lanes(second[i * group : (i + 1) * group], source), strips)
+    for i, at in enumerate(range(0, rows, group)):
+        here = jnp.logical_and(lane >= 2 * STRIP * i, lane < 2 * STRIP * (i + 1))
+        part = take_lanes(second[at : at + group], source)
+        if part.shape[0] < group:
+            spare = jnp.zeros((group - part.shape[0], width), jnp.float32)
+            part = jnp.concatenate((part, spare), axis=0)
+        strips = jnp.where(here, part, strips)
     payload_ref[rows:] = strips
 
 
@@ -249,8 +260,12 @@
     group = strips.shape[0]
     columns = []
     for j, x in enumerate((main, left(main, half))):
-        ends = [right(strips, half - (2 * i + j) * STRIP) for i in range(rows // group)]
-        x = jnp.where(lane < half, x, jnp.where(lane < half + STRIP, jnp.concatenate(ends), 0.0))
+        ends = [
+            right(strips, half - (2 * i + j) * STRIP)[: rows - at]
+            for i, at in enumerate(range(0, rows, group))
+        ]
+        ends = jnp.concatenate(ends, axis=0)
+        x = jnp.where(lane < half, x, jnp.where(lane < half + STRIP, ends, 0.0))
         columns.append(jnp.where(second, right(x, half - STRIP), x))
     return columns
 
@@ -472,25 +487,30 @@
 
 
 def cross_partial(x_even, x_odd, y_even, y_odd, x_second, y_second):
-    rows, width = x_even.shape
+    width = x_even.shape[1]
+    half = width // 2
     x_starts, y_starts = near_starts(width)
-    lane = lanes_of(x_even)
-
-    def window(even, odd, flag, starts):
-        start = jnp.where(flag, starts[1], starts[0])
-        at_zero = pltpu.roll(even, (width - start) % width, 1)
-        at_next = pltpu.roll(odd, (width - start + WINDOW) % width, 1)
-        return jnp.where(lane < WINDOW, at_zero, jnp.where(lane < 2 * WINDOW, at_next, 0.0))
-
-    corner = lax.dot_general(
-        window(y_even, y_odd, y_second, y_starts),
-        window(x_even, x_odd, x_second, x_starts),
+    lane = line_lanes(x_even)
+
+    def window(even, odd, start):
+        here = jnp.logical_and(lane >= start, lane < start + WINDOW)
+        return jnp.where(here, even, right(odd, half))
+
+    x_start = jnp.where(x_second, x_starts[1], x_starts[0])
+    y_start = jnp.where(y_second, y_starts[1], y_starts[0])
+    product = lax.dot_general(
+        window(y_even, y_odd, y_start),
+        window(x_even, x_odd, x_start),
         (((0,), (0,)), ((), ())),
         precision=lax.Precision.HIGHEST,
         preferred_element_type=jnp.float32,
     )
-    low = lax.broadcasted_iota(jnp.int32, (WINDOW, width), 1) < 2 * WINDOW
-    return jnp.where(low, corner[:WINDOW], right(corner[WINDOW : 2 * WINDOW], 2 * WINDOW))
+    product = pltpu.roll(product, (width - y_start) % width, 0)
+    product = pltpu.roll(product, (width - x_start) % width, 1)
+    upper, lower = product[:WINDOW], product[half : half + WINDOW]
+    upper = jnp.where(lane < WINDOW, upper, left(upper, half - WINDOW))
+    lower = jnp.where(lane < half + WINDOW, right(lower, half), right(lower, WINDOW))
+    return jnp.where(lane < half, upper, lower)
 
 
 def own_rotation(angles, second, swapped, first_pair):
@@ -773,7 +793,7 @@
     pair_total = lax.axis_size("pair")
     column = (rows, width)
     opened = (column,) * 4 + ((NEAR, width), (4 * PACKED + NEAR, width))
-    payload = (rows + rows * 2 * STRIP // width, width)
+    payload = (rows + strip_rows(rows, width), width)
 
     sends, sends_second, gets_second, own_second, is_second = first_moves(pair_total)
     (sent,) = call(functools.partial(payload_kernel, sends_second), (payload,), basis)

time: 53 us -> 52.8 us (level)
  no operation moved by 1% of the time
where the time goes in v17:
time: 52.8 us; the launch traced here: 52.7 us
  waiting for transfers between devices  23.3 us (44%)
  starting transfers between devices  16.6 us (31%)
  Pallas kernels  11 us (21%)
  local copies, waits for them, and re-layouts  0.95 us (2%)
  other arithmetic  0.75 us (1%)
    pallas_call x12, Pallas kernels, call(): pl.pallas_call(kernel, out_shape=out, compiler_params=pltpu.CompilerParam...  11 us
    ppermute x10, waiting for transfers between devices, swap(): lax.ppermute(x, axis, [(i, i ^ mask) for i in range(lax.axis_size(axis))])  8.91 us
    ppermute x2, waiting for transfers between devices, per_device(): came = lax.ppermute(sent, 'pair', sends)  7.79 us
    ppermute x10, starting transfers between devices, swap(): lax.ppermute(x, axis, [(i, i ^ mask) for i in range(lax.axis_size(axis))])  7.26 us
    ppermute x2, waiting for transfers between devices, per_device(): came = [lax.ppermute(x, 'pair', s) for x, s in zip((sent, kept), sends)]  6.56 us
    ppermute x2, starting transfers between devices, per_device(): came = lax.ppermute(sent, 'pair', sends)  5.88 us
    ppermute x2, starting transfers between devices, per_device(): came = [lax.ppermute(x, 'pair', s) for x, s in zip((sent, kept), sends)]  3.5 us
  transfers between devices with their start and end apart: 14, of which 14 were waited for; matrix products, arithmetic and copies ran while one was open for 0% of the time, Pallas kernels for 6%

profile of v17, /device:TPU:0, one launch (start us, length us, event | category | flops | bytes accessed | tf_op | source)
XLA Modules:
  0.0 52.7 jit_solution(4999308089436987004)
XLA Ops:
  0.0 0.9 %copy-done = f32[256,256]{1,0:T(8,128)S(1)} copy-done((f32[256,256]{1,0:T(8,128)S(1)}, f32[256,256]{1,0:T(8,128)}, u32[]{:S(2)}) %copy-start) | copy-done | bytes 262168
  1.1 4.1 %collective-permute-start = (f32[304,128]{1,0:T(8,128)S(1)}, f32[304,128]{1,0:T(8,128)S(1)}, u32[]{:S(2)}, u32[]{:S(2)}) collective-permute-start(f32[304,128]{1,0:T(8,128)S(1)} %shard_map.18), channel_id=1, source_target_pairs={{1,0},{0,2},{3,1},{2,3},{5,4},{4,6},{7,5},{6,7},{9,8},{8,10},{11,9... | collective-permute-start | bytes 466952 | tf_op jit(solution)/shard_map/ppermute | solution.py:800
  5.4 3.1 %collective-permute-done.payload_ref = f32[304,128]{1,0:T(8,128)S(1)} collective-permute-done((f32[304,128]{1,0:T(8,128)S(1)}, f32[304,128]{1,0:T(8,128)S(1)}, u32[]{:S(2)}, u32[]{:S(2)}) %collective-permute-start) | collective-permute-done | bytes 155680 | tf_op jit(solution)/shard_map/ppermute | solution.py:800
  8.5 1.2 %shard_map.19 = (f32[256,128]{1,0:T(8,128)S(1)}, f32[256,128]{1,0:T(8,128)S(1)}, f32[256,128]{1,0:T(8,128)S(1)}, f32[256,128]{1,0:T(8,128)S(1)}, f32[16,128]{1,0:T(8,128)S(1)}, /*index=5*/f32[80,128]{1,0:T(8,128)S(1)}) custom-call(f32[256,128]{1,0:T(8,128)S(1)} %get-tuple-element.27.even_ref, f32[256,128]{1,0:T(8,128)S(1)} %get-tuple-element.28.odd_ref, ...), custom_call_target="tpu_custom_call" | custom-call | tf_op jit(solution)/shard_map/pallas_call | solution.py:765
  9.8 0.8 %shard_map.20 = f32[80,128]{1,0:T(8,128)S(1)} custom-call(f32[256,128]{1,0:T(8,128)S(1)} %get-tuple-element.29.even_ref, f32[256,128]{1,0:T(8,128)S(1)} %get-tuple-element.30.odd_ref, f32[16,128]{1,0:T(8,128)S(1)} %get-tuple-element.31.corner_ref), custom_call_target="tpu_custom_call" | custom-call | tf_op jit(solution)/shard_map/pallas_call | solution.py:765
  11.0 1.5 %collective-permute-start.2 = (f32[80,128]{1,0:T(8,128)S(1)}, f32[80,128]{1,0:T(8,128)S(1)}, u32[]{:S(2)}, u32[]{:S(2)}) collective-permute-start(f32[80,128]{1,0:T(8,128)S(1)} %add.6.refs_0_), channel_id=1, source_target_pairs={{0,8},{4,12},{8,0},{12,4},{16,24},{20,28},{24,16},{28,20},{1,9},{5... | collective-permute-start | bytes 122888 | tf_op jit(solution)/shard_map/ppermute | solution.py:748
  12.5 1.5 %collective-permute-start.3 = (f32[80,128]{1,0:T(8,128)S(1)}, f32[80,128]{1,0:T(8,128)S(1)}, u32[]{:S(2)}, u32[]{:S(2)}) collective-permute-start(f32[80,128]{1,0:T(8,128)S(1)} %add.6.refs_0_), channel_id=1, source_target_pairs={{0,16},{4,20},{8,24},{12,28},{16,0},{20,4},{24,8},{28,12},{1,17},{... | collective-permute-start | bytes 122888 | tf_op jit(solution)/shard_map/ppermute | solution.py:748
  14.5 0.5 collective-permute-done.2.refs_1_
  15.0 1.5 %collective-permute-done.3.refs_2_ = f32[80,128]{1,0:T(8,128)S(1)} collective-permute-done((f32[80,128]{1,0:T(8,128)S(1)}, f32[80,128]{1,0:T(8,128)S(1)}, u32[]{:S(2)}, u32[]{:S(2)}) %collective-permute-start.3) | collective-permute-done | bytes 40992 | tf_op jit(solution)/shard_map/ppermute | solution.py:748
  16.5 2.4 %collective-permute-done.4.refs_3_ = f32[80,128]{1,0:T(8,128)S(1)} collective-permute-done((f32[80,128]{1,0:T(8,128)S(1)}, f32[80,128]{1,0:T(8,128)S(1)}, u32[]{:S(2)}, u32[]{:S(2)}) %collective-permute-start.4) | collective-permute-done | bytes 40992 | tf_op jit(solution)/shard_map/ppermute | solution.py:748
  18.9 1.0 %shard_map.21.found_ref.refs_4_ = f32[160,128]{1,0:T(8,128)S(1)} custom-call(f32[80,128]{1,0:T(8,128)S(1)} %add.6.refs_0_, f32[80,128]{1,0:T(8,128)S(1)} %collective-permute-done.2.refs_1_, f32[80,128]{1,0:T(8,128)S(1)} %collective-permute-done.3.refs_2_, f32[80,128]{1,0:T(8,128)S(1)} %collective-permute-done.4.refs_3_), custom_call_target="tpu_custom_call" | custom-call | tf_op jit(solution)/shard_map/pallas_call | solution.py:765
  20.1 0.7 %shard_map.22 = (f32[256,128]{1,0:T(8,128)S(1)}, f32[256,128]{1,0:T(8,128)S(1)}) custom-call(f32[256,128]{1,0:T(8,128)S(1)} %get-tuple-element.29.even_ref, f32[256,128]{1,0:T(8,128)S(1)} %get-tuple-element.30.odd_ref, f32[160,128]{1,0:T(8,128)S(1)} %shard_map.21.found_ref.refs_4_), custom_call_target="tpu_custom_call" | custom-call | tf_op jit(solution)/shard_map/pallas_call | solution.py:765
  20.8 0.6 %collective-permute-done.5.refs_5_ = f32[160,128]{1,0:T(8,128)S(1)} collective-permute-done((f32[160,128]{1,0:T(8,128)S(1)}, f32[160,128]{1,0:T(8,128)S(1)}, u32[]{:S(2)}, u32[]{:S(2)}) %collective-permute-start.5) | collective-permute-done | bytes 81952 | tf_op jit(solution)/shard_map/ppermute | solution.py:748
  21.3 1.6 %shard_map.23 = (f32[256,128]{1,0:T(8,128)S(1)}, f32[256,128]{1,0:T(8,128)S(1)}) custom-call(f32[256,128]{1,0:T(8,128)S(1)} %get-tuple-element.33.refs_0_, f32[256,128]{1,0:T(8,128)S(1)} %get-tuple-element.34.refs_1_, f32[256,128]{1,0:T(8,128)S(1)} %get-tuple-element.35.refs_2_, f32[256,128]{1,0:T(8,128)S(1)} %get-tuple-element.36.refs_3_, ...), custom_call_target="tpu_custom_call" | custom-call | tf_op jit(solution)/shard_map/pallas_call | solution.py:765
  22.9 2.4 %collective-permute-start.6 = (f32[256,128]{1,0:T(8,128)S(1)}, f32[256,128]{1,0:T(8,128)S(1)}, u32[]{:S(2)}, u32[]{:S(2)}) collective-permute-start(f32[256,128]{1,0:T(8,128)S(1)} %get-tuple-element.38.sent_ref), channel_id=1, source_target_pairs={{2,0},{3,2},{0,1},{1,3},{6,4},{7,6},{4,5},{5,7},{10,8},{11,10},{8,... | collective-permute-start | bytes 393224 | tf_op jit(solution)/shard_map/ppermute | solution.py:807
  25.3 1.1 %collective-permute-start.7 = (f32[256,128]{1,0:T(8,128)S(1)}, f32[256,128]{1,0:T(8,128)S(1)}, u32[]{:S(2)}, u32[]{:S(2)}) collective-permute-start(f32[256,128]{1,0:T(8,128)S(1)} %get-tuple-element.37.kept_ref), channel_id=1, source_target_pairs={{1,0},{0,2},{3,1},{2,3},{5,4},{4,6},{7,5},{6,7},{9,8},{8,10},{11,9... | collective-permute-start | bytes 393224 | tf_op jit(solution)/shard_map/ppermute | solution.py:807
  26.4 3.9 %collective-permute-done.6.came0_ref = f32[256,128]{1,0:T(8,128)S(1)} collective-permute-done((f32[256,128]{1,0:T(8,128)S(1)}, f32[256,128]{1,0:T(8,128)S(1)}, u32[]{:S(2)}, u32[]{:S(2)}) %collective-permute-start.6) | collective-permute-done | bytes 131104 | tf_op jit(solution)/shard_map/ppermute | solution.py:807
  30.3 2.7 %collective-permute-done.7.came1_ref = f32[256,128]{1,0:T(8,128)S(1)} collective-permute-done((f32[256,128]{1,0:T(8,128)S(1)}, f32[256,128]{1,0:T(8,128)S(1)}, u32[]{:S(2)}, u32[]{:S(2)}) %collective-permute-start.7) | collective-permute-done | bytes 131104 | tf_op jit(solution)/shard_map/ppermute | solution.py:807
  33.0 1.1 %shard_map.24 = (f32[256,128]{1,0:T(8,128)S(1)}, f32[256,128]{1,0:T(8,128)S(1)}, f32[256,128]{1,0:T(8,128)S(1)}, f32[256,128]{1,0:T(8,128)S(1)}, f32[16,128]{1,0:T(8,128)S(1)}, /*index=5*/f32[80,128]{1,0:T(8,128)S(1)}) custom-call(f32[256,128]{1,0:T(8,128)S(1)} %get-tuple-element.37.kept_ref, f32[256,128]{1,0:T(8,128)S(1)} %get-tuple-element.38.sent_ref, ...), custom_call_target="tpu_custom_call" | custom-call | tf_op jit(solution)/shard_map/pallas_call | solution.py:765
  34.2 0.8 %shard_map.25 = f32[80,128]{1,0:T(8,128)S(1)} custom-call(f32[256,128]{1,0:T(8,128)S(1)} %get-tuple-element.39.even_ref, f32[256,128]{1,0:T(8,128)S(1)} %get-tuple-element.40.odd_ref, f32[16,128]{1,0:T(8,128)S(1)} %get-tuple-element.41.corner_ref), custom_call_target="tpu_custom_call" | custom-call | tf_op jit(solution)/shard_map/pallas_call | solution.py:765
  35.9 1.5 %collective-permute-start.11 = (f32[80,128]{1,0:T(8,128)S(1)}, f32[80,128]{1,0:T(8,128)S(1)}, u32[]{:S(2)}, u32[]{:S(2)}) collective-permute-start(f32[80,128]{1,0:T(8,128)S(1)} %add.7.refs_0_), channel_id=1, source_target_pairs={{0,24},{4,28},{8,16},{12,20},{16,8},{20,12},{24,0},{28,4},{1,25},{... | collective-permute-start | bytes 122888 | tf_op jit(solution)/shard_map/ppermute | solution.py:748
  37.4 1.5 %collective-permute-start.9 = (f32[80,128]{1,0:T(8,128)S(1)}, f32[80,128]{1,0:T(8,128)S(1)}, u32[]{:S(2)}, u32[]{:S(2)}) collective-permute-start(f32[80,128]{1,0:T(8,128)S(1)} %add.7.refs_0_), channel_id=1, source_target_pairs={{0,8},{4,12},{8,0},{12,4},{16,24},{20,28},{24,16},{28,20},{1,9},{5... | collective-permute-start | bytes 122888 | tf_op jit(solution)/shard_map/ppermute | solution.py:748
  38.9 1.0 %collective-permute-done.10.refs_2_ = f32[80,128]{1,0:T(8,128)S(1)} collective-permute-done((f32[80,128]{1,0:T(8,128)S(1)}, f32[80,128]{1,0:T(8,128)S(1)}, u32[]{:S(2)}, u32[]{:S(2)}) %collective-permute-start.10) | collective-permute-done | bytes 40992 | tf_op jit(solution)/shard_map/ppermute | solution.py:748
  39.8 1.0 %collective-permute-done.11.refs_3_ = f32[80,128]{1,0:T(8,128)S(1)} collective-permute-done((f32[80,128]{1,0:T(8,128)S(1)}, f32[80,128]{1,0:T(8,128)S(1)}, u32[]{:S(2)}, u32[]{:S(2)}) %collective-permute-start.11) | collective-permute-done | bytes 40992 | tf_op jit(solution)/shard_map/ppermute | solution.py:748
  40.8 0.6 %collective-permute-done.9.refs_1_ = f32[80,128]{1,0:T(8,128)S(1)} collective-permute-done((f32[80,128]{1,0:T(8,128)S(1)}, f32[80,128]{1,0:T(8,128)S(1)}, u32[]{:S(2)}, u32[]{:S(2)}) %collective-permute-start.9) | collective-permute-done | bytes 40992 | tf_op jit(solution)/shard_map/ppermute | solution.py:748
  41.4 1.0 %shard_map.26.found_ref.refs_4_ = f32[160,128]{1,0:T(8,128)S(1)} custom-call(f32[80,128]{1,0:T(8,128)S(1)} %add.7.refs_0_, f32[80,128]{1,0:T(8,128)S(1)} %collective-permute-done.9.refs_1_, f32[80,128]{1,0:T(8,128)S(1)} %collective-permute-done.10.refs_2_, f32[80,128]{1,0:T(8,128)S(1)} %collective-permute-done.11.refs_3_), custom_call_target="tpu_custom_call" | custom-call | tf_op jit(solution)/shard_map/pallas_call | solution.py:765
  42.5 0.7 %shard_map.27 = (f32[256,128]{1,0:T(8,128)S(1)}, f32[256,128]{1,0:T(8,128)S(1)}) custom-call(f32[256,128]{1,0:T(8,128)S(1)} %get-tuple-element.39.even_ref, f32[256,128]{1,0:T(8,128)S(1)} %get-tuple-element.40.odd_ref, f32[160,128]{1,0:T(8,128)S(1)} %shard_map.26.found_ref.refs_4_), custom_call_target="tpu_custom_call" | custom-call | tf_op jit(solution)/shard_map/pallas_call | solution.py:765
  43.2 0.6 %collective-permute-done.12.refs_5_ = f32[160,128]{1,0:T(8,128)S(1)} collective-permute-done((f32[160,128]{1,0:T(8,128)S(1)}, f32[160,128]{1,0:T(8,128)S(1)}, u32[]{:S(2)}, u32[]{:S(2)}) %collective-permute-start.12) | collective-permute-done | bytes 81952 | tf_op jit(solution)/shard_map/ppermute | solution.py:748
  43.8 1.6 %shard_map.28 = (f32[256,128]{1,0:T(8,128)S(1)}, f32[256,128]{1,0:T(8,128)S(1)}) custom-call(f32[256,128]{1,0:T(8,128)S(1)} %get-tuple-element.43.refs_0_, f32[256,128]{1,0:T(8,128)S(1)} %get-tuple-element.44.refs_1_, f32[256,128]{1,0:T(8,128)S(1)} %get-tuple-element.45.refs_2_, f32[256,128]{1,0:T(8,128)S(1)} %get-tuple-element.46.refs_3_, ...), custom_call_target="tpu_custom_call" | custom-call | tf_op jit(solution)/shard_map/pallas_call | solution.py:765
  45.4 1.8 %collective-permute-start.13 = (f32[256,128]{1,0:T(8,128)S(1)}, f32[256,128]{1,0:T(8,128)S(1)}, u32[]{:S(2)}, u32[]{:S(2)}) collective-permute-start(f32[256,128]{1,0:T(8,128)S(1)} %get-tuple-element.47), channel_id=1, source_target_pairs={{2,0},{0,1},{3,2},{1,3},{6,4},{4,5},{7,6},{5,7},{10,8},{8,9},{11,1... | collective-permute-start | bytes 393224 | tf_op jit(solution)/shard_map/ppermute | solution.py:813
  47.2 4.7 %collective-permute-done.13 = f32[256,128]{1,0:T(8,128)S(1)} collective-permute-done((f32[256,128]{1,0:T(8,128)S(1)}, f32[256,128]{1,0:T(8,128)S(1)}, u32[]{:S(2)}, u32[]{:S(2)}) %collective-permute-start.13) | collective-permute-done | bytes 131104 | tf_op jit(solution)/shard_map/ppermute | solution.py:813
  51.9 0.7 %pad_maximum_fusion = f32[256,256]{1,0:T(8,128)} fusion(f32[256,128]{1,0:T(8,128)S(1)} %get-tuple-element.50, f32[256,128]{1,0:T(8,128)S(1)} %get-tuple-element.49), kind=kLoop, calls=%fused_computation | loop fusion | flops 65536 | bytes 524288 | tf_op jit(solution)/shard_map/concatenate | solution.py:817
  (14 shorter events, 2.6 us)
Async XLA Ops:
  0.0 0.9 %copy-start = (f32[256,256]{1,0:T(8,128)S(1)}, f32[256,256]{1,0:T(8,128)}, u32[]{:S(2)}) copy-start(f32[256,256]{1,0:T(8,128)} %basis_ref.3) | copy-start | bytes 786436
  1.1 7.4 %collective-permute-start = (f32[304,128]{1,0:T(8,128)S(1)}, f32[304,128]{1,0:T(8,128)S(1)}, u32[]{:S(2)}, u32[]{:S(2)}) collective-permute-start(f32[304,128]{1,0:T(8,128)S(1)} %shard_map.18), channel_id=1, source_target_pairs={{1,0},{0,2},{3,1},{2,3},{5,4},{4,6},{7,5},{6,7},{9,8},{8,10},{11,9... | collective-permute-start | bytes 466952 | tf_op jit(solution)/shard_map/ppermute | solution.py:800
  9.7 1.3 %collective-permute-start.1 = (f32[80,128]{1,0:T(8,128)S(1)}, f32[80,128]{1,0:T(8,128)S(1)}, u32[]{:S(2)}, u32[]{:S(2)}) collective-permute-start(f32[80,128]{1,0:T(8,128)S(1)} %get-tuple-element.32), channel_id=1, source_target_pairs={{0,4},{4,0},{8,12},{12,8},{16,20},{20,16},{24,28},{28,24},{1,5},{5... | collective-permute-start | bytes 122888 | tf_op jit(solution)/shard_map/ppermute | solution.py:748
  11.0 4.0 %collective-permute-start.2 = (f32[80,128]{1,0:T(8,128)S(1)}, f32[80,128]{1,0:T(8,128)S(1)}, u32[]{:S(2)}, u32[]{:S(2)}) collective-permute-start(f32[80,128]{1,0:T(8,128)S(1)} %add.6.refs_0_), channel_id=1, source_target_pairs={{0,8},{4,12},{8,0},{12,4},{16,24},{20,28},{24,16},{28,20},{1,9},{5... | collective-permute-start | bytes 122888 | tf_op jit(solution)/shard_map/ppermute | solution.py:748
  12.5 4.0 %collective-permute-start.3 = (f32[80,128]{1,0:T(8,128)S(1)}, f32[80,128]{1,0:T(8,128)S(1)}, u32[]{:S(2)}, u32[]{:S(2)}) collective-permute-start(f32[80,128]{1,0:T(8,128)S(1)} %add.6.refs_0_), channel_id=1, source_target_pairs={{0,16},{4,20},{8,24},{12,28},{16,0},{20,4},{24,8},{28,12},{1,17},{... | collective-permute-start | bytes 122888 | tf_op jit(solution)/shard_map/ppermute | solution.py:748
  14.0 4.9 %collective-permute-start.4 = (f32[80,128]{1,0:T(8,128)S(1)}, f32[80,128]{1,0:T(8,128)S(1)}, u32[]{:S(2)}, u32[]{:S(2)}) collective-permute-start(f32[80,128]{1,0:T(8,128)S(1)} %add.6.refs_0_), channel_id=1, source_target_pairs={{0,24},{4,28},{8,16},{12,20},{16,8},{20,12},{24,0},{28,4},{1,25},{... | collective-permute-start | bytes 122888 | tf_op jit(solution)/shard_map/ppermute | solution.py:748
  20.0 1.3 %collective-permute-start.5 = (f32[160,128]{1,0:T(8,128)S(1)}, f32[160,128]{1,0:T(8,128)S(1)}, u32[]{:S(2)}, u32[]{:S(2)}) collective-permute-start(f32[160,128]{1,0:T(8,128)S(1)} %shard_map.21.found_ref.refs_4_), channel_id=1, source_target_pairs={{0,4},{4,0},{8,12},{12,8},{16,20},{20,16},{24,28},{28,24},{1,5},{5... | collective-permute-start | bytes 245768 | tf_op jit(solution)/shard_map/ppermute | solution.py:748
  22.9 7.4 %collective-permute-start.6 = (f32[256,128]{1,0:T(8,128)S(1)}, f32[256,128]{1,0:T(8,128)S(1)}, u32[]{:S(2)}, u32[]{:S(2)}) collective-permute-start(f32[256,128]{1,0:T(8,128)S(1)} %get-tuple-element.38.sent_ref), channel_id=1, source_target_pairs={{2,0},{3,2},{0,1},{1,3},{6,4},{7,6},{4,5},{5,7},{10,8},{11,10},{8,... | collective-permute-start | bytes 393224 | tf_op jit(solution)/shard_map/ppermute | solution.py:807
  25.3 7.6 %collective-permute-start.7 = (f32[256,128]{1,0:T(8,128)S(1)}, f32[256,128]{1,0:T(8,128)S(1)}, u32[]{:S(2)}, u32[]{:S(2)}) collective-permute-start(f32[256,128]{1,0:T(8,128)S(1)} %get-tuple-element.37.kept_ref), channel_id=1, source_target_pairs={{1,0},{0,2},{3,1},{2,3},{5,4},{4,6},{7,5},{6,7},{9,8},{8,10},{11,9... | collective-permute-start | bytes 393224 | tf_op jit(solution)/shard_map/ppermute | solution.py:807
  34.1 1.3 %collective-permute-start.8 = (f32[80,128]{1,0:T(8,128)S(1)}, f32[80,128]{1,0:T(8,128)S(1)}, u32[]{:S(2)}, u32[]{:S(2)}) collective-permute-start(f32[80,128]{1,0:T(8,128)S(1)} %get-tuple-element.42), channel_id=1, source_target_pairs={{0,4},{4,0},{8,12},{12,8},{16,20},{20,16},{24,28},{28,24},{1,5},{5... | collective-permute-start | bytes 122888 | tf_op jit(solution)/shard_map/ppermute | solution.py:748
  35.4 4.4 %collective-permute-start.10 = (f32[80,128]{1,0:T(8,128)S(1)}, f32[80,128]{1,0:T(8,128)S(1)}, u32[]{:S(2)}, u32[]{:S(2)}) collective-permute-start(f32[80,128]{1,0:T(8,128)S(1)} %add.7.refs_0_), channel_id=1, source_target_pairs={{0,16},{4,20},{8,24},{12,28},{16,0},{20,4},{24,8},{28,12},{1,17},{... | collective-permute-start | bytes 122888 | tf_op jit(solution)/shard_map/ppermute | solution.py:748
  35.9 4.9 %collective-permute-start.11 = (f32[80,128]{1,0:T(8,128)S(1)}, f32[80,128]{1,0:T(8,128)S(1)}, u32[]{:S(2)}, u32[]{:S(2)}) collective-permute-start(f32[80,128]{1,0:T(8,128)S(1)} %add.7.refs_0_), channel_id=1, source_target_pairs={{0,24},{4,28},{8,16},{12,20},{16,8},{20,12},{24,0},{28,4},{1,25},{... | collective-permute-start | bytes 122888 | tf_op jit(solution)/shard_map/ppermute | solution.py:748
  37.4 4.0 %collective-permute-start.9 = (f32[80,128]{1,0:T(8,128)S(1)}, f32[80,128]{1,0:T(8,128)S(1)}, u32[]{:S(2)}, u32[]{:S(2)}) collective-permute-start(f32[80,128]{1,0:T(8,128)S(1)} %add.7.refs_0_), channel_id=1, source_target_pairs={{0,8},{4,12},{8,0},{12,4},{16,24},{20,28},{24,16},{28,20},{1,9},{5... | collective-permute-start | bytes 122888 | tf_op jit(solution)/shard_map/ppermute | solution.py:748
  42.5 1.3 %collective-permute-start.12 = (f32[160,128]{1,0:T(8,128)S(1)}, f32[160,128]{1,0:T(8,128)S(1)}, u32[]{:S(2)}, u32[]{:S(2)}) collective-permute-start(f32[160,128]{1,0:T(8,128)S(1)} %shard_map.26.found_ref.refs_4_), channel_id=1, source_target_pairs={{0,4},{4,0},{8,12},{12,8},{16,20},{20,16},{24,28},{28,24},{1,5},{5... | collective-permute-start | bytes 245768 | tf_op jit(solution)/shard_map/ppermute | solution.py:748
  45.4 6.5 %collective-permute-start.13 = (f32[256,128]{1,0:T(8,128)S(1)}, f32[256,128]{1,0:T(8,128)S(1)}, u32[]{:S(2)}, u32[]{:S(2)}) collective-permute-start(f32[256,128]{1,0:T(8,128)S(1)} %get-tuple-element.47), channel_id=1, source_target_pairs={{2,0},{0,1},{3,2},{1,3},{6,4},{4,5},{7,6},{5,7},{10,8},{8,9},{11,1... | collective-permute-start | bytes 393224 | tf_op jit(solution)/shard_map/ppermute | solution.py:813

commit v18 on v16

--- a/solution.py
+++ b/solution.py
@@ -669,6 +669,8 @@
     flag = own_second_flag(is_second)
     quadrants = [unpack_far(part[q * PACKED : (q + 1) * PACKED], flag) for q in range(4)]
     angles = angles_of(quadrants)
+    first_pair = jnp.logical_not(on_odd_core())
+    found_ref[ROTATION:, :] = own_rotation(angles, flag, swapped_flag(is_second), first_pair)
     bands = carried(quadrants, angles)
     for step, pair in enumerate(angles):
         for i in (0, 1):
@@ -678,8 +680,6 @@
     for q in range(4):
         found_ref[NEAR + q * DIAGS : NEAR + (q + 1) * DIAGS, :] = bands[q][:DIAGS]
     found_ref[CORNER:ROTATION, :] = part[4 * PACKED :]
-    first_pair = jnp.logical_not(on_odd_core())
-    found_ref[ROTATION:, :] = own_rotation(angles, flag, swapped_flag(is_second), first_pair)
 
 
 CORNER = NEAR + 4 * DIAGS
@@ -755,7 +755,8 @@
     for group in groups[first_bit:]:
         x = pair_sums(arrays)
         masks = [group[0]] if len(group) == 1 else [group[0], group[1], group[0] | group[1]]
-        arrays = [x] + [swap(x, axis, mask) for mask in masks]
+        came = {mask: swap(x, axis, mask) for mask in reversed(masks)}
+        arrays = [x] + [came[mask] for mask in masks]
     return arrays
 
 

time: 52.7 us -> 52.6 us (level)
  no operation moved by 1% of the time
where the time goes in v18:
time: 52.6 us; the launch traced here: 52.5 us
  waiting for transfers between devices  23.1 us (44%)
  starting transfers between devices  16.8 us (32%)
  Pallas kernels  10.8 us (21%)
  local copies, waits for them, and re-layouts  0.95 us (2%)
  other arithmetic  0.76 us (1%)
    pallas_call x12, Pallas kernels, call(): pl.pallas_call(kernel, out_shape=out, compiler_params=pltpu.CompilerParam...  10.8 us
    ppermute x10, waiting for transfers between devices, swap(): lax.ppermute(x, axis, [(i, i ^ mask) for i in range(lax.axis_size(axis))])  8.81 us
    ppermute x2, waiting for transfers between devices, per_device(): came = lax.ppermute(sent, 'pair', sends)  7.78 us
    ppermute x10, starting transfers between devices, swap(): lax.ppermute(x, axis, [(i, i ^ mask) for i in range(lax.axis_size(axis))])  7.38 us
    ppermute x2, waiting for transfers between devices, per_device(): came = [lax.ppermute(x, 'pair', s) for x, s in zip((sent, kept), sends)]  6.56 us
    ppermute x2, starting transfers between devices, per_device(): came = lax.ppermute(sent, 'pair', sends)  5.88 us
    ppermute x2, starting transfers between devices, per_device(): came = [lax.ppermute(x, 'pair', s) for x, s in zip((sent, kept), sends)]  3.5 us
  transfers between devices with their start and end apart: 14, of which 14 were waited for; matrix products, arithmetic and copies ran while one was open for 0% of the time, Pallas kernels for 7%

profile of v18, /device:TPU:0, one launch (start us, length us, event | category | flops | bytes accessed | tf_op | source)
XLA Modules:
  0.0 52.5 jit_solution(6413537799635797208)
XLA Ops:
  0.0 0.9 %copy-done = f32[256,256]{1,0:T(8,128)S(1)} copy-done((f32[256,256]{1,0:T(8,128)S(1)}, f32[256,256]{1,0:T(8,128)}, u32[]{:S(2)}) %copy-start) | copy-done | bytes 262168
  1.1 4.1 %collective-permute-start = (f32[304,128]{1,0:T(8,128)S(1)}, f32[304,128]{1,0:T(8,128)S(1)}, u32[]{:S(2)}, u32[]{:S(2)}) collective-permute-start(f32[304,128]{1,0:T(8,128)S(1)} %shard_map.18), channel_id=1, source_target_pairs={{1,0},{0,2},{3,1},{2,3},{5,4},{4,6},{7,5},{6,7},{9,8},{8,10},{11,9... | collective-permute-start | bytes 466952 | tf_op jit(solution)/shard_map/ppermute | solution.py:800
  5.4 3.1 %collective-permute-done.payload_ref = f32[304,128]{1,0:T(8,128)S(1)} collective-permute-done((f32[304,128]{1,0:T(8,128)S(1)}, f32[304,128]{1,0:T(8,128)S(1)}, u32[]{:S(2)}, u32[]{:S(2)}) %collective-permute-start) | collective-permute-done | bytes 155680 | tf_op jit(solution)/shard_map/ppermute | solution.py:800
  8.5 1.0 %shard_map.19 = (f32[256,128]{1,0:T(8,128)S(1)}, f32[256,128]{1,0:T(8,128)S(1)}, f32[256,128]{1,0:T(8,128)S(1)}, f32[256,128]{1,0:T(8,128)S(1)}, f32[96,128]{1,0:T(8,128)S(1)}) custom-call(f32[256,128]{1,0:T(8,128)S(1)} %get-tuple-element.25.even_ref, f32[256,128]{1,0:T(8,128)S(1)} %get-tuple-element.26.odd_ref, f32[304,128]{1,0:T(8,128)S(1)} %collective-permute-done.payload_ref), custom_call_target="tpu_custom_call" | custom-call | tf_op jit(solution)/shard_map/pallas_call | solution.py:765
  9.6 1.0 %shard_map.20 = f32[96,128]{1,0:T(8,128)S(1)} custom-call(f32[256,128]{1,0:T(8,128)S(1)} %get-tuple-element.27.refs_0_.even_ref, f32[256,128]{1,0:T(8,128)S(1)} %get-tuple-element.28.refs_1_.odd_ref, f32[256,128]{1,0:T(8,128)S(1)} %get-tuple-element.29.refs_2_, f32[256,128]{1,0:T(8,128)S(1)} %get-tuple-element.30.refs_3_), custom_call_target="tpu_custom_call" | custom-call | tf_op jit(solution)/shard_map/pallas_call | solution.py:765
  10.8 1.6 %collective-permute-start.2 = (f32[96,128]{1,0:T(8,128)S(1)}, f32[96,128]{1,0:T(8,128)S(1)}, u32[]{:S(2)}, u32[]{:S(2)}) collective-permute-start(f32[96,128]{1,0:T(8,128)S(1)} %add.6.refs_0_), channel_id=1, source_target_pairs={{0,8},{4,12},{8,0},{12,4},{16,24},{20,28},{24,16},{28,20},{1,9},{5... | collective-permute-start | bytes 147464 | tf_op jit(solution)/shard_map/ppermute | solution.py:747
  12.4 1.5 %collective-permute-start.3 = (f32[96,128]{1,0:T(8,128)S(1)}, f32[96,128]{1,0:T(8,128)S(1)}, u32[]{:S(2)}, u32[]{:S(2)}) collective-permute-start(f32[96,128]{1,0:T(8,128)S(1)} %add.6.refs_0_), channel_id=1, source_target_pairs={{0,16},{4,20},{8,24},{12,28},{16,0},{20,4},{24,8},{28,12},{1,17},{... | collective-permute-start | bytes 147464 | tf_op jit(solution)/shard_map/ppermute | solution.py:747
  14.4 0.6 %collective-permute-done.2.refs_1_ = f32[96,128]{1,0:T(8,128)S(1)} collective-permute-done((f32[96,128]{1,0:T(8,128)S(1)}, f32[96,128]{1,0:T(8,128)S(1)}, u32[]{:S(2)}, u32[]{:S(2)}) %collective-permute-start.2) | collective-permute-done | bytes 49184 | tf_op jit(solution)/shard_map/ppermute | solution.py:747
  15.0 1.5 %collective-permute-done.3.refs_2_ = f32[96,128]{1,0:T(8,128)S(1)} collective-permute-done((f32[96,128]{1,0:T(8,128)S(1)}, f32[96,128]{1,0:T(8,128)S(1)}, u32[]{:S(2)}, u32[]{:S(2)}) %collective-permute-start.3) | collective-permute-done | bytes 49184 | tf_op jit(solution)/shard_map/ppermute | solution.py:747
  16.5 2.4 %collective-permute-done.4.refs_3_ = f32[96,128]{1,0:T(8,128)S(1)} collective-permute-done((f32[96,128]{1,0:T(8,128)S(1)}, f32[96,128]{1,0:T(8,128)S(1)}, u32[]{:S(2)}, u32[]{:S(2)}) %collective-permute-start.4) | collective-permute-done | bytes 49184 | tf_op jit(solution)/shard_map/ppermute | solution.py:747
  18.9 1.0 %shard_map.21.found_ref.refs_4_ = f32[176,128]{1,0:T(8,128)S(1)} custom-call(f32[96,128]{1,0:T(8,128)S(1)} %add.6.refs_0_, f32[96,128]{1,0:T(8,128)S(1)} %collective-permute-done.2.refs_1_, f32[96,128]{1,0:T(8,128)S(1)} %collective-permute-done.3.refs_2_, f32[96,128]{1,0:T(8,128)S(1)} %collective-permute-done.4.refs_3_), custom_call_target="tpu_custom_call" | custom-call | tf_op jit(solution)/shard_map/pallas_call | solution.py:765
  20.0 0.7 %shard_map.22 = (f32[256,128]{1,0:T(8,128)S(1)}, f32[256,128]{1,0:T(8,128)S(1)}) custom-call(f32[256,128]{1,0:T(8,128)S(1)} %get-tuple-element.27.refs_0_.even_ref, f32[256,128]{1,0:T(8,128)S(1)} %get-tuple-element.28.refs_1_.odd_ref, f32[176,128]{1,0:T(8,128)S(1)} %shard_map.21.found_ref.refs_4_), custom_call_target="tpu_custom_call" | custom-call | tf_op jit(solution)/shard_map/pallas_call | solution.py:765
  20.7 0.6 %collective-permute-done.5.refs_5_ = f32[176,128]{1,0:T(8,128)S(1)} collective-permute-done((f32[176,128]{1,0:T(8,128)S(1)}, f32[176,128]{1,0:T(8,128)S(1)}, u32[]{:S(2)}, u32[]{:S(2)}) %collective-permute-start.5) | collective-permute-done | bytes 90144 | tf_op jit(solution)/shard_map/ppermute | solution.py:747
  21.2 1.6 %shard_map.23 = (f32[256,128]{1,0:T(8,128)S(1)}, f32[256,128]{1,0:T(8,128)S(1)}) custom-call(f32[256,128]{1,0:T(8,128)S(1)} %get-tuple-element.32.refs_0_, f32[256,128]{1,0:T(8,128)S(1)} %get-tuple-element.33.refs_1_, f32[256,128]{1,0:T(8,128)S(1)} %get-tuple-element.29.refs_2_, f32[256,128]{1,0:T(8,128)S(1)} %get-tuple-element.30.refs_3_, ...), custom_call_target="tpu_custom_call" | custom-call | tf_op jit(solution)/shard_map/pallas_call | solution.py:765
  22.8 2.4 %collective-permute-start.6 = (f32[256,128]{1,0:T(8,128)S(1)}, f32[256,128]{1,0:T(8,128)S(1)}, u32[]{:S(2)}, u32[]{:S(2)}) collective-permute-start(f32[256,128]{1,0:T(8,128)S(1)} %get-tuple-element.35.sent_ref), channel_id=1, source_target_pairs={{2,0},{3,2},{0,1},{1,3},{6,4},{7,6},{4,5},{5,7},{10,8},{11,10},{8,... | collective-permute-start | bytes 393224 | tf_op jit(solution)/shard_map/ppermute | solution.py:807
  25.2 1.1 %collective-permute-start.7 = (f32[256,128]{1,0:T(8,128)S(1)}, f32[256,128]{1,0:T(8,128)S(1)}, u32[]{:S(2)}, u32[]{:S(2)}) collective-permute-start(f32[256,128]{1,0:T(8,128)S(1)} %get-tuple-element.34.kept_ref), channel_id=1, source_target_pairs={{1,0},{0,2},{3,1},{2,3},{5,4},{4,6},{7,5},{6,7},{9,8},{8,10},{11,9... | collective-permute-start | bytes 393224 | tf_op jit(solution)/shard_map/ppermute | solution.py:807
  26.3 3.9 %collective-permute-done.6.came0_ref = f32[256,128]{1,0:T(8,128)S(1)} collective-permute-done((f32[256,128]{1,0:T(8,128)S(1)}, f32[256,128]{1,0:T(8,128)S(1)}, u32[]{:S(2)}, u32[]{:S(2)}) %collective-permute-start.6) | collective-permute-done | bytes 131104 | tf_op jit(solution)/shard_map/ppermute | solution.py:807
  30.2 2.7 %collective-permute-done.7.came1_ref = f32[256,128]{1,0:T(8,128)S(1)} collective-permute-done((f32[256,128]{1,0:T(8,128)S(1)}, f32[256,128]{1,0:T(8,128)S(1)}, u32[]{:S(2)}, u32[]{:S(2)}) %collective-permute-start.7) | collective-permute-done | bytes 131104 | tf_op jit(solution)/shard_map/ppermute | solution.py:807
  32.9 0.9 %shard_map.24 = (f32[256,128]{1,0:T(8,128)S(1)}, f32[256,128]{1,0:T(8,128)S(1)}, f32[256,128]{1,0:T(8,128)S(1)}, f32[256,128]{1,0:T(8,128)S(1)}, f32[96,128]{1,0:T(8,128)S(1)}) custom-call(f32[256,128]{1,0:T(8,128)S(1)} %get-tuple-element.34.kept_ref, f32[256,128]{1,0:T(8,128)S(1)} %get-tuple-element.35.sent_ref, ...), custom_call_target="tpu_custom_call" | custom-call | tf_op jit(solution)/shard_map/pallas_call | solution.py:765
  33.9 0.9 %shard_map.25 = f32[96,128]{1,0:T(8,128)S(1)} custom-call(f32[256,128]{1,0:T(8,128)S(1)} %get-tuple-element.36.refs_0_.even_ref, f32[256,128]{1,0:T(8,128)S(1)} %get-tuple-element.37.refs_1_.odd_ref, f32[256,128]{1,0:T(8,128)S(1)} %get-tuple-element.38.refs_2_, f32[256,128]{1,0:T(8,128)S(1)} %get-tuple-element.39.refs_3_), custom_call_target="tpu_custom_call" | custom-call | tf_op jit(solution)/shard_map/pallas_call | solution.py:765
  35.1 0.6 %collective-permute-start.10 = (f32[96,128]{1,0:T(8,128)S(1)}, f32[96,128]{1,0:T(8,128)S(1)}, u32[]{:S(2)}, u32[]{:S(2)}) collective-permute-start(f32[96,128]{1,0:T(8,128)S(1)} %add.7.refs_0_), channel_id=1, source_target_pairs={{0,16},{4,20},{8,24},{12,28},{16,0},{20,4},{24,8},{28,12},{1,17},{... | collective-permute-start | bytes 147464 | tf_op jit(solution)/shard_map/ppermute | solution.py:747
  35.7 1.5 %collective-permute-start.11 = (f32[96,128]{1,0:T(8,128)S(1)}, f32[96,128]{1,0:T(8,128)S(1)}, u32[]{:S(2)}, u32[]{:S(2)}) collective-permute-start(f32[96,128]{1,0:T(8,128)S(1)} %add.7.refs_0_), channel_id=1, source_target_pairs={{0,24},{4,28},{8,16},{12,20},{16,8},{20,12},{24,0},{28,4},{1,25},{... | collective-permute-start | bytes 147464 | tf_op jit(solution)/shard_map/ppermute | solution.py:747
  37.2 1.5 %collective-permute-start.9 = (f32[96,128]{1,0:T(8,128)S(1)}, f32[96,128]{1,0:T(8,128)S(1)}, u32[]{:S(2)}, u32[]{:S(2)}) collective-permute-start(f32[96,128]{1,0:T(8,128)S(1)} %add.7.refs_0_), channel_id=1, source_target_pairs={{0,8},{4,12},{8,0},{12,4},{16,24},{20,28},{24,16},{28,20},{1,9},{5... | collective-permute-start | bytes 147464 | tf_op jit(solution)/shard_map/ppermute | solution.py:747
  38.7 1.1 %collective-permute-done.10.refs_2_ = f32[96,128]{1,0:T(8,128)S(1)} collective-permute-done((f32[96,128]{1,0:T(8,128)S(1)}, f32[96,128]{1,0:T(8,128)S(1)}, u32[]{:S(2)}, u32[]{:S(2)}) %collective-permute-start.10) | collective-permute-done | bytes 49184 | tf_op jit(solution)/shard_map/ppermute | solution.py:747
  39.8 0.9 %collective-permute-done.11.refs_3_ = f32[96,128]{1,0:T(8,128)S(1)} collective-permute-done((f32[96,128]{1,0:T(8,128)S(1)}, f32[96,128]{1,0:T(8,128)S(1)}, u32[]{:S(2)}, u32[]{:S(2)}) %collective-permute-start.11) | collective-permute-done | bytes 49184 | tf_op jit(solution)/shard_map/ppermute | solution.py:747
  40.7 0.6 %collective-permute-done.9.refs_1_ = f32[96,128]{1,0:T(8,128)S(1)} collective-permute-done((f32[96,128]{1,0:T(8,128)S(1)}, f32[96,128]{1,0:T(8,128)S(1)}, u32[]{:S(2)}, u32[]{:S(2)}) %collective-permute-start.9) | collective-permute-done | bytes 49184 | tf_op jit(solution)/shard_map/ppermute | solution.py:747
  41.3 1.0 %shard_map.26.found_ref.refs_4_ = f32[176,128]{1,0:T(8,128)S(1)} custom-call(f32[96,128]{1,0:T(8,128)S(1)} %add.7.refs_0_, f32[96,128]{1,0:T(8,128)S(1)} %collective-permute-done.9.refs_1_, f32[96,128]{1,0:T(8,128)S(1)} %collective-permute-done.10.refs_2_, f32[96,128]{1,0:T(8,128)S(1)} %collective-permute-done.11.refs_3_), custom_call_target="tpu_custom_call" | custom-call | tf_op jit(solution)/shard_map/pallas_call | solution.py:765
  42.4 0.7 %shard_map.27 = (f32[256,128]{1,0:T(8,128)S(1)}, f32[256,128]{1,0:T(8,128)S(1)}) custom-call(f32[256,128]{1,0:T(8,128)S(1)} %get-tuple-element.36.refs_0_.even_ref, f32[256,128]{1,0:T(8,128)S(1)} %get-tuple-element.37.refs_1_.odd_ref, f32[176,128]{1,0:T(8,128)S(1)} %shard_map.26.found_ref.refs_4_), custom_call_target="tpu_custom_call" | custom-call | tf_op jit(solution)/shard_map/pallas_call | solution.py:765
  43.7 1.6 %shard_map.28 = (f32[256,128]{1,0:T(8,128)S(1)}, f32[256,128]{1,0:T(8,128)S(1)}) custom-call(f32[256,128]{1,0:T(8,128)S(1)} %get-tuple-element.41.refs_0_, f32[256,128]{1,0:T(8,128)S(1)} %get-tuple-element.42.refs_1_, f32[256,128]{1,0:T(8,128)S(1)} %get-tuple-element.38.refs_2_, f32[256,128]{1,0:T(8,128)S(1)} %get-tuple-element.39.refs_3_, ...), custom_call_target="tpu_custom_call" | custom-call | tf_op jit(solution)/shard_map/pallas_call | solution.py:765
  45.2 1.8 %collective-permute-start.13 = (f32[256,128]{1,0:T(8,128)S(1)}, f32[256,128]{1,0:T(8,128)S(1)}, u32[]{:S(2)}, u32[]{:S(2)}) collective-permute-start(f32[256,128]{1,0:T(8,128)S(1)} %get-tuple-element.43), channel_id=1, source_target_pairs={{2,0},{0,1},{3,2},{1,3},{6,4},{4,5},{7,6},{5,7},{10,8},{8,9},{11,1... | collective-permute-start | bytes 393224 | tf_op jit(solution)/shard_map/ppermute | solution.py:813
  47.0 4.7 %collective-permute-done.13 = f32[256,128]{1,0:T(8,128)S(1)} collective-permute-done((f32[256,128]{1,0:T(8,128)S(1)}, f32[256,128]{1,0:T(8,128)S(1)}, u32[]{:S(2)}, u32[]{:S(2)}) %collective-permute-start.13) | collective-permute-done | bytes 131104 | tf_op jit(solution)/shard_map/ppermute | solution.py:813
  51.8 0.7 %pad_maximum_fusion = f32[256,256]{1,0:T(8,128)} fusion(f32[256,128]{1,0:T(8,128)S(1)} %get-tuple-element.46, f32[256,128]{1,0:T(8,128)S(1)} %get-tuple-element.45), kind=kLoop, calls=%fused_computation | loop fusion | flops 65536 | bytes 524288 | tf_op jit(solution)/shard_map/concatenate | solution.py:817
  (14 shorter events, 2.3 us)
Async XLA Ops:
  0.0 0.9 %copy-start = (f32[256,256]{1,0:T(8,128)S(1)}, f32[256,256]{1,0:T(8,128)}, u32[]{:S(2)}) copy-start(f32[256,256]{1,0:T(8,128)} %basis_ref.3) | copy-start | bytes 786436
  1.1 7.4 %collective-permute-start = (f32[304,128]{1,0:T(8,128)S(1)}, f32[304,128]{1,0:T(8,128)S(1)}, u32[]{:S(2)}, u32[]{:S(2)}) collective-permute-start(f32[304,128]{1,0:T(8,128)S(1)} %shard_map.18), channel_id=1, source_target_pairs={{1,0},{0,2},{3,1},{2,3},{5,4},{4,6},{7,5},{6,7},{9,8},{8,10},{11,9... | collective-permute-start | bytes 466952 | tf_op jit(solution)/shard_map/ppermute | solution.py:800
  9.5 1.3 %collective-permute-start.1 = (f32[96,128]{1,0:T(8,128)S(1)}, f32[96,128]{1,0:T(8,128)S(1)}, u32[]{:S(2)}, u32[]{:S(2)}) collective-permute-start(f32[96,128]{1,0:T(8,128)S(1)} %get-tuple-element.31), channel_id=1, source_target_pairs={{0,4},{4,0},{8,12},{12,8},{16,20},{20,16},{24,28},{28,24},{1,5},{5... | collective-permute-start | bytes 147464 | tf_op jit(solution)/shard_map/ppermute | solution.py:747
  10.8 4.1 %collective-permute-start.2 = (f32[96,128]{1,0:T(8,128)S(1)}, f32[96,128]{1,0:T(8,128)S(1)}, u32[]{:S(2)}, u32[]{:S(2)}) collective-permute-start(f32[96,128]{1,0:T(8,128)S(1)} %add.6.refs_0_), channel_id=1, source_target_pairs={{0,8},{4,12},{8,0},{12,4},{16,24},{20,28},{24,16},{28,20},{1,9},{5... | collective-permute-start | bytes 147464 | tf_op jit(solution)/shard_map/ppermute | solution.py:747
  12.4 4.1 %collective-permute-start.3 = (f32[96,128]{1,0:T(8,128)S(1)}, f32[96,128]{1,0:T(8,128)S(1)}, u32[]{:S(2)}, u32[]{:S(2)}) collective-permute-start(f32[96,128]{1,0:T(8,128)S(1)} %add.6.refs_0_), channel_id=1, source_target_pairs={{0,16},{4,20},{8,24},{12,28},{16,0},{20,4},{24,8},{28,12},{1,17},{... | collective-permute-start | bytes 147464 | tf_op jit(solution)/shard_map/ppermute | solution.py:747
  13.9 5.0 %collective-permute-start.4 = (f32[96,128]{1,0:T(8,128)S(1)}, f32[96,128]{1,0:T(8,128)S(1)}, u32[]{:S(2)}, u32[]{:S(2)}) collective-permute-start(f32[96,128]{1,0:T(8,128)S(1)} %add.6.refs_0_), channel_id=1, source_target_pairs={{0,24},{4,28},{8,16},{12,20},{16,8},{20,12},{24,0},{28,4},{1,25},{... | collective-permute-start | bytes 147464 | tf_op jit(solution)/shard_map/ppermute | solution.py:747
  19.9 1.4 %collective-permute-start.5 = (f32[176,128]{1,0:T(8,128)S(1)}, f32[176,128]{1,0:T(8,128)S(1)}, u32[]{:S(2)}, u32[]{:S(2)}) collective-permute-start(f32[176,128]{1,0:T(8,128)S(1)} %shard_map.21.found_ref.refs_4_), channel_id=1, source_target_pairs={{0,4},{4,0},{8,12},{12,8},{16,20},{20,16},{24,28},{28,24},{1,5},{5... | collective-permute-start | bytes 270344 | tf_op jit(solution)/shard_map/ppermute | solution.py:747
  22.8 7.4 %collective-permute-start.6 = (f32[256,128]{1,0:T(8,128)S(1)}, f32[256,128]{1,0:T(8,128)S(1)}, u32[]{:S(2)}, u32[]{:S(2)}) collective-permute-start(f32[256,128]{1,0:T(8,128)S(1)} %get-tuple-element.35.sent_ref), channel_id=1, source_target_pairs={{2,0},{3,2},{0,1},{1,3},{6,4},{7,6},{4,5},{5,7},{10,8},{11,10},{8,... | collective-permute-start | bytes 393224 | tf_op jit(solution)/shard_map/ppermute | solution.py:807
  25.2 7.6 %collective-permute-start.7 = (f32[256,128]{1,0:T(8,128)S(1)}, f32[256,128]{1,0:T(8,128)S(1)}, u32[]{:S(2)}, u32[]{:S(2)}) collective-permute-start(f32[256,128]{1,0:T(8,128)S(1)} %get-tuple-element.34.kept_ref), channel_id=1, source_target_pairs={{1,0},{0,2},{3,1},{2,3},{5,4},{4,6},{7,5},{6,7},{9,8},{8,10},{11,9... | collective-permute-start | bytes 393224 | tf_op jit(solution)/shard_map/ppermute | solution.py:807
  33.8 1.3 %collective-permute-start.8 = (f32[96,128]{1,0:T(8,128)S(1)}, f32[96,128]{1,0:T(8,128)S(1)}, u32[]{:S(2)}, u32[]{:S(2)}) collective-permute-start(f32[96,128]{1,0:T(8,128)S(1)} %get-tuple-element.40), channel_id=1, source_target_pairs={{0,4},{4,0},{8,12},{12,8},{16,20},{20,16},{24,28},{28,24},{1,5},{5... | collective-permute-start | bytes 147464 | tf_op jit(solution)/shard_map/ppermute | solution.py:747
  35.1 4.7 %collective-permute-start.10 = (f32[96,128]{1,0:T(8,128)S(1)}, f32[96,128]{1,0:T(8,128)S(1)}, u32[]{:S(2)}, u32[]{:S(2)}) collective-permute-start(f32[96,128]{1,0:T(8,128)S(1)} %add.7.refs_0_), channel_id=1, source_target_pairs={{0,16},{4,20},{8,24},{12,28},{16,0},{20,4},{24,8},{28,12},{1,17},{... | collective-permute-start | bytes 147464 | tf_op jit(solution)/shard_map/ppermute | solution.py:747
  35.7 5.0 %collective-permute-start.11 = (f32[96,128]{1,0:T(8,128)S(1)}, f32[96,128]{1,0:T(8,128)S(1)}, u32[]{:S(2)}, u32[]{:S(2)}) collective-permute-start(f32[96,128]{1,0:T(8,128)S(1)} %add.7.refs_0_), channel_id=1, source_target_pairs={{0,24},{4,28},{8,16},{12,20},{16,8},{20,12},{24,0},{28,4},{1,25},{... | collective-permute-start | bytes 147464 | tf_op jit(solution)/shard_map/ppermute | solution.py:747
  37.2 4.1 %collective-permute-start.9 = (f32[96,128]{1,0:T(8,128)S(1)}, f32[96,128]{1,0:T(8,128)S(1)}, u32[]{:S(2)}, u32[]{:S(2)}) collective-permute-start(f32[96,128]{1,0:T(8,128)S(1)} %add.7.refs_0_), channel_id=1, source_target_pairs={{0,8},{4,12},{8,0},{12,4},{16,24},{20,28},{24,16},{28,20},{1,9},{5... | collective-permute-start | bytes 147464 | tf_op jit(solution)/shard_map/ppermute | solution.py:747
  42.3 1.4 %collective-permute-start.12 = (f32[176,128]{1,0:T(8,128)S(1)}, f32[176,128]{1,0:T(8,128)S(1)}, u32[]{:S(2)}, u32[]{:S(2)}) collective-permute-start(f32[176,128]{1,0:T(8,128)S(1)} %shard_map.26.found_ref.refs_4_), channel_id=1, source_target_pairs={{0,4},{4,0},{8,12},{12,8},{16,20},{20,16},{24,28},{28,24},{1,5},{5... | collective-permute-start | bytes 270344 | tf_op jit(solution)/shard_map/ppermute | solution.py:747
  45.2 6.5 %collective-permute-start.13 = (f32[256,128]{1,0:T(8,128)S(1)}, f32[256,128]{1,0:T(8,128)S(1)}, u32[]{:S(2)}, u32[]{:S(2)}) collective-permute-start(f32[256,128]{1,0:T(8,128)S(1)} %get-tuple-element.43), channel_id=1, source_target_pairs={{2,0},{0,1},{3,2},{1,3},{6,4},{4,5},{7,6},{5,7},{10,8},{8,9},{11,1... | collective-permute-start | bytes 393224 | tf_op jit(solution)/shard_map/ppermute | solution.py:813

commit v19 on v18

--- a/solution.py
+++ b/solution.py
@@ -615,32 +615,39 @@
         part_ref[q * PACKED : (q + 1) * PACKED, :] = band
 
 
-def open_pairs(is_second, x, y, column_refs, other_ref):
-    flag = on_odd_core()
-    mine = [jnp.where(flag, b, a) for a, b in zip(x, y)]
-    theirs = [jnp.where(flag, a, b) for a, b in zip(x, y)]
-    for ref, value in zip(column_refs, mine + theirs):
+def open_pairs(is_second, theirs, mine, column_refs, other_ref):
+    second = either(on_odd_core(), among(is_second[0]), among(is_second[1]))
+    store_part(*theirs, second, other_ref)
+    other_ref[4 * PACKED :, :] = jnp.zeros((WINDOW, theirs[0].shape[1]), jnp.float32)
+    for ref, value in zip(column_refs, mine() + theirs):
         ref[...] = value
-    store_part(*theirs, either(flag, among(is_second[0]), among(is_second[1])), other_ref)
-    other_ref[4 * PACKED :, :] = jnp.zeros((WINDOW, theirs[0].shape[1]), jnp.float32)
 
 
 def first_open(own_second, gets_second, is_second, even_ref, odd_ref, payload_ref, *refs):
     *column_refs, other_ref = refs
     own = even_ref[...], odd_ref[...]
     came = unpacked(payload_ref[...], own[0].shape[0], among(gets_second))
-    flag = among(own_second)
-    x = [jnp.where(flag, b, a) for a, b in zip(own, came)]
-    y = [jnp.where(flag, a, b) for a, b in zip(own, came)]
-    open_pairs(is_second, x, y, column_refs, other_ref)
+    flag = jnp.logical_xor(among(own_second), jnp.logical_not(on_odd_core()))
+    theirs = [jnp.where(flag, b, a) for a, b in zip(own, came)]
+
+    def mine():
+        return [jnp.where(flag, a, b) for a, b in zip(own, came)]
+
+    open_pairs(is_second, theirs, mine, column_refs, other_ref)
 
 
 def fused_open(picks, is_second, kept_ref, sent_ref, came0_ref, came1_ref, *refs):
     *column_refs, other_ref = refs
     arrays = [ref[...] for ref in (sent_ref, kept_ref, came0_ref, came1_ref)]
     blocks = [choose(pick, arrays) for pick in picks]
-    x, y = split_pair(*blocks[:2]), split_pair(*blocks[2:])
-    open_pairs(is_second, x, y, column_refs, other_ref)
+    flag = on_odd_core()
+    theirs = split_pair(*(jnp.where(flag, a, b) for a, b in zip(blocks[:2], blocks[2:])))
+
+    def mine():
+        own = split_pair(*(jnp.where(flag, b, a) for a, b in zip(blocks[:2], blocks[2:])))
+        return list(own)
+
+    open_pairs(is_second, list(theirs), mine, column_refs, other_ref)
 
 
 def swapped_flag(is_second):

time: 52.6 us -> 52.6 us (level)
  no operation moved by 1% of the time
where the time goes in v19:
time: 52.6 us; the launch traced here: 52.4 us
  waiting for transfers between devices  23.1 us (44%)
  starting transfers between devices  16.8 us (32%)
  Pallas kernels  10.7 us (20%)
  local copies, waits for them, and re-layouts  0.95 us (2%)
  other arithmetic  0.76 us (1%)
    pallas_call x12, Pallas kernels, call(): pl.pallas_call(kernel, out_shape=out, compiler_params=pltpu.CompilerParam...  10.7 us
    ppermute x10, waiting for transfers between devices, swap(): lax.ppermute(x, axis, [(i, i ^ mask) for i in range(lax.axis_size(axis))])  8.8 us
    ppermute x2, waiting for transfers between devices, per_device(): came = lax.ppermute(sent, 'pair', sends)  7.78 us
    ppermute x10, starting transfers between devices, swap(): lax.ppermute(x, axis, [(i, i ^ mask) for i in range(lax.axis_size(axis))])  7.38 us
    ppermute x2, waiting for transfers between devices, per_device(): came = [lax.ppermute(x, 'pair', s) for x, s in zip((sent, kept), sends)]  6.56 us
    ppermute x2, starting transfers between devices, per_device(): came = lax.ppermute(sent, 'pair', sends)  5.89 us
    ppermute x2, starting transfers between devices, per_device(): came = [lax.ppermute(x, 'pair', s) for x, s in zip((sent, kept), sends)]  3.5 us
  transfers between devices with their start and end apart: 14, of which 14 were waited for; matrix products, arithmetic and copies ran while one was open for 0% of the time, Pallas kernels for 7%

profile of v19, /device:TPU:0, one launch (start us, length us, event | category | flops | bytes accessed | tf_op | source)
XLA Modules:
  0.0 52.4 jit_solution(12593126013098053525)
XLA Ops:
  0.0 0.9 %copy-done = f32[256,256]{1,0:T(8,128)S(1)} copy-done((f32[256,256]{1,0:T(8,128)S(1)}, f32[256,256]{1,0:T(8,128)}, u32[]{:S(2)}) %copy-start) | copy-done | bytes 262168
  1.1 4.1 %collective-permute-start = (f32[304,128]{1,0:T(8,128)S(1)}, f32[304,128]{1,0:T(8,128)S(1)}, u32[]{:S(2)}, u32[]{:S(2)}) collective-permute-start(f32[304,128]{1,0:T(8,128)S(1)} %shard_map.18), channel_id=1, source_target_pairs={{1,0},{0,2},{3,1},{2,3},{5,4},{4,6},{7,5},{6,7},{9,8},{8,10},{11,9... | collective-permute-start | bytes 466952 | tf_op jit(solution)/shard_map/ppermute | solution.py:807
  5.4 3.1 %collective-permute-done.payload_ref = f32[304,128]{1,0:T(8,128)S(1)} collective-permute-done((f32[304,128]{1,0:T(8,128)S(1)}, f32[304,128]{1,0:T(8,128)S(1)}, u32[]{:S(2)}, u32[]{:S(2)}) %collective-permute-start) | collective-permute-done | bytes 155680 | tf_op jit(solution)/shard_map/ppermute | solution.py:807
  8.5 1.0 %shard_map.19 = (f32[256,128]{1,0:T(8,128)S(1)}, f32[256,128]{1,0:T(8,128)S(1)}, f32[256,128]{1,0:T(8,128)S(1)}, f32[256,128]{1,0:T(8,128)S(1)}, f32[96,128]{1,0:T(8,128)S(1)}) custom-call(f32[256,128]{1,0:T(8,128)S(1)} %get-tuple-element.25.even_ref, f32[256,128]{1,0:T(8,128)S(1)} %get-tuple-element.26.odd_ref, f32[304,128]{1,0:T(8,128)S(1)} %collective-permute-done.payload_ref), custom_call_target="tpu_custom_call" | custom-call | tf_op jit(solution)/shard_map/pallas_call | solution.py:772
  9.6 1.0 %shard_map.20 = f32[96,128]{1,0:T(8,128)S(1)} custom-call(f32[256,128]{1,0:T(8,128)S(1)} %get-tuple-element.27.refs_0_.even_ref, f32[256,128]{1,0:T(8,128)S(1)} %get-tuple-element.28.refs_1_.odd_ref, f32[256,128]{1,0:T(8,128)S(1)} %get-tuple-element.29.refs_2_, f32[256,128]{1,0:T(8,128)S(1)} %get-tuple-element.30.refs_3_), custom_call_target="tpu_custom_call" | custom-call | tf_op jit(solution)/shard_map/pallas_call | solution.py:772
  10.8 1.6 %collective-permute-start.2 = (f32[96,128]{1,0:T(8,128)S(1)}, f32[96,128]{1,0:T(8,128)S(1)}, u32[]{:S(2)}, u32[]{:S(2)}) collective-permute-start(f32[96,128]{1,0:T(8,128)S(1)} %add.6.refs_0_), channel_id=1, source_target_pairs={{0,8},{4,12},{8,0},{12,4},{16,24},{20,28},{24,16},{28,20},{1,9},{5... | collective-permute-start | bytes 147464 | tf_op jit(solution)/shard_map/ppermute | solution.py:754
  12.4 1.5 %collective-permute-start.3 = (f32[96,128]{1,0:T(8,128)S(1)}, f32[96,128]{1,0:T(8,128)S(1)}, u32[]{:S(2)}, u32[]{:S(2)}) collective-permute-start(f32[96,128]{1,0:T(8,128)S(1)} %add.6.refs_0_), channel_id=1, source_target_pairs={{0,16},{4,20},{8,24},{12,28},{16,0},{20,4},{24,8},{28,12},{1,17},{... | collective-permute-start | bytes 147464 | tf_op jit(solution)/shard_map/ppermute | solution.py:754
  14.4 0.6 %collective-permute-done.2.refs_1_ = f32[96,128]{1,0:T(8,128)S(1)} collective-permute-done((f32[96,128]{1,0:T(8,128)S(1)}, f32[96,128]{1,0:T(8,128)S(1)}, u32[]{:S(2)}, u32[]{:S(2)}) %collective-permute-start.2) | collective-permute-done | bytes 49184 | tf_op jit(solution)/shard_map/ppermute | solution.py:754
  15.0 1.5 %collective-permute-done.3.refs_2_ = f32[96,128]{1,0:T(8,128)S(1)} collective-permute-done((f32[96,128]{1,0:T(8,128)S(1)}, f32[96,128]{1,0:T(8,128)S(1)}, u32[]{:S(2)}, u32[]{:S(2)}) %collective-permute-start.3) | collective-permute-done | bytes 49184 | tf_op jit(solution)/shard_map/ppermute | solution.py:754
  16.5 2.4 %collective-permute-done.4.refs_3_ = f32[96,128]{1,0:T(8,128)S(1)} collective-permute-done((f32[96,128]{1,0:T(8,128)S(1)}, f32[96,128]{1,0:T(8,128)S(1)}, u32[]{:S(2)}, u32[]{:S(2)}) %collective-permute-start.4) | collective-permute-done | bytes 49184 | tf_op jit(solution)/shard_map/ppermute | solution.py:754
  18.9 1.0 %shard_map.21.found_ref.refs_4_ = f32[176,128]{1,0:T(8,128)S(1)} custom-call(f32[96,128]{1,0:T(8,128)S(1)} %add.6.refs_0_, f32[96,128]{1,0:T(8,128)S(1)} %collective-permute-done.2.refs_1_, f32[96,128]{1,0:T(8,128)S(1)} %collective-permute-done.3.refs_2_, f32[96,128]{1,0:T(8,128)S(1)} %collective-permute-done.4.refs_3_), custom_call_target="tpu_custom_call" | custom-call | tf_op jit(solution)/shard_map/pallas_call | solution.py:772
  20.0 0.7 %shard_map.22 = (f32[256,128]{1,0:T(8,128)S(1)}, f32[256,128]{1,0:T(8,128)S(1)}) custom-call(f32[256,128]{1,0:T(8,128)S(1)} %get-tuple-element.27.refs_0_.even_ref, f32[256,128]{1,0:T(8,128)S(1)} %get-tuple-element.28.refs_1_.odd_ref, f32[176,128]{1,0:T(8,128)S(1)} %shard_map.21.found_ref.refs_4_), custom_call_target="tpu_custom_call" | custom-call | tf_op jit(solution)/shard_map/pallas_call | solution.py:772
  20.7 0.6 %collective-permute-done.5.refs_5_ = f32[176,128]{1,0:T(8,128)S(1)} collective-permute-done((f32[176,128]{1,0:T(8,128)S(1)}, f32[176,128]{1,0:T(8,128)S(1)}, u32[]{:S(2)}, u32[]{:S(2)}) %collective-permute-start.5) | collective-permute-done | bytes 90144 | tf_op jit(solution)/shard_map/ppermute | solution.py:754
  21.2 1.6 %shard_map.23 = (f32[256,128]{1,0:T(8,128)S(1)}, f32[256,128]{1,0:T(8,128)S(1)}) custom-call(f32[256,128]{1,0:T(8,128)S(1)} %get-tuple-element.32.refs_0_, f32[256,128]{1,0:T(8,128)S(1)} %get-tuple-element.33.refs_1_, f32[256,128]{1,0:T(8,128)S(1)} %get-tuple-element.29.refs_2_, f32[256,128]{1,0:T(8,128)S(1)} %get-tuple-element.30.refs_3_, ...), custom_call_target="tpu_custom_call" | custom-call | tf_op jit(solution)/shard_map/pallas_call | solution.py:772
  22.8 2.4 %collective-permute-start.6 = (f32[256,128]{1,0:T(8,128)S(1)}, f32[256,128]{1,0:T(8,128)S(1)}, u32[]{:S(2)}, u32[]{:S(2)}) collective-permute-start(f32[256,128]{1,0:T(8,128)S(1)} %get-tuple-element.35.sent_ref), channel_id=1, source_target_pairs={{2,0},{3,2},{0,1},{1,3},{6,4},{7,6},{4,5},{5,7},{10,8},{11,10},{8,... | collective-permute-start | bytes 393224 | tf_op jit(solution)/shard_map/ppermute | solution.py:814
  25.2 1.1 %collective-permute-start.7 = (f32[256,128]{1,0:T(8,128)S(1)}, f32[256,128]{1,0:T(8,128)S(1)}, u32[]{:S(2)}, u32[]{:S(2)}) collective-permute-start(f32[256,128]{1,0:T(8,128)S(1)} %get-tuple-element.34.kept_ref), channel_id=1, source_target_pairs={{1,0},{0,2},{3,1},{2,3},{5,4},{4,6},{7,5},{6,7},{9,8},{8,10},{11,9... | collective-permute-start | bytes 393224 | tf_op jit(solution)/shard_map/ppermute | solution.py:814
  26.3 3.9 %collective-permute-done.6.came0_ref = f32[256,128]{1,0:T(8,128)S(1)} collective-permute-done((f32[256,128]{1,0:T(8,128)S(1)}, f32[256,128]{1,0:T(8,128)S(1)}, u32[]{:S(2)}, u32[]{:S(2)}) %collective-permute-start.6) | collective-permute-done | bytes 131104 | tf_op jit(solution)/shard_map/ppermute | solution.py:814
  30.2 2.7 %collective-permute-done.7.came1_ref = f32[256,128]{1,0:T(8,128)S(1)} collective-permute-done((f32[256,128]{1,0:T(8,128)S(1)}, f32[256,128]{1,0:T(8,128)S(1)}, u32[]{:S(2)}, u32[]{:S(2)}) %collective-permute-start.7) | collective-permute-done | bytes 131104 | tf_op jit(solution)/shard_map/ppermute | solution.py:814
  32.9 0.9 %shard_map.24 = (f32[256,128]{1,0:T(8,128)S(1)}, f32[256,128]{1,0:T(8,128)S(1)}, f32[256,128]{1,0:T(8,128)S(1)}, f32[256,128]{1,0:T(8,128)S(1)}, f32[96,128]{1,0:T(8,128)S(1)}) custom-call(f32[256,128]{1,0:T(8,128)S(1)} %get-tuple-element.34.kept_ref, f32[256,128]{1,0:T(8,128)S(1)} %get-tuple-element.35.sent_ref, ...), custom_call_target="tpu_custom_call" | custom-call | tf_op jit(solution)/shard_map/pallas_call | solution.py:772
  33.8 0.9 %shard_map.25 = f32[96,128]{1,0:T(8,128)S(1)} custom-call(f32[256,128]{1,0:T(8,128)S(1)} %get-tuple-element.36.refs_0_.even_ref, f32[256,128]{1,0:T(8,128)S(1)} %get-tuple-element.37.refs_1_.odd_ref, f32[256,128]{1,0:T(8,128)S(1)} %get-tuple-element.38.refs_2_, f32[256,128]{1,0:T(8,128)S(1)} %get-tuple-element.39.refs_3_), custom_call_target="tpu_custom_call" | custom-call | tf_op jit(solution)/shard_map/pallas_call | solution.py:772
  35.0 0.6 %collective-permute-start.10 = (f32[96,128]{1,0:T(8,128)S(1)}, f32[96,128]{1,0:T(8,128)S(1)}, u32[]{:S(2)}, u32[]{:S(2)}) collective-permute-start(f32[96,128]{1,0:T(8,128)S(1)} %add.7.refs_0_), channel_id=1, source_target_pairs={{0,16},{4,20},{8,24},{12,28},{16,0},{20,4},{24,8},{28,12},{1,17},{... | collective-permute-start | bytes 147464 | tf_op jit(solution)/shard_map/ppermute | solution.py:754
  35.6 1.5 %collective-permute-start.11 = (f32[96,128]{1,0:T(8,128)S(1)}, f32[96,128]{1,0:T(8,128)S(1)}, u32[]{:S(2)}, u32[]{:S(2)}) collective-permute-start(f32[96,128]{1,0:T(8,128)S(1)} %add.7.refs_0_), channel_id=1, source_target_pairs={{0,24},{4,28},{8,16},{12,20},{16,8},{20,12},{24,0},{28,4},{1,25},{... | collective-permute-start | bytes 147464 | tf_op jit(solution)/shard_map/ppermute | solution.py:754
  37.1 1.5 %collective-permute-start.9 = (f32[96,128]{1,0:T(8,128)S(1)}, f32[96,128]{1,0:T(8,128)S(1)}, u32[]{:S(2)}, u32[]{:S(2)}) collective-permute-start(f32[96,128]{1,0:T(8,128)S(1)} %add.7.refs_0_), channel_id=1, source_target_pairs={{0,8},{4,12},{8,0},{12,4},{16,24},{20,28},{24,16},{28,20},{1,9},{5... | collective-permute-start | bytes 147464 | tf_op jit(solution)/shard_map/ppermute | solution.py:754
  38.6 1.1 %collective-permute-done.10.refs_2_ = f32[96,128]{1,0:T(8,128)S(1)} collective-permute-done((f32[96,128]{1,0:T(8,128)S(1)}, f32[96,128]{1,0:T(8,128)S(1)}, u32[]{:S(2)}, u32[]{:S(2)}) %collective-permute-start.10) | collective-permute-done | bytes 49184 | tf_op jit(solution)/shard_map/ppermute | solution.py:754
  39.7 0.9 %collective-permute-done.11.refs_3_ = f32[96,128]{1,0:T(8,128)S(1)} collective-permute-done((f32[96,128]{1,0:T(8,128)S(1)}, f32[96,128]{1,0:T(8,128)S(1)}, u32[]{:S(2)}, u32[]{:S(2)}) %collective-permute-start.11) | collective-permute-done | bytes 49184 | tf_op jit(solution)/shard_map/ppermute | solution.py:754
  40.7 0.6 %collective-permute-done.9.refs_1_ = f32[96,128]{1,0:T(8,128)S(1)} collective-permute-done((f32[96,128]{1,0:T(8,128)S(1)}, f32[96,128]{1,0:T(8,128)S(1)}, u32[]{:S(2)}, u32[]{:S(2)}) %collective-permute-start.9) | collective-permute-done | bytes 49184 | tf_op jit(solution)/shard_map/ppermute | solution.py:754
  41.2 1.0 %shard_map.26.found_ref.refs_4_ = f32[176,128]{1,0:T(8,128)S(1)} custom-call(f32[96,128]{1,0:T(8,128)S(1)} %add.7.refs_0_, f32[96,128]{1,0:T(8,128)S(1)} %collective-permute-done.9.refs_1_, f32[96,128]{1,0:T(8,128)S(1)} %collective-permute-done.10.refs_2_, f32[96,128]{1,0:T(8,128)S(1)} %collective-permute-done.11.refs_3_), custom_call_target="tpu_custom_call" | custom-call | tf_op jit(solution)/shard_map/pallas_call | solution.py:772
  42.3 0.7 %shard_map.27 = (f32[256,128]{1,0:T(8,128)S(1)}, f32[256,128]{1,0:T(8,128)S(1)}) custom-call(f32[256,128]{1,0:T(8,128)S(1)} %get-tuple-element.36.refs_0_.even_ref, f32[256,128]{1,0:T(8,128)S(1)} %get-tuple-element.37.refs_1_.odd_ref, f32[176,128]{1,0:T(8,128)S(1)} %shard_map.26.found_ref.refs_4_), custom_call_target="tpu_custom_call" | custom-call | tf_op jit(solution)/shard_map/pallas_call | solution.py:772
  43.6 1.6 %shard_map.28 = (f32[256,128]{1,0:T(8,128)S(1)}, f32[256,128]{1,0:T(8,128)S(1)}) custom-call(f32[256,128]{1,0:T(8,128)S(1)} %get-tuple-element.41.refs_0_, f32[256,128]{1,0:T(8,128)S(1)} %get-tuple-element.42.refs_1_, f32[256,128]{1,0:T(8,128)S(1)} %get-tuple-element.38.refs_2_, f32[256,128]{1,0:T(8,128)S(1)} %get-tuple-element.39.refs_3_, ...), custom_call_target="tpu_custom_call" | custom-call | tf_op jit(solution)/shard_map/pallas_call | solution.py:772
  45.2 1.8 %collective-permute-start.13 = (f32[256,128]{1,0:T(8,128)S(1)}, f32[256,128]{1,0:T(8,128)S(1)}, u32[]{:S(2)}, u32[]{:S(2)}) collective-permute-start(f32[256,128]{1,0:T(8,128)S(1)} %get-tuple-element.43), channel_id=1, source_target_pairs={{2,0},{0,1},{3,2},{1,3},{6,4},{4,5},{7,6},{5,7},{10,8},{8,9},{11,1... | collective-permute-start | bytes 393224 | tf_op jit(solution)/shard_map/ppermute | solution.py:820
  47.0 4.7 %collective-permute-done.13 = f32[256,128]{1,0:T(8,128)S(1)} collective-permute-done((f32[256,128]{1,0:T(8,128)S(1)}, f32[256,128]{1,0:T(8,128)S(1)}, u32[]{:S(2)}, u32[]{:S(2)}) %collective-permute-start.13) | collective-permute-done | bytes 131104 | tf_op jit(solution)/shard_map/ppermute | solution.py:820
  51.7 0.7 %pad_maximum_fusion = f32[256,256]{1,0:T(8,128)} fusion(f32[256,128]{1,0:T(8,128)S(1)} %get-tuple-element.46, f32[256,128]{1,0:T(8,128)S(1)} %get-tuple-element.45), kind=kLoop, calls=%fused_computation | loop fusion | flops 65536 | bytes 524288 | tf_op jit(solution)/shard_map/concatenate | solution.py:824
  (14 shorter events, 2.3 us)
Async XLA Ops:
  0.0 0.9 %copy-start = (f32[256,256]{1,0:T(8,128)S(1)}, f32[256,256]{1,0:T(8,128)}, u32[]{:S(2)}) copy-start(f32[256,256]{1,0:T(8,128)} %basis_ref.3) | copy-start | bytes 786436
  1.1 7.4 %collective-permute-start = (f32[304,128]{1,0:T(8,128)S(1)}, f32[304,128]{1,0:T(8,128)S(1)}, u32[]{:S(2)}, u32[]{:S(2)}) collective-permute-start(f32[304,128]{1,0:T(8,128)S(1)} %shard_map.18), channel_id=1, source_target_pairs={{1,0},{0,2},{3,1},{2,3},{5,4},{4,6},{7,5},{6,7},{9,8},{8,10},{11,9... | collective-permute-start | bytes 466952 | tf_op jit(solution)/shard_map/ppermute | solution.py:807
  9.5 1.3 %collective-permute-start.1 = (f32[96,128]{1,0:T(8,128)S(1)}, f32[96,128]{1,0:T(8,128)S(1)}, u32[]{:S(2)}, u32[]{:S(2)}) collective-permute-start(f32[96,128]{1,0:T(8,128)S(1)} %get-tuple-element.31), channel_id=1, source_target_pairs={{0,4},{4,0},{8,12},{12,8},{16,20},{20,16},{24,28},{28,24},{1,5},{5... | collective-permute-start | bytes 147464 | tf_op jit(solution)/shard_map/ppermute | solution.py:754
  10.8 4.1 %collective-permute-start.2 = (f32[96,128]{1,0:T(8,128)S(1)}, f32[96,128]{1,0:T(8,128)S(1)}, u32[]{:S(2)}, u32[]{:S(2)}) collective-permute-start(f32[96,128]{1,0:T(8,128)S(1)} %add.6.refs_0_), channel_id=1, source_target_pairs={{0,8},{4,12},{8,0},{12,4},{16,24},{20,28},{24,16},{28,20},{1,9},{5... | collective-permute-start | bytes 147464 | tf_op jit(solution)/shard_map/ppermute | solution.py:754
  12.4 4.1 %collective-permute-start.3 = (f32[96,128]{1,0:T(8,128)S(1)}, f32[96,128]{1,0:T(8,128)S(1)}, u32[]{:S(2)}, u32[]{:S(2)}) collective-permute-start(f32[96,128]{1,0:T(8,128)S(1)} %add.6.refs_0_), channel_id=1, source_target_pairs={{0,16},{4,20},{8,24},{12,28},{16,0},{20,4},{24,8},{28,12},{1,17},{... | collective-permute-start | bytes 147464 | tf_op jit(solution)/shard_map/ppermute | solution.py:754
  13.9 5.0 %collective-permute-start.4 = (f32[96,128]{1,0:T(8,128)S(1)}, f32[96,128]{1,0:T(8,128)S(1)}, u32[]{:S(2)}, u32[]{:S(2)}) collective-permute-start(f32[96,128]{1,0:T(8,128)S(1)} %add.6.refs_0_), channel_id=1, source_target_pairs={{0,24},{4,28},{8,16},{12,20},{16,8},{20,12},{24,0},{28,4},{1,25},{... | collective-permute-start | bytes 147464 | tf_op jit(solution)/shard_map/ppermute | solution.py:754
  19.9 1.4 %collective-permute-start.5 = (f32[176,128]{1,0:T(8,128)S(1)}, f32[176,128]{1,0:T(8,128)S(1)}, u32[]{:S(2)}, u32[]{:S(2)}) collective-permute-start(f32[176,128]{1,0:T(8,128)S(1)} %shard_map.21.found_ref.refs_4_), channel_id=1, source_target_pairs={{0,4},{4,0},{8,12},{12,8},{16,20},{20,16},{24,28},{28,24},{1,5},{5... | collective-permute-start | bytes 270344 | tf_op jit(solution)/shard_map/ppermute | solution.py:754
  22.8 7.4 %collective-permute-start.6 = (f32[256,128]{1,0:T(8,128)S(1)}, f32[256,128]{1,0:T(8,128)S(1)}, u32[]{:S(2)}, u32[]{:S(2)}) collective-permute-start(f32[256,128]{1,0:T(8,128)S(1)} %get-tuple-element.35.sent_ref), channel_id=1, source_target_pairs={{2,0},{3,2},{0,1},{1,3},{6,4},{7,6},{4,5},{5,7},{10,8},{11,10},{8,... | collective-permute-start | bytes 393224 | tf_op jit(solution)/shard_map/ppermute | solution.py:814
  25.2 7.6 %collective-permute-start.7 = (f32[256,128]{1,0:T(8,128)S(1)}, f32[256,128]{1,0:T(8,128)S(1)}, u32[]{:S(2)}, u32[]{:S(2)}) collective-permute-start(f32[256,128]{1,0:T(8,128)S(1)} %get-tuple-element.34.kept_ref), channel_id=1, source_target_pairs={{1,0},{0,2},{3,1},{2,3},{5,4},{4,6},{7,5},{6,7},{9,8},{8,10},{11,9... | collective-permute-start | bytes 393224 | tf_op jit(solution)/shard_map/ppermute | solution.py:814
  33.7 1.3 %collective-permute-start.8 = (f32[96,128]{1,0:T(8,128)S(1)}, f32[96,128]{1,0:T(8,128)S(1)}, u32[]{:S(2)}, u32[]{:S(2)}) collective-permute-start(f32[96,128]{1,0:T(8,128)S(1)} %get-tuple-element.40), channel_id=1, source_target_pairs={{0,4},{4,0},{8,12},{12,8},{16,20},{20,16},{24,28},{28,24},{1,5},{5... | collective-permute-start | bytes 147464 | tf_op jit(solution)/shard_map/ppermute | solution.py:754
  35.0 4.7 %collective-permute-start.10 = (f32[96,128]{1,0:T(8,128)S(1)}, f32[96,128]{1,0:T(8,128)S(1)}, u32[]{:S(2)}, u32[]{:S(2)}) collective-permute-start(f32[96,128]{1,0:T(8,128)S(1)} %add.7.refs_0_), channel_id=1, source_target_pairs={{0,16},{4,20},{8,24},{12,28},{16,0},{20,4},{24,8},{28,12},{1,17},{... | collective-permute-start | bytes 147464 | tf_op jit(solution)/shard_map/ppermute | solution.py:754
  35.6 5.0 %collective-permute-start.11 = (f32[96,128]{1,0:T(8,128)S(1)}, f32[96,128]{1,0:T(8,128)S(1)}, u32[]{:S(2)}, u32[]{:S(2)}) collective-permute-start(f32[96,128]{1,0:T(8,128)S(1)} %add.7.refs_0_), channel_id=1, source_target_pairs={{0,24},{4,28},{8,16},{12,20},{16,8},{20,12},{24,0},{28,4},{1,25},{... | collective-permute-start | bytes 147464 | tf_op jit(solution)/shard_map/ppermute | solution.py:754
  37.1 4.1 %collective-permute-start.9 = (f32[96,128]{1,0:T(8,128)S(1)}, f32[96,128]{1,0:T(8,128)S(1)}, u32[]{:S(2)}, u32[]{:S(2)}) collective-permute-start(f32[96,128]{1,0:T(8,128)S(1)} %add.7.refs_0_), channel_id=1, source_target_pairs={{0,8},{4,12},{8,0},{12,4},{16,24},{20,28},{24,16},{28,20},{1,9},{5... | collective-permute-start | bytes 147464 | tf_op jit(solution)/shard_map/ppermute | solution.py:754
  42.3 1.4 %collective-permute-start.12 = (f32[176,128]{1,0:T(8,128)S(1)}, f32[176,128]{1,0:T(8,128)S(1)}, u32[]{:S(2)}, u32[]{:S(2)}) collective-permute-start(f32[176,128]{1,0:T(8,128)S(1)} %shard_map.26.found_ref.refs_4_), channel_id=1, source_target_pairs={{0,4},{4,0},{8,12},{12,8},{16,20},{20,16},{24,28},{28,24},{1,5},{5... | collective-permute-start | bytes 270344 | tf_op jit(solution)/shard_map/ppermute | solution.py:754
  45.2 6.5 %collective-permute-start.13 = (f32[256,128]{1,0:T(8,128)S(1)}, f32[256,128]{1,0:T(8,128)S(1)}, u32[]{:S(2)}, u32[]{:S(2)}) collective-permute-start(f32[256,128]{1,0:T(8,128)S(1)} %get-tuple-element.43), channel_id=1, source_target_pairs={{2,0},{0,1},{3,2},{1,3},{6,4},{4,5},{7,6},{5,7},{10,8},{8,9},{11,1... | collective-permute-start | bytes 393224 | tf_op jit(solution)/shard_map/ppermute | solution.py:820
